TPU v7x, 32 devices: a whole 2x2x4 slice. The times are simulated.
32 devices in a mesh: gz: 4 (over y, x), dom: 8 (over z, core).
Axes of the slice: x: 2, y: 2, z: 4, core: 2. Of those that a mesh axis runs over, the one named last changes fastest.
Arguments:
- volume: float32 [768, 4, 384], P('gz'), may hold values from -6 to 6
- observed: bfloat16 [512, 4, 384], P(('gz', 'dom')), may hold values from -6 to 6
- ctf_table: float32 [32, 2, 384], replicated, may hold values from -1 to 1
- ctf_class: int32 [512], P(('gz', 'dom')), may hold values from 0 to 31
- bin_ids: int32 [512], P(('gz', 'dom')), may hold values from 0 to 63
Outputs:
- pose_score: float32 [512], P(('gz', 'dom'))
- backprojection: float32 [768, 4, 384], P(('gz', 'dom'))
All inputs are finite; a program needn't handle non-finite values.
Results may differ from a plain program's by a relative error of at most 0.0034.
Values may be sent and summed in bfloat16 or wider, within the bound.
No kernel may reach another device: no remote copies, remote signals or barrier semaphores. Data moves between devices by JAX's collectives and lax.ppermute only.
A program may use at most 64 MiB of HBM per device.

v0:
```python
import math

import jax
import jax.numpy as jnp
from jax import lax
from jax.sharding import PartitionSpec as P

NZ = 768
NB_DEV = 8
NCTF = 32
ITERS = 3


epsilon = 1e-05


def kernel(offset):
    inside = jnp.abs(offset) < 1.0
    falloff = 1.0 - offset * offset
    return (
        jnp.where(inside, falloff * falloff, 0.0),
        jnp.where(inside, -4.0 * offset * falloff, 0.0),
    )


def geometry(bin_index, planes, total_bins, samples, columns):
    tilt_angle = -0.5 * math.pi + math.pi * (bin_index.astype(jnp.float32) + 0.5) / total_bins
    sine_value = jnp.sin(tilt_angle)
    cosine = jnp.cos(tilt_angle)
    radius = jnp.arange(samples).astype(jnp.float32)
    centre = 0.5 * NZ + radius * sine_value
    z_value, z_slope = kernel(planes[None, :] - centre[:, None])
    z_slope = z_slope * (-radius * cosine / samples)[:, None]
    x_value, x_slope = kernel(
        jnp.arange(columns).astype(jnp.float32)[None, :] - (radius * cosine)[:, None]
    )
    x_slope = x_slope * (radius * sine_value / samples)[:, None]
    return (z_value, z_slope, jnp.concatenate([x_value, x_slope], 0))


def contrast_of(classes, ctf_table, count, stacked_rows, samples):
    class_onehot = (classes[:, None] == jnp.arange(NCTF, dtype=jnp.int32)[None, :]).astype(
        jnp.float32
    )
    contrast = jnp.dot(
        class_onehot,
        ctf_table.reshape(NCTF, -1),
        precision=lax.Precision.HIGHEST,
        preferred_element_type=jnp.float32,
    )
    contrast = contrast.reshape(count, stacked_rows // 2, samples)
    return jnp.concatenate([contrast, contrast], 1)


def local(volume, observed, ctf_table, ctf_class, bin_ids):
    depth_local = volume.shape[0]
    stacked_rows = volume.shape[1]
    columns = volume.shape[2]
    samples = observed.shape[2]
    particles = observed.shape[0]
    total_bins = NB_DEV * lax.axis_size("dom")
    first_bin = lax.axis_index("dom") * NB_DEV
    planes = (lax.axis_index("gz") * depth_local + jnp.arange(depth_local, dtype=jnp.int32)).astype(
        jnp.float32
    )
    flat_volume = volume.reshape(depth_local * stacked_rows, columns)

    def extract(offset):
        z_value, z_slope, x_weights = geometry(
            first_bin + offset, planes, total_bins, samples, columns
        )
        resampled = jnp.dot(
            flat_volume,
            x_weights.T,
            precision=lax.Precision.HIGHEST,
            preferred_element_type=jnp.float32,
        )
        resampled = resampled.reshape(depth_local, stacked_rows, 2 * samples)
        direct = resampled[:, :, :samples]
        tilted = resampled[:, :, samples:]
        leading = jnp.sum(direct * z_value.T[:, None, :], axis=0)
        second = jnp.sum(direct * z_slope.T[:, None, :] + tilted * z_value.T[:, None, :], axis=0)
        return jnp.concatenate([leading, second], 0)

    partial_slices = lax.map(extract, jnp.arange(NB_DEV, dtype=jnp.int32))
    reduced = lax.psum(partial_slices, "gz")
    gathered = lax.all_gather(reduced.astype(jnp.bfloat16), "dom", axis=0, tiled=True)
    bin_onehot = bin_ids[:, None] == jnp.arange(total_bins, dtype=jnp.int32)[None, :]
    picked = jnp.dot(
        bin_onehot.astype(jnp.bfloat16),
        gathered.reshape(total_bins, -1),
        preferred_element_type=jnp.float32,
    )
    picked = picked.reshape(particles, 2 * stacked_rows, samples)
    contrast = contrast_of(ctf_class, ctf_table, particles, stacked_rows, samples)
    measured = observed.astype(jnp.float32)
    predicted = contrast * picked[:, :stacked_rows]
    tangent = contrast * picked[:, stacked_rows:]
    curvature = jnp.sum(tangent * tangent, axis=(1, 2)) + epsilon
    shift = jnp.zeros((particles,), jnp.float32)
    for iteration in range(ITERS):
        residual_map = measured - predicted - shift[:, None, None] * tangent
        shift = shift + 0.5 * jnp.sum(residual_map * tangent, axis=(1, 2)) / curvature
    pose_score = shift * jnp.sqrt(curvature)
    onehot_float = bin_onehot.astype(jnp.float32)
    weighted = contrast * measured
    contributions = jnp.concatenate([weighted, shift[:, None, None] * weighted], 1).reshape(
        particles, -1
    )
    totals = jnp.dot(
        onehot_float.T,
        contributions,
        precision=lax.Precision.HIGHEST,
        preferred_element_type=jnp.float32,
    )
    totals = lax.psum(totals, ("gz", "dom"))
    owned = lax.dynamic_slice_in_dim(totals, first_bin, NB_DEV, 0)
    owned = owned.reshape(NB_DEV, 2 * stacked_rows, samples)

    def spread_back(offset, accumulated):
        z_value, z_slope, x_weights = geometry(
            first_bin + offset, planes, total_bins, samples, columns
        )
        summed = lax.dynamic_index_in_dim(owned, offset, 0, keepdims=False)
        direct = summed[:stacked_rows]
        tilted = summed[stacked_rows:]
        z_plain = z_value.T[:, None, :]
        z_tilted = z_slope.T[:, None, :]
        leading = z_plain * direct[None] + z_tilted * tilted[None]
        second = z_plain * tilted[None]
        stacked = jnp.concatenate([leading, second], 2).reshape(
            depth_local * stacked_rows, 2 * samples
        )
        return accumulated + jnp.dot(
            stacked, x_weights, precision=lax.Precision.HIGHEST, preferred_element_type=jnp.float32
        )

    backprojected = lax.fori_loop(
        0, NB_DEV, spread_back, jnp.zeros((depth_local * stacked_rows, columns), jnp.float32)
    )
    backprojected = backprojected.reshape(depth_local, stacked_rows, columns)
    plane_share = lax.psum_scatter(backprojected, "dom", scatter_dimension=0, tiled=True)
    return (pose_score, plane_share)


def solution(mesh):
    return jax.shard_map(
        local,
        mesh=mesh,
        in_specs=(
            P("gz", None, None),
            P(("gz", "dom"), None, None),
            P(),
            P(("gz", "dom")),
            P(("gz", "dom")),
        ),
        out_specs=(P(("gz", "dom")), P(("gz", "dom"), None, None)),
        check_vma=False,
    )
```

profile of v0, /device:TPU:4, one launch (start us, length us, event | category | flops | bytes accessed | tf_op | source)
XLA Modules:
  0.0 402.5 jit_solution(4547380727115613800)
XLA Ops:
  7.2 1.7 reshape.295
  9.0 88.1 %while.29 = (s32[]{:T(128)}, f32[8,8,384]{2,1,0:T(8,128)}, s32[8]{0:T(128)S(1)}, s32[]{:T(128)}, f32[768,384]{1,0:T(8,128)S(1)}, /*index=5*/s32[]{:T(128)}, s32[]{:T(128)}, f32[]{:T(128)}, f32[]{:T(128)}, f32[]{:T(128)}) while((s32[]{:T(128)}, f32[8,8,384]{2,1,0:T(8,128)}, s32[8]{0:T(128)S(1)}, s32[]{:T(128)}, ...), condition=%wide.region_3.4_spmd.clone, body=%wide.region_0.3_spmd.clone.sunk | while | flops 2722410496 | bytes 14210245 | solution.py:85
  9.0 0.6 dynamic_slice.26
  10.6 5.3 %convolution_bitcast_fusion.2 = f32[768,768]{1,0:T(8,128)} fusion(f32[768,384]{1,0:T(8,128)S(1)} %get-tuple-element.435, f32[384,384]{1,0:T(8,128)S(1)} %get-tuple-element.386, f32[384,384]{1,0:T(8,128)S(1)} %get-tuple-element.387), kind=kOutput, calls=%fused_computation.2.clone.1 | convolution fusion | flops 2718203904 | bytes 4718592 | tf_op jit(solution)/shard_map/while/body/eval_jaxpr/dot_general | solution.py:72
  15.9 2.6 reshape.305
  18.7 0.7 multiply_reduce_fusion.6
  19.4 0.6 fusion.91
  20.0 0.6 dynamic_slice.26
  21.6 5.3 %convolution_bitcast_fusion.2 = f32[768,768]{1,0:T(8,128)} fusion(f32[768,384]{1,0:T(8,128)S(1)} %get-tuple-element.435, f32[384,384]{1,0:T(8,128)S(1)} %get-tuple-element.386, f32[384,384]{1,0:T(8,128)S(1)} %get-tuple-element.387), kind=kOutput, calls=%fused_computation.2.clone.1 | convolution fusion | flops 2718203904 | bytes 4718592 | tf_op jit(solution)/shard_map/while/body/eval_jaxpr/dot_general | solution.py:72
  26.9 2.6 reshape.305
  29.7 0.7 multiply_reduce_fusion.6
  30.4 0.6 fusion.91
  32.6 5.3 %convolution_bitcast_fusion.2 = f32[768,768]{1,0:T(8,128)} fusion(f32[768,384]{1,0:T(8,128)S(1)} %get-tuple-element.435, f32[384,384]{1,0:T(8,128)S(1)} %get-tuple-element.386, f32[384,384]{1,0:T(8,128)S(1)} %get-tuple-element.387), kind=kOutput, calls=%fused_computation.2.clone.1 | convolution fusion | flops 2718203904 | bytes 4718592 | tf_op jit(solution)/shard_map/while/body/eval_jaxpr/dot_general | solution.py:72
  37.9 2.6 reshape.305
  40.7 0.7 multiply_reduce_fusion.6
  41.4 0.6 fusion.91
  43.6 5.3 %convolution_bitcast_fusion.2 = f32[768,768]{1,0:T(8,128)} fusion(f32[768,384]{1,0:T(8,128)S(1)} %get-tuple-element.435, f32[384,384]{1,0:T(8,128)S(1)} %get-tuple-element.386, f32[384,384]{1,0:T(8,128)S(1)} %get-tuple-element.387), kind=kOutput, calls=%fused_computation.2.clone.1 | convolution fusion | flops 2718203904 | bytes 4718592 | tf_op jit(solution)/shard_map/while/body/eval_jaxpr/dot_general | solution.py:72
  48.9 2.6 reshape.305
  51.7 0.7 multiply_reduce_fusion.6
  52.4 0.6 fusion.91
  54.6 5.3 %convolution_bitcast_fusion.2 = f32[768,768]{1,0:T(8,128)} fusion(f32[768,384]{1,0:T(8,128)S(1)} %get-tuple-element.435, f32[384,384]{1,0:T(8,128)S(1)} %get-tuple-element.386, f32[384,384]{1,0:T(8,128)S(1)} %get-tuple-element.387), kind=kOutput, calls=%fused_computation.2.clone.1 | convolution fusion | flops 2718203904 | bytes 4718592 | tf_op jit(solution)/shard_map/while/body/eval_jaxpr/dot_general | solution.py:72
  59.9 2.6 reshape.305
  62.7 0.7 multiply_reduce_fusion.6
  63.4 0.6 fusion.91
  65.6 5.3 %convolution_bitcast_fusion.2 = f32[768,768]{1,0:T(8,128)} fusion(f32[768,384]{1,0:T(8,128)S(1)} %get-tuple-element.435, f32[384,384]{1,0:T(8,128)S(1)} %get-tuple-element.386, f32[384,384]{1,0:T(8,128)S(1)} %get-tuple-element.387), kind=kOutput, calls=%fused_computation.2.clone.1 | convolution fusion | flops 2718203904 | bytes 4718592 | tf_op jit(solution)/shard_map/while/body/eval_jaxpr/dot_general | solution.py:72
  70.9 2.6 reshape.305
  73.7 0.7 multiply_reduce_fusion.6
  74.4 0.6 fusion.91
  76.7 5.3 %convolution_bitcast_fusion.2 = f32[768,768]{1,0:T(8,128)} fusion(f32[768,384]{1,0:T(8,128)S(1)} %get-tuple-element.435, f32[384,384]{1,0:T(8,128)S(1)} %get-tuple-element.386, f32[384,384]{1,0:T(8,128)S(1)} %get-tuple-element.387), kind=kOutput, calls=%fused_computation.2.clone.1 | convolution fusion | flops 2718203904 | bytes 4718592 | tf_op jit(solution)/shard_map/while/body/eval_jaxpr/dot_general | solution.py:72
  81.9 2.6 reshape.305
  84.7 0.7 multiply_reduce_fusion.6
  85.4 0.6 fusion.91
  87.7 5.3 %convolution_bitcast_fusion.2 = f32[768,768]{1,0:T(8,128)} fusion(f32[768,384]{1,0:T(8,128)S(1)} %get-tuple-element.435, f32[384,384]{1,0:T(8,128)S(1)} %get-tuple-element.386, f32[384,384]{1,0:T(8,128)S(1)} %get-tuple-element.387), kind=kOutput, calls=%fused_computation.2.clone.1 | convolution fusion | flops 2718203904 | bytes 4718592 | tf_op jit(solution)/shard_map/while/body/eval_jaxpr/dot_general | solution.py:72
  92.9 2.6 reshape.305
  95.7 0.7 multiply_reduce_fusion.6
  96.4 0.6 fusion.91
  97.0 17.3 %psum.14 = bf16[8,8,384]{2,1,0:T(8,128)(2,1)S(1)} all-reduce(f32[8,8,384]{2,1,0:T(8,128)} %get-tuple-element.211), channel_id=1, replica_groups=mesh['gz'=4,'dom'=8] {'gz'}, use_global_device_ids=true, to_apply=%region_4.5 | all-reduce | flops 24576 | bytes 147456 | tf_op jit(solution)/shard_map/psum | solution.py:86
  114.3 14.9 %all_gather.3 = bf16[64,8,384]{2,1,0:T(8,128)(2,1)S(1)} all-gather(bf16[8,8,384]{2,1,0:T(8,128)(2,1)S(1)} %psum.14), channel_id=1, replica_groups=mesh['gz'=4,'dom'=8] {'dom'}, dimensions={0}, use_global_device_ids=true | all-gather | bytes 442368 | tf_op jit(solution)/shard_map/all_gather | solution.py:87
  130.9 1.5 fusion.64
  132.7 129.0 %all-reduce.4.cloned.1.call-done = f32[64,3072]{1,0:T(8,128)} async-done(((f32[64,3072]{1,0:T(8,128)}), f32[64,3072]{1,0:T(8,128)}) %all-reduce.4.cloned.1.call-update) | async-done | bytes 786448 | tf_op jit(solution)/shard_map/psum | solution.py:116
  261.6 0.9 constant_dynamic-slice_fusion.1
  262.5 0.7 copy.47
  263.2 69.6 %while.30 = (s32[]{:T(128)}, f32[768,384]{1,0:T(8,128)}, s32[]{:T(128)}, f32[8,8,384]{2,1,0:T(8,128)}, s32[]{:T(128)}, /*index=5*/s32[]{:T(128)}, s32[]{:T(128)}, s32[]{}, f32[]{:T(128)}, f32[]{:T(128)}, /*index=10*/f32[]{:T(128)}) while((s32[]{:T(128)}, f32[768,384]{1,0:T(8,128)}, s32[]{:T(128)}, f32[8,8,384]{2,1,0:T(8,128)}, ...), condition=%wide.region_11.12_spmd.clone, body=%wide.region_10.11_spmd.clone.sunk | while | flops 2723000576 | bytes 15389407 | solution.py:138
  263.6 0.8 dynamic-slice_bitcast_fusion.3
  265.9 4.9 %fusion.97 = f32[768,384]{1,0:T(8,128)} fusion(f32[768,384]{1,0:T(8,128)S(1)} %mul.923, f32[768,384]{1,0:T(8,128)S(1)} %add.278, f32[384,384]{1,0:T(8,128)S(1)} %get-tuple-element.409, f32[384,384]{1,0:T(8,128)S(1)} %get-tuple-element.410, f32[768,384]{1,0:T(8,128)} %get-tuple-element.453, pred[]{:T(512)S(6)} %compare.3), kind=kOutput, calls=%fused_computation.44.clone.1 | convolution fusion | flops 2719383552 | bytes 5898241 | tf_op jit(solution)/shard_map/while/body/eval_jaxpr/dot_general | solution.py:134
  271.2 0.8 dynamic-slice_bitcast_fusion.3
  273.5 6.1 %fusion.97 = f32[768,384]{1,0:T(8,128)} fusion(f32[768,384]{1,0:T(8,128)S(1)} %mul.923, f32[768,384]{1,0:T(8,128)S(1)} %add.278, f32[384,384]{1,0:T(8,128)S(1)} %get-tuple-element.409, f32[384,384]{1,0:T(8,128)S(1)} %get-tuple-element.410, f32[768,384]{1,0:T(8,128)} %get-tuple-element.453, pred[]{:T(512)S(6)} %compare.3), kind=kOutput, calls=%fused_computation.44.clone.1 | convolution fusion | flops 2719383552 | bytes 5898241 | tf_op jit(solution)/shard_map/while/body/eval_jaxpr/dot_general | solution.py:134
  280.0 0.8 dynamic-slice_bitcast_fusion.3
  282.4 6.1 %fusion.97 = f32[768,384]{1,0:T(8,128)} fusion(f32[768,384]{1,0:T(8,128)S(1)} %mul.923, f32[768,384]{1,0:T(8,128)S(1)} %add.278, f32[384,384]{1,0:T(8,128)S(1)} %get-tuple-element.409, f32[384,384]{1,0:T(8,128)S(1)} %get-tuple-element.410, f32[768,384]{1,0:T(8,128)} %get-tuple-element.453, pred[]{:T(512)S(6)} %compare.3), kind=kOutput, calls=%fused_computation.44.clone.1 | convolution fusion | flops 2719383552 | bytes 5898241 | tf_op jit(solution)/shard_map/while/body/eval_jaxpr/dot_general | solution.py:134
  288.9 0.8 dynamic-slice_bitcast_fusion.3
  291.2 6.1 %fusion.97 = f32[768,384]{1,0:T(8,128)} fusion(f32[768,384]{1,0:T(8,128)S(1)} %mul.923, f32[768,384]{1,0:T(8,128)S(1)} %add.278, f32[384,384]{1,0:T(8,128)S(1)} %get-tuple-element.409, f32[384,384]{1,0:T(8,128)S(1)} %get-tuple-element.410, f32[768,384]{1,0:T(8,128)} %get-tuple-element.453, pred[]{:T(512)S(6)} %compare.3), kind=kOutput, calls=%fused_computation.44.clone.1 | convolution fusion | flops 2719383552 | bytes 5898241 | tf_op jit(solution)/shard_map/while/body/eval_jaxpr/dot_general | solution.py:134
  297.7 0.8 dynamic-slice_bitcast_fusion.3
  300.1 6.1 %fusion.97 = f32[768,384]{1,0:T(8,128)} fusion(f32[768,384]{1,0:T(8,128)S(1)} %mul.923, f32[768,384]{1,0:T(8,128)S(1)} %add.278, f32[384,384]{1,0:T(8,128)S(1)} %get-tuple-element.409, f32[384,384]{1,0:T(8,128)S(1)} %get-tuple-element.410, f32[768,384]{1,0:T(8,128)} %get-tuple-element.453, pred[]{:T(512)S(6)} %compare.3), kind=kOutput, calls=%fused_computation.44.clone.1 | convolution fusion | flops 2719383552 | bytes 5898241 | tf_op jit(solution)/shard_map/while/body/eval_jaxpr/dot_general | solution.py:134
  306.6 0.8 dynamic-slice_bitcast_fusion.3
  308.9 6.1 %fusion.97 = f32[768,384]{1,0:T(8,128)} fusion(f32[768,384]{1,0:T(8,128)S(1)} %mul.923, f32[768,384]{1,0:T(8,128)S(1)} %add.278, f32[384,384]{1,0:T(8,128)S(1)} %get-tuple-element.409, f32[384,384]{1,0:T(8,128)S(1)} %get-tuple-element.410, f32[768,384]{1,0:T(8,128)} %get-tuple-element.453, pred[]{:T(512)S(6)} %compare.3), kind=kOutput, calls=%fused_computation.44.clone.1 | convolution fusion | flops 2719383552 | bytes 5898241 | tf_op jit(solution)/shard_map/while/body/eval_jaxpr/dot_general | solution.py:134
  315.4 0.8 dynamic-slice_bitcast_fusion.3
  317.8 6.1 %fusion.97 = f32[768,384]{1,0:T(8,128)} fusion(f32[768,384]{1,0:T(8,128)S(1)} %mul.923, f32[768,384]{1,0:T(8,128)S(1)} %add.278, f32[384,384]{1,0:T(8,128)S(1)} %get-tuple-element.409, f32[384,384]{1,0:T(8,128)S(1)} %get-tuple-element.410, f32[768,384]{1,0:T(8,128)} %get-tuple-element.453, pred[]{:T(512)S(6)} %compare.3), kind=kOutput, calls=%fused_computation.44.clone.1 | convolution fusion | flops 2719383552 | bytes 5898241 | tf_op jit(solution)/shard_map/while/body/eval_jaxpr/dot_general | solution.py:134
  324.3 0.8 dynamic-slice_bitcast_fusion.3
  326.6 6.1 %fusion.97 = f32[768,384]{1,0:T(8,128)} fusion(f32[768,384]{1,0:T(8,128)S(1)} %mul.923, f32[768,384]{1,0:T(8,128)S(1)} %add.278, f32[384,384]{1,0:T(8,128)S(1)} %get-tuple-element.409, f32[384,384]{1,0:T(8,128)S(1)} %get-tuple-element.410, f32[768,384]{1,0:T(8,128)} %get-tuple-element.453, pred[]{:T(512)S(6)} %compare.3), kind=kOutput, calls=%fused_computation.44.clone.1 | convolution fusion | flops 2719383552 | bytes 5898241 | tf_op jit(solution)/shard_map/while/body/eval_jaxpr/dot_general | solution.py:134
  332.8 2.6 reshape.299
  335.4 0.6 copy-done.4
  336.0 0.6 dynamic-slice
  337.3 56.9 %all-reduce.6.cloned.1.call-done = f32[192,4,384]{2,1,0:T(4,128)} async-done(((f32[192,4,384]{2,1,0:T(4,128)}), f32[192,4,384]{2,1,0:T(4,128)}) %all-reduce.6.cloned.1.call-update) | async-done | bytes 1179664
  394.1 1.6 constant_dynamic-slice_fusion
  (153 shorter events, 23.0 us)
Async XLA Ops:
  7.2 254.5 %all-reduce.4.cloned.1.call-start = ((), (), s32[]{:S(2)}) async-start(), calls=%async_computation | async-start | bytes 1572864 | tf_op jit(solution)/shard_map/psum | solution.py:116
  8.9 120.3 %copy-start.2 = (s32[16]{0:T(128)S(1)}, s32[16]{0:T(128)}, u32[]{:S(2)}) copy-start(s32[16]{0:T(128)} %param.13) | copy-start | bytes 196
  97.0 32.4 %copy-start.1 = (f32[32,2,384]{2,1,0:T(2,128)S(1)}, f32[32,2,384]{2,1,0:T(2,128)}, u32[]{:S(2)}) copy-start(f32[32,2,384]{2,1,0:T(2,128)} %param.11) | copy-start | bytes 294916
  97.0 32.4 %copy-start.3 = (s32[16]{0:T(128)S(1)}, s32[16]{0:T(128)}, u32[]{:S(2)}) copy-start(s32[16]{0:T(128)} %param.12) | copy-start | bytes 196
  97.0 32.6 %copy-start = (bf16[16,4,384]{2,1,0:T(4,128)(2,1)S(1)}, bf16[16,4,384]{2,1,0:T(4,128)(2,1)}, u32[]{:S(2)}) copy-start(bf16[16,4,384]{2,1,0:T(4,128)(2,1)} %param.10) | copy-start | bytes 147460
  132.4 261.7 %all-reduce.6.cloned.1.call-start = ((), (), s32[]{:S(2)}) async-start(), calls=%async_computation.1 | async-start | bytes 2359296
  335.4 0.7 copy-start.4
Sparse Core Ops, SparseCore 0:
  132.5 129.0 all-reduce.3
  335.5 58.5 all-reduce.5
where the time goes:
time: 406 us; the launch traced here: 403 us
  waiting for transfers between devices  186 us (46%)
  matrix products  91.8 us (23%)
  local copies, waits for them, and re-layouts  47 us (12%)
  blocking collectives  32.2 us (8%)
  other arithmetic  22.6 us (6%)
  between operations  14.8 us (4%)
  loops' own time  8.04 us (2%)
    psum x1, waiting for transfers between devices, local(): totals = lax.psum(totals, ('gz', 'dom'))  129 us
    unnamed x3, waiting for transfers between devices  56.9 us
    dot_general x8, matrix products, spread_back(): jnp.dot(stacked, x_weights, precision=lax.Precision.HIGHEST, preferred_el...  47.7 us
    dot_general x8, matrix products, extract(): jnp.dot(flat_volume, x_weights.T, precision=lax.Precision.HIGHEST, prefer...  42.2 us
    reshape x8, local copies, waits for them, and re-layouts, extract(): resampled = resampled.reshape(depth_local, stacked_rows, 2 * samples)  20.8 us
    psum x1, blocking collectives, local(): reduced = lax.psum(partial_slices, 'gz')  17.3 us
    all_gather x1, blocking collectives, local(): lax.all_gather(reduced.astype(jnp.bfloat16), 'dom', axis=0, tiled=True)  14.9 us
  transfers between devices with their start and end apart: 2, of which 2 were waited for; matrix products, arithmetic and copies ran while one was open for 0% of the time, Pallas kernels for 0%

commit v1 on v0

v1 whole, which is shorter than its diff:
```python
import functools
import math

import jax
import jax.numpy as jnp
import numpy as np
from jax import lax
from jax.experimental import pallas as pl
from jax.experimental.pallas import tpu as pltpu
from jax.sharding import PartitionSpec as P

NZ = 768
NB_DEV = 8
NCTF = 32
ITERS = 3
EPS = 1e-05
TILE = 128
GROUP = 4
CHUNK = 512
VMEM = 56 * 2**20
f32 = jnp.float32
bf16 = jnp.bfloat16
NT = (((1,), (1,)), ((), ()))
TN = (((0,), (0,)), ((), ()))


def round_up(n, m):
    return -(-n // m) * m


def make_plan(devices, bins, samples, columns):
    planes = NZ // devices
    ut_count, xt_count = samples // TILE, columns // TILE
    theta = -0.5 * math.pi + math.pi * (np.arange(bins) + 0.5) / bins
    u = np.arange(samples)
    rows = []
    for device in range(devices):
        z0 = device * planes
        lists = [[] for _ in range(xt_count)]
        for b in range(bins):
            s, c = math.sin(theta[b]), math.cos(theta[b])
            centre = 0.5 * NZ + u * s
            near = (centre > z0 - 1.01) & (centre < z0 + planes + 0.01)
            for ut in range(ut_count):
                hit = u[ut * TILE : (ut + 1) * TILE][near[ut * TILE : (ut + 1) * TILE]]
                if hit.size == 0:
                    continue
                first = max(0, int((hit.min() * c - 1.01) // TILE))
                last = min(xt_count - 1, int((hit.max() * c + 1.01) // TILE))
                for xt in range(first, last + 1):
                    lists[xt].append(b * 4 + ut)
        idle = (bins - 1 if 2 * z0 < NZ else 0) * 4 + ut_count - 1
        tiles, codes = [], []
        for xt, entries in enumerate(lists):
            entries = entries + [idle] * (-len(entries) % GROUP)
            tiles += [xt] * (len(entries) // GROUP)
            codes += entries
        rows.append((tiles, codes))
    groups = max(len(tiles) for tiles, _ in rows)
    table = np.zeros((devices, 1 + groups * (1 + GROUP)), np.int32)
    for device, (tiles, codes) in enumerate(rows):
        table[device, 0] = len(tiles)
        table[device, 1 : 1 + len(tiles)] = tiles
        table[device, 1 + groups : 1 + groups + len(codes)] = codes
    return table, groups


def lanes_of(shape, axis):
    return lax.broadcasted_iota(jnp.int32, shape, axis).astype(f32)


def block_of(table, trig, groups, j, k):
    code = table[1 + groups + j * GROUP + k]
    b = lax.shift_right_logical(code, 2)
    ut = lax.bitwise_and(code, 3)
    return b, ut, trig[0, b], trig[1, b], (ut * TILE).astype(f32)


def bump(t):
    falloff = jnp.maximum(1.0 - t * t, 0.0)
    return falloff * falloff, -4.0 * t * falloff


def z_weights(z0, rows, u, s, c, samples):
    centre = 0.5 * NZ + u * s
    kz, kzd = bump((z0 + lanes_of((rows, TILE), 0)) - centre)
    return centre, kz, kzd * (-u * c * (1.0 / samples))


def extract_kernel(groups, planes, samples, table, trig, where, vhi, vlo, out):
    depth = vhi.shape[1] // 4
    ut_count = samples // TILE
    z0 = where[0].astype(f32)
    out[...] = jnp.zeros_like(out)

    def step(j, carry):
        xt = table[1 + j]
        hi_rows, lo_rows = vhi[xt], vlo[xt]
        xx = lanes_of((TILE, TILE), 0) + (xt * TILE).astype(f32)
        for k in range(GROUP):
            b, ut, s, c, base = block_of(table, trig, groups, j, k)
            u = lanes_of((1, TILE), 1) + base
            centre, kz, kzd = z_weights(z0, depth, u, s, c, samples)
            lower = jnp.floor(centre)
            own = jnp.where((lower >= z0) & (lower < z0 + planes), 1.0, 0.0)
            kz, kzd = kz * own, kzd * own
            kx, kxd = bump(xx - u * c)
            weights = jnp.concatenate([kx, kxd * (u * s * (1.0 / samples))], 1)
            whi = weights.astype(bf16)
            wlo = (weights - whi.astype(f32)).astype(bf16)
            sampled = (
                jnp.dot(hi_rows, whi, preferred_element_type=f32)
                + jnp.dot(lo_rows, whi, preferred_element_type=f32)
                + jnp.dot(hi_rows, wlo, preferred_element_type=f32)
            )
            leading, second = [], []
            for r in range(4):
                direct = sampled[r * depth : (r + 1) * depth, :TILE]
                tilted = sampled[r * depth : (r + 1) * depth, TILE:]
                leading.append(jnp.sum(direct * kz, axis=0, keepdims=True))
                second.append(jnp.sum(direct * kzd + tilted * kz, axis=0, keepdims=True))
            at = b * ut_count + ut
            out[at] = out[at] + jnp.concatenate(leading + second, 0)
        return carry

    lax.fori_loop(0, table[0], step, 0)


def particle_kernel(width, packed, ctf_hi, ctf_lo, slope, pairs, weighted, parts, bins_row, plain):
    count = packed.shape[0]
    bins = slope.shape[0]
    ids = packed[:, width:]
    classes = ids[:, 0:1].astype(f32)
    onehot_class = jnp.where(lanes_of((count, NCTF), 1) == classes, 1.0, 0.0)
    onehot_bin = jnp.where(lanes_of((count, bins), 1) == ids[:, 1:2].astype(f32), 1.0, 0.0)
    half = onehot_class.astype(bf16)
    contrast = jnp.dot(half, ctf_hi[...], preferred_element_type=f32) + jnp.dot(
        half, ctf_lo[...], preferred_element_type=f32
    )
    contrast = jnp.concatenate([contrast, contrast], 1)
    w = contrast * packed[:, :width].astype(f32)
    whi = w.astype(bf16)
    wlo = (w - whi.astype(f32)).astype(bf16)
    weighted[...] = whi
    slopes = slope[...]
    along = lax.dot_general(whi, slopes, NT, preferred_element_type=f32) + lax.dot_general(
        wlo, slopes, NT, preferred_element_type=f32
    )
    tables = jnp.dot(
        onehot_class, pairs[...], precision=lax.Precision.HIGHEST, preferred_element_type=f32
    )
    square = tables[:, :bins] * onehot_bin
    pull = (along - tables[:, bins:]) * onehot_bin
    ones = jnp.ones((8, bins), f32)
    rows = [
        lax.dot_general(
            ones, m, NT, precision=lax.Precision.HIGHEST, preferred_element_type=f32
        )[0:1]
        for m in (square, pull)
    ]
    parts[...] = jnp.concatenate(rows, 0)
    pick = jnp.where(lanes_of((8, TILE), 1) == 1.0, 1.0, 0.0).astype(bf16)
    bins_row[...] = lax.dot_general(pick, ids, NT, preferred_element_type=f32)[0:1]
    sums = lax.dot_general(onehot_bin.astype(bf16), whi, TN, preferred_element_type=f32)

    @pl.when(pl.program_id(0) == 0)
    def _():
        plain[...] = sums

    @pl.when(pl.program_id(0) > 0)
    def _():
        plain[...] = plain[...] + sums


def spread_kernel(
    groups, planes, samples, table, trig, where, parts, bins_row, weighted, plain, pose, out, sums, total
):
    bins, width = plain.shape
    tiles = width // TILE
    ut_count = samples // TILE
    depth = total.shape[1] // 4
    count = parts.shape[1]
    chunk = min(CHUNK, count)
    z0 = where[0].astype(f32)

    square, pull = parts[0:1, :], parts[1:2, :]
    curvature = square + EPS
    shift = jnp.zeros_like(square)
    for _ in range(ITERS):
        shift = shift + 0.5 * (pull - shift * square) / curvature
    pose[...] = shift * jnp.sqrt(curvature)

    slope_sum = jnp.zeros((bins, width), f32)
    for i in range(count // chunk):
        span = slice(i * chunk, (i + 1) * chunk)
        belongs = lanes_of((bins, chunk), 0) == bins_row[:, span]
        scaled = jnp.where(belongs, shift[:, span], 0.0)
        hi = scaled.astype(bf16)
        lo = (scaled - hi.astype(f32)).astype(bf16)
        rows = weighted[span, :]
        slope_sum = (
            slope_sum
            + jnp.dot(hi, rows, preferred_element_type=f32)
            + jnp.dot(lo, rows, preferred_element_type=f32)
        )
    for q in range(tiles):
        sums[q] = plain[:, q * TILE : (q + 1) * TILE]
        sums[tiles + q] = slope_sum[:, q * TILE : (q + 1) * TILE]
    total[...] = jnp.zeros_like(total)

    def step(j, carry):
        xt = table[1 + j]
        xx = lanes_of((TILE, TILE), 1) + (xt * TILE).astype(f32)
        left, right = [], []
        for k in range(GROUP):
            b, ut, s, c, base = block_of(table, trig, groups, j, k)
            u = lanes_of((1, TILE), 1) + base
            _, kz, kzd = z_weights(z0, depth, u, s, c, samples)
            first, second = [], []
            for r in range(4):
                direct = sums[r * ut_count + ut, pl.ds(b, 1), :]
                tilted = sums[tiles + r * ut_count + ut, pl.ds(b, 1), :]
                first.append(kz * direct + kzd * tilted)
                second.append(kz * tilted)
            left += [jnp.concatenate(first, 0).astype(bf16), jnp.concatenate(second, 0).astype(bf16)]
            uu = lanes_of((TILE, TILE), 0) + base
            kx, kxd = bump(xx - uu * c)
            right += [kx.astype(bf16), (kxd * (uu * (s * (1.0 / samples)))).astype(bf16)]
        total[xt] = total[xt] + jnp.dot(
            jnp.concatenate(left, 1), jnp.concatenate(right, 0), preferred_element_type=f32
        )
        return carry

    lax.fori_loop(0, table[0], step, 0)
    for xt in range(total.shape[0]):
        for r in range(4):
            out[:, r, xt * TILE : (xt + 1) * TILE] = total[xt, r * depth : r * depth + planes, :]


def local(volume, observed, ctf_table, ctf_class, bin_ids):
    slab, rows, columns = volume.shape
    mine, _, samples = observed.shape
    n_gz, n_dom = lax.axis_size("gz"), lax.axis_size("dom")
    devices = n_gz * n_dom
    bins = NB_DEV * n_dom
    planes = NZ // devices
    count = mine * devices
    width = rows * samples
    xt_count, ut_count = columns // TILE, samples // TILE
    gz, dom = lax.axis_index("gz"), lax.axis_index("dom")
    device = gz * n_dom + dom

    ids = jnp.stack([ctf_class, bin_ids], 1).astype(bf16)
    ids = jnp.pad(ids, ((0, 0), (0, TILE - 2)))
    packed = jnp.concatenate([observed.reshape(mine, width), ids], 1)
    packed = lax.all_gather(packed, ("gz", "dom"), axis=0, tiled=True)

    table, groups = make_plan(devices, bins, samples, columns)
    table = lax.dynamic_index_in_dim(jnp.asarray(table), device, 0, keepdims=False)
    where = (device * planes)[None].astype(jnp.int32)
    theta = -0.5 * math.pi + math.pi * (jnp.arange(bins, dtype=f32) + 0.5) / bins
    trig = jnp.stack([jnp.sin(theta), jnp.cos(theta)])

    above = lax.ppermute(volume[:1], "gz", [(i, i - 1) for i in range(1, n_gz)])
    own = lax.dynamic_slice_in_dim(volume, dom * planes, planes, 0)
    inner = lax.dynamic_slice_in_dim(volume, jnp.minimum((dom + 1) * planes, slab - 1), 1, 0)
    halo = jnp.where(dom == n_dom - 1, above, inner)
    depth_in = round_up(planes + 1, 8)
    field = jnp.concatenate([own, halo, jnp.zeros((depth_in - planes - 1, rows, columns), f32)], 0)
    field = field.reshape(depth_in, rows, xt_count, TILE).transpose(2, 1, 0, 3)
    field = field.reshape(xt_count, rows * depth_in, TILE)
    field_hi = lax.reduce_precision(field, 8, 7)
    field_lo = (field - field_hi).astype(bf16)
    field_hi = field_hi.astype(bf16)

    smem = pl.BlockSpec(memory_space=pltpu.SMEM)
    vmem = pl.BlockSpec(memory_space=pltpu.VMEM)
    params = pltpu.CompilerParams(vmem_limit_bytes=VMEM)
    slices = pl.pallas_call(
        functools.partial(extract_kernel, groups, planes, samples),
        out_shape=jax.ShapeDtypeStruct((bins * ut_count, 2 * rows, TILE), f32),
        in_specs=[smem, smem, smem, vmem, vmem],
        out_specs=vmem,
        compiler_params=params,
        name="extract",
    )(table, trig, where, field_hi, field_lo)

    slices = lax.reduce_precision(slices, 8, 7)
    slices = slices.reshape(bins, ut_count, 2 * rows, TILE).transpose(0, 2, 1, 3)
    slices = slices.reshape(bins, 2, 2, rows // 2, samples)
    direct, slope = slices[:, 0], slices[:, 1]
    squares = jnp.stack([jnp.sum(slope * slope, 1), jnp.sum(direct * slope, 1)])
    pairs = lax.dot_general(
        (ctf_table * ctf_table).reshape(NCTF, -1),
        squares.reshape(2 * bins, -1),
        NT,
        precision=lax.Precision.HIGHEST,
        preferred_element_type=f32,
    )
    slope = slope.reshape(bins, width).astype(bf16)
    flat_ctf = ctf_table.reshape(NCTF, -1)
    ctf_hi = lax.reduce_precision(flat_ctf, 8, 7)
    ctf_lo = (flat_ctf - ctf_hi).astype(bf16)
    ctf_hi = ctf_hi.astype(bf16)

    chunk = min(CHUNK, count)
    whole = lambda shape: pl.BlockSpec(shape, lambda i: (0,) * len(shape))
    weighted, parts, bins_row, plain = pl.pallas_call(
        functools.partial(particle_kernel, width),
        grid=(count // chunk,),
        out_shape=[
            jax.ShapeDtypeStruct((count, width), bf16),
            jax.ShapeDtypeStruct((2, count), f32),
            jax.ShapeDtypeStruct((1, count), f32),
            jax.ShapeDtypeStruct((bins, width), f32),
        ],
        in_specs=[
            pl.BlockSpec((chunk, width + TILE), lambda i: (i, 0)),
            whole(ctf_hi.shape),
            whole(ctf_lo.shape),
            whole(slope.shape),
            whole(pairs.shape),
        ],
        out_specs=[
            pl.BlockSpec((chunk, width), lambda i: (i, 0)),
            pl.BlockSpec((2, chunk), lambda i: (0, i)),
            pl.BlockSpec((1, chunk), lambda i: (0, i)),
            whole((bins, width)),
        ],
        compiler_params=params,
        name="particles",
    )(packed, ctf_hi, ctf_lo, slope, pairs)

    parts = lax.psum(parts, ("gz", "dom"))

    depth = round_up(planes, 8)
    pose, spread = pl.pallas_call(
        functools.partial(spread_kernel, groups, planes, samples),
        out_shape=[
            jax.ShapeDtypeStruct((1, count), f32),
            jax.ShapeDtypeStruct((planes, rows, columns), f32),
        ],
        in_specs=[smem, smem, smem, vmem, vmem, vmem, vmem],
        out_specs=[vmem, vmem],
        scratch_shapes=[
            pltpu.VMEM((2 * width // TILE, bins, TILE), f32),
            pltpu.VMEM((xt_count, rows * depth, TILE), f32),
        ],
        compiler_params=params,
        name="spread",
    )(table, trig, where, parts, bins_row, weighted, plain)
    pose = lax.dynamic_slice_in_dim(pose.reshape(count), device * mine, mine, 0)
    return pose, spread


def solution(mesh):
    return jax.shard_map(
        local,
        mesh=mesh,
        in_specs=(
            P("gz", None, None),
            P(("gz", "dom"), None, None),
            P(),
            P(("gz", "dom")),
            P(("gz", "dom")),
        ),
        out_specs=(P(("gz", "dom")), P(("gz", "dom"), None, None)),
        check_vma=False,
    )
```

time: 406 us -> 131 us (0.32)
  waiting for transfers between devices: 186 us -> 32.2 us
  matrix products: 91.8 us -> 1.1 us
  local copies, waits for them, and re-layouts: 47 us -> 8.09 us
  Pallas kernels: 0 us -> 24.4 us
  other arithmetic: 22.6 us -> 6.41 us
  loops' own time: 8.04 us -> 0 us
  blocking collectives: 32.2 us -> 40.2 us
    psum x1 -> x0, waiting for transfers between devices: 129 us -> none  [local(): totals = lax.psum(totals, ('gz', 'dom'))]
    dot_general x19 -> x1, matrix products: 91.8 us -> 1.1 us  [local(): lax.dot_general((ctf_table * ctf_table).reshape(NCTF, -1), squares.reshap...]
    unnamed x3 -> x1, waiting for transfers between devices: 56.9 us -> 0.02 us
    all_gather x0 -> x1, waiting for transfers between devices: none -> 32.2 us  [local(): packed = lax.all_gather(packed, ('gz', 'dom'), axis=0, tiled=True)]
    pallas_call x0 -> x3, Pallas kernels: none -> 24.4 us  [the longest x1 10.2 us: local(): pl.pallas_call(functools.partial(extract_kernel, groups, planes, samples)...]
    reshape x11 -> x3, local copies, waits for them, and re-layouts: 25.1 us -> 0.77 us  [the longest x1 0.42 us: local(): slices = slices.reshape(bins, 2, 2, rows // 2, samples)]
    psum x1, blocking collectives: 17.3 us -> 40.2 us  [local(): parts = lax.psum(parts, ('gz', 'dom'))]
    all_gather x1 -> x0, blocking collectives: 14.9 us -> none  [local(): lax.all_gather(reduced.astype(jnp.bfloat16), 'dom', axis=0, tiled=True)]
  transfers between devices with their start and end apart: 2 -> 2, of which waited for: 2 -> 1; matrix products, arithmetic and copies ran while one was open for 0% -> 9% of each run, Pallas kernels for 0% -> 8%
where the time goes in v1:
time: 131 us; the launch traced here: 130 us
  blocking collectives  40.2 us (31%)
  waiting for transfers between devices  32.2 us (25%)
  Pallas kernels  24.4 us (19%)
  between operations  14.2 us (11%)
  local copies, waits for them, and re-layouts  8.09 us (6%)
  other arithmetic  6.41 us (5%)
  starting transfers between devices  3.37 us (3%)
    psum x1, blocking collectives, local(): parts = lax.psum(parts, ('gz', 'dom'))  40.2 us
    all_gather x1, waiting for transfers between devices, local(): packed = lax.all_gather(packed, ('gz', 'dom'), axis=0, tiled=True)  32.2 us
    pallas_call x1, Pallas kernels, local(): pl.pallas_call(functools.partial(extract_kernel, groups, planes, samples)...  10.2 us
    pallas_call x1, Pallas kernels, local(): pl.pallas_call(functools.partial(spread_kernel, groups, planes, samples),...  8.78 us
    pallas_call x1, Pallas kernels, local(): pl.pallas_call(functools.partial(particle_kernel, width), grid=(count //...  5.44 us
    ppermute x1, starting transfers between devices, local(): above = lax.ppermute(volume[:1], 'gz', [(i, i - 1) for i in range(1, n_gz)])  3.33 us
  transfers between devices with their start and end apart: 2, of which 1 were waited for; matrix products, arithmetic and copies ran while one was open for 9% of the time, Pallas kernels for 8%

profile of v1, /device:TPU:4, one launch (start us, length us, event | category | flops | bytes accessed | tf_op | source)
XLA Modules:
  0.0 130.0 jit_solution(2794057698635501191)
XLA Ops:
  7.2 0.0 all-gather.2.cloned.1.call-start
  7.2 0.7 convert_bitcast_fusion
  7.9 0.1 copy.22
  8.0 0.8 copy.28
  8.8 0.6 fusion.4
  9.4 0.0 all-gather.2.cloned.1.call-update
  9.5 0.7 slice.9
  10.2 3.3 %collective-permute-start = (f32[1,4,384]{2,1,0:T(4,128)S(1)}, f32[1,4,384]{2,1,0:T(4,128)S(1)}, u32[]{:S(2)}, u32[]{:S(2)}) collective-permute-start(f32[1,4,384]{2,1,0:T(4,128)S(1)} %slice.9), channel_id=1, source_target_pairs={{8,0},{16,8},{24,16},{9,1},{17,9},{25,17},{10,2},{18,10},{26,18},{... | collective-permute-start | bytes 18440 | tf_op jit(solution)/shard_map/ppermute | solution.py:264
  13.5 0.9 copy.29
  14.4 0.6 pad_maximum_fusion.1.trig
  15.0 0.9 constant_dynamic-slice_fusion.1
  16.0 0.7 fusion.3
  16.6 1.2 fusion.5.table
  17.8 1.0 mul.34
  18.9 0.1 pad.9.clone
  19.0 0.0 collective-permute-done
  19.0 0.7 dynamic-slice_select_fusion
  19.7 0.1 maximum_maximum_fusion
  19.8 0.1 reshape.55
  19.9 0.7 fusion.1
  20.6 10.2 %extract.1 = f32[192,8,128]{2,1,0:T(8,128)} custom-call(s32[101]{0:T(128)} %fusion.5.table, f32[2,64]{1,0:T(2,128)} %pad_maximum_fusion.1.trig, s32[1]{0:T(128)} %bitcast.1.where, bf16[3,128,128]{2,1,0:T(8,128)(2,1)} %get-tuple-element.17.vhi, bf16[3,128,128]{2,1,0:T(8,128)(2,1)} %get-tuple-element.16.vlo), custom_call_target="tpu_custom_call" | custom-call | tf_op jit(solution)/shard_map/extract/pallas_call | solution.py:279
  30.8 1.2 reduce_precision.11
  32.0 0.3 copy.33
  32.3 0.4 reshape.58
  32.8 0.1 multiply_reduce_fusion
  32.9 0.3 copy.27
  33.2 0.2 copy.26
  33.4 0.8 convert_element_type.25.slope
  34.2 1.1 fusion.9.pairs
  35.3 32.2 %all-gather.2.cloned.1.call-done.packed = bf16[512,1664]{1,0:T(8,128)(2,1)} async-done(((bf16[16,1664]{1,0:T(8,128)(2,1)}), bf16[512,1664]{1,0:T(8,128)(2,1)}) %all-gather.2.cloned.1.call-update) | async-done | bytes 1703952 | tf_op jit(solution)/shard_map/all_gather | solution.py:256
  67.5 5.4 %particles.1 = (bf16[512,1536]{1,0:T(8,128)(2,1)}, f32[2,512]{1,0:T(2,128)}, f32[1,512]{1,0:T(1,128)}, f32[64,1536]{1,0:T(8,128)}) custom-call(bf16[512,1664]{1,0:T(8,128)(2,1)} %all-gather.2.cloned.1.call-done.packed, bf16[32,768]{1,0:T(8,128)(2,1)} %get-tuple-element.19.ctf_hi, bf16[32,768]{1,0:T(8,128)(2,1)} %get-tuple-element.18.ctf_lo, ...), custom_call_target="tpu_custom_call" | custom-call | tf_op jit(solution)/shard_map/particles/pallas_call | solution.py:308
  73.0 40.2 %psum.7.parts = f32[2,512]{1,0:T(2,128)} all-reduce(f32[2,512]{1,0:T(2,128)} %get-tuple-element.8), channel_id=1, replica_groups=mesh['gz'=4,'dom'=8] {'gz','dom'}, use_global_device_ids=true, to_apply=%region_2.3 | all-reduce | flops 1024 | bytes 8192 | tf_op jit(solution)/shard_map/psum | solution.py:334
  113.2 8.8 %spread.1 = (f32[1,512]{1,0:T(1,128)}, f32[24,4,384]{2,1,0:T(4,128)}) custom-call(s32[101]{0:T(128)} %fusion.5.table, f32[2,64]{1,0:T(2,128)} %pad_maximum_fusion.1.trig, s32[1]{0:T(128)} %bitcast.1.where, f32[2,512]{1,0:T(2,128)} %psum.7.parts, f32[1,512]{1,0:T(1,128)} %get-tuple-element.9.bins_row, bf16[512,1536]{1,0:T(8,128)(2,1)} %get-tuple-element.10.weighted, ...), custom_call_target="tpu_custom_call" | custom-call | tf_op jit(solution)/shard_map/spread/pallas_call | solution.py:337
  122.0 1.2 fusion.6
  (9 shorter events, 0.2 us)
Async XLA Ops:
  7.2 60.4 %all-gather.2.cloned.1.call-start = ((), (), s32[]{:S(2)}) async-start(), calls=%async_computation | async-start | bytes 1757184 | tf_op jit(solution)/shard_map/all_gather | solution.py:256
  10.2 8.8 %collective-permute-start = (f32[1,4,384]{2,1,0:T(4,128)S(1)}, f32[1,4,384]{2,1,0:T(4,128)S(1)}, u32[]{:S(2)}, u32[]{:S(2)}) collective-permute-start(f32[1,4,384]{2,1,0:T(4,128)S(1)} %slice.9), channel_id=1, source_target_pairs={{8,0},{16,8},{24,16},{9,1},{17,9},{25,17},{10,2},{18,10},{26,18},{... | collective-permute-start | bytes 18440 | tf_op jit(solution)/shard_map/ppermute | solution.py:264
Sparse Core Ops, SparseCore 0:
  10.8 56.6 all-gather.1

commit v2 on v1

--- a/solution.py
+++ b/solution.py
@@ -126,50 +126,74 @@
     lax.fori_loop(0, table[0], step, 0)
 
 
-def particle_kernel(width, packed, ctf_hi, ctf_lo, slope, pairs, weighted, parts, bins_row, plain):
-    count = packed.shape[0]
+def particle_kernel(width, mine, n_gz, n_dom, place, *refs):
+    blocks = refs[: 2 * n_gz]
+    ctf_hi, ctf_lo, slope, pairs, weighted, parts, bins_row, plain, packed, sems = refs[2 * n_gz :]
+    n_z = n_dom // 2
+    gz, z, core = place[0], place[1], place[2]
+    copies = []
+    for c in range(2):
+        for j in range(n_gz):
+            for k in range(n_z):
+                owner = ((gz ^ j) * n_z + (z ^ k)) * 2 + (core ^ c)
+                start = pl.multiple_of(owner * mine, mine)
+                copies.append(
+                    pltpu.make_async_copy(
+                        blocks[c * n_gz + j].at[pl.ds(k * mine, mine), :],
+                        packed.at[pl.ds(start, mine), :],
+                        sems.at[len(copies)],
+                    )
+                )
+    for copy in copies:
+        copy.start()
+    for copy in copies:
+        copy.wait()
+
+    total = packed.shape[0]
+    count = min(CHUNK, total)
     bins = slope.shape[0]
-    ids = packed[:, width:]
-    classes = ids[:, 0:1].astype(f32)
-    onehot_class = jnp.where(lanes_of((count, NCTF), 1) == classes, 1.0, 0.0)
-    onehot_bin = jnp.where(lanes_of((count, bins), 1) == ids[:, 1:2].astype(f32), 1.0, 0.0)
-    half = onehot_class.astype(bf16)
-    contrast = jnp.dot(half, ctf_hi[...], preferred_element_type=f32) + jnp.dot(
-        half, ctf_lo[...], preferred_element_type=f32
-    )
-    contrast = jnp.concatenate([contrast, contrast], 1)
-    w = contrast * packed[:, :width].astype(f32)
-    whi = w.astype(bf16)
-    wlo = (w - whi.astype(f32)).astype(bf16)
-    weighted[...] = whi
-    slopes = slope[...]
-    along = lax.dot_general(whi, slopes, NT, preferred_element_type=f32) + lax.dot_general(
-        wlo, slopes, NT, preferred_element_type=f32
-    )
-    tables = jnp.dot(
-        onehot_class, pairs[...], precision=lax.Precision.HIGHEST, preferred_element_type=f32
-    )
-    square = tables[:, :bins] * onehot_bin
-    pull = (along - tables[:, bins:]) * onehot_bin
-    ones = jnp.ones((8, bins), f32)
-    rows = [
-        lax.dot_general(
-            ones, m, NT, precision=lax.Precision.HIGHEST, preferred_element_type=f32
-        )[0:1]
-        for m in (square, pull)
-    ]
-    parts[...] = jnp.concatenate(rows, 0)
-    pick = jnp.where(lanes_of((8, TILE), 1) == 1.0, 1.0, 0.0).astype(bf16)
-    bins_row[...] = lax.dot_general(pick, ids, NT, preferred_element_type=f32)[0:1]
-    sums = lax.dot_general(onehot_bin.astype(bf16), whi, TN, preferred_element_type=f32)
-
-    @pl.when(pl.program_id(0) == 0)
-    def _():
-        plain[...] = sums
-
-    @pl.when(pl.program_id(0) > 0)
-    def _():
-        plain[...] = plain[...] + sums
+    plain[...] = jnp.zeros_like(plain)
+
+    def step(i, carry):
+        span = pl.ds(pl.multiple_of(i * count, count), count)
+        ids = packed[span, width:]
+        classes = ids[:, 0:1].astype(f32)
+        onehot_class = jnp.where(lanes_of((count, NCTF), 1) == classes, 1.0, 0.0)
+        onehot_bin = jnp.where(lanes_of((count, bins), 1) == ids[:, 1:2].astype(f32), 1.0, 0.0)
+        half = onehot_class.astype(bf16)
+        contrast = jnp.dot(half, ctf_hi[...], preferred_element_type=f32) + jnp.dot(
+            half, ctf_lo[...], preferred_element_type=f32
+        )
+        contrast = jnp.concatenate([contrast, contrast], 1)
+        w = contrast * packed[span, :width].astype(f32)
+        whi = w.astype(bf16)
+        wlo = (w - whi.astype(f32)).astype(bf16)
+        weighted[span, :] = whi
+        slopes = slope[...]
+        along = lax.dot_general(whi, slopes, NT, preferred_element_type=f32) + lax.dot_general(
+            wlo, slopes, NT, preferred_element_type=f32
+        )
+        tables = jnp.dot(
+            onehot_class, pairs[...], precision=lax.Precision.HIGHEST, preferred_element_type=f32
+        )
+        square = tables[:, :bins] * onehot_bin
+        pull = (along - tables[:, bins:]) * onehot_bin
+        ones = jnp.ones((8, bins), f32)
+        for n, m in enumerate((square, pull)):
+            row = lax.dot_general(
+                ones, m, NT, precision=lax.Precision.HIGHEST, preferred_element_type=f32
+            )[0:1]
+            for q in range(count // TILE):
+                at = n * (total // TILE) + i * (count // TILE) + q
+                parts[pl.ds(at, 1), :] = row[:, q * TILE : (q + 1) * TILE]
+        pick = jnp.where(lanes_of((8, TILE), 1) == 1.0, 1.0, 0.0).astype(bf16)
+        bins_row[:, span] = lax.dot_general(pick, ids, NT, preferred_element_type=f32)[0:1]
+        plain[...] = plain[...] + lax.dot_general(
+            onehot_bin.astype(bf16), whi, TN, preferred_element_type=f32
+        )
+        return carry
+
+    lax.fori_loop(0, total // count, step, 0)
 
 
 def spread_kernel(
@@ -179,11 +203,14 @@
     tiles = width // TILE
     ut_count = samples // TILE
     depth = total.shape[1] // 4
-    count = parts.shape[1]
+    count = bins_row.shape[1]
     chunk = min(CHUNK, count)
     z0 = where[0].astype(f32)
 
-    square, pull = parts[0:1, :], parts[1:2, :]
+    rows = 2 * count // TILE
+    scalars = jnp.sum(parts[...].reshape(parts.shape[0] // rows, rows, TILE), axis=0)
+    square = jnp.concatenate([scalars[q : q + 1] for q in range(rows // 2)], 1)
+    pull = jnp.concatenate([scalars[q : q + 1] for q in range(rows // 2, rows)], 1)
     curvature = square + EPS
     shift = jnp.zeros_like(square)
     for _ in range(ITERS):
@@ -222,19 +249,27 @@
                 tilted = sums[tiles + r * ut_count + ut, pl.ds(b, 1), :]
                 first.append(kz * direct + kzd * tilted)
                 second.append(kz * tilted)
-            left += [jnp.concatenate(first, 0).astype(bf16), jnp.concatenate(second, 0).astype(bf16)]
+            left += [jnp.concatenate(first, 0), jnp.concatenate(second, 0)]
             uu = lanes_of((TILE, TILE), 0) + base
             kx, kxd = bump(xx - uu * c)
             right += [kx.astype(bf16), (kxd * (uu * (s * (1.0 / samples)))).astype(bf16)]
-        total[xt] = total[xt] + jnp.dot(
-            jnp.concatenate(left, 1), jnp.concatenate(right, 0), preferred_element_type=f32
-        )
+        left = jnp.concatenate(left, 1)
+        hi = left.astype(bf16)
+        lo = (left - hi.astype(f32)).astype(bf16)
+        both = jnp.dot(
+            jnp.concatenate([hi, lo], 0), jnp.concatenate(right, 0), preferred_element_type=f32
+        )
+        total[xt] = total[xt] + both[: 4 * depth] + both[4 * depth :]
         return carry
 
     lax.fori_loop(0, table[0], step, 0)
     for xt in range(total.shape[0]):
         for r in range(4):
             out[:, r, xt * TILE : (xt + 1) * TILE] = total[xt, r * depth : r * depth + planes, :]
+
+
+def swap(x, axis, size, distance):
+    return lax.ppermute(x, axis, [(i, i ^ distance) for i in range(size)])
 
 
 def local(volume, observed, ctf_table, ctf_class, bin_ids):
@@ -253,7 +288,13 @@
     ids = jnp.stack([ctf_class, bin_ids], 1).astype(bf16)
     ids = jnp.pad(ids, ((0, 0), (0, TILE - 2)))
     packed = jnp.concatenate([observed.reshape(mine, width), ids], 1)
-    packed = lax.all_gather(packed, ("gz", "dom"), axis=0, tiled=True)
+    n_z = n_dom // 2
+    column = jnp.concatenate(
+        [packed] + [swap(packed, "dom", n_dom, 2 * k) for k in range(1, n_z)], 0
+    )
+    planes_of = [column] + [swap(column, "gz", n_gz, j) for j in range(1, n_gz)]
+    gathered = planes_of + [swap(part, "dom", n_dom, 1) for part in planes_of]
+    place = jnp.stack([gz, dom // 2, dom % 2]).astype(jnp.int32)
 
     table, groups = make_plan(devices, bins, samples, columns)
     table = lax.dynamic_index_in_dim(jnp.asarray(table), device, 0, keepdims=False)
@@ -303,35 +344,26 @@
     ctf_lo = (flat_ctf - ctf_hi).astype(bf16)
     ctf_hi = ctf_hi.astype(bf16)
 
-    chunk = min(CHUNK, count)
-    whole = lambda shape: pl.BlockSpec(shape, lambda i: (0,) * len(shape))
+    hbm = pl.BlockSpec(memory_space=pl.ANY)
     weighted, parts, bins_row, plain = pl.pallas_call(
-        functools.partial(particle_kernel, width),
-        grid=(count // chunk,),
+        functools.partial(particle_kernel, width, mine, n_gz, n_dom),
         out_shape=[
             jax.ShapeDtypeStruct((count, width), bf16),
-            jax.ShapeDtypeStruct((2, count), f32),
+            jax.ShapeDtypeStruct((2 * count // TILE, TILE), f32),
             jax.ShapeDtypeStruct((1, count), f32),
             jax.ShapeDtypeStruct((bins, width), f32),
         ],
-        in_specs=[
-            pl.BlockSpec((chunk, width + TILE), lambda i: (i, 0)),
-            whole(ctf_hi.shape),
-            whole(ctf_lo.shape),
-            whole(slope.shape),
-            whole(pairs.shape),
-        ],
-        out_specs=[
-            pl.BlockSpec((chunk, width), lambda i: (i, 0)),
-            pl.BlockSpec((2, chunk), lambda i: (0, i)),
-            pl.BlockSpec((1, chunk), lambda i: (0, i)),
-            whole((bins, width)),
+        in_specs=[smem] + [hbm] * len(gathered) + [vmem] * 4,
+        out_specs=[vmem] * 4,
+        scratch_shapes=[
+            pltpu.VMEM((count, width + TILE), bf16),
+            pltpu.SemaphoreType.DMA((devices,)),
         ],
         compiler_params=params,
         name="particles",
-    )(packed, ctf_hi, ctf_lo, slope, pairs)
-
-    parts = lax.psum(parts, ("gz", "dom"))
+    )(place, *gathered, ctf_hi, ctf_lo, slope, pairs)
+
+    parts = lax.all_gather(parts, ("gz", "dom"), axis=0, tiled=True)
 
     depth = round_up(planes, 8)
     pose, spread = pl.pallas_call(

time: 131 us -> 105 us (0.80)
  waiting for transfers between devices: 32.2 us -> 3.36 us
  between operations: 14.2 us -> 0.94 us
  starting transfers between devices: 3.37 us -> 11.8 us
  blocking collectives: 40.2 us -> 44.8 us
  Pallas kernels: 24.4 us -> 26.6 us
    all_gather x0 -> x1, blocking collectives: none -> 44.8 us  [local(): parts = lax.all_gather(parts, ('gz', 'dom'), axis=0, tiled=True)]
    psum x1 -> x0, blocking collectives: 40.2 us -> none  [local(): parts = lax.psum(parts, ('gz', 'dom'))]
    all_gather x1 -> x0, waiting for transfers between devices: 32.2 us -> none  [local(): packed = lax.all_gather(packed, ('gz', 'dom'), axis=0, tiled=True)]
    ppermute x0 -> x10, starting transfers between devices: none -> 8.5 us  [swap(): return lax.ppermute(x, axis, [(i, i ^ distance) for i in range(size)])]
    ppermute x0 -> x10, waiting for transfers between devices: none -> 3.36 us  [swap(): return lax.ppermute(x, axis, [(i, i ^ distance) for i in range(size)])]
  transfers between devices with their start and end apart: 2 -> 11, of which waited for: 1 -> 3; matrix products, arithmetic and copies ran while one was open for 9% -> 12% of each run, Pallas kernels for 8% -> 10%
where the time goes in v2:
time: 105 us; the launch traced here: 104 us
  blocking collectives  44.8 us (43%)
  Pallas kernels  26.6 us (25%)
  starting transfers between devices  11.8 us (11%)
  local copies, waits for them, and re-layouts  8.92 us (8%)
  other arithmetic  6.42 us (6%)
  waiting for transfers between devices  3.36 us (3%)
  matrix products  1.1 us (1%)
    all_gather x1, blocking collectives, local(): parts = lax.all_gather(parts, ('gz', 'dom'), axis=0, tiled=True)  44.8 us
    pallas_call x1, Pallas kernels, local(): pl.pallas_call(functools.partial(extract_kernel, groups, planes, samples)...  10.2 us
    pallas_call x1, Pallas kernels, local(): pl.pallas_call(functools.partial(spread_kernel, groups, planes, samples),...  9.83 us
    ppermute x10, starting transfers between devices, swap(): return lax.ppermute(x, axis, [(i, i ^ distance) for i in range(size)])  8.5 us
    pallas_call x1, Pallas kernels, local(): pl.pallas_call(functools.partial(particle_kernel, width, mine, n_gz, n_do...  6.56 us
    ppermute x10, waiting for transfers between devices, swap(): return lax.ppermute(x, axis, [(i, i ^ distance) for i in range(size)])  3.36 us
    ppermute x1, starting transfers between devices, local(): above = lax.ppermute(volume[:1], 'gz', [(i, i - 1) for i in range(1, n_gz)])  3.33 us
    unnamed x20, local copies, waits for them, and re-layouts  2.5 us
  transfers between devices with their start and end apart: 11, of which 3 were waited for; matrix products, arithmetic and copies ran while one was open for 12% of the time, Pallas kernels for 10%

profile of v2, /device:TPU:4, one launch (start us, length us, event | category | flops | bytes accessed | tf_op | source)
XLA Modules:
  0.0 104.0 jit_solution(13883427754274419443)
XLA Ops:
  0.6 0.7 convert_bitcast_fusion
  1.3 0.1 copy.22
  1.4 0.8 copy.28
  2.2 3.7 %collective-permute-start.2 = (bf16[16,1664]{1,0:T(8,128)(2,1)S(1)}, bf16[16,1664]{1,0:T(8,128)(2,1)S(1)}, u32[]{:S(2)}, u32[]{:S(2)}) collective-permute-start(bf16[16,1664]{1,0:T(8,128)(2,1)S(1)} %pad_maximum_fusion.2), channel_id=1, source_target_pairs={{0,6},{1,7},{2,4},{3,5},{4,2},{5,3},{6,0},{7,1},{8,14},{9,15},{10,... | collective-permute-start | bytes 159752 | tf_op jit(solution)/shard_map/ppermute | solution.py:272
  5.9 0.0 collective-permute-start.1
  5.9 0.8 collective-permute-start
  6.7 0.7 slice.9
  7.4 3.3 %collective-permute-start.10 = (f32[1,4,384]{2,1,0:T(4,128)S(1)}, f32[1,4,384]{2,1,0:T(4,128)S(1)}, u32[]{:S(2)}, u32[]{:S(2)}) collective-permute-start(f32[1,4,384]{2,1,0:T(4,128)S(1)} %slice.9), channel_id=1, source_target_pairs={{8,0},{16,8},{24,16},{9,1},{17,9},{25,17},{10,2},{18,10},{26,18},{... | collective-permute-start | bytes 18440 | tf_op jit(solution)/shard_map/ppermute | solution.py:305
  10.8 0.9 copy.29
  11.7 0.7 fusion.2
  12.4 0.9 constant_dynamic-slice_fusion.1
  13.3 1.2 %fusion.3.table = s32[101]{0:T(128)} fusion(s32[32,101]{1,0:T(8,128)} %constant.71.clone, s32[]{:T(128)S(6)} %select_n.32), kind=kLoop, calls=%fused_computation.20 | loop fusion | bytes 812 | tf_op jit(solution)/shard_map/jit(dynamic_index_in_dim)/squeeze | solution.py:300
  14.5 0.5 pad_maximum_fusion.3.trig
  15.1 0.7 pad_add_fusion.place
  15.7 1.0 mul.34
  16.8 0.1 pad.9.clone
  16.9 0.0 collective-permute-done.10
  16.9 0.7 dynamic-slice_select_fusion
  17.6 0.1 maximum_maximum_fusion
  17.7 0.1 reshape.55
  17.8 0.7 fusion.1
  18.5 10.2 %extract.1 = f32[192,8,128]{2,1,0:T(8,128)} custom-call(s32[101]{0:T(128)} %fusion.3.table, f32[2,64]{1,0:T(2,128)} %pad_maximum_fusion.3.trig, s32[1]{0:T(128)} %bitcast.1.where, bf16[3,128,128]{2,1,0:T(8,128)(2,1)} %get-tuple-element.17.vhi, bf16[3,128,128]{2,1,0:T(8,128)(2,1)} %get-tuple-element.16.vlo), custom_call_target="tpu_custom_call" | custom-call | tf_op jit(solution)/shard_map/extract/pallas_call | solution.py:320
  28.7 1.2 %reduce_precision.11 = f32[192,8,128]{2,1,0:T(8,128)S(1)} reduce-precision(f32[192,8,128]{2,1,0:T(8,128)} %extract.1), exponent_bits=8, mantissa_bits=7 | non-fusion elementwise | flops 196608 | bytes 1572864 | tf_op jit(solution)/shard_map/reduce_precision | solution.py:329
  29.9 0.3 copy.33
  30.2 0.4 reshape.58
  30.7 0.0 collective-permute-done.2
  30.7 0.0 collective-permute-done.1
  30.7 0.0 collective-permute-done
  30.7 0.0 copy-start
  30.7 0.1 collective-permute-start.5
  30.8 0.1 collective-permute-start.4
  30.9 3.4 %collective-permute-start.3 = (bf16[64,1664]{1,0:T(8,128)(2,1)S(1)}, bf16[64,1664]{1,0:T(8,128)(2,1)S(1)}, u32[]{:S(2)}, u32[]{:S(2)}) collective-permute-start(bf16[64,1664]{1,0:T(8,128)(2,1)S(1)} %pad_maximum_fusion.1.refs_0_), channel_id=1, source_target_pairs={{0,8},{8,0},{16,24},{24,16},{1,9},{9,1},{17,25},{25,17},{2,10},{10... | collective-permute-start | bytes 638984 | tf_op jit(solution)/shard_map/ppermute | solution.py:272
  34.3 0.1 multiply_reduce_fusion
  34.4 0.3 copy.27
  34.7 0.2 copy.26
  34.9 0.8 convert_element_type.25.refs_10_
  35.8 0.0 copy-done
  35.8 0.0 collective-permute-start.6
  35.8 1.9 %collective-permute-done.5.refs_3_ = bf16[64,1664]{1,0:T(8,128)(2,1)S(1)} collective-permute-done((bf16[64,1664]{1,0:T(8,128)(2,1)S(1)}, bf16[64,1664]{1,0:T(8,128)(2,1)S(1)}, u32[]{:S(2)}, u32[]{:S(2)}) %collective-permute-start.5) | collective-permute-done | bytes 213024 | tf_op jit(solution)/shard_map/ppermute | solution.py:272
  37.6 0.0 copy-start.1
  37.6 0.0 collective-permute-start.9
  37.6 1.3 %collective-permute-done.4.refs_2_ = bf16[64,1664]{1,0:T(8,128)(2,1)S(1)} collective-permute-done((bf16[64,1664]{1,0:T(8,128)(2,1)S(1)}, bf16[64,1664]{1,0:T(8,128)(2,1)S(1)}, u32[]{:S(2)}, u32[]{:S(2)}) %collective-permute-start.4) | collective-permute-done | bytes 213024 | tf_op jit(solution)/shard_map/ppermute | solution.py:272
  39.0 0.0 collective-permute-start.8
  39.0 0.0 collective-permute-done.3.refs_1_
  39.0 0.0 copy-start.3
  39.0 0.5 collective-permute-start.7
  39.5 1.1 %fusion.7.refs_11_ = f32[32,128]{1,0:T(8,128)} fusion(f32[32,768]{1,0:T(8,128)S(1)} %bitcast.51, f32[128,768]{1,0:T(8,128)S(1)} %bitcast.42), kind=kOutput, calls=%fused_computation.29 | convolution fusion | flops 37748736 | bytes 507904 | tf_op jit(solution)/shard_map/dot_general | solution.py:334
  40.6 0.0 collective-permute-done.6.refs_4_
  40.6 0.0 collective-permute-done.9.refs_7_
  40.6 0.0 copy-start.5
  40.6 0.0 collective-permute-done.8.refs_6_
  40.6 0.0 copy-start.6
  40.7 0.1 collective-permute-done.7.refs_5_
  40.8 0.0 copy-done.1
  40.8 0.0 copy-done.2
  40.8 0.0 copy-done.3
  40.8 0.5 copy-done.4
  41.3 0.1 copy-done.5
  41.4 0.1 copy-done.6
  41.5 0.1 copy-done.7
  41.5 6.6 %particles.1 = (bf16[512,1536]{1,0:T(8,128)(2,1)}, f32[8,128]{1,0:T(8,128)}, f32[1,512]{1,0:T(1,128)}, f32[64,1536]{1,0:T(8,128)}) custom-call(s32[3]{0:T(128)} %pad_add_fusion.place, bf16[64,1664]{1,0:T(8,128)(2,1)} %copy-done, bf16[64,1664]{1,0:T(8,128)(2,1)} %copy-done.3, bf16[64,1664]{1,0:T(8,128)(2,1)} %copy-done.2, bf16[64,1664]{1,0:T(8,128)(2,1)} %copy-done.1, ...), custom_call_target="tpu_custom_call" | custom-call | tf_op jit(solution)/shard_map/particles/pallas_call | solution.py:348
  48.1 44.8 %all_gather.3.parts = f32[256,128]{1,0:T(8,128)} all-gather(f32[8,128]{1,0:T(8,128)} %get-tuple-element.8), channel_id=1, replica_groups=mesh['gz'=4,'dom'=8] {'gz','dom'}, dimensions={0}, use_global_device_ids=true | all-gather | bytes 135168 | tf_op jit(solution)/shard_map/all_gather | solution.py:366
  92.9 9.8 %spread.1 = (f32[1,512]{1,0:T(1,128)}, f32[24,4,384]{2,1,0:T(4,128)}) custom-call(s32[101]{0:T(128)} %fusion.3.table, f32[2,64]{1,0:T(2,128)} %pad_maximum_fusion.3.trig, s32[1]{0:T(128)} %bitcast.1.where, f32[256,128]{1,0:T(8,128)} %all_gather.3.parts, f32[1,512]{1,0:T(1,128)} %get-tuple-element.9.bins_row, bf16[512,1536]{1,0:T(8,128)(2,1)} %get-tuple-element.10.weighted, ...), custom_call_target="tpu_custom_call" | custom-call | tf_op jit(solution)/shard_map/spread/pallas_call | solution.py:369
  102.8 1.3 %fusion.4 = f32[16]{0:T(128)} fusion(f32[1,512]{1,0:T(1,128)} %get-tuple-element.12, s32[]{:T(128)S(6)} %select_n.39), kind=kLoop, calls=%fused_computation.21 | loop fusion | bytes 132 | tf_op jit(solution)/shard_map/dynamic_slice | solution.py:384
  (15 shorter events, 0.2 us)
Async XLA Ops:
  2.2 28.4 %collective-permute-start.2 = (bf16[16,1664]{1,0:T(8,128)(2,1)S(1)}, bf16[16,1664]{1,0:T(8,128)(2,1)S(1)}, u32[]{:S(2)}, u32[]{:S(2)}) collective-permute-start(bf16[16,1664]{1,0:T(8,128)(2,1)S(1)} %pad_maximum_fusion.2), channel_id=1, source_target_pairs={{0,6},{1,7},{2,4},{3,5},{4,2},{5,3},{6,0},{7,1},{8,14},{9,15},{10,... | collective-permute-start | bytes 159752 | tf_op jit(solution)/shard_map/ppermute | solution.py:272
  5.9 24.8 %collective-permute-start.1 = (bf16[16,1664]{1,0:T(8,128)(2,1)S(1)}, bf16[16,1664]{1,0:T(8,128)(2,1)S(1)}, u32[]{:S(2)}, u32[]{:S(2)}) collective-permute-start(bf16[16,1664]{1,0:T(8,128)(2,1)S(1)} %pad_maximum_fusion.2), channel_id=1, source_target_pairs={{0,4},{1,5},{2,6},{3,7},{4,0},{5,1},{6,2},{7,3},{8,12},{9,13},{10,... | collective-permute-start | bytes 159752 | tf_op jit(solution)/shard_map/ppermute | solution.py:272
  5.9 24.8 %collective-permute-start = (bf16[16,1664]{1,0:T(8,128)(2,1)S(1)}, bf16[16,1664]{1,0:T(8,128)(2,1)S(1)}, u32[]{:S(2)}, u32[]{:S(2)}) collective-permute-start(bf16[16,1664]{1,0:T(8,128)(2,1)S(1)} %pad_maximum_fusion.2), channel_id=1, source_target_pairs={{0,2},{1,3},{2,0},{3,1},{4,6},{5,7},{6,4},{7,5},{8,10},{9,11},{10,... | collective-permute-start | bytes 159752 | tf_op jit(solution)/shard_map/ppermute | solution.py:272
  7.4 9.5 %collective-permute-start.10 = (f32[1,4,384]{2,1,0:T(4,128)S(1)}, f32[1,4,384]{2,1,0:T(4,128)S(1)}, u32[]{:S(2)}, u32[]{:S(2)}) collective-permute-start(f32[1,4,384]{2,1,0:T(4,128)S(1)} %slice.9), channel_id=1, source_target_pairs={{8,0},{16,8},{24,16},{9,1},{17,9},{25,17},{10,2},{18,10},{26,18},{... | collective-permute-start | bytes 18440 | tf_op jit(solution)/shard_map/ppermute | solution.py:305
  30.7 5.0 %copy-start = (bf16[64,1664]{1,0:T(8,128)(2,1)}, bf16[64,1664]{1,0:T(8,128)(2,1)S(1)}, u32[]{:S(2)}) copy-start(bf16[64,1664]{1,0:T(8,128)(2,1)S(1)} %pad_maximum_fusion.1.refs_0_) | copy-start | bytes 638980
  30.7 6.9 %collective-permute-start.5 = (bf16[64,1664]{1,0:T(8,128)(2,1)S(1)}, bf16[64,1664]{1,0:T(8,128)(2,1)S(1)}, u32[]{:S(2)}, u32[]{:S(2)}) collective-permute-start(bf16[64,1664]{1,0:T(8,128)(2,1)S(1)} %pad_maximum_fusion.1.refs_0_), channel_id=1, source_target_pairs={{0,24},{8,16},{16,8},{24,0},{1,25},{9,17},{17,9},{25,1},{2,26},{10... | collective-permute-start | bytes 638984 | tf_op jit(solution)/shard_map/ppermute | solution.py:272
  30.8 8.2 %collective-permute-start.4 = (bf16[64,1664]{1,0:T(8,128)(2,1)S(1)}, bf16[64,1664]{1,0:T(8,128)(2,1)S(1)}, u32[]{:S(2)}, u32[]{:S(2)}) collective-permute-start(bf16[64,1664]{1,0:T(8,128)(2,1)S(1)} %pad_maximum_fusion.1.refs_0_), channel_id=1, source_target_pairs={{0,16},{8,24},{16,0},{24,8},{1,17},{9,25},{17,1},{25,9},{2,18},{10... | collective-permute-start | bytes 638984 | tf_op jit(solution)/shard_map/ppermute | solution.py:272
  30.9 8.1 %collective-permute-start.3 = (bf16[64,1664]{1,0:T(8,128)(2,1)S(1)}, bf16[64,1664]{1,0:T(8,128)(2,1)S(1)}, u32[]{:S(2)}, u32[]{:S(2)}) collective-permute-start(bf16[64,1664]{1,0:T(8,128)(2,1)S(1)} %pad_maximum_fusion.1.refs_0_), channel_id=1, source_target_pairs={{0,8},{8,0},{16,24},{24,16},{1,9},{9,1},{17,25},{25,17},{2,10},{10... | collective-permute-start | bytes 638984 | tf_op jit(solution)/shard_map/ppermute | solution.py:272
  35.8 4.9 %collective-permute-start.6 = (bf16[64,1664]{1,0:T(8,128)(2,1)S(1)}, bf16[64,1664]{1,0:T(8,128)(2,1)S(1)}, u32[]{:S(2)}, u32[]{:S(2)}) collective-permute-start(bf16[64,1664]{1,0:T(8,128)(2,1)S(1)} %pad_maximum_fusion.1.refs_0_), channel_id=1, source_target_pairs={{0,1},{1,0},{2,3},{3,2},{4,5},{5,4},{6,7},{7,6},{8,9},{9,8},{10,11... | collective-permute-start | bytes 638984 | tf_op jit(solution)/shard_map/ppermute | solution.py:272
  37.6 3.1 %copy-start.1 = (bf16[64,1664]{1,0:T(8,128)(2,1)}, bf16[64,1664]{1,0:T(8,128)(2,1)S(1)}, u32[]{:S(2)}) copy-start(bf16[64,1664]{1,0:T(8,128)(2,1)S(1)} %collective-permute-done.5.refs_3_) | copy-start | bytes 638980
  37.6 3.0 %collective-permute-start.9 = (bf16[64,1664]{1,0:T(8,128)(2,1)S(1)}, bf16[64,1664]{1,0:T(8,128)(2,1)S(1)}, u32[]{:S(2)}, u32[]{:S(2)}) collective-permute-start(bf16[64,1664]{1,0:T(8,128)(2,1)S(1)} %collective-permute-done.5.refs_3_), channel_id=1, source_target_pairs={{0,1},{1,0},{2,3},{3,2},{4,5},{5,4},{6,7},{7,6},{8,9},{9,8},{10,11... | collective-permute-start | bytes 638984 | tf_op jit(solution)/shard_map/ppermute | solution.py:272
  39.0 1.8 %copy-start.2 = (bf16[64,1664]{1,0:T(8,128)(2,1)}, bf16[64,1664]{1,0:T(8,128)(2,1)S(1)}, u32[]{:S(2)}) copy-start(bf16[64,1664]{1,0:T(8,128)(2,1)S(1)} %collective-permute-done.4.refs_2_) | copy-start | bytes 638980
  39.0 1.6 %collective-permute-start.8 = (bf16[64,1664]{1,0:T(8,128)(2,1)S(1)}, bf16[64,1664]{1,0:T(8,128)(2,1)S(1)}, u32[]{:S(2)}, u32[]{:S(2)}) collective-permute-start(bf16[64,1664]{1,0:T(8,128)(2,1)S(1)} %collective-permute-done.4.refs_2_), channel_id=1, source_target_pairs={{0,1},{1,0},{2,3},{3,2},{4,5},{5,4},{6,7},{7,6},{8,9},{9,8},{10,11... | collective-permute-start | bytes 638984 | tf_op jit(solution)/shard_map/ppermute | solution.py:272
  39.0 1.8 %copy-start.3 = (bf16[64,1664]{1,0:T(8,128)(2,1)}, bf16[64,1664]{1,0:T(8,128)(2,1)S(1)}, u32[]{:S(2)}) copy-start(bf16[64,1664]{1,0:T(8,128)(2,1)S(1)} %collective-permute-done.3.refs_1_) | copy-start | bytes 638980
  39.0 1.8 %collective-permute-start.7 = (bf16[64,1664]{1,0:T(8,128)(2,1)S(1)}, bf16[64,1664]{1,0:T(8,128)(2,1)S(1)}, u32[]{:S(2)}, u32[]{:S(2)}) collective-permute-start(bf16[64,1664]{1,0:T(8,128)(2,1)S(1)} %collective-permute-done.3.refs_1_), channel_id=1, source_target_pairs={{0,1},{1,0},{2,3},{3,2},{4,5},{5,4},{6,7},{7,6},{8,9},{9,8},{10,11... | collective-permute-start | bytes 638984 | tf_op jit(solution)/shard_map/ppermute | solution.py:272
  40.6 0.7 copy-start.4
  40.6 0.8 copy-start.5
  40.6 0.8 copy-start.6
  40.8 0.7 copy-start.7

commit v3 on v2

--- a/solution.py
+++ b/solution.py
@@ -21,7 +21,6 @@
 f32 = jnp.float32
 bf16 = jnp.bfloat16
 NT = (((1,), (1,)), ((), ()))
-TN = (((0,), (0,)), ((), ()))
 
 
 def round_up(n, m):
@@ -87,7 +86,7 @@
     return centre, kz, kzd * (-u * c * (1.0 / samples))
 
 
-def extract_kernel(groups, planes, samples, table, trig, where, vhi, vlo, out):
+def extract_kernel(groups, planes, samples, table, trig, where, vhi, vlo, after, out):
     depth = vhi.shape[1] // 4
     ut_count = samples // TILE
     z0 = where[0].astype(f32)
@@ -128,7 +127,7 @@
 
 def particle_kernel(width, mine, n_gz, n_dom, place, *refs):
     blocks = refs[: 2 * n_gz]
-    ctf_hi, ctf_lo, slope, pairs, weighted, parts, bins_row, plain, packed, sems = refs[2 * n_gz :]
+    ctf_hi, ctf_lo, slope, pairs, weighted, parts, bins_row, packed, sems = refs[2 * n_gz :]
     n_z = n_dom // 2
     gz, z, core = place[0], place[1], place[2]
     copies = []
@@ -152,7 +151,6 @@
     total = packed.shape[0]
     count = min(CHUNK, total)
     bins = slope.shape[0]
-    plain[...] = jnp.zeros_like(plain)
 
     def step(i, carry):
         span = pl.ds(pl.multiple_of(i * count, count), count)
@@ -188,17 +186,28 @@
                 parts[pl.ds(at, 1), :] = row[:, q * TILE : (q + 1) * TILE]
         pick = jnp.where(lanes_of((8, TILE), 1) == 1.0, 1.0, 0.0).astype(bf16)
         bins_row[:, span] = lax.dot_general(pick, ids, NT, preferred_element_type=f32)[0:1]
-        plain[...] = plain[...] + lax.dot_general(
-            onehot_bin.astype(bf16), whi, TN, preferred_element_type=f32
-        )
         return carry
 
     lax.fori_loop(0, total // count, step, 0)
 
 
+def plain_kernel(bins_row, weighted, plain):
+    count = weighted.shape[0]
+    chunk = min(CHUNK, count)
+    sums = jnp.zeros(plain.shape, f32)
+    for i in range(count // chunk):
+        span = slice(i * chunk, (i + 1) * chunk)
+        belongs = lanes_of((plain.shape[0], chunk), 0) == bins_row[:, span]
+        onehot = jnp.where(belongs, 1.0, 0.0).astype(bf16)
+        sums = sums + jnp.dot(onehot, weighted[span, :], preferred_element_type=f32)
+    plain[...] = sums
+
+
 def spread_kernel(
-    groups, planes, samples, table, trig, where, parts, bins_row, weighted, plain, pose, out, sums, total
+    groups, planes, samples, mine, n_gz, table, trig, where, bins_row, weighted, plain, *refs
 ):
+    parts = refs[:n_gz]
+    pose, out, sums, total, poses = refs[n_gz:]
     bins, width = plain.shape
     tiles = width // TILE
     ut_count = samples // TILE
@@ -207,15 +216,18 @@
     chunk = min(CHUNK, count)
     z0 = where[0].astype(f32)
 
-    rows = 2 * count // TILE
-    scalars = jnp.sum(parts[...].reshape(parts.shape[0] // rows, rows, TILE), axis=0)
-    square = jnp.concatenate([scalars[q : q + 1] for q in range(rows // 2)], 1)
-    pull = jnp.concatenate([scalars[q : q + 1] for q in range(rows // 2, rows)], 1)
+    rows = count // TILE
+    scalars = sum([part[...] for part in parts[1:]], parts[0][...])
+    square, pull = scalars[:rows], scalars[rows:]
     curvature = square + EPS
     shift = jnp.zeros_like(square)
     for _ in range(ITERS):
         shift = shift + 0.5 * (pull - shift * square) / curvature
-    pose[...] = shift * jnp.sqrt(curvature)
+    poses[...] = shift * jnp.sqrt(curvature)
+    first = (where[0] // planes) * mine
+    row = poses[pl.ds(first // TILE, 1), :]
+    pose[...] = pltpu.roll(row, TILE - lax.rem(first, TILE), 1)[:, :mine]
+    shift = jnp.concatenate([shift[q : q + 1] for q in range(rows)], 1)
 
     slope_sum = jnp.zeros((bins, width), f32)
     for i in range(count // chunk):
@@ -316,15 +328,17 @@
 
     smem = pl.BlockSpec(memory_space=pltpu.SMEM)
     vmem = pl.BlockSpec(memory_space=pltpu.VMEM)
+    hbm = pl.BlockSpec(memory_space=pl.ANY)
     params = pltpu.CompilerParams(vmem_limit_bytes=VMEM)
     slices = pl.pallas_call(
         functools.partial(extract_kernel, groups, planes, samples),
         out_shape=jax.ShapeDtypeStruct((bins * ut_count, 2 * rows, TILE), f32),
-        in_specs=[smem, smem, smem, vmem, vmem],
+        in_specs=[smem, smem, smem, vmem, vmem, hbm],
         out_specs=vmem,
         compiler_params=params,
+        cost_estimate=pl.CostEstimate(flops=6 * 10**9, bytes_accessed=2**20, transcendentals=0),
         name="extract",
-    )(table, trig, where, field_hi, field_lo)
+    )(table, trig, where, field_hi, field_lo, column)
 
     slices = lax.reduce_precision(slices, 8, 7)
     slices = slices.reshape(bins, ut_count, 2 * rows, TILE).transpose(0, 2, 1, 3)
@@ -344,17 +358,15 @@
     ctf_lo = (flat_ctf - ctf_hi).astype(bf16)
     ctf_hi = ctf_hi.astype(bf16)
 
-    hbm = pl.BlockSpec(memory_space=pl.ANY)
-    weighted, parts, bins_row, plain = pl.pallas_call(
+    weighted, parts, bins_row = pl.pallas_call(
         functools.partial(particle_kernel, width, mine, n_gz, n_dom),
         out_shape=[
             jax.ShapeDtypeStruct((count, width), bf16),
             jax.ShapeDtypeStruct((2 * count // TILE, TILE), f32),
             jax.ShapeDtypeStruct((1, count), f32),
-            jax.ShapeDtypeStruct((bins, width), f32),
         ],
         in_specs=[smem] + [hbm] * len(gathered) + [vmem] * 4,
-        out_specs=[vmem] * 4,
+        out_specs=[vmem] * 3,
         scratch_shapes=[
             pltpu.VMEM((count, width + TILE), bf16),
             pltpu.SemaphoreType.DMA((devices,)),
@@ -363,25 +375,37 @@
         name="particles",
     )(place, *gathered, ctf_hi, ctf_lo, slope, pairs)
 
-    parts = lax.all_gather(parts, ("gz", "dom"), axis=0, tiled=True)
+    plain = pl.pallas_call(
+        plain_kernel,
+        out_shape=jax.ShapeDtypeStruct((bins, width), f32),
+        in_specs=[vmem, vmem],
+        out_specs=vmem,
+        compiler_params=params,
+        cost_estimate=pl.CostEstimate(flops=2 * 10**9, bytes_accessed=2**21, transcendentals=0),
+        name="plain_sums",
+    )(bins_row, weighted)
+
+    parts = sum([swap(parts, "dom", n_dom, k) for k in range(1, n_dom)], parts)
+    parts = [parts] + [swap(parts, "gz", n_gz, j) for j in range(1, n_gz)]
 
     depth = round_up(planes, 8)
     pose, spread = pl.pallas_call(
-        functools.partial(spread_kernel, groups, planes, samples),
+        functools.partial(spread_kernel, groups, planes, samples, mine, n_gz),
         out_shape=[
-            jax.ShapeDtypeStruct((1, count), f32),
+            jax.ShapeDtypeStruct((1, mine), f32),
             jax.ShapeDtypeStruct((planes, rows, columns), f32),
         ],
-        in_specs=[smem, smem, smem, vmem, vmem, vmem, vmem],
+        in_specs=[smem, smem, smem] + [vmem] * (3 + n_gz),
         out_specs=[vmem, vmem],
         scratch_shapes=[
             pltpu.VMEM((2 * width // TILE, bins, TILE), f32),
             pltpu.VMEM((xt_count, rows * depth, TILE), f32),
+            pltpu.VMEM((count // TILE, TILE), f32),
         ],
         compiler_params=params,
         name="spread",
-    )(table, trig, where, parts, bins_row, weighted, plain)
-    pose = lax.dynamic_slice_in_dim(pose.reshape(count), device * mine, mine, 0)
+    )(table, trig, where, bins_row, weighted, plain, *parts)
+    pose = pose.reshape(mine)
     return pose, spread
 
 

time: 105 us -> 75.6 us (0.72)
  blocking collectives: 44.8 us -> 0 us
  starting transfers between devices: 11.8 us -> 24.4 us
  Pallas kernels: 26.6 us -> 28.7 us
  waiting for transfers between devices: 3.36 us -> 4.55 us
    all_gather x1 -> x0, blocking collectives: 44.8 us -> none  [local(): parts = lax.all_gather(parts, ('gz', 'dom'), axis=0, tiled=True)]
    ppermute x10 -> x20, starting transfers between devices: 8.5 us -> 21.1 us  [swap(): return lax.ppermute(x, axis, [(i, i ^ distance) for i in range(size)])]
    pallas_call x1 -> x2, Pallas kernels: 9.83 us -> 12.3 us  [the longest x1 9.75 us: local(): pl.pallas_call(functools.partial(spread_kernel, groups, planes, samples,...]
    dynamic_slice x1 -> x0, local copies, waits for them, and re-layouts: 1.26 us -> none  [local(): pose = lax.dynamic_slice_in_dim(pose.reshape(count), device * mine, mine, 0)]
    ppermute x10 -> x20, waiting for transfers between devices: 3.36 us -> 4.55 us  [swap(): return lax.ppermute(x, axis, [(i, i ^ distance) for i in range(size)])]
    unnamed x20 -> x28, local copies, waits for them, and re-layouts: 2.5 us -> 3.03 us
  transfers between devices with their start and end apart: 11 -> 21, of which waited for: 3 -> 3; matrix products, arithmetic and copies ran while one was open for 12% -> 17% of each run, Pallas kernels for 10% -> 17%
where the time goes in v3:
time: 75.6 us; the launch traced here: 75 us
  Pallas kernels  28.7 us (38%)
  starting transfers between devices  24.4 us (32%)
  local copies, waits for them, and re-layouts  8.17 us (11%)
  other arithmetic  7.11 us (9%)
  waiting for transfers between devices  4.55 us (6%)
  matrix products  1.1 us (1%)
  between operations  0.93 us (1%)
    ppermute x20, starting transfers between devices, swap(): return lax.ppermute(x, axis, [(i, i ^ distance) for i in range(size)])  21.1 us
    pallas_call x1, Pallas kernels, local(): pl.pallas_call(functools.partial(extract_kernel, groups, planes, samples)...  10.3 us
    pallas_call x1, Pallas kernels, local(): pl.pallas_call(functools.partial(spread_kernel, groups, planes, samples,...  9.75 us
    pallas_call x1, Pallas kernels, local(): pl.pallas_call(functools.partial(particle_kernel, width, mine, n_gz, n_do...  6.13 us
    ppermute x20, waiting for transfers between devices, swap(): return lax.ppermute(x, axis, [(i, i ^ distance) for i in range(size)])  4.55 us
    ppermute x1, starting transfers between devices, local(): above = lax.ppermute(volume[:1], 'gz', [(i, i - 1) for i in range(1, n_gz)])  3.33 us
    unnamed x28, local copies, waits for them, and re-layouts  3.03 us
    pallas_call x1, Pallas kernels, local(): pl.pallas_call(plain_kernel, out_shape=jax.ShapeDtypeStruct((bins, width)...  2.55 us
  transfers between devices with their start and end apart: 21, of which 3 were waited for; matrix products, arithmetic and copies ran while one was open for 17% of the time, Pallas kernels for 17%

profile of v3, /device:TPU:4, one launch (start us, length us, event | category | flops | bytes accessed | tf_op | source)
XLA Modules:
  0.0 75.0 jit_solution(17479761074251818315)
XLA Ops:
  0.6 0.7 convert_bitcast_fusion
  1.3 0.1 copy.22
  1.4 0.8 %copy.28 = bf16[2,8,4,384]{3,1,2,0:T(8,128)(2,1)S(1)} copy(bf16[2,8,4,384]{3,2,1,0:T(4,128)(2,1)} %bitcast.51) | data formatting | bytes 98304
  2.2 1.6 %collective-permute-start = (bf16[16,1664]{1,0:T(8,128)(2,1)S(1)}, bf16[16,1664]{1,0:T(8,128)(2,1)S(1)}, u32[]{:S(2)}, u32[]{:S(2)}) collective-permute-start(bf16[16,1664]{1,0:T(8,128)(2,1)S(1)} %pad_maximum_fusion.2), channel_id=1, source_target_pairs={{0,2},{1,3},{2,0},{3,1},{4,6},{5,7},{6,4},{7,5},{8,10},{9,11},{10,... | collective-permute-start | bytes 159752 | tf_op jit(solution)/shard_map/ppermute | solution.py:284
  3.9 2.6 %collective-permute-start.1 = (bf16[16,1664]{1,0:T(8,128)(2,1)S(1)}, bf16[16,1664]{1,0:T(8,128)(2,1)S(1)}, u32[]{:S(2)}, u32[]{:S(2)}) collective-permute-start(bf16[16,1664]{1,0:T(8,128)(2,1)S(1)} %pad_maximum_fusion.2), channel_id=1, source_target_pairs={{0,4},{1,5},{2,6},{3,7},{4,0},{5,1},{6,2},{7,3},{8,12},{9,13},{10,... | collective-permute-start | bytes 159752 | tf_op jit(solution)/shard_map/ppermute | solution.py:284
  6.5 0.2 collective-permute-start.2
  6.7 0.7 slice.9
  7.4 3.3 %collective-permute-start.10 = (f32[1,4,384]{2,1,0:T(4,128)S(1)}, f32[1,4,384]{2,1,0:T(4,128)S(1)}, u32[]{:S(2)}, u32[]{:S(2)}) collective-permute-start(f32[1,4,384]{2,1,0:T(4,128)S(1)} %slice.9), channel_id=1, source_target_pairs={{8,0},{16,8},{24,16},{9,1},{17,9},{25,17},{10,2},{18,10},{26,18},{... | collective-permute-start | bytes 18440 | tf_op jit(solution)/shard_map/ppermute | solution.py:317
  10.8 0.9 %constant_dynamic-slice_fusion = f32[24,4,384]{2,1,0:T(4,128)S(1)} fusion(f32[192,4,384]{2,1,0:T(4,128)} %param.6, s32[]{:T(128)S(6)} %select_n.32), kind=kLoop, calls=%fused_computation.18 | loop fusion | bytes 294916 | tf_op jit(solution)/shard_map/dynamic_slice | solution.py:318
  11.8 0.9 %copy.29 = f32[4,8,2,384]{3,1,2,0:T(8,128)S(1)} copy(f32[4,8,2,384]{3,2,1,0:T(2,128)} %bitcast.43) | data formatting | bytes 196608
  12.7 0.7 fusion.2
  13.3 1.2 %fusion.3.table = s32[101]{0:T(128)} fusion(s32[32,101]{1,0:T(8,128)} %constant.66.clone, s32[]{:T(128)S(6)} %select_n.29), kind=kLoop, calls=%fused_computation.20 | loop fusion | bytes 812 | tf_op jit(solution)/shard_map/jit(dynamic_index_in_dim)/squeeze | solution.py:312
  14.5 0.5 pad_maximum_fusion.3.trig
  15.1 0.7 pad_add_fusion.place
  15.7 1.0 %mul.31 = f32[32,2,384]{2,1,0:T(2,128)S(1)} multiply(f32[32,2,384]{2,1,0:T(2,128)} %param.8, f32[32,2,384]{2,1,0:T(2,128)} %param.8) | non-fusion elementwise | flops 24576 | bytes 294912 | tf_op jit(solution)/shard_map/mul | solution.py:349
  16.8 0.1 pad.9.clone
  16.9 0.0 collective-permute-done.10
  16.9 0.7 dynamic-slice_select_fusion
  17.6 0.1 maximum_maximum_fusion
  17.7 0.1 reshape.56
  17.8 0.7 fusion.1
  18.5 0.0 collective-permute-done
  18.5 0.0 collective-permute-done.1
  18.6 0.7 collective-permute-start.3
  19.2 0.3 collective-permute-start.4
  19.5 2.6 %collective-permute-start.5 = (bf16[64,1664]{1,0:T(8,128)(2,1)S(1)}, bf16[64,1664]{1,0:T(8,128)(2,1)S(1)}, u32[]{:S(2)}, u32[]{:S(2)}) collective-permute-start(bf16[64,1664]{1,0:T(8,128)(2,1)S(1)} %pad_maximum_fusion.1.after.refs_0_), channel_id=1, source_target_pairs={{0,24},{8,16},{16,8},{24,0},{1,25},{9,17},{17,9},{25,1},{2,26},{10... | collective-permute-start | bytes 638984 | tf_op jit(solution)/shard_map/ppermute | solution.py:284
  22.1 0.0 collective-permute-start.6
  22.1 10.3 %extract.1 = f32[192,8,128]{2,1,0:T(8,128)} custom-call(s32[101]{0:T(128)} %fusion.3.table, f32[2,64]{1,0:T(2,128)} %pad_maximum_fusion.3.trig, s32[1]{0:T(128)} %bitcast.1.where, bf16[3,128,128]{2,1,0:T(8,128)(2,1)} %get-tuple-element.15.vhi, bf16[3,128,128]{2,1,0:T(8,128)(2,1)} %get-tuple-element.14.vlo, bf16[64,1664]{1,0:T(8,128)(2,1)} %copy-done), custom_call_target="tpu_custom_call" | custom-call | flops 6000000000 | bytes 1048576 | tf_op jit(solution)/shard_map/extract/pallas_call | solution.py:333
  32.4 1.2 %reduce_precision.11 = f32[192,8,128]{2,1,0:T(8,128)S(1)} reduce-precision(f32[192,8,128]{2,1,0:T(8,128)} %extract.1), exponent_bits=8, mantissa_bits=7 | non-fusion elementwise | flops 196608 | bytes 1572864 | tf_op jit(solution)/shard_map/reduce_precision | solution.py:343
  33.6 0.3 copy.33
  33.8 0.4 reshape.59
  34.3 0.1 multiply_reduce_fusion
  34.4 0.3 copy.27
  34.8 0.2 copy.26
  35.0 0.8 %convert_element_type.25.refs_10_ = bf16[64,1536]{1,0:T(8,128)(2,1)} reshape(bf16[64,1,2,2,384]{4,3,2,0,1:T(2,128)(2,1)S(1)} %copy.26) | data formatting | bytes 393216 | tf_op jit(solution)/shard_map/convert_element_type | solution.py:355
  35.8 0.0 collective-permute-start.7
  35.8 0.0 collective-permute-done.4.refs_2_
  35.8 0.5 collective-permute-start.8
  36.3 0.0 collective-permute-done.5.refs_3_
  36.3 0.1 collective-permute-start.9
  36.4 1.1 %fusion.6.refs_11_ = f32[32,128]{1,0:T(8,128)} fusion(f32[32,768]{1,0:T(8,128)S(1)} %bitcast.50, f32[128,768]{1,0:T(8,128)S(1)} %bitcast.41), kind=kOutput, calls=%fused_computation.28 | convolution fusion | flops 37748736 | bytes 507904 | tf_op jit(solution)/shard_map/dot_general | solution.py:348
  37.5 0.0 collective-permute-done.8.refs_6_
  37.5 0.3 collective-permute-done.9.refs_7_
  37.9 0.3 copy-done.4
  38.2 0.1 copy-done.5
  38.3 0.1 copy-done.6
  38.3 0.2 copy-done.7
  38.5 6.1 %particles.1 = (bf16[512,1536]{1,0:T(8,128)(2,1)}, f32[8,128]{1,0:T(8,128)}, f32[1,512]{1,0:T(1,128)}) custom-call(s32[3]{0:T(128)} %pad_add_fusion.place, bf16[64,1664]{1,0:T(8,128)(2,1)} %copy-done, bf16[64,1664]{1,0:T(8,128)(2,1)} %copy-done.1, bf16[64,1664]{1,0:T(8,128)(2,1)} %copy-done.2, bf16[64,1664]{1,0:T(8,128)(2,1)} %copy-done.3, ...), custom_call_target="tpu_custom_call" | custom-call | tf_op jit(solution)/shard_map/particles/pallas_call | solution.py:361
  44.7 0.4 collective-permute-start.11
  45.0 1.6 %collective-permute-start.13 = (f32[8,128]{1,0:T(8,128)}, f32[8,128]{1,0:T(8,128)S(1)}, u32[]{:S(2)}, u32[]{:S(2)}) collective-permute-start(f32[8,128]{1,0:T(8,128)} %get-tuple-element.9), channel_id=1, source_target_pairs={{0,3},{1,2},{2,1},{3,0},{4,7},{5,6},{6,5},{7,4},{8,11},{9,10},{10,... | collective-permute-start | bytes 12296 | tf_op jit(solution)/shard_map/ppermute | solution.py:284
  46.6 0.0 collective-permute-start.14
  46.6 2.8 %collective-permute-start.15 = (f32[8,128]{1,0:T(8,128)}, f32[8,128]{1,0:T(8,128)S(1)}, u32[]{:S(2)}, u32[]{:S(2)}) collective-permute-start(f32[8,128]{1,0:T(8,128)} %get-tuple-element.9), channel_id=1, source_target_pairs={{0,5},{1,4},{2,7},{3,6},{4,1},{5,0},{6,3},{7,2},{8,13},{9,12},{10,... | collective-permute-start | bytes 12296 | tf_op jit(solution)/shard_map/ppermute | solution.py:284
  49.4 0.0 collective-permute-done.11
  49.4 0.0 collective-permute-start.16
  49.4 0.0 collective-permute-done.12
  49.4 3.4 %collective-permute-start.17 = (f32[8,128]{1,0:T(8,128)}, f32[8,128]{1,0:T(8,128)S(1)}, u32[]{:S(2)}, u32[]{:S(2)}) collective-permute-start(f32[8,128]{1,0:T(8,128)} %get-tuple-element.9), channel_id=1, source_target_pairs={{0,7},{1,6},{2,5},{3,4},{4,3},{5,2},{6,1},{7,0},{8,15},{9,14},{10,... | collective-permute-start | bytes 12296 | tf_op jit(solution)/shard_map/ppermute | solution.py:284
  52.8 2.2 %collective-permute-done.16 = f32[8,128]{1,0:T(8,128)S(1)} collective-permute-done((f32[8,128]{1,0:T(8,128)}, f32[8,128]{1,0:T(8,128)S(1)}, u32[]{:S(2)}, u32[]{:S(2)}) %collective-permute-start.16) | collective-permute-done | bytes 4128 | tf_op jit(solution)/shard_map/ppermute | solution.py:284
  55.0 0.7 add_add_fusion.refs_0_
  55.7 0.1 collective-permute-start.18
  55.8 4.3 %collective-permute-start.19 = (f32[8,128]{1,0:T(8,128)S(1)}, f32[8,128]{1,0:T(8,128)S(1)}, u32[]{:S(2)}, u32[]{:S(2)}) collective-permute-start(f32[8,128]{1,0:T(8,128)S(1)} %add_add_fusion.refs_0_), channel_id=1, source_target_pairs={{0,16},{8,24},{16,0},{24,8},{1,17},{9,25},{17,1},{25,9},{2,18},{10... | collective-permute-start | bytes 12296 | tf_op jit(solution)/shard_map/ppermute | solution.py:284
  60.1 2.5 %plain_sums.1.plain = f32[64,1536]{1,0:T(8,128)} custom-call(f32[1,512]{1,0:T(1,128)} %get-tuple-element.7.bins_row, bf16[512,1536]{1,0:T(8,128)(2,1)} %get-tuple-element.8.weighted), custom_call_target="tpu_custom_call" | custom-call | flops 2000000000 | bytes 2097152 | tf_op jit(solution)/shard_map/plain_sums/pallas_call | solution.py:378
  62.7 1.9 %collective-permute-done.20.refs_3_ = f32[8,128]{1,0:T(8,128)S(1)} collective-permute-done((f32[8,128]{1,0:T(8,128)S(1)}, f32[8,128]{1,0:T(8,128)S(1)}, u32[]{:S(2)}, u32[]{:S(2)}) %collective-permute-start.20) | collective-permute-done | bytes 4128 | tf_op jit(solution)/shard_map/ppermute | solution.py:284
  64.7 0.6 copy-done.11
  65.2 9.7 %spread.1 = (f32[1,16]{1,0:T(1,128)}, f32[24,4,384]{2,1,0:T(4,128)}) custom-call(s32[101]{0:T(128)} %fusion.3.table, f32[2,64]{1,0:T(2,128)} %pad_maximum_fusion.3.trig, s32[1]{0:T(128)} %bitcast.1.where, f32[1,512]{1,0:T(1,128)} %get-tuple-element.7.bins_row, bf16[512,1536]{1,0:T(8,128)(2,1)} %get-tuple-element.8.weighted, f32[64,1536]{1,0:T(8,128)} %plain_sums.1.plain, ...), custom_call_target="tpu_custom_call" | custom-call | tf_op jit(solution)/shard_map/spread/pallas_call | solution.py:392
  (43 shorter events, 0.3 us)
Async XLA Ops:
  2.2 16.3 %collective-permute-start = (bf16[16,1664]{1,0:T(8,128)(2,1)S(1)}, bf16[16,1664]{1,0:T(8,128)(2,1)S(1)}, u32[]{:S(2)}, u32[]{:S(2)}) collective-permute-start(bf16[16,1664]{1,0:T(8,128)(2,1)S(1)} %pad_maximum_fusion.2), channel_id=1, source_target_pairs={{0,2},{1,3},{2,0},{3,1},{4,6},{5,7},{6,4},{7,5},{8,10},{9,11},{10,... | collective-permute-start | bytes 159752 | tf_op jit(solution)/shard_map/ppermute | solution.py:284
  3.9 14.6 %collective-permute-start.1 = (bf16[16,1664]{1,0:T(8,128)(2,1)S(1)}, bf16[16,1664]{1,0:T(8,128)(2,1)S(1)}, u32[]{:S(2)}, u32[]{:S(2)}) collective-permute-start(bf16[16,1664]{1,0:T(8,128)(2,1)S(1)} %pad_maximum_fusion.2), channel_id=1, source_target_pairs={{0,4},{1,5},{2,6},{3,7},{4,0},{5,1},{6,2},{7,3},{8,12},{9,13},{10,... | collective-permute-start | bytes 159752 | tf_op jit(solution)/shard_map/ppermute | solution.py:284
  6.5 12.0 %collective-permute-start.2 = (bf16[16,1664]{1,0:T(8,128)(2,1)S(1)}, bf16[16,1664]{1,0:T(8,128)(2,1)S(1)}, u32[]{:S(2)}, u32[]{:S(2)}) collective-permute-start(bf16[16,1664]{1,0:T(8,128)(2,1)S(1)} %pad_maximum_fusion.2), channel_id=1, source_target_pairs={{0,6},{1,7},{2,4},{3,5},{4,2},{5,3},{6,0},{7,1},{8,14},{9,15},{10,... | collective-permute-start | bytes 159752 | tf_op jit(solution)/shard_map/ppermute | solution.py:284
  7.4 9.5 %collective-permute-start.10 = (f32[1,4,384]{2,1,0:T(4,128)S(1)}, f32[1,4,384]{2,1,0:T(4,128)S(1)}, u32[]{:S(2)}, u32[]{:S(2)}) collective-permute-start(f32[1,4,384]{2,1,0:T(4,128)S(1)} %slice.9), channel_id=1, source_target_pairs={{8,0},{16,8},{24,16},{9,1},{17,9},{25,17},{10,2},{18,10},{26,18},{... | collective-permute-start | bytes 18440 | tf_op jit(solution)/shard_map/ppermute | solution.py:317
  18.5 3.6 %copy-start = (bf16[64,1664]{1,0:T(8,128)(2,1)}, bf16[64,1664]{1,0:T(8,128)(2,1)S(1)}, u32[]{:S(2)}) copy-start(bf16[64,1664]{1,0:T(8,128)(2,1)S(1)} %pad_maximum_fusion.1.after.refs_0_) | copy-start | bytes 638980
  18.6 17.2 %collective-permute-start.3 = (bf16[64,1664]{1,0:T(8,128)(2,1)S(1)}, bf16[64,1664]{1,0:T(8,128)(2,1)S(1)}, u32[]{:S(2)}, u32[]{:S(2)}) collective-permute-start(bf16[64,1664]{1,0:T(8,128)(2,1)S(1)} %pad_maximum_fusion.1.after.refs_0_), channel_id=1, source_target_pairs={{0,8},{8,0},{16,24},{24,16},{1,9},{9,1},{17,25},{25,17},{2,10},{10... | collective-permute-start | bytes 638984 | tf_op jit(solution)/shard_map/ppermute | solution.py:284
  19.2 16.6 %collective-permute-start.4 = (bf16[64,1664]{1,0:T(8,128)(2,1)S(1)}, bf16[64,1664]{1,0:T(8,128)(2,1)S(1)}, u32[]{:S(2)}, u32[]{:S(2)}) collective-permute-start(bf16[64,1664]{1,0:T(8,128)(2,1)S(1)} %pad_maximum_fusion.1.after.refs_0_), channel_id=1, source_target_pairs={{0,16},{8,24},{16,0},{24,8},{1,17},{9,25},{17,1},{25,9},{2,18},{10... | collective-permute-start | bytes 638984 | tf_op jit(solution)/shard_map/ppermute | solution.py:284
  19.5 16.8 %collective-permute-start.5 = (bf16[64,1664]{1,0:T(8,128)(2,1)S(1)}, bf16[64,1664]{1,0:T(8,128)(2,1)S(1)}, u32[]{:S(2)}, u32[]{:S(2)}) collective-permute-start(bf16[64,1664]{1,0:T(8,128)(2,1)S(1)} %pad_maximum_fusion.1.after.refs_0_), channel_id=1, source_target_pairs={{0,24},{8,16},{16,8},{24,0},{1,25},{9,17},{17,9},{25,1},{2,26},{10... | collective-permute-start | bytes 638984 | tf_op jit(solution)/shard_map/ppermute | solution.py:284
  22.1 15.4 %collective-permute-start.6 = (bf16[64,1664]{1,0:T(8,128)(2,1)S(1)}, bf16[64,1664]{1,0:T(8,128)(2,1)S(1)}, u32[]{:S(2)}, u32[]{:S(2)}) collective-permute-start(bf16[64,1664]{1,0:T(8,128)(2,1)S(1)} %pad_maximum_fusion.1.after.refs_0_), channel_id=1, source_target_pairs={{0,1},{1,0},{2,3},{3,2},{4,5},{5,4},{6,7},{7,6},{8,9},{9,8},{10,11... | collective-permute-start | bytes 638984 | tf_op jit(solution)/shard_map/ppermute | solution.py:284
  35.8 2.1 %copy-start.1 = (bf16[64,1664]{1,0:T(8,128)(2,1)}, bf16[64,1664]{1,0:T(8,128)(2,1)S(1)}, u32[]{:S(2)}) copy-start(bf16[64,1664]{1,0:T(8,128)(2,1)S(1)} %collective-permute-done.3.refs_1_) | copy-start | bytes 638980
  35.8 1.7 %collective-permute-start.7 = (bf16[64,1664]{1,0:T(8,128)(2,1)S(1)}, bf16[64,1664]{1,0:T(8,128)(2,1)S(1)}, u32[]{:S(2)}, u32[]{:S(2)}) collective-permute-start(bf16[64,1664]{1,0:T(8,128)(2,1)S(1)} %collective-permute-done.3.refs_1_), channel_id=1, source_target_pairs={{0,1},{1,0},{2,3},{3,2},{4,5},{5,4},{6,7},{7,6},{8,9},{9,8},{10,11... | collective-permute-start | bytes 638984 | tf_op jit(solution)/shard_map/ppermute | solution.py:284
  35.8 2.1 %copy-start.2 = (bf16[64,1664]{1,0:T(8,128)(2,1)}, bf16[64,1664]{1,0:T(8,128)(2,1)S(1)}, u32[]{:S(2)}) copy-start(bf16[64,1664]{1,0:T(8,128)(2,1)S(1)} %collective-permute-done.4.refs_2_) | copy-start | bytes 638980
  35.8 1.7 %collective-permute-start.8 = (bf16[64,1664]{1,0:T(8,128)(2,1)S(1)}, bf16[64,1664]{1,0:T(8,128)(2,1)S(1)}, u32[]{:S(2)}, u32[]{:S(2)}) collective-permute-start(bf16[64,1664]{1,0:T(8,128)(2,1)S(1)} %collective-permute-done.4.refs_2_), channel_id=1, source_target_pairs={{0,1},{1,0},{2,3},{3,2},{4,5},{5,4},{6,7},{7,6},{8,9},{9,8},{10,11... | collective-permute-start | bytes 638984 | tf_op jit(solution)/shard_map/ppermute | solution.py:284
  36.3 1.6 %copy-start.3 = (bf16[64,1664]{1,0:T(8,128)(2,1)}, bf16[64,1664]{1,0:T(8,128)(2,1)S(1)}, u32[]{:S(2)}) copy-start(bf16[64,1664]{1,0:T(8,128)(2,1)S(1)} %collective-permute-done.5.refs_3_) | copy-start | bytes 638980
  36.3 1.6 %collective-permute-start.9 = (bf16[64,1664]{1,0:T(8,128)(2,1)S(1)}, bf16[64,1664]{1,0:T(8,128)(2,1)S(1)}, u32[]{:S(2)}, u32[]{:S(2)}) collective-permute-start(bf16[64,1664]{1,0:T(8,128)(2,1)S(1)} %collective-permute-done.5.refs_3_), channel_id=1, source_target_pairs={{0,1},{1,0},{2,3},{3,2},{4,5},{5,4},{6,7},{7,6},{8,9},{9,8},{10,11... | collective-permute-start | bytes 638984 | tf_op jit(solution)/shard_map/ppermute | solution.py:284
  37.5 0.7 copy-start.4
  37.5 0.8 %copy-start.5 = (bf16[64,1664]{1,0:T(8,128)(2,1)}, bf16[64,1664]{1,0:T(8,128)(2,1)S(1)}, u32[]{:S(2)}) copy-start(bf16[64,1664]{1,0:T(8,128)(2,1)S(1)} %collective-permute-done.7.refs_5_) | copy-start | bytes 638980
  37.5 0.8 %copy-start.6 = (bf16[64,1664]{1,0:T(8,128)(2,1)}, bf16[64,1664]{1,0:T(8,128)(2,1)S(1)}, u32[]{:S(2)}) copy-start(bf16[64,1664]{1,0:T(8,128)(2,1)S(1)} %collective-permute-done.8.refs_6_) | copy-start | bytes 638980
  37.8 0.7 copy-start.7
  44.7 4.8 %collective-permute-start.11 = (f32[8,128]{1,0:T(8,128)}, f32[8,128]{1,0:T(8,128)S(1)}, u32[]{:S(2)}, u32[]{:S(2)}) collective-permute-start(f32[8,128]{1,0:T(8,128)} %get-tuple-element.9), channel_id=1, source_target_pairs={{0,1},{1,0},{2,3},{3,2},{4,5},{5,4},{6,7},{7,6},{8,9},{9,8},{10,11... | collective-permute-start | bytes 12296 | tf_op jit(solution)/shard_map/ppermute | solution.py:284
  45.0 4.4 %collective-permute-start.12 = (f32[8,128]{1,0:T(8,128)}, f32[8,128]{1,0:T(8,128)S(1)}, u32[]{:S(2)}, u32[]{:S(2)}) collective-permute-start(f32[8,128]{1,0:T(8,128)} %get-tuple-element.9), channel_id=1, source_target_pairs={{0,2},{1,3},{2,0},{3,1},{4,6},{5,7},{6,4},{7,5},{8,10},{9,11},{10,... | collective-permute-start | bytes 12296 | tf_op jit(solution)/shard_map/ppermute | solution.py:284
  45.0 7.8 %collective-permute-start.13 = (f32[8,128]{1,0:T(8,128)}, f32[8,128]{1,0:T(8,128)S(1)}, u32[]{:S(2)}, u32[]{:S(2)}) collective-permute-start(f32[8,128]{1,0:T(8,128)} %get-tuple-element.9), channel_id=1, source_target_pairs={{0,3},{1,2},{2,1},{3,0},{4,7},{5,6},{6,5},{7,4},{8,11},{9,10},{10,... | collective-permute-start | bytes 12296 | tf_op jit(solution)/shard_map/ppermute | solution.py:284
  46.6 6.2 %collective-permute-start.14 = (f32[8,128]{1,0:T(8,128)}, f32[8,128]{1,0:T(8,128)S(1)}, u32[]{:S(2)}, u32[]{:S(2)}) collective-permute-start(f32[8,128]{1,0:T(8,128)} %get-tuple-element.9), channel_id=1, source_target_pairs={{0,4},{1,5},{2,6},{3,7},{4,0},{5,1},{6,2},{7,3},{8,12},{9,13},{10,... | collective-permute-start | bytes 12296 | tf_op jit(solution)/shard_map/ppermute | solution.py:284
  46.6 6.2 %collective-permute-start.15 = (f32[8,128]{1,0:T(8,128)}, f32[8,128]{1,0:T(8,128)S(1)}, u32[]{:S(2)}, u32[]{:S(2)}) collective-permute-start(f32[8,128]{1,0:T(8,128)} %get-tuple-element.9), channel_id=1, source_target_pairs={{0,5},{1,4},{2,7},{3,6},{4,1},{5,0},{6,3},{7,2},{8,13},{9,12},{10,... | collective-permute-start | bytes 12296 | tf_op jit(solution)/shard_map/ppermute | solution.py:284
  49.4 5.6 %collective-permute-start.16 = (f32[8,128]{1,0:T(8,128)}, f32[8,128]{1,0:T(8,128)S(1)}, u32[]{:S(2)}, u32[]{:S(2)}) collective-permute-start(f32[8,128]{1,0:T(8,128)} %get-tuple-element.9), channel_id=1, source_target_pairs={{0,6},{1,7},{2,4},{3,5},{4,2},{5,3},{6,0},{7,1},{8,14},{9,15},{10,... | collective-permute-start | bytes 12296 | tf_op jit(solution)/shard_map/ppermute | solution.py:284
  49.4 5.6 %collective-permute-start.17 = (f32[8,128]{1,0:T(8,128)}, f32[8,128]{1,0:T(8,128)S(1)}, u32[]{:S(2)}, u32[]{:S(2)}) collective-permute-start(f32[8,128]{1,0:T(8,128)} %get-tuple-element.9), channel_id=1, source_target_pairs={{0,7},{1,6},{2,5},{3,4},{4,3},{5,2},{6,1},{7,0},{8,15},{9,14},{10,... | collective-permute-start | bytes 12296 | tf_op jit(solution)/shard_map/ppermute | solution.py:284
  55.7 7.0 %copy-start.8 = (f32[8,128]{1,0:T(8,128)}, f32[8,128]{1,0:T(8,128)S(1)}, u32[]{:S(2)}) copy-start(f32[8,128]{1,0:T(8,128)S(1)} %add_add_fusion.refs_0_) | copy-start | bytes 12292
  55.7 7.0 %collective-permute-start.18 = (f32[8,128]{1,0:T(8,128)S(1)}, f32[8,128]{1,0:T(8,128)S(1)}, u32[]{:S(2)}, u32[]{:S(2)}) collective-permute-start(f32[8,128]{1,0:T(8,128)S(1)} %add_add_fusion.refs_0_), channel_id=1, source_target_pairs={{0,8},{8,0},{16,24},{24,16},{1,9},{9,1},{17,25},{25,17},{2,10},{10... | collective-permute-start | bytes 12296 | tf_op jit(solution)/shard_map/ppermute | solution.py:284
  55.8 6.9 %collective-permute-start.19 = (f32[8,128]{1,0:T(8,128)S(1)}, f32[8,128]{1,0:T(8,128)S(1)}, u32[]{:S(2)}, u32[]{:S(2)}) collective-permute-start(f32[8,128]{1,0:T(8,128)S(1)} %add_add_fusion.refs_0_), channel_id=1, source_target_pairs={{0,16},{8,24},{16,0},{24,8},{1,17},{9,25},{17,1},{25,9},{2,18},{10... | collective-permute-start | bytes 12296 | tf_op jit(solution)/shard_map/ppermute | solution.py:284
  60.1 4.5 %collective-permute-start.20 = (f32[8,128]{1,0:T(8,128)S(1)}, f32[8,128]{1,0:T(8,128)S(1)}, u32[]{:S(2)}, u32[]{:S(2)}) collective-permute-start(f32[8,128]{1,0:T(8,128)S(1)} %add_add_fusion.refs_0_), channel_id=1, source_target_pairs={{0,24},{8,16},{16,8},{24,0},{1,25},{9,17},{17,9},{25,1},{2,26},{10... | collective-permute-start | bytes 12296 | tf_op jit(solution)/shard_map/ppermute | solution.py:284
  62.7 2.0 %copy-start.9 = (f32[8,128]{1,0:T(8,128)}, f32[8,128]{1,0:T(8,128)S(1)}, u32[]{:S(2)}) copy-start(f32[8,128]{1,0:T(8,128)S(1)} %collective-permute-done.18.refs_1_) | copy-start | bytes 12292
  62.7 1.9 %copy-start.10 = (f32[8,128]{1,0:T(8,128)}, f32[8,128]{1,0:T(8,128)S(1)}, u32[]{:S(2)}) copy-start(f32[8,128]{1,0:T(8,128)S(1)} %collective-permute-done.19.refs_2_) | copy-start | bytes 12292
  64.7 0.6 copy-start.11

commit v4 on v3

v4 whole, which is shorter than its diff:
```python
import functools
import math

import jax
import jax.numpy as jnp
import numpy as np
from jax import lax
from jax.experimental import pallas as pl
from jax.experimental.pallas import tpu as pltpu
from jax.sharding import PartitionSpec as P

NZ = 768
NB_DEV = 8
NCTF = 32
ITERS = 3
EPS = 1e-05
TILE = 128
GROUP = 4
CHUNK = 512
VMEM = 56 * 2**20
f32 = jnp.float32
bf16 = jnp.bfloat16
NT = (((1,), (1,)), ((), ()))


def round_up(n, m):
    return -(-n // m) * m


def make_plan(devices, bins, samples, columns):
    planes = NZ // devices
    middle = NZ // 2
    ut_count, xt_count = samples // TILE, columns // TILE
    theta = -0.5 * math.pi + math.pi * (np.arange(bins) + 0.5) / bins
    trig = np.concatenate([np.sin(theta), np.cos(theta)]).astype(np.float32)
    u = np.arange(samples)
    slack = 1e-3
    reach = 0
    plans = []
    for spread in (False, True):
        rows = []
        for device in range(devices):
            z0 = device * planes
            z1 = z0 + planes
            lists = [[] for _ in range(xt_count)]
            edge = []
            for b in range(bins):
                s, c = math.sin(theta[b]), math.cos(theta[b])
                centre = middle + u * s
                near = (centre > z0 - slack - (1 if spread else 0)) & (centre < z1 + slack)
                if spread:
                    near[0] = z0 - 1 < middle < z1
                else:
                    near[0] = z0 <= middle < z1 if s > 0 else z0 < middle <= z1
                if not near.any():
                    continue
                if spread and s < 0 and z0 == middle:
                    edge.append(b * 4)
                    reach = max(reach, int(u[near].max()) + 1)
                    continue
                for ut in range(ut_count):
                    hit = u[ut * TILE : (ut + 1) * TILE][near[ut * TILE : (ut + 1) * TILE]]
                    if hit.size == 0:
                        continue
                    first = max(0, int((hit.min() * c - 1.01) // TILE))
                    last = min(xt_count - 1, int((hit.max() * c + 1.01) // TILE))
                    for xt in range(first, last + 1):
                        lists[xt].append(b * 4 + ut)
            idle = (bins - 1 if z0 < middle else 0) * 4 + ut_count - 1
            tiles, codes = [], []
            for xt, entries in enumerate(lists):
                entries = entries + [idle] * (-len(entries) % GROUP)
                tiles += [xt] * (len(entries) // GROUP)
                codes += entries
            rows.append((tiles, codes, edge))
        groups = max(len(tiles) for tiles, _, _ in rows)
        start = 1 + groups * (1 + GROUP)
        table = np.zeros((devices, start + 1 + max(len(edge) for _, _, edge in rows)), np.int32)
        for device, (tiles, codes, edge) in enumerate(rows):
            table[device, 0] = len(tiles)
            table[device, 1 : 1 + len(tiles)] = tiles
            table[device, 1 + groups : 1 + groups + len(codes)] = codes
            table[device, start] = len(edge) // GROUP
            table[device, start + 1 : start + 1 + len(edge)] = edge
        plans.append((table, groups))
    edge_samples = round_up(reach, 16)
    assert edge_samples <= TILE and (bins // 2) % GROUP == 0
    return plans[0], plans[1], edge_samples, trig


def lanes_of(shape, axis):
    return lax.broadcasted_iota(jnp.int32, shape, axis).astype(f32)


def block_of(table, trig, at, bins):
    code = table[at]
    b = lax.shift_right_logical(code, 2)
    ut = lax.bitwise_and(code, 3)
    return b, ut, trig[b], trig[bins + b], (ut * TILE).astype(f32)


def split3(x):
    hi = x.astype(bf16)
    rest = x - hi.astype(f32)
    mid = rest.astype(bf16)
    return [hi, mid, (rest - mid.astype(f32)).astype(bf16)]


def bump(t):
    falloff = jnp.maximum(1.0 - t * t, 0.0)
    return falloff * falloff, -4.0 * t * falloff


def z_weights(z0, rows, u, s, c, samples):
    centre = 0.5 * NZ + u * s
    kz, kzd = bump((z0 + lanes_of((rows, TILE), 0)) - centre)
    return centre, kz, kzd * (-u * c * (1.0 / samples))


def extract_kernel(
    groups, length, samples, bins, planes, n_dom,
    table, trig, volume, above, ctf, slope, pairs, field, vhi, vlo, out, sem,
):
    depth = field.shape[0]
    xt_count = vhi.shape[0]
    ut_count = samples // TILE
    dom = lax.axis_index("dom")
    device = lax.axis_index("gz") * n_dom + dom
    row = device * length
    first = device * planes
    z0, z1 = first.astype(f32), (first + planes).astype(f32)

    own = pltpu.make_async_copy(
        volume.at[pl.ds(dom * planes, planes)], field.at[pl.ds(0, planes)], sem.at[0]
    )
    own.start()

    @pl.when(dom < n_dom - 1)
    def _():
        copy = pltpu.make_async_copy(
            volume.at[pl.ds((dom + 1) * planes, 1)], field.at[pl.ds(planes, 1)], sem.at[1]
        )
        copy.start()
        copy.wait()

    @pl.when(dom == n_dom - 1)
    def _():
        copy = pltpu.make_async_copy(above, field.at[pl.ds(planes, 1)], sem.at[1])
        copy.start()
        copy.wait()

    for z in range(planes + 1, depth):
        field[z] = jnp.zeros(field.shape[1:], f32)
    out[...] = jnp.zeros_like(out)
    own.wait()
    for xt in range(xt_count):
        stacked = jnp.concatenate(
            [field[:, r, xt * TILE : (xt + 1) * TILE] for r in range(4)], 0
        )
        hi = stacked.astype(bf16)
        vhi[xt] = hi
        vlo[xt] = (stacked - hi.astype(f32)).astype(bf16)

    def step(j, carry):
        xt = table[row + 1 + j]
        hi_rows, lo_rows = vhi[xt], vlo[xt]
        xx = lanes_of((TILE, TILE), 0) + (xt * TILE).astype(f32)
        for k in range(GROUP):
            at = row + 1 + groups + j * GROUP + k
            b, ut, s, c, base = block_of(table, trig, at, bins)
            u = lanes_of((1, TILE), 1) + base
            centre, kz, kzd = z_weights(z0, depth, u, s, c, samples)
            below = s < 0.0
            place = centre * jnp.where(below, -1.0, 1.0)
            least, most = jnp.where(below, -z1, z0), jnp.where(below, -z0, z1)
            own = jnp.where((place >= least) & (place < most), 1.0, 0.0)
            kz, kzd = kz * own, kzd * own
            kx, kxd = bump(xx - u * c)
            weights = jnp.concatenate([kx, kxd * (u * s * (1.0 / samples))], 1)
            whi = weights.astype(bf16)
            wlo = (weights - whi.astype(f32)).astype(bf16)
            sampled = (
                jnp.dot(hi_rows, whi, preferred_element_type=f32)
                + jnp.dot(lo_rows, whi, preferred_element_type=f32)
                + jnp.dot(hi_rows, wlo, preferred_element_type=f32)
            )
            leading, second = [], []
            for r in range(4):
                direct = sampled[r * depth : (r + 1) * depth, :TILE]
                tilted = sampled[r * depth : (r + 1) * depth, TILE:]
                leading.append(jnp.sum(direct * kz, axis=0, keepdims=True))
                second.append(jnp.sum(direct * kzd + tilted * kz, axis=0, keepdims=True))
            span = pl.ds(pl.multiple_of((b * ut_count + ut) * 8, 8), 8)
            out[span, :] = out[span, :] + jnp.concatenate(leading + second, 0)
        return carry

    lax.fori_loop(0, table[row], step, 0)

    slope[...] = jnp.zeros_like(slope)
    square, mixed = [], []
    for y in range(2):
        for ut in range(ut_count):
            square_sum, mixed_sum = 0.0, 0.0
            for r in (y, 2 + y):
                direct = out[pl.ds(ut * 8 + r, bins, stride=ut_count * 8), :].astype(bf16).astype(f32)
                tilted = out[pl.ds(ut * 8 + 4 + r, bins, stride=ut_count * 8), :].astype(bf16)
                at = (r * ut_count + ut) * TILE
                slope[bins:, at : at + TILE] = tilted
                tilted = tilted.astype(f32)
                square_sum = square_sum + tilted * tilted
                mixed_sum = mixed_sum - direct * tilted
            square.append(square_sum)
            mixed.append(mixed_sum)
    moments = jnp.concatenate([jnp.concatenate(square, 1), jnp.concatenate(mixed, 1)], 0)
    flat = jnp.concatenate([ctf[:, 0, :], ctf[:, 1, :]], 1)
    product = lax.dot_general(
        flat * flat, moments, NT, precision=lax.Precision.HIGHEST, preferred_element_type=f32
    )
    pairs[...] = jnp.concatenate(split3(product), 1)


def particle_kernel(width, mine, n_gz, n_dom, *refs):
    blocks = refs[: 2 * n_gz]
    ctf, slope, pairs, weighted, parts, bins_row, packed, sems = refs[2 * n_gz :]
    n_z = n_dom // 2
    gz, dom = lax.axis_index("gz"), lax.axis_index("dom")
    z, core = lax.shift_right_logical(dom, 1), lax.bitwise_and(dom, 1)
    copies = []
    for c in range(2):
        for j in range(n_gz):
            for k in range(n_z):
                owner = ((gz ^ j) * n_z + (z ^ k)) * 2 + (core ^ c)
                start = pl.multiple_of(owner * mine, mine)
                copies.append(
                    pltpu.make_async_copy(
                        blocks[c * n_gz + j].at[pl.ds(k * mine, mine), :],
                        packed.at[pl.ds(start, mine), :],
                        sems.at[len(copies)],
                    )
                )
    for copy in copies:
        copy.start()
    for copy in copies:
        copy.wait()

    total = packed.shape[0]
    count = min(CHUNK, total)
    both = slope.shape[0]
    bins = both // 2
    flat = jnp.concatenate([ctf[:, 0, :], ctf[:, 1, :]], 1)
    ctf_hi = flat.astype(bf16)
    ctf_lo = (flat - ctf_hi.astype(f32)).astype(bf16)
    upper = jnp.where(lanes_of((8, both), 1) >= bins, 1.0, 0.0)
    select = jnp.where(lanes_of((8, both), 0) == upper, 1.0, 0.0).astype(bf16)
    select = jnp.concatenate([select] * 3, 1)

    def step(i, carry):
        span = pl.ds(pl.multiple_of(i * count, count), count)
        ids = packed[span, width:]
        classes = ids[:, 0:1].astype(f32)
        onehot_class = jnp.where(lanes_of((count, NCTF), 1) == classes, 1.0, 0.0).astype(bf16)
        bin_of = ids[:, 1:2].astype(f32)
        lane = lanes_of((count, both), 1)
        chosen = (lane == bin_of) | (lane == bin_of + bins)
        contrast = jnp.dot(onehot_class, ctf_hi, preferred_element_type=f32) + jnp.dot(
            onehot_class, ctf_lo, preferred_element_type=f32
        )
        contrast = jnp.concatenate([contrast, contrast], 1)
        w = contrast * packed[span, :width].astype(f32)
        whi = w.astype(bf16)
        wlo = (w - whi.astype(f32)).astype(bf16)
        weighted[span, :] = whi
        slopes = slope[...]
        along = lax.dot_general(whi, slopes, NT, preferred_element_type=f32) + lax.dot_general(
            wlo, slopes, NT, preferred_element_type=f32
        )
        tables = jnp.dot(onehot_class, pairs[...], preferred_element_type=f32)
        tables = tables[:, :both] + tables[:, both : 2 * both] + tables[:, 2 * both :]
        terms = jnp.concatenate(split3(jnp.where(chosen, along + tables, 0.0)), 1)
        rows = lax.dot_general(select, terms, NT, preferred_element_type=f32)
        for n in range(2):
            row = rows[n : n + 1]
            for q in range(count // TILE):
                at = n * (total // TILE) + i * (count // TILE) + q
                parts[pl.ds(at, 1), :] = row[:, q * TILE : (q + 1) * TILE]
        pick = jnp.where(lanes_of((8, TILE), 1) == 1.0, 1.0, 0.0).astype(bf16)
        bins_row[:, span] = lax.dot_general(pick, ids, NT, preferred_element_type=f32)[0:1]
        return carry

    lax.fori_loop(0, total // count, step, 0)


def plain_kernel(bins_row, weighted, plain):
    count = weighted.shape[0]
    chunk = min(CHUNK, count)
    sums = jnp.zeros(plain.shape, f32)
    for i in range(count // chunk):
        span = slice(i * chunk, (i + 1) * chunk)
        belongs = lanes_of((plain.shape[0], chunk), 0) == bins_row[:, span]
        onehot = jnp.where(belongs, 1.0, 0.0).astype(bf16)
        sums = sums + jnp.dot(onehot, weighted[span, :], preferred_element_type=f32)
    plain[...] = sums


def spread_kernel(
    groups, length, planes, samples, edge_samples, mine, n_gz, n_dom,
    table, trig, bins_row, weighted, plain, *refs
):
    parts = refs[:n_gz]
    pose, out, sums, total, poses = refs[n_gz:]
    bins, width = plain.shape
    tiles = width // TILE
    ut_count = samples // TILE
    depth = total.shape[1] // 4
    count = bins_row.shape[1]
    chunk = min(CHUNK, count)
    device = lax.axis_index("gz") * n_dom + lax.axis_index("dom")
    row = device * length
    z0 = (device * planes).astype(f32)

    rows = count // TILE
    scalars = sum([part[...] for part in parts[1:]], parts[0][...])
    square, pull = scalars[:rows], scalars[rows:]
    curvature = square + EPS
    shift = jnp.zeros_like(square)
    for _ in range(ITERS):
        shift = shift + 0.5 * (pull - shift * square) / curvature
    poses[...] = shift * jnp.sqrt(curvature)
    first = device * mine
    line = poses[pl.ds(lax.div(first, TILE), 1), :]
    pose[...] = pltpu.roll(line, TILE - lax.rem(first, TILE), 1)[:, :mine]
    shift = jnp.concatenate([shift[q : q + 1] for q in range(rows)], 1)

    slope_sum = jnp.zeros((bins, width), f32)
    for i in range(count // chunk):
        span = slice(i * chunk, (i + 1) * chunk)
        belongs = lanes_of((bins, chunk), 0) == bins_row[:, span]
        scaled = jnp.where(belongs, shift[:, span], 0.0)
        hi = scaled.astype(bf16)
        lo = (scaled - hi.astype(f32)).astype(bf16)
        rows = weighted[span, :]
        slope_sum = (
            slope_sum
            + jnp.dot(hi, rows, preferred_element_type=f32)
            + jnp.dot(lo, rows, preferred_element_type=f32)
        )
    for q in range(tiles):
        sums[q] = plain[:, q * TILE : (q + 1) * TILE]
        sums[tiles + q] = slope_sum[:, q * TILE : (q + 1) * TILE]
    total[...] = jnp.zeros_like(total)

    def step(j, carry):
        xt = table[row + 1 + j]
        xx = lanes_of((TILE, TILE), 1) + (xt * TILE).astype(f32)
        left, right = [], []
        for k in range(GROUP):
            at = row + 1 + groups + j * GROUP + k
            b, ut, s, c, base = block_of(table, trig, at, bins)
            u = lanes_of((1, TILE), 1) + base
            _, kz, kzd = z_weights(z0, depth, u, s, c, samples)
            first, second = [], []
            for r in range(4):
                direct = sums[r * ut_count + ut, pl.ds(b, 1), :]
                tilted = sums[tiles + r * ut_count + ut, pl.ds(b, 1), :]
                first.append(kz * direct + kzd * tilted)
                second.append(kz * tilted)
            left += [jnp.concatenate(first, 0), jnp.concatenate(second, 0)]
            uu = lanes_of((TILE, TILE), 0) + base
            kx, kxd = bump(xx - uu * c)
            right += [kx.astype(bf16), (kxd * (uu * (s * (1.0 / samples)))).astype(bf16)]
        left = jnp.concatenate(left, 1)
        hi = left.astype(bf16)
        lo = (left - hi.astype(f32)).astype(bf16)
        both = jnp.dot(
            jnp.concatenate([hi, lo], 0), jnp.concatenate(right, 0), preferred_element_type=f32
        )
        total[xt] = total[xt] + both[: 4 * depth] + both[4 * depth :]
        return carry

    lax.fori_loop(0, table[row], step, 0)
    tail = row + 1 + groups * (1 + GROUP)

    def edge(j, carry):
        left, right = [], []
        rest = jnp.zeros((TILE - edge_samples, TILE), f32)
        for k in range(GROUP):
            b, _, s, c, _ = block_of(table, trig, tail + 1 + j * GROUP + k, bins)
            u = lanes_of((1, TILE), 1)
            _, kz, kzd = z_weights(z0, 1, u, s, c, samples)
            direct = jnp.concatenate(
                [sums[r * ut_count, pl.ds(b, 1), :] for r in range(4)], 0
            )
            tilted = jnp.concatenate(
                [sums[tiles + r * ut_count, pl.ds(b, 1), :] for r in range(4)], 0
            )
            left += [kz * direct + kzd * tilted, kz * tilted]
            uu = lanes_of((edge_samples, TILE), 0)
            kx, kxd = bump(lanes_of((edge_samples, TILE), 1) - uu * c)
            for part in (kx, kxd * (uu * (s * (1.0 / samples)))):
                right.append(jnp.concatenate([part, rest], 0).astype(bf16))
        left = jnp.concatenate(left, 1)
        hi = left.astype(bf16).astype(f32)
        split = jnp.concatenate([hi, left - hi], 0).astype(bf16)
        both = jnp.dot(split, jnp.concatenate(right, 0), preferred_element_type=f32)
        return carry + both[:4] + both[4:]

    extra = lax.fori_loop(0, table[tail], edge, jnp.zeros((4, TILE), f32))
    for xt in range(total.shape[0]):
        for r in range(4):
            out[:, r, xt * TILE : (xt + 1) * TILE] = total[xt, r * depth : r * depth + planes, :]
    out[0, :, :TILE] = out[0, :, :TILE] + extra


def swap(x, axis, size, distance):
    return lax.ppermute(x, axis, [(i, i ^ distance) for i in range(size)])


def local(volume, observed, ctf_table, ctf_class, bin_ids):
    slab, rows, columns = volume.shape
    mine, _, samples = observed.shape
    n_gz, n_dom = lax.axis_size("gz"), lax.axis_size("dom")
    devices = n_gz * n_dom
    bins = NB_DEV * n_dom
    planes = NZ // devices
    count = mine * devices
    width = rows * samples
    xt_count, ut_count = columns // TILE, samples // TILE
    ids = jnp.stack([ctf_class, bin_ids], 1).astype(bf16)
    ids = jnp.pad(ids, ((0, 0), (0, TILE - 2)))
    packed = jnp.concatenate([observed.reshape(mine, width), ids], 1)
    n_z = n_dom // 2
    above = lax.ppermute(volume[:1], "gz", [(i, i - 1) for i in range(1, n_gz)])
    column = jnp.concatenate(
        [packed] + [swap(packed, "dom", n_dom, 2 * k) for k in range(1, n_z)], 0
    )
    column, above = lax.optimization_barrier((column, above))
    planes_of = [column] + [swap(column, "gz", n_gz, j) for j in range(1, n_gz)]

    extract_plan, spread_plan, edge_samples, trig = make_plan(devices, bins, samples, columns)
    trig = jnp.asarray(trig)
    depth_in = round_up(planes + 1, 8)

    smem = pl.BlockSpec(memory_space=pltpu.SMEM)
    vmem = pl.BlockSpec(memory_space=pltpu.VMEM)
    hbm = pl.BlockSpec(memory_space=pl.ANY)
    params = pltpu.CompilerParams(vmem_limit_bytes=VMEM)
    table, groups = extract_plan
    slope, pairs = pl.pallas_call(
        functools.partial(
            extract_kernel, groups, table.shape[1], samples, bins, planes, n_dom
        ),
        out_shape=[
            jax.ShapeDtypeStruct((2 * bins, width), bf16),
            jax.ShapeDtypeStruct((NCTF, 6 * bins), bf16),
        ],
        in_specs=[smem, smem, hbm, hbm, vmem],
        out_specs=[vmem, vmem],
        scratch_shapes=[
            pltpu.VMEM((depth_in, rows, columns), f32),
            pltpu.VMEM((xt_count, rows * depth_in, TILE), bf16),
            pltpu.VMEM((xt_count, rows * depth_in, TILE), bf16),
            pltpu.VMEM((bins * ut_count * 2 * rows, TILE), f32),
            pltpu.SemaphoreType.DMA((2,)),
        ],
        compiler_params=params,
        cost_estimate=pl.CostEstimate(flops=6 * 10**9, bytes_accessed=2**20, transcendentals=0),
        name="extract",
    )(jnp.asarray(table.reshape(-1)), trig, volume, above, ctf_table)

    planes_of, slope = lax.optimization_barrier((planes_of, slope))
    gathered = planes_of + [swap(part, "dom", n_dom, 1) for part in planes_of]
    weighted, parts, bins_row = pl.pallas_call(
        functools.partial(particle_kernel, width, mine, n_gz, n_dom),
        out_shape=[
            jax.ShapeDtypeStruct((count, width), bf16),
            jax.ShapeDtypeStruct((2 * count // TILE, TILE), f32),
            jax.ShapeDtypeStruct((1, count), f32),
        ],
        in_specs=[hbm] * len(gathered) + [vmem] * 3,
        out_specs=[vmem] * 3,
        scratch_shapes=[
            pltpu.VMEM((count, width + TILE), bf16),
            pltpu.SemaphoreType.DMA((devices,)),
        ],
        compiler_params=params,
        name="particles",
    )(*gathered, ctf_table, slope, pairs)

    plain = pl.pallas_call(
        plain_kernel,
        out_shape=jax.ShapeDtypeStruct((bins, width), f32),
        in_specs=[vmem, vmem],
        out_specs=vmem,
        compiler_params=params,
        cost_estimate=pl.CostEstimate(flops=2 * 10**9, bytes_accessed=2**21, transcendentals=0),
        name="plain_sums",
    )(bins_row, weighted)

    parts = sum([swap(parts, "dom", n_dom, k) for k in range(1, n_dom)], parts)
    parts = [parts] + [swap(parts, "gz", n_gz, j) for j in range(1, n_gz)]

    depth = round_up(planes, 8)
    table, groups = spread_plan
    pose, spread = pl.pallas_call(
        functools.partial(
            spread_kernel, groups, table.shape[1], planes, samples, edge_samples, mine, n_gz, n_dom
        ),
        out_shape=[
            jax.ShapeDtypeStruct((1, mine), f32),
            jax.ShapeDtypeStruct((planes, rows, columns), f32),
        ],
        in_specs=[smem, smem] + [vmem] * (3 + n_gz),
        out_specs=[vmem, vmem],
        scratch_shapes=[
            pltpu.VMEM((2 * width // TILE, bins, TILE), f32),
            pltpu.VMEM((xt_count, rows * depth, TILE), f32),
            pltpu.VMEM((count // TILE, TILE), f32),
        ],
        compiler_params=params,
        name="spread",
    )(jnp.asarray(table.reshape(-1)), trig, bins_row, weighted, plain, *parts)
    pose = pose.reshape(mine)
    return pose, spread


def solution(mesh):
    return jax.shard_map(
        local,
        mesh=mesh,
        in_specs=(
            P("gz", None, None),
            P(("gz", "dom"), None, None),
            P(),
            P(("gz", "dom")),
            P(("gz", "dom")),
        ),
        out_specs=(P(("gz", "dom")), P(("gz", "dom"), None, None)),
        check_vma=False,
    )
```

time: 75.6 us -> 61.6 us (0.81)
  other arithmetic: 7.11 us -> 1.4 us
  local copies, waits for them, and re-layouts: 8.17 us -> 3.46 us
  Pallas kernels: 28.7 us -> 25.2 us
  waiting for transfers between devices: 4.55 us -> 5.9 us
  matrix products: 1.1 us -> 0 us
    pallas_call x2, Pallas kernels: 20 us -> 16.8 us  [the longest x1 8.55 us: local(): pl.pallas_call(functools.partial(spread_kernel, groups, table.shape[1], p...]
    ppermute x1, waiting for transfers between devices: 0.01 us -> 1.92 us  [local(): above = lax.ppermute(volume[:1], 'gz', [(i, i - 1) for i in range(1, n_gz)])]
    convert_element_type x2 -> x0, other arithmetic: 1.37 us -> none  [the longest x1 0.71 us: local(): field_lo = (field - field_hi).astype(bf16)]
    another operation x3 -> x0, other arithmetic: 1.23 us -> none  [the longest x1 0.66 us: local(): place = jnp.stack([gz, dom // 2, dom % 2]).astype(jnp.int32)]
    squeeze x1 -> x0, local copies, waits for them, and re-layouts: 1.21 us -> none  [local(): lax.dynamic_index_in_dim(jnp.asarray(table), device, 0, keepdims=False)]
    reduce_precision x1 -> x0, other arithmetic: 1.18 us -> none  [local(): slices = lax.reduce_precision(slices, 8, 7)]
    dot_general x1 -> x0, matrix products: 1.1 us -> none  [local(): lax.dot_general((ctf_table * ctf_table).reshape(NCTF, -1), squares.reshap...]
    mul x1 -> x0, other arithmetic: 1.02 us -> none  [local(): ctf_table * ctf_table]
  transfers between devices with their start and end apart: 21 -> 21, of which waited for: 3 -> 10; matrix products, arithmetic and copies ran while one was open for 17% -> 1% of each run, Pallas kernels for 17% -> 18%
where the time goes in v4:
time: 61.6 us; the launch traced here: 61.1 us
  Pallas kernels  25.2 us (41%)
  starting transfers between devices  24.4 us (40%)
  waiting for transfers between devices  5.9 us (10%)
  local copies, waits for them, and re-layouts  3.46 us (6%)
  other arithmetic  1.4 us (2%)
  between operations  0.79 us (1%)
    ppermute x20, starting transfers between devices, swap(): return lax.ppermute(x, axis, [(i, i ^ distance) for i in range(size)])  21 us
    pallas_call x1, Pallas kernels, local(): pl.pallas_call(functools.partial(spread_kernel, groups, table.shape[1], p...  8.55 us
    pallas_call x1, Pallas kernels, local(): pl.pallas_call(functools.partial(extract_kernel, groups, table.shape[1],...  8.24 us
    pallas_call x1, Pallas kernels, local(): pl.pallas_call(functools.partial(particle_kernel, width, mine, n_gz, n_do...  5.85 us
    ppermute x20, waiting for transfers between devices, swap(): return lax.ppermute(x, axis, [(i, i ^ distance) for i in range(size)])  3.98 us
    ppermute x1, starting transfers between devices, local(): above = lax.ppermute(volume[:1], 'gz', [(i, i - 1) for i in range(1, n_gz)])  3.33 us
    unnamed x27, local copies, waits for them, and re-layouts  2.67 us
    pallas_call x1, Pallas kernels, local(): pl.pallas_call(plain_kernel, out_shape=jax.ShapeDtypeStruct((bins, width)...  2.53 us
  transfers between devices with their start and end apart: 21, of which 10 were waited for; matrix products, arithmetic and copies ran while one was open for 1% of the time, Pallas kernels for 18%

profile of v4, /device:TPU:4, one launch (start us, length us, event | category | flops | bytes accessed | tf_op | source)
XLA Modules:
  0.0 61.1 jit_solution(4251557568720215434)
XLA Ops:
  0.6 0.7 %convert_bitcast_fusion = (bf16[16,1]{0,1:T(2,128)(2,1)S(1)}, bf16[16,1]{0,1:T(2,128)(2,1)S(1)}) fusion(s32[16]{0:T(128)} %param.12, s32[16]{0:T(128)} %param.11), kind=kLoop, calls=%fused_computation.4 | loop fusion | flops 32 | bytes 192 | tf_op jit(solution)/shard_map/stack | solution.py:428
  1.3 0.1 copy.12
  1.4 0.8 %copy.13 = bf16[2,8,4,384]{3,1,2,0:T(8,128)(2,1)S(1)} copy(bf16[2,8,4,384]{3,2,1,0:T(4,128)(2,1)} %bitcast.9) | data formatting | bytes 98304
  2.2 3.7 %collective-permute-start.2 = (bf16[16,1664]{1,0:T(8,128)(2,1)S(1)}, bf16[16,1664]{1,0:T(8,128)(2,1)S(1)}, u32[]{:S(2)}, u32[]{:S(2)}) collective-permute-start(bf16[16,1664]{1,0:T(8,128)(2,1)S(1)} %pad_maximum_fusion.1), channel_id=1, source_target_pairs={{0,6},{1,7},{2,4},{3,5},{4,2},{5,3},{6,0},{7,1},{8,14},{9,15},{10,... | collective-permute-start | bytes 159752 | tf_op jit(solution)/shard_map/ppermute | solution.py:415
  5.9 0.0 collective-permute-start.1
  5.9 0.8 %collective-permute-start = (bf16[16,1664]{1,0:T(8,128)(2,1)S(1)}, bf16[16,1664]{1,0:T(8,128)(2,1)S(1)}, u32[]{:S(2)}, u32[]{:S(2)}) collective-permute-start(bf16[16,1664]{1,0:T(8,128)(2,1)S(1)} %pad_maximum_fusion.1), channel_id=1, source_target_pairs={{0,2},{1,3},{2,0},{3,1},{4,6},{5,7},{6,4},{7,5},{8,10},{9,11},{10,... | collective-permute-start | bytes 159752 | tf_op jit(solution)/shard_map/ppermute | solution.py:415
  6.7 0.7 %slice.3 = f32[1,4,384]{2,1,0:T(4,128)S(1)} slice(f32[192,4,384]{2,1,0:T(4,128)} %volume.1), slice={[0:1], [0:4], [0:384]} | slice | bytes 12288 | tf_op jit(solution)/shard_map/slice | solution.py:432
  7.4 3.3 %collective-permute-start.3 = (f32[1,4,384]{2,1,0:T(4,128)S(1)}, f32[1,4,384]{2,1,0:T(4,128)S(1)}, u32[]{:S(2)}, u32[]{:S(2)}) collective-permute-start(f32[1,4,384]{2,1,0:T(4,128)S(1)} %slice.3), channel_id=1, source_target_pairs={{8,0},{16,8},{24,16},{9,1},{17,9},{25,17},{10,2},{18,10},{26,18},{... | collective-permute-start | bytes 18440 | tf_op jit(solution)/shard_map/ppermute | solution.py:432
  10.7 0.0 collective-permute-done.2
  10.7 0.2 collective-permute-done.1
  10.9 0.0 collective-permute-done
  11.0 1.9 %collective-permute-done.3.above = f32[1,4,384]{2,1,0:T(4,128)S(1)} collective-permute-done((f32[1,4,384]{2,1,0:T(4,128)S(1)}, f32[1,4,384]{2,1,0:T(4,128)S(1)}, u32[]{:S(2)}, u32[]{:S(2)}) %collective-permute-start.3) | collective-permute-done | bytes 6176 | tf_op jit(solution)/shard_map/ppermute | solution.py:432
  12.9 2.3 %collective-permute-start.6 = (bf16[64,1664]{1,0:T(8,128)(2,1)S(1)}, bf16[64,1664]{1,0:T(8,128)(2,1)S(1)}, u32[]{:S(2)}, u32[]{:S(2)}) collective-permute-start(bf16[64,1664]{1,0:T(8,128)(2,1)S(1)} %pad_maximum_fusion.refs_0_), channel_id=1, source_target_pairs={{0,24},{8,16},{16,8},{24,0},{1,25},{9,17},{17,9},{25,1},{2,26},{10... | collective-permute-start | bytes 638984 | tf_op jit(solution)/shard_map/ppermute | solution.py:415
  15.2 0.0 collective-permute-start.5
  15.2 1.2 %collective-permute-start.4 = (bf16[64,1664]{1,0:T(8,128)(2,1)S(1)}, bf16[64,1664]{1,0:T(8,128)(2,1)S(1)}, u32[]{:S(2)}, u32[]{:S(2)}) collective-permute-start(bf16[64,1664]{1,0:T(8,128)(2,1)S(1)} %pad_maximum_fusion.refs_0_), channel_id=1, source_target_pairs={{0,8},{8,0},{16,24},{24,16},{1,9},{9,1},{17,25},{25,17},{2,10},{10... | collective-permute-start | bytes 638984 | tf_op jit(solution)/shard_map/ppermute | solution.py:415
  16.4 0.0 copy-done.12
  16.4 8.2 %extract.1 = (bf16[128,1536]{1,0:T(8,128)(2,1)}, bf16[32,384]{1,0:T(8,128)(2,1)}) custom-call(s32[1984]{0:T(1024)} %constant.10.clone.table, f32[128]{0:T(128)} %constant.9.clone.trig, f32[192,4,384]{2,1,0:T(4,128)} %volume.1, f32[1,4,384]{2,1,0:T(4,128)} %copy-done.12, f32[32,2,384]{2,1,0:T(2,128)} %refs_8_.1), custom_call_target="tpu_custom_call" | custom-call | flops 6000000000 | bytes 1048576 | tf_op jit(solution)/shard_map/extract/pallas_call | solution.py:448
  24.6 0.0 collective-permute-done.6.refs_3_
  24.7 0.0 copy-start.1
  24.7 0.0 collective-permute-done.5.refs_2_
  24.7 0.0 copy-start.2
  24.7 0.0 collective-permute-done.4.refs_1_
  24.7 0.0 copy-start.3
  24.7 0.0 copy-done
  24.7 0.1 collective-permute-start.7
  24.8 0.5 collective-permute-start.8
  25.3 0.1 collective-permute-start.9
  25.4 0.4 collective-permute-start.10
  25.8 0.4 collective-permute-done.7.refs_4_
  26.2 0.3 collective-permute-done.8.refs_5_
  26.6 0.3 collective-permute-done.9.refs_6_
  26.9 0.3 collective-permute-done.10.refs_7_
  27.2 0.0 copy-done.1
  27.2 0.0 copy-done.2
  27.2 0.1 copy-done.5
  27.3 0.3 copy-done.6
  27.5 0.3 copy-done.7
  27.8 5.8 %particles.1 = (bf16[512,1536]{1,0:T(8,128)(2,1)}, f32[8,128]{1,0:T(8,128)}, f32[1,512]{1,0:T(1,128)}) custom-call(bf16[64,1664]{1,0:T(8,128)(2,1)} %copy-done, bf16[64,1664]{1,0:T(8,128)(2,1)} %copy-done.3, bf16[64,1664]{1,0:T(8,128)(2,1)} %copy-done.2, bf16[64,1664]{1,0:T(8,128)(2,1)} %copy-done.1, bf16[64,1664]{1,0:T(8,128)(2,1)} %copy-done.4, ...), custom_call_target="tpu_custom_call" | custom-call | tf_op jit(solution)/shard_map/particles/pallas_call | solution.py:472
  33.7 2.1 %collective-permute-start.17 = (f32[8,128]{1,0:T(8,128)}, f32[8,128]{1,0:T(8,128)S(1)}, u32[]{:S(2)}, u32[]{:S(2)}) collective-permute-start(f32[8,128]{1,0:T(8,128)} %get-tuple-element.27), channel_id=1, source_target_pairs={{0,7},{1,6},{2,5},{3,4},{4,3},{5,2},{6,1},{7,0},{8,15},{9,14},{10,... | collective-permute-start | bytes 12296 | tf_op jit(solution)/shard_map/ppermute | solution.py:415
  35.8 1.6 %collective-permute-start.16 = (f32[8,128]{1,0:T(8,128)}, f32[8,128]{1,0:T(8,128)S(1)}, u32[]{:S(2)}, u32[]{:S(2)}) collective-permute-start(f32[8,128]{1,0:T(8,128)} %get-tuple-element.27), channel_id=1, source_target_pairs={{0,6},{1,7},{2,4},{3,5},{4,2},{5,3},{6,0},{7,1},{8,14},{9,15},{10,... | collective-permute-start | bytes 12296 | tf_op jit(solution)/shard_map/ppermute | solution.py:415
  37.4 0.0 collective-permute-start.15
  37.4 2.6 %collective-permute-start.14 = (f32[8,128]{1,0:T(8,128)}, f32[8,128]{1,0:T(8,128)S(1)}, u32[]{:S(2)}, u32[]{:S(2)}) collective-permute-start(f32[8,128]{1,0:T(8,128)} %get-tuple-element.27), channel_id=1, source_target_pairs={{0,4},{1,5},{2,6},{3,7},{4,0},{5,1},{6,2},{7,3},{8,12},{9,13},{10,... | collective-permute-start | bytes 12296 | tf_op jit(solution)/shard_map/ppermute | solution.py:415
  39.9 0.0 collective-permute-start.13
  40.0 0.0 collective-permute-done.17
  40.0 1.8 %collective-permute-start.12 = (f32[8,128]{1,0:T(8,128)}, f32[8,128]{1,0:T(8,128)S(1)}, u32[]{:S(2)}, u32[]{:S(2)}) collective-permute-start(f32[8,128]{1,0:T(8,128)} %get-tuple-element.27), channel_id=1, source_target_pairs={{0,2},{1,3},{2,0},{3,1},{4,6},{5,7},{6,4},{7,5},{8,10},{9,11},{10,... | collective-permute-start | bytes 12296 | tf_op jit(solution)/shard_map/ppermute | solution.py:415
  41.8 0.0 collective-permute-done.16
  41.8 0.0 collective-permute-start.11
  41.8 0.0 collective-permute-done.15
  41.8 0.3 collective-permute-done.14
  42.1 1.1 %collective-permute-done.13 = f32[8,128]{1,0:T(8,128)S(1)} collective-permute-done((f32[8,128]{1,0:T(8,128)}, f32[8,128]{1,0:T(8,128)S(1)}, u32[]{:S(2)}, u32[]{:S(2)}) %collective-permute-start.13) | collective-permute-done | bytes 4128 | tf_op jit(solution)/shard_map/ppermute | solution.py:415
  43.2 0.6 collective-permute-done.12
  43.8 0.0 collective-permute-done.11
  43.8 0.7 %add_add_fusion.refs_0_ = f32[8,128]{1,0:T(8,128)S(1)} fusion(f32[8,128]{1,0:T(8,128)S(1)} %collective-permute-done.17, f32[8,128]{1,0:T(8,128)S(1)} %collective-permute-done.16, f32[8,128]{1,0:T(8,128)S(1)} %collective-permute-done.15, f32[8,128]{1,0:T(8,128)S(1)} %collective-permute-done.14, f32[8,128]{1,0:T(8,128)S(1)} %collective-permute-done.13, ...), kind=kLoop, calls=%fused_computation.2 | loop fusion | flops 7168 | bytes 36864 | tf_op jit(solution)/shard_map/add | solution.py:499
  44.5 3.3 %collective-permute-start.20 = (f32[8,128]{1,0:T(8,128)S(1)}, f32[8,128]{1,0:T(8,128)S(1)}, u32[]{:S(2)}, u32[]{:S(2)}) collective-permute-start(f32[8,128]{1,0:T(8,128)S(1)} %add_add_fusion.refs_0_), channel_id=1, source_target_pairs={{0,24},{8,16},{16,8},{24,0},{1,25},{9,17},{17,9},{25,1},{2,26},{10... | collective-permute-start | bytes 12296 | tf_op jit(solution)/shard_map/ppermute | solution.py:415
  47.8 0.0 collective-permute-start.19
  47.8 0.6 %collective-permute-start.18 = (f32[8,128]{1,0:T(8,128)S(1)}, f32[8,128]{1,0:T(8,128)S(1)}, u32[]{:S(2)}, u32[]{:S(2)}) collective-permute-start(f32[8,128]{1,0:T(8,128)S(1)} %add_add_fusion.refs_0_), channel_id=1, source_target_pairs={{0,8},{8,0},{16,24},{24,16},{1,9},{9,1},{17,25},{25,17},{2,10},{10... | collective-permute-start | bytes 12296 | tf_op jit(solution)/shard_map/ppermute | solution.py:415
  48.4 2.5 %plain_sums.1.plain = f32[64,1536]{1,0:T(8,128)} custom-call(f32[1,512]{1,0:T(1,128)} %get-tuple-element.25.bins_row, bf16[512,1536]{1,0:T(8,128)(2,1)} %get-tuple-element.26.weighted), custom_call_target="tpu_custom_call" | custom-call | flops 2000000000 | bytes 2097152 | tf_op jit(solution)/shard_map/plain_sums/pallas_call | solution.py:489
  50.9 0.0 collective-permute-done.20.refs_3_
  50.9 0.4 collective-permute-done.19.refs_2_
  51.4 0.0 collective-permute-done.18.refs_1_
  51.4 0.2 copy-done.9
  51.5 0.4 copy-done.10
  52.0 0.6 copy-done.11
  52.5 8.5 %spread.1 = (f32[1,16]{1,0:T(1,128)}, f32[24,4,384]{2,1,0:T(4,128)}) custom-call(s32[3008]{0:T(1024)} %constant.11.clone.table, f32[128]{0:T(128)} %constant.9.clone.trig, f32[1,512]{1,0:T(1,128)} %get-tuple-element.25.bins_row, bf16[512,1536]{1,0:T(8,128)(2,1)} %get-tuple-element.26.weighted, f32[64,1536]{1,0:T(8,128)} %plain_sums.1.plain, ...), custom_call_target="tpu_custom_call" | custom-call | tf_op jit(solution)/shard_map/spread/pallas_call | solution.py:504
  (17 shorter events, 0.1 us)
Async XLA Ops:
  2.2 8.5 %collective-permute-start.2 = (bf16[16,1664]{1,0:T(8,128)(2,1)S(1)}, bf16[16,1664]{1,0:T(8,128)(2,1)S(1)}, u32[]{:S(2)}, u32[]{:S(2)}) collective-permute-start(bf16[16,1664]{1,0:T(8,128)(2,1)S(1)} %pad_maximum_fusion.1), channel_id=1, source_target_pairs={{0,6},{1,7},{2,4},{3,5},{4,2},{5,3},{6,0},{7,1},{8,14},{9,15},{10,... | collective-permute-start | bytes 159752 | tf_op jit(solution)/shard_map/ppermute | solution.py:415
  5.9 5.0 %collective-permute-start.1 = (bf16[16,1664]{1,0:T(8,128)(2,1)S(1)}, bf16[16,1664]{1,0:T(8,128)(2,1)S(1)}, u32[]{:S(2)}, u32[]{:S(2)}) collective-permute-start(bf16[16,1664]{1,0:T(8,128)(2,1)S(1)} %pad_maximum_fusion.1), channel_id=1, source_target_pairs={{0,4},{1,5},{2,6},{3,7},{4,0},{5,1},{6,2},{7,3},{8,12},{9,13},{10,... | collective-permute-start | bytes 159752 | tf_op jit(solution)/shard_map/ppermute | solution.py:415
  5.9 5.0 %collective-permute-start = (bf16[16,1664]{1,0:T(8,128)(2,1)S(1)}, bf16[16,1664]{1,0:T(8,128)(2,1)S(1)}, u32[]{:S(2)}, u32[]{:S(2)}) collective-permute-start(bf16[16,1664]{1,0:T(8,128)(2,1)S(1)} %pad_maximum_fusion.1), channel_id=1, source_target_pairs={{0,2},{1,3},{2,0},{3,1},{4,6},{5,7},{6,4},{7,5},{8,10},{9,11},{10,... | collective-permute-start | bytes 159752 | tf_op jit(solution)/shard_map/ppermute | solution.py:415
  7.4 5.5 %collective-permute-start.3 = (f32[1,4,384]{2,1,0:T(4,128)S(1)}, f32[1,4,384]{2,1,0:T(4,128)S(1)}, u32[]{:S(2)}, u32[]{:S(2)}) collective-permute-start(f32[1,4,384]{2,1,0:T(4,128)S(1)} %slice.3), channel_id=1, source_target_pairs={{8,0},{16,8},{24,16},{9,1},{17,9},{25,17},{10,2},{18,10},{26,18},{... | collective-permute-start | bytes 18440 | tf_op jit(solution)/shard_map/ppermute | solution.py:432
  11.0 13.7 %copy-start = (bf16[64,1664]{1,0:T(8,128)(2,1)}, bf16[64,1664]{1,0:T(8,128)(2,1)S(1)}, u32[]{:S(2)}) copy-start(bf16[64,1664]{1,0:T(8,128)(2,1)S(1)} %pad_maximum_fusion.refs_0_) | copy-start | bytes 638980
  12.9 3.5 %copy-start.12 = (f32[1,4,384]{2,1,0:T(4,128)}, f32[1,4,384]{2,1,0:T(4,128)S(1)}, u32[]{:S(2)}) copy-start(f32[1,4,384]{2,1,0:T(4,128)S(1)} %collective-permute-done.3.above) | copy-start | bytes 18436
  12.9 11.7 %collective-permute-start.6 = (bf16[64,1664]{1,0:T(8,128)(2,1)S(1)}, bf16[64,1664]{1,0:T(8,128)(2,1)S(1)}, u32[]{:S(2)}, u32[]{:S(2)}) collective-permute-start(bf16[64,1664]{1,0:T(8,128)(2,1)S(1)} %pad_maximum_fusion.refs_0_), channel_id=1, source_target_pairs={{0,24},{8,16},{16,8},{24,0},{1,25},{9,17},{17,9},{25,1},{2,26},{10... | collective-permute-start | bytes 638984 | tf_op jit(solution)/shard_map/ppermute | solution.py:415
  15.2 9.4 %collective-permute-start.5 = (bf16[64,1664]{1,0:T(8,128)(2,1)S(1)}, bf16[64,1664]{1,0:T(8,128)(2,1)S(1)}, u32[]{:S(2)}, u32[]{:S(2)}) collective-permute-start(bf16[64,1664]{1,0:T(8,128)(2,1)S(1)} %pad_maximum_fusion.refs_0_), channel_id=1, source_target_pairs={{0,16},{8,24},{16,0},{24,8},{1,17},{9,25},{17,1},{25,9},{2,18},{10... | collective-permute-start | bytes 638984 | tf_op jit(solution)/shard_map/ppermute | solution.py:415
  15.2 9.4 %collective-permute-start.4 = (bf16[64,1664]{1,0:T(8,128)(2,1)S(1)}, bf16[64,1664]{1,0:T(8,128)(2,1)S(1)}, u32[]{:S(2)}, u32[]{:S(2)}) collective-permute-start(bf16[64,1664]{1,0:T(8,128)(2,1)S(1)} %pad_maximum_fusion.refs_0_), channel_id=1, source_target_pairs={{0,8},{8,0},{16,24},{24,16},{1,9},{9,1},{17,25},{25,17},{2,10},{10... | collective-permute-start | bytes 638984 | tf_op jit(solution)/shard_map/ppermute | solution.py:415
  24.7 2.5 %copy-start.1 = (bf16[64,1664]{1,0:T(8,128)(2,1)}, bf16[64,1664]{1,0:T(8,128)(2,1)S(1)}, u32[]{:S(2)}) copy-start(bf16[64,1664]{1,0:T(8,128)(2,1)S(1)} %collective-permute-done.6.refs_3_) | copy-start | bytes 638980
  24.7 2.5 %copy-start.2 = (bf16[64,1664]{1,0:T(8,128)(2,1)}, bf16[64,1664]{1,0:T(8,128)(2,1)S(1)}, u32[]{:S(2)}) copy-start(bf16[64,1664]{1,0:T(8,128)(2,1)S(1)} %collective-permute-done.5.refs_2_) | copy-start | bytes 638980
  24.7 2.5 %copy-start.3 = (bf16[64,1664]{1,0:T(8,128)(2,1)}, bf16[64,1664]{1,0:T(8,128)(2,1)S(1)}, u32[]{:S(2)}) copy-start(bf16[64,1664]{1,0:T(8,128)(2,1)S(1)} %collective-permute-done.4.refs_1_) | copy-start | bytes 638980
  24.7 1.5 %collective-permute-start.7 = (bf16[64,1664]{1,0:T(8,128)(2,1)S(1)}, bf16[64,1664]{1,0:T(8,128)(2,1)S(1)}, u32[]{:S(2)}, u32[]{:S(2)}) collective-permute-start(bf16[64,1664]{1,0:T(8,128)(2,1)S(1)} %pad_maximum_fusion.refs_0_), channel_id=1, source_target_pairs={{0,1},{1,0},{2,3},{3,2},{4,5},{5,4},{6,7},{7,6},{8,9},{9,8},{10,11... | collective-permute-start | bytes 638984 | tf_op jit(solution)/shard_map/ppermute | solution.py:415
  24.8 1.8 %collective-permute-start.8 = (bf16[64,1664]{1,0:T(8,128)(2,1)S(1)}, bf16[64,1664]{1,0:T(8,128)(2,1)S(1)}, u32[]{:S(2)}, u32[]{:S(2)}) collective-permute-start(bf16[64,1664]{1,0:T(8,128)(2,1)S(1)} %collective-permute-done.4.refs_1_), channel_id=1, source_target_pairs={{0,1},{1,0},{2,3},{3,2},{4,5},{5,4},{6,7},{7,6},{8,9},{9,8},{10,11... | collective-permute-start | bytes 638984 | tf_op jit(solution)/shard_map/ppermute | solution.py:415
  25.3 1.6 %collective-permute-start.9 = (bf16[64,1664]{1,0:T(8,128)(2,1)S(1)}, bf16[64,1664]{1,0:T(8,128)(2,1)S(1)}, u32[]{:S(2)}, u32[]{:S(2)}) collective-permute-start(bf16[64,1664]{1,0:T(8,128)(2,1)S(1)} %collective-permute-done.5.refs_2_), channel_id=1, source_target_pairs={{0,1},{1,0},{2,3},{3,2},{4,5},{5,4},{6,7},{7,6},{8,9},{9,8},{10,11... | collective-permute-start | bytes 638984 | tf_op jit(solution)/shard_map/ppermute | solution.py:415
  25.4 1.8 %collective-permute-start.10 = (bf16[64,1664]{1,0:T(8,128)(2,1)S(1)}, bf16[64,1664]{1,0:T(8,128)(2,1)S(1)}, u32[]{:S(2)}, u32[]{:S(2)}) collective-permute-start(bf16[64,1664]{1,0:T(8,128)(2,1)S(1)} %collective-permute-done.6.refs_3_), channel_id=1, source_target_pairs={{0,1},{1,0},{2,3},{3,2},{4,5},{5,4},{6,7},{7,6},{8,9},{9,8},{10,11... | collective-permute-start | bytes 638984 | tf_op jit(solution)/shard_map/ppermute | solution.py:415
  26.2 0.9 %copy-start.4 = (bf16[64,1664]{1,0:T(8,128)(2,1)}, bf16[64,1664]{1,0:T(8,128)(2,1)S(1)}, u32[]{:S(2)}) copy-start(bf16[64,1664]{1,0:T(8,128)(2,1)S(1)} %collective-permute-done.7.refs_4_) | copy-start | bytes 638980
  26.6 0.7 %copy-start.5 = (bf16[64,1664]{1,0:T(8,128)(2,1)}, bf16[64,1664]{1,0:T(8,128)(2,1)S(1)}, u32[]{:S(2)}) copy-start(bf16[64,1664]{1,0:T(8,128)(2,1)S(1)} %collective-permute-done.8.refs_5_) | copy-start | bytes 638980
  26.9 0.7 %copy-start.6 = (bf16[64,1664]{1,0:T(8,128)(2,1)}, bf16[64,1664]{1,0:T(8,128)(2,1)S(1)}, u32[]{:S(2)}) copy-start(bf16[64,1664]{1,0:T(8,128)(2,1)S(1)} %collective-permute-done.9.refs_6_) | copy-start | bytes 638980
  27.2 0.7 %copy-start.7 = (bf16[64,1664]{1,0:T(8,128)(2,1)}, bf16[64,1664]{1,0:T(8,128)(2,1)S(1)}, u32[]{:S(2)}) copy-start(bf16[64,1664]{1,0:T(8,128)(2,1)S(1)} %collective-permute-done.10.refs_7_) | copy-start | bytes 638980
  33.7 6.3 %collective-permute-start.17 = (f32[8,128]{1,0:T(8,128)}, f32[8,128]{1,0:T(8,128)S(1)}, u32[]{:S(2)}, u32[]{:S(2)}) collective-permute-start(f32[8,128]{1,0:T(8,128)} %get-tuple-element.27), channel_id=1, source_target_pairs={{0,7},{1,6},{2,5},{3,4},{4,3},{5,2},{6,1},{7,0},{8,15},{9,14},{10,... | collective-permute-start | bytes 12296 | tf_op jit(solution)/shard_map/ppermute | solution.py:415
  35.8 6.0 %collective-permute-start.16 = (f32[8,128]{1,0:T(8,128)}, f32[8,128]{1,0:T(8,128)S(1)}, u32[]{:S(2)}, u32[]{:S(2)}) collective-permute-start(f32[8,128]{1,0:T(8,128)} %get-tuple-element.27), channel_id=1, source_target_pairs={{0,6},{1,7},{2,4},{3,5},{4,2},{5,3},{6,0},{7,1},{8,14},{9,15},{10,... | collective-permute-start | bytes 12296 | tf_op jit(solution)/shard_map/ppermute | solution.py:415
  37.4 4.4 %collective-permute-start.15 = (f32[8,128]{1,0:T(8,128)}, f32[8,128]{1,0:T(8,128)S(1)}, u32[]{:S(2)}, u32[]{:S(2)}) collective-permute-start(f32[8,128]{1,0:T(8,128)} %get-tuple-element.27), channel_id=1, source_target_pairs={{0,5},{1,4},{2,7},{3,6},{4,1},{5,0},{6,3},{7,2},{8,13},{9,12},{10,... | collective-permute-start | bytes 12296 | tf_op jit(solution)/shard_map/ppermute | solution.py:415
  37.4 4.7 %collective-permute-start.14 = (f32[8,128]{1,0:T(8,128)}, f32[8,128]{1,0:T(8,128)S(1)}, u32[]{:S(2)}, u32[]{:S(2)}) collective-permute-start(f32[8,128]{1,0:T(8,128)} %get-tuple-element.27), channel_id=1, source_target_pairs={{0,4},{1,5},{2,6},{3,7},{4,0},{5,1},{6,2},{7,3},{8,12},{9,13},{10,... | collective-permute-start | bytes 12296 | tf_op jit(solution)/shard_map/ppermute | solution.py:415
  39.9 3.2 %collective-permute-start.13 = (f32[8,128]{1,0:T(8,128)}, f32[8,128]{1,0:T(8,128)S(1)}, u32[]{:S(2)}, u32[]{:S(2)}) collective-permute-start(f32[8,128]{1,0:T(8,128)} %get-tuple-element.27), channel_id=1, source_target_pairs={{0,3},{1,2},{2,1},{3,0},{4,7},{5,6},{6,5},{7,4},{8,11},{9,10},{10,... | collective-permute-start | bytes 12296 | tf_op jit(solution)/shard_map/ppermute | solution.py:415
  40.0 3.8 %collective-permute-start.12 = (f32[8,128]{1,0:T(8,128)}, f32[8,128]{1,0:T(8,128)S(1)}, u32[]{:S(2)}, u32[]{:S(2)}) collective-permute-start(f32[8,128]{1,0:T(8,128)} %get-tuple-element.27), channel_id=1, source_target_pairs={{0,2},{1,3},{2,0},{3,1},{4,6},{5,7},{6,4},{7,5},{8,10},{9,11},{10,... | collective-permute-start | bytes 12296 | tf_op jit(solution)/shard_map/ppermute | solution.py:415
  41.8 2.0 %collective-permute-start.11 = (f32[8,128]{1,0:T(8,128)}, f32[8,128]{1,0:T(8,128)S(1)}, u32[]{:S(2)}, u32[]{:S(2)}) collective-permute-start(f32[8,128]{1,0:T(8,128)} %get-tuple-element.27), channel_id=1, source_target_pairs={{0,1},{1,0},{2,3},{3,2},{4,5},{5,4},{6,7},{7,6},{8,9},{9,8},{10,11... | collective-permute-start | bytes 12296 | tf_op jit(solution)/shard_map/ppermute | solution.py:415
  44.5 6.5 %copy-start.8 = (f32[8,128]{1,0:T(8,128)}, f32[8,128]{1,0:T(8,128)S(1)}, u32[]{:S(2)}) copy-start(f32[8,128]{1,0:T(8,128)S(1)} %add_add_fusion.refs_0_) | copy-start | bytes 12292
  44.5 6.5 %collective-permute-start.20 = (f32[8,128]{1,0:T(8,128)S(1)}, f32[8,128]{1,0:T(8,128)S(1)}, u32[]{:S(2)}, u32[]{:S(2)}) collective-permute-start(f32[8,128]{1,0:T(8,128)S(1)} %add_add_fusion.refs_0_), channel_id=1, source_target_pairs={{0,24},{8,16},{16,8},{24,0},{1,25},{9,17},{17,9},{25,1},{2,26},{10... | collective-permute-start | bytes 12296 | tf_op jit(solution)/shard_map/ppermute | solution.py:415
  47.8 3.6 %collective-permute-start.19 = (f32[8,128]{1,0:T(8,128)S(1)}, f32[8,128]{1,0:T(8,128)S(1)}, u32[]{:S(2)}, u32[]{:S(2)}) collective-permute-start(f32[8,128]{1,0:T(8,128)S(1)} %add_add_fusion.refs_0_), channel_id=1, source_target_pairs={{0,16},{8,24},{16,0},{24,8},{1,17},{9,25},{17,1},{25,9},{2,18},{10... | collective-permute-start | bytes 12296 | tf_op jit(solution)/shard_map/ppermute | solution.py:415
  47.8 3.6 %collective-permute-start.18 = (f32[8,128]{1,0:T(8,128)S(1)}, f32[8,128]{1,0:T(8,128)S(1)}, u32[]{:S(2)}, u32[]{:S(2)}) collective-permute-start(f32[8,128]{1,0:T(8,128)S(1)} %add_add_fusion.refs_0_), channel_id=1, source_target_pairs={{0,8},{8,0},{16,24},{24,16},{1,9},{9,1},{17,25},{25,17},{2,10},{10... | collective-permute-start | bytes 12296 | tf_op jit(solution)/shard_map/ppermute | solution.py:415
  50.9 0.6 copy-start.9
  51.4 0.6 copy-start.10
  52.0 0.6 copy-start.11

commit v5 on v4

--- a/solution.py
+++ b/solution.py
@@ -16,8 +16,8 @@
 EPS = 1e-05
 TILE = 128
 GROUP = 4
+EDGE_GROUP = 8
 CHUNK = 512
-VMEM = 56 * 2**20
 f32 = jnp.float32
 bf16 = jnp.bfloat16
 NT = (((1,), (1,)), ((), ()))
@@ -80,11 +80,11 @@
             table[device, 0] = len(tiles)
             table[device, 1 : 1 + len(tiles)] = tiles
             table[device, 1 + groups : 1 + groups + len(codes)] = codes
-            table[device, start] = len(edge) // GROUP
+            table[device, start] = len(edge) // EDGE_GROUP
             table[device, start + 1 : start + 1 + len(edge)] = edge
         plans.append((table, groups))
     edge_samples = round_up(reach, 16)
-    assert edge_samples <= TILE and (bins // 2) % GROUP == 0
+    assert edge_samples <= TILE and (bins // 2) % EDGE_GROUP == 0
     return plans[0], plans[1], edge_samples, trig
 
 
@@ -108,13 +108,41 @@
 
 def bump(t):
     falloff = jnp.maximum(1.0 - t * t, 0.0)
-    return falloff * falloff, -4.0 * t * falloff
-
-
-def z_weights(z0, rows, u, s, c, samples):
+    return falloff * falloff, t * falloff
+
+
+def row_weights(z0, rows, u, s, c, samples):
     centre = 0.5 * NZ + u * s
     kz, kzd = bump((z0 + lanes_of((rows, TILE), 0)) - centre)
-    return centre, kz, kzd * (-u * c * (1.0 / samples))
+    return centre, kz, kzd, u * (c * (4.0 / samples)), u * (s * (-4.0 / samples))
+
+
+def reorder(x, device, mine):
+    lane = lax.broadcasted_iota(jnp.int32, x.shape, 1)
+    rows = x.shape[0]
+    size = mine
+    bit = 0
+    while size < rows // 2 * TILE:
+        if size < TILE:
+            moved = jnp.where(
+                lax.bitwise_and(lane, size) != 0,
+                pltpu.roll(x, size, 1),
+                pltpu.roll(x, TILE - size, 1),
+            )
+        else:
+            step = size // TILE
+            moved = jnp.concatenate([x[r ^ step : (r ^ step) + 1] for r in range(rows)], 0)
+        flag = lax.bitwise_and(lax.shift_right_logical(device, bit), 1)
+        x = jnp.where(flag == 1, moved, x)
+        size, bit = 2 * size, bit + 1
+    return x
+
+
+def position(n_gz, n_dom):
+    dom = lax.axis_index("dom")
+    n_z = n_dom // 2
+    core, z = lax.bitwise_and(dom, 1), lax.shift_right_logical(dom, 1)
+    return (core * n_gz + lax.axis_index("gz")) * n_z + z
 
 
 def extract_kernel(
@@ -135,20 +163,7 @@
     )
     own.start()
 
-    @pl.when(dom < n_dom - 1)
-    def _():
-        copy = pltpu.make_async_copy(
-            volume.at[pl.ds((dom + 1) * planes, 1)], field.at[pl.ds(planes, 1)], sem.at[1]
-        )
-        copy.start()
-        copy.wait()
-
-    @pl.when(dom == n_dom - 1)
-    def _():
-        copy = pltpu.make_async_copy(above, field.at[pl.ds(planes, 1)], sem.at[1])
-        copy.start()
-        copy.wait()
-
+    field[planes] = above[0]
     for z in range(planes + 1, depth):
         field[z] = jnp.zeros(field.shape[1:], f32)
     out[...] = jnp.zeros_like(out)
@@ -169,14 +184,13 @@
             at = row + 1 + groups + j * GROUP + k
             b, ut, s, c, base = block_of(table, trig, at, bins)
             u = lanes_of((1, TILE), 1) + base
-            centre, kz, kzd = z_weights(z0, depth, u, s, c, samples)
+            centre, kz, kzd, z_factor, x_factor = row_weights(z0, depth, u, s, c, samples)
             below = s < 0.0
             place = centre * jnp.where(below, -1.0, 1.0)
             least, most = jnp.where(below, -z1, z0), jnp.where(below, -z0, z1)
             own = jnp.where((place >= least) & (place < most), 1.0, 0.0)
-            kz, kzd = kz * own, kzd * own
-            kx, kxd = bump(xx - u * c)
-            weights = jnp.concatenate([kx, kxd * (u * s * (1.0 / samples))], 1)
+            z_factor, x_factor = z_factor * own, x_factor * own
+            weights = jnp.concatenate(bump(xx - u * c), 1)
             whi = weights.astype(bf16)
             wlo = (weights - whi.astype(f32)).astype(bf16)
             sampled = (
@@ -188,8 +202,11 @@
             for r in range(4):
                 direct = sampled[r * depth : (r + 1) * depth, :TILE]
                 tilted = sampled[r * depth : (r + 1) * depth, TILE:]
-                leading.append(jnp.sum(direct * kz, axis=0, keepdims=True))
-                second.append(jnp.sum(direct * kzd + tilted * kz, axis=0, keepdims=True))
+                leading.append(own * jnp.sum(direct * kz, axis=0, keepdims=True))
+                second.append(
+                    z_factor * jnp.sum(direct * kzd, axis=0, keepdims=True)
+                    + x_factor * jnp.sum(tilted * kz, axis=0, keepdims=True)
+                )
             span = pl.ds(pl.multiple_of((b * ut_count + ut) * 8, 8), 8)
             out[span, :] = out[span, :] + jnp.concatenate(leading + second, 0)
         return carry
@@ -221,30 +238,9 @@
 
 def particle_kernel(width, mine, n_gz, n_dom, *refs):
     blocks = refs[: 2 * n_gz]
-    ctf, slope, pairs, weighted, parts, bins_row, packed, sems = refs[2 * n_gz :]
-    n_z = n_dom // 2
-    gz, dom = lax.axis_index("gz"), lax.axis_index("dom")
-    z, core = lax.shift_right_logical(dom, 1), lax.bitwise_and(dom, 1)
-    copies = []
-    for c in range(2):
-        for j in range(n_gz):
-            for k in range(n_z):
-                owner = ((gz ^ j) * n_z + (z ^ k)) * 2 + (core ^ c)
-                start = pl.multiple_of(owner * mine, mine)
-                copies.append(
-                    pltpu.make_async_copy(
-                        blocks[c * n_gz + j].at[pl.ds(k * mine, mine), :],
-                        packed.at[pl.ds(start, mine), :],
-                        sems.at[len(copies)],
-                    )
-                )
-    for copy in copies:
-        copy.start()
-    for copy in copies:
-        copy.wait()
-
-    total = packed.shape[0]
-    count = min(CHUNK, total)
+    ctf, slope, pairs, weighted, parts, bins_row = refs[2 * n_gz :]
+    size = blocks[0].shape[0]
+    joined = max(1, CHUNK // size)
     both = slope.shape[0]
     bins = both // 2
     flat = jnp.concatenate([ctf[:, 0, :], ctf[:, 1, :]], 1)
@@ -253,10 +249,14 @@
     upper = jnp.where(lanes_of((8, both), 1) >= bins, 1.0, 0.0)
     select = jnp.where(lanes_of((8, both), 0) == upper, 1.0, 0.0).astype(bf16)
     select = jnp.concatenate([select] * 3, 1)
-
-    def step(i, carry):
-        span = pl.ds(pl.multiple_of(i * count, count), count)
-        ids = packed[span, width:]
+    slopes = slope[...]
+    scalars = [[], []]
+
+    for i in range(0, 2 * n_gz, joined):
+        packed = jnp.concatenate([ref[...] for ref in blocks[i : i + joined]], 0)
+        count = packed.shape[0]
+        span = slice(i * size, i * size + count)
+        ids = packed[:, width:]
         classes = ids[:, 0:1].astype(f32)
         onehot_class = jnp.where(lanes_of((count, NCTF), 1) == classes, 1.0, 0.0).astype(bf16)
         bin_of = ids[:, 1:2].astype(f32)
@@ -266,11 +266,10 @@
             onehot_class, ctf_lo, preferred_element_type=f32
         )
         contrast = jnp.concatenate([contrast, contrast], 1)
-        w = contrast * packed[span, :width].astype(f32)
+        w = contrast * packed[:, :width].astype(f32)
         whi = w.astype(bf16)
         wlo = (w - whi.astype(f32)).astype(bf16)
         weighted[span, :] = whi
-        slopes = slope[...]
         along = lax.dot_general(whi, slopes, NT, preferred_element_type=f32) + lax.dot_general(
             wlo, slopes, NT, preferred_element_type=f32
         )
@@ -279,37 +278,23 @@
         terms = jnp.concatenate(split3(jnp.where(chosen, along + tables, 0.0)), 1)
         rows = lax.dot_general(select, terms, NT, preferred_element_type=f32)
         for n in range(2):
-            row = rows[n : n + 1]
             for q in range(count // TILE):
-                at = n * (total // TILE) + i * (count // TILE) + q
-                parts[pl.ds(at, 1), :] = row[:, q * TILE : (q + 1) * TILE]
+                scalars[n].append(rows[n : n + 1, q * TILE : (q + 1) * TILE])
         pick = jnp.where(lanes_of((8, TILE), 1) == 1.0, 1.0, 0.0).astype(bf16)
         bins_row[:, span] = lax.dot_general(pick, ids, NT, preferred_element_type=f32)[0:1]
-        return carry
-
-    lax.fori_loop(0, total // count, step, 0)
-
-
-def plain_kernel(bins_row, weighted, plain):
-    count = weighted.shape[0]
-    chunk = min(CHUNK, count)
-    sums = jnp.zeros(plain.shape, f32)
-    for i in range(count // chunk):
-        span = slice(i * chunk, (i + 1) * chunk)
-        belongs = lanes_of((plain.shape[0], chunk), 0) == bins_row[:, span]
-        onehot = jnp.where(belongs, 1.0, 0.0).astype(bf16)
-        sums = sums + jnp.dot(onehot, weighted[span, :], preferred_element_type=f32)
-    plain[...] = sums
+
+    scalars = jnp.concatenate(scalars[0] + scalars[1], 0)
+    scalars = reorder(scalars, position(n_gz, n_dom), mine)
+    rows = scalars.shape[0]
+    for n in range(parts.shape[0] // rows):
+        parts[n * rows : (n + 1) * rows, :] = scalars
 
 
 def spread_kernel(
     groups, length, planes, samples, edge_samples, mine, n_gz, n_dom,
-    table, trig, bins_row, weighted, plain, *refs
+    table, trig, parts, bins_row, weighted, pose, out, sums, total, poses,
 ):
-    parts = refs[:n_gz]
-    pose, out, sums, total, poses = refs[n_gz:]
-    bins, width = plain.shape
-    tiles = width // TILE
+    tiles, bins = sums.shape[0] // 2, sums.shape[1]
     ut_count = samples // TILE
     depth = total.shape[1] // 4
     count = bins_row.shape[1]
@@ -319,31 +304,33 @@
     z0 = (device * planes).astype(f32)
 
     rows = count // TILE
-    scalars = sum([part[...] for part in parts[1:]], parts[0][...])
+    scalars = jnp.sum(parts[...].reshape(parts.shape[0] // (2 * rows), 2 * rows, TILE), axis=0)
     square, pull = scalars[:rows], scalars[rows:]
     curvature = square + EPS
     shift = jnp.zeros_like(square)
     for _ in range(ITERS):
         shift = shift + 0.5 * (pull - shift * square) / curvature
+    here = position(n_gz, n_dom)
     poses[...] = shift * jnp.sqrt(curvature)
-    first = device * mine
+    first = here * mine
     line = poses[pl.ds(lax.div(first, TILE), 1), :]
     pose[...] = pltpu.roll(line, TILE - lax.rem(first, TILE), 1)[:, :mine]
+    shift = reorder(jnp.concatenate([shift, shift], 0), here, mine)
     shift = jnp.concatenate([shift[q : q + 1] for q in range(rows)], 1)
 
-    slope_sum = jnp.zeros((bins, width), f32)
+    bin_sums = jnp.zeros((3 * bins, tiles * TILE), f32)
     for i in range(count // chunk):
         span = slice(i * chunk, (i + 1) * chunk)
         belongs = lanes_of((bins, chunk), 0) == bins_row[:, span]
         scaled = jnp.where(belongs, shift[:, span], 0.0)
         hi = scaled.astype(bf16)
         lo = (scaled - hi.astype(f32)).astype(bf16)
-        rows = weighted[span, :]
-        slope_sum = (
-            slope_sum
-            + jnp.dot(hi, rows, preferred_element_type=f32)
-            + jnp.dot(lo, rows, preferred_element_type=f32)
+        onehot = jnp.where(belongs, 1.0, 0.0).astype(bf16)
+        bin_sums = bin_sums + jnp.dot(
+            jnp.concatenate([onehot, hi, lo], 0), weighted[span, :], preferred_element_type=f32
         )
+    plain = bin_sums[:bins]
+    slope_sum = bin_sums[bins : 2 * bins] + bin_sums[2 * bins :]
     for q in range(tiles):
         sums[q] = plain[:, q * TILE : (q + 1) * TILE]
         sums[tiles + q] = slope_sum[:, q * TILE : (q + 1) * TILE]
@@ -351,23 +338,22 @@
 
     def step(j, carry):
         xt = table[row + 1 + j]
-        xx = lanes_of((TILE, TILE), 1) + (xt * TILE).astype(f32)
+        xx = lanes_of((1, TILE), 1) + (xt * TILE).astype(f32)
+        uu = lanes_of((TILE, TILE), 0)
         left, right = [], []
         for k in range(GROUP):
             at = row + 1 + groups + j * GROUP + k
             b, ut, s, c, base = block_of(table, trig, at, bins)
             u = lanes_of((1, TILE), 1) + base
-            _, kz, kzd = z_weights(z0, depth, u, s, c, samples)
+            _, kz, kzd, z_factor, x_factor = row_weights(z0, depth, u, s, c, samples)
             first, second = [], []
             for r in range(4):
                 direct = sums[r * ut_count + ut, pl.ds(b, 1), :]
                 tilted = sums[tiles + r * ut_count + ut, pl.ds(b, 1), :]
-                first.append(kz * direct + kzd * tilted)
-                second.append(kz * tilted)
+                first.append(kz * direct + kzd * (tilted * z_factor))
+                second.append(kz * (tilted * x_factor))
             left += [jnp.concatenate(first, 0), jnp.concatenate(second, 0)]
-            uu = lanes_of((TILE, TILE), 0) + base
-            kx, kxd = bump(xx - uu * c)
-            right += [kx.astype(bf16), (kxd * (uu * (s * (1.0 / samples)))).astype(bf16)]
+            right += [k.astype(bf16) for k in bump((xx - base * c) - uu * c)]
         left = jnp.concatenate(left, 1)
         hi = left.astype(bf16)
         lo = (left - hi.astype(f32)).astype(bf16)
@@ -383,20 +369,19 @@
     def edge(j, carry):
         left, right = [], []
         rest = jnp.zeros((TILE - edge_samples, TILE), f32)
-        for k in range(GROUP):
-            b, _, s, c, _ = block_of(table, trig, tail + 1 + j * GROUP + k, bins)
+        for k in range(EDGE_GROUP):
+            b, _, s, c, _ = block_of(table, trig, tail + 1 + j * EDGE_GROUP + k, bins)
             u = lanes_of((1, TILE), 1)
-            _, kz, kzd = z_weights(z0, 1, u, s, c, samples)
+            _, kz, kzd, z_factor, x_factor = row_weights(z0, 1, u, s, c, samples)
             direct = jnp.concatenate(
                 [sums[r * ut_count, pl.ds(b, 1), :] for r in range(4)], 0
             )
             tilted = jnp.concatenate(
                 [sums[tiles + r * ut_count, pl.ds(b, 1), :] for r in range(4)], 0
             )
-            left += [kz * direct + kzd * tilted, kz * tilted]
+            left += [kz * direct + (kzd * z_factor) * tilted, (kz * x_factor) * tilted]
             uu = lanes_of((edge_samples, TILE), 0)
-            kx, kxd = bump(lanes_of((edge_samples, TILE), 1) - uu * c)
-            for part in (kx, kxd * (uu * (s * (1.0 / samples)))):
+            for part in bump(lanes_of((1, TILE), 1) - uu * c):
                 right.append(jnp.concatenate([part, rest], 0).astype(bf16))
         left = jnp.concatenate(left, 1)
         hi = left.astype(bf16).astype(f32)
@@ -433,6 +418,10 @@
     column = jnp.concatenate(
         [packed] + [swap(packed, "dom", n_dom, 2 * k) for k in range(1, n_z)], 0
     )
+    inner = lax.dynamic_slice_in_dim(
+        volume, jnp.minimum((lax.axis_index("dom") + 1) * planes, slab - 1), 1, 0
+    )
+    above = jnp.where(lax.axis_index("dom") == n_dom - 1, above, inner)
     column, above = lax.optimization_barrier((column, above))
     planes_of = [column] + [swap(column, "gz", n_gz, j) for j in range(1, n_gz)]
 
@@ -443,7 +432,7 @@
     smem = pl.BlockSpec(memory_space=pltpu.SMEM)
     vmem = pl.BlockSpec(memory_space=pltpu.VMEM)
     hbm = pl.BlockSpec(memory_space=pl.ANY)
-    params = pltpu.CompilerParams(vmem_limit_bytes=VMEM)
+    params = pltpu.CompilerParams(vmem_limit_bytes=min(56, 19 + 37 * count // 4096) * 2**20)
     table, groups = extract_plan
     slope, pairs = pl.pallas_call(
         functools.partial(
@@ -453,14 +442,14 @@
             jax.ShapeDtypeStruct((2 * bins, width), bf16),
             jax.ShapeDtypeStruct((NCTF, 6 * bins), bf16),
         ],
-        in_specs=[smem, smem, hbm, hbm, vmem],
+        in_specs=[smem, smem, hbm, vmem, vmem],
         out_specs=[vmem, vmem],
         scratch_shapes=[
             pltpu.VMEM((depth_in, rows, columns), f32),
             pltpu.VMEM((xt_count, rows * depth_in, TILE), bf16),
             pltpu.VMEM((xt_count, rows * depth_in, TILE), bf16),
             pltpu.VMEM((bins * ut_count * 2 * rows, TILE), f32),
-            pltpu.SemaphoreType.DMA((2,)),
+            pltpu.SemaphoreType.DMA((1,)),
         ],
         compiler_params=params,
         cost_estimate=pl.CostEstimate(flops=6 * 10**9, bytes_accessed=2**20, transcendentals=0),
@@ -473,31 +462,16 @@
         functools.partial(particle_kernel, width, mine, n_gz, n_dom),
         out_shape=[
             jax.ShapeDtypeStruct((count, width), bf16),
-            jax.ShapeDtypeStruct((2 * count // TILE, TILE), f32),
+            jax.ShapeDtypeStruct((devices * 2 * count // TILE, TILE), f32),
             jax.ShapeDtypeStruct((1, count), f32),
         ],
-        in_specs=[hbm] * len(gathered) + [vmem] * 3,
+        in_specs=[vmem] * (len(gathered) + 3),
         out_specs=[vmem] * 3,
-        scratch_shapes=[
-            pltpu.VMEM((count, width + TILE), bf16),
-            pltpu.SemaphoreType.DMA((devices,)),
-        ],
         compiler_params=params,
         name="particles",
     )(*gathered, ctf_table, slope, pairs)
 
-    plain = pl.pallas_call(
-        plain_kernel,
-        out_shape=jax.ShapeDtypeStruct((bins, width), f32),
-        in_specs=[vmem, vmem],
-        out_specs=vmem,
-        compiler_params=params,
-        cost_estimate=pl.CostEstimate(flops=2 * 10**9, bytes_accessed=2**21, transcendentals=0),
-        name="plain_sums",
-    )(bins_row, weighted)
-
-    parts = sum([swap(parts, "dom", n_dom, k) for k in range(1, n_dom)], parts)
-    parts = [parts] + [swap(parts, "gz", n_gz, j) for j in range(1, n_gz)]
+    parts = lax.all_to_all(parts, ("gz", "dom"), 0, 0, tiled=True)
 
     depth = round_up(planes, 8)
     table, groups = spread_plan
@@ -509,7 +483,7 @@
             jax.ShapeDtypeStruct((1, mine), f32),
             jax.ShapeDtypeStruct((planes, rows, columns), f32),
         ],
-        in_specs=[smem, smem] + [vmem] * (3 + n_gz),
+        in_specs=[smem, smem, vmem, vmem, vmem],
         out_specs=[vmem, vmem],
         scratch_shapes=[
             pltpu.VMEM((2 * width // TILE, bins, TILE), f32),
@@ -518,7 +492,7 @@
         ],
         compiler_params=params,
         name="spread",
-    )(jnp.asarray(table.reshape(-1)), trig, bins_row, weighted, plain, *parts)
+    )(jnp.asarray(table.reshape(-1)), trig, parts, bins_row, weighted)
     pose = pose.reshape(mine)
     return pose, spread
 

time: 61.6 us -> 51.4 us (0.83)
  starting transfers between devices: 24.4 us -> 12.4 us
  blocking collectives: 0 us -> 10.2 us
  Pallas kernels: 25.2 us -> 16.1 us
  local copies, waits for them, and re-layouts: 3.46 us -> 5.12 us
  waiting for transfers between devices: 5.9 us -> 4.91 us
    ppermute x20 -> x10, starting transfers between devices: 21 us -> 9.08 us  [swap(): return lax.ppermute(x, axis, [(i, i ^ distance) for i in range(size)])]
    all_to_all x0 -> x1, blocking collectives: none -> 10.2 us  [local(): parts = lax.all_to_all(parts, ('gz', 'dom'), 0, 0, tiled=True)]
    pallas_call x1, Pallas kernels: 5.85 us -> 2.73 us  [local(): pl.pallas_call(functools.partial(particle_kernel, width, mine, n_gz, n_do...]
    pallas_call x1 -> x0, Pallas kernels: 2.53 us -> none  [local(): pl.pallas_call(plain_kernel, out_shape=jax.ShapeDtypeStruct((bins, width)...]
    ppermute x1, waiting for transfers between devices: 1.92 us -> 0.01 us  [local(): above = lax.ppermute(volume[:1], 'gz', [(i, i - 1) for i in range(1, n_gz)])]
    pallas_call x1, Pallas kernels: 8.55 us -> 6.86 us  [local(): pl.pallas_call(functools.partial(spread_kernel, groups, table.shape[1], p...]
    pallas_call x1, Pallas kernels: 8.24 us -> 6.55 us  [local(): pl.pallas_call(functools.partial(extract_kernel, groups, table.shape[1],...]
    unnamed x27 -> x11, local copies, waits for them, and re-layouts: 2.67 us -> 4.32 us
  transfers between devices with their start and end apart: 21 -> 11, of which waited for: 10 -> 6; matrix products, arithmetic and copies ran while one was open for 1% -> 5% of each run, Pallas kernels for 18% -> 13%
where the time goes in v5:
time: 51.4 us; the launch traced here: 51 us
  Pallas kernels  16.1 us (31%)
  starting transfers between devices  12.4 us (24%)
  blocking collectives  10.2 us (20%)
  local copies, waits for them, and re-layouts  5.12 us (10%)
  waiting for transfers between devices  4.91 us (10%)
  other arithmetic  1.42 us (3%)
  between operations  0.71 us (1%)
    all_to_all x1, blocking collectives, local(): parts = lax.all_to_all(parts, ('gz', 'dom'), 0, 0, tiled=True)  10.2 us
    ppermute x10, starting transfers between devices, swap(): return lax.ppermute(x, axis, [(i, i ^ distance) for i in range(size)])  9.08 us
    pallas_call x1, Pallas kernels, local(): pl.pallas_call(functools.partial(spread_kernel, groups, table.shape[1], p...  6.86 us
    pallas_call x1, Pallas kernels, local(): pl.pallas_call(functools.partial(extract_kernel, groups, table.shape[1],...  6.55 us
    ppermute x10, waiting for transfers between devices, swap(): return lax.ppermute(x, axis, [(i, i ^ distance) for i in range(size)])  4.91 us
    unnamed x11, local copies, waits for them, and re-layouts  4.32 us
    ppermute x1, starting transfers between devices, local(): above = lax.ppermute(volume[:1], 'gz', [(i, i - 1) for i in range(1, n_gz)])  3.33 us
    pallas_call x1, Pallas kernels, local(): pl.pallas_call(functools.partial(particle_kernel, width, mine, n_gz, n_do...  2.73 us
  transfers between devices with their start and end apart: 11, of which 6 were waited for; matrix products, arithmetic and copies ran while one was open for 5% of the time, Pallas kernels for 13%

profile of v5, /device:TPU:4, one launch (start us, length us, event | category | flops | bytes accessed | tf_op | source)
XLA Modules:
  0.0 51.0 jit_solution(6422696956274695869)
XLA Ops:
  0.6 0.7 %slice.3 = f32[1,4,384]{2,1,0:T(4,128)S(1)} slice(f32[192,4,384]{2,1,0:T(4,128)} %volume.1), slice={[0:1], [0:4], [0:384]} | slice | bytes 12288 | tf_op jit(solution)/shard_map/slice | solution.py:417
  1.3 3.3 %collective-permute-start.3 = (f32[1,4,384]{2,1,0:T(4,128)S(1)}, f32[1,4,384]{2,1,0:T(4,128)S(1)}, u32[]{:S(2)}, u32[]{:S(2)}) collective-permute-start(f32[1,4,384]{2,1,0:T(4,128)S(1)} %slice.3), channel_id=1, source_target_pairs={{8,0},{16,8},{24,16},{9,1},{17,9},{25,17},{10,2},{18,10},{26,18},{... | collective-permute-start | bytes 18440 | tf_op jit(solution)/shard_map/ppermute | solution.py:417
  4.7 0.7 %convert_bitcast_fusion = (bf16[16,1]{0,1:T(2,128)(2,1)S(1)}, bf16[16,1]{0,1:T(2,128)(2,1)S(1)}) fusion(s32[16]{0:T(128)} %param.12, s32[16]{0:T(128)} %param.11), kind=kLoop, calls=%fused_computation.4 | loop fusion | flops 32 | bytes 192 | tf_op jit(solution)/shard_map/stack | solution.py:413
  5.4 0.1 copy.12
  5.5 0.8 %copy.13 = bf16[2,8,4,384]{3,1,2,0:T(8,128)(2,1)S(1)} copy(bf16[2,8,4,384]{3,2,1,0:T(4,128)(2,1)} %bitcast.13) | data formatting | bytes 98304
  6.3 3.7 %collective-permute-start.2 = (bf16[16,1664]{1,0:T(8,128)(2,1)S(1)}, bf16[16,1664]{1,0:T(8,128)(2,1)S(1)}, u32[]{:S(2)}, u32[]{:S(2)}) collective-permute-start(bf16[16,1664]{1,0:T(8,128)(2,1)S(1)} %pad_maximum_fusion.1), channel_id=1, source_target_pairs={{0,6},{1,7},{2,4},{3,5},{4,2},{5,3},{6,0},{7,1},{8,14},{9,15},{10,... | collective-permute-start | bytes 159752 | tf_op jit(solution)/shard_map/ppermute | solution.py:400
  9.9 0.0 collective-permute-start.1
  10.0 0.8 %collective-permute-start = (bf16[16,1664]{1,0:T(8,128)(2,1)S(1)}, bf16[16,1664]{1,0:T(8,128)(2,1)S(1)}, u32[]{:S(2)}, u32[]{:S(2)}) collective-permute-start(bf16[16,1664]{1,0:T(8,128)(2,1)S(1)} %pad_maximum_fusion.1), channel_id=1, source_target_pairs={{0,2},{1,3},{2,0},{3,1},{4,6},{5,7},{6,4},{7,5},{8,10},{9,11},{10,... | collective-permute-start | bytes 159752 | tf_op jit(solution)/shard_map/ppermute | solution.py:400
  10.7 0.0 collective-permute-done.3
  10.7 0.7 %dynamic-slice_select_fusion.above = f32[1,4,384]{2,1,0:T(4,128)S(1)} fusion(f32[1,4,384]{2,1,0:T(4,128)S(1)} %collective-permute-done.3, f32[192,4,384]{2,1,0:T(4,128)} %volume.1, s32[]{:T(128)S(6)} %select_n.12, pred[]{:T(512)S(6)} %eq.3), kind=kLoop, calls=%fused_computation.2 | loop fusion | flops 1536 | bytes 18437 | tf_op jit(solution)/shard_map/jit(_where)/select_n | solution.py:424
  11.4 1.5 %collective-permute-done.2 = bf16[16,1664]{1,0:T(8,128)(2,1)S(1)} collective-permute-done((bf16[16,1664]{1,0:T(8,128)(2,1)S(1)}, bf16[16,1664]{1,0:T(8,128)(2,1)S(1)}, u32[]{:S(2)}, u32[]{:S(2)}) %collective-permute-start.2) | collective-permute-done | bytes 53280 | tf_op jit(solution)/shard_map/ppermute | solution.py:400
  12.9 2.1 %collective-permute-done.1 = bf16[16,1664]{1,0:T(8,128)(2,1)S(1)} collective-permute-done((bf16[16,1664]{1,0:T(8,128)(2,1)S(1)}, bf16[16,1664]{1,0:T(8,128)(2,1)S(1)}, u32[]{:S(2)}, u32[]{:S(2)}) %collective-permute-start.1) | collective-permute-done | bytes 53280 | tf_op jit(solution)/shard_map/ppermute | solution.py:400
  15.0 0.0 collective-permute-done
  15.0 0.6 %collective-permute-start.6 = (bf16[64,1664]{1,0:T(8,128)(2,1)S(1)}, bf16[64,1664]{1,0:T(8,128)(2,1)S(1)}, u32[]{:S(2)}, u32[]{:S(2)}) collective-permute-start(bf16[64,1664]{1,0:T(8,128)(2,1)S(1)} %pad_maximum_fusion.refs_0_), channel_id=1, source_target_pairs={{0,24},{8,16},{16,8},{24,0},{1,25},{9,17},{17,9},{25,1},{2,26},{10... | collective-permute-start | bytes 638984 | tf_op jit(solution)/shard_map/ppermute | solution.py:400
  15.6 1.5 %collective-permute-start.5 = (bf16[64,1664]{1,0:T(8,128)(2,1)S(1)}, bf16[64,1664]{1,0:T(8,128)(2,1)S(1)}, u32[]{:S(2)}, u32[]{:S(2)}) collective-permute-start(bf16[64,1664]{1,0:T(8,128)(2,1)S(1)} %pad_maximum_fusion.refs_0_), channel_id=1, source_target_pairs={{0,16},{8,24},{16,0},{24,8},{1,17},{9,25},{17,1},{25,9},{2,18},{10... | collective-permute-start | bytes 638984 | tf_op jit(solution)/shard_map/ppermute | solution.py:400
  17.1 1.4 %collective-permute-start.4 = (bf16[64,1664]{1,0:T(8,128)(2,1)S(1)}, bf16[64,1664]{1,0:T(8,128)(2,1)S(1)}, u32[]{:S(2)}, u32[]{:S(2)}) collective-permute-start(bf16[64,1664]{1,0:T(8,128)(2,1)S(1)} %pad_maximum_fusion.refs_0_), channel_id=1, source_target_pairs={{0,8},{8,0},{16,24},{24,16},{1,9},{9,1},{17,25},{25,17},{2,10},{10... | collective-permute-start | bytes 638984 | tf_op jit(solution)/shard_map/ppermute | solution.py:400
  18.6 0.0 copy-start
  18.6 0.9 %copy-done = f32[32,2,384]{2,1,0:T(2,128)S(1)} copy-done((f32[32,2,384]{2,1,0:T(2,128)S(1)}, f32[32,2,384]{2,1,0:T(2,128)}, u32[]{:S(2)}) %copy-start) | copy-done | bytes 98328
  19.5 0.0 copy-start.2
  19.5 0.7 %copy-done.2 = f32[128]{0:T(128)S(1)} copy-done((f32[128]{0:T(128)S(1)}, f32[128]{0:T(128)}, u32[]{:S(2)}) %copy-start.2) | copy-done | bytes 536
  20.1 0.0 copy-start.3
  20.1 1.3 %copy-done.3 = f32[192,4,384]{2,1,0:T(4,128)S(1)} copy-done((f32[192,4,384]{2,1,0:T(4,128)S(1)}, f32[192,4,384]{2,1,0:T(4,128)}, u32[]{:S(2)}) %copy-start.3) | copy-done | bytes 1179672
  21.4 0.0 copy-start.4
  21.4 0.7 %copy-done.4 = s32[1984]{0:T(1024)S(1)} copy-done((s32[1984]{0:T(1024)S(1)}, s32[1984]{0:T(1024)}, u32[]{:S(2)}) %copy-start.4) | copy-done | bytes 7960
  22.1 6.6 %extract.1 = (bf16[128,1536]{1,0:T(8,128)(2,1)S(1)}, bf16[32,384]{1,0:T(8,128)(2,1)S(1)}) custom-call(s32[1984]{0:T(1024)S(1)} %copy-done.4, f32[128]{0:T(128)S(1)} %copy-done.2, f32[192,4,384]{2,1,0:T(4,128)S(1)} %copy-done.3, f32[1,4,384]{2,1,0:T(4,128)S(1)} %dynamic-slice_select_fusion.above, f32[32,2,384]{2,1,0:T(2,128)S(1)} %copy-done), custom_call_target="tpu_custom_call" | custom-call | flops 6000000000 | bytes 1048576 | tf_op jit(solution)/shard_map/extract/pallas_call | solution.py:437
  28.6 0.0 collective-permute-done.6.refs_3_
  28.7 0.0 collective-permute-done.5.refs_2_
  28.7 0.0 collective-permute-done.4.refs_1_
  28.7 0.1 collective-permute-start.7
  28.8 0.5 collective-permute-start.8
  29.3 0.1 collective-permute-start.9
  29.3 0.4 collective-permute-start.10
  29.8 0.4 collective-permute-done.7.refs_4_
  30.2 0.3 collective-permute-done.8.refs_5_
  30.5 0.3 collective-permute-done.9.refs_6_
  30.8 0.3 collective-permute-done.10.refs_7_
  31.1 0.0 copy-start.1
  31.1 2.7 %particles.1 = (bf16[512,1536]{1,0:T(8,128)(2,1)S(1)}, f32[256,128]{1,0:T(8,128)S(1)}, f32[1,512]{1,0:T(1,128)S(1)}) custom-call(bf16[64,1664]{1,0:T(8,128)(2,1)S(1)} %pad_maximum_fusion.refs_0_, bf16[64,1664]{1,0:T(8,128)(2,1)S(1)} %collective-permute-done.4.refs_1_, bf16[64,1664]{1,0:T(8,128)(2,1)S(1)} %collective-permute-done.5.refs_2_, ...), custom_call_target="tpu_custom_call" | custom-call | tf_op jit(solution)/shard_map/particles/pallas_call | solution.py:461
  33.9 10.2 %all_to_all.11 = f32[32,8,128]{2,1,0:T(8,128)S(1)} all-to-all(f32[32,8,128]{2,1,0:T(8,128)S(1)} %bitcast.10), channel_id=1, replica_groups=mesh['gz'=4,'dom'=8] {'gz','dom'}, dimensions={0} | all-to-all | bytes 262144 | tf_op jit(solution)/shard_map/all_to_all | solution.py:474
  44.1 0.0 copy-done.1
  44.1 6.9 %spread.1 = (f32[1,16]{1,0:T(1,128)}, f32[24,4,384]{2,1,0:T(4,128)}) custom-call(s32[3008]{0:T(1024)S(1)} %copy-done.1, f32[128]{0:T(128)S(1)} %copy-done.2, f32[256,128]{1,0:T(8,128)S(1)} %bitcast.9, f32[1,512]{1,0:T(1,128)S(1)} %get-tuple-element.26.bins_row, bf16[512,1536]{1,0:T(8,128)(2,1)S(1)} %get-tuple-element.27.weighted), custom_call_target="tpu_custom_call" | custom-call | tf_op jit(solution)/shard_map/spread/pallas_call | solution.py:478
  (4 shorter events, 0.0 us)
Async XLA Ops:
  1.3 9.4 %collective-permute-start.3 = (f32[1,4,384]{2,1,0:T(4,128)S(1)}, f32[1,4,384]{2,1,0:T(4,128)S(1)}, u32[]{:S(2)}, u32[]{:S(2)}) collective-permute-start(f32[1,4,384]{2,1,0:T(4,128)S(1)} %slice.3), channel_id=1, source_target_pairs={{8,0},{16,8},{24,16},{9,1},{17,9},{25,17},{10,2},{18,10},{26,18},{... | collective-permute-start | bytes 18440 | tf_op jit(solution)/shard_map/ppermute | solution.py:417
  6.3 6.6 %collective-permute-start.2 = (bf16[16,1664]{1,0:T(8,128)(2,1)S(1)}, bf16[16,1664]{1,0:T(8,128)(2,1)S(1)}, u32[]{:S(2)}, u32[]{:S(2)}) collective-permute-start(bf16[16,1664]{1,0:T(8,128)(2,1)S(1)} %pad_maximum_fusion.1), channel_id=1, source_target_pairs={{0,6},{1,7},{2,4},{3,5},{4,2},{5,3},{6,0},{7,1},{8,14},{9,15},{10,... | collective-permute-start | bytes 159752 | tf_op jit(solution)/shard_map/ppermute | solution.py:400
  9.9 5.0 %collective-permute-start.1 = (bf16[16,1664]{1,0:T(8,128)(2,1)S(1)}, bf16[16,1664]{1,0:T(8,128)(2,1)S(1)}, u32[]{:S(2)}, u32[]{:S(2)}) collective-permute-start(bf16[16,1664]{1,0:T(8,128)(2,1)S(1)} %pad_maximum_fusion.1), channel_id=1, source_target_pairs={{0,4},{1,5},{2,6},{3,7},{4,0},{5,1},{6,2},{7,3},{8,12},{9,13},{10,... | collective-permute-start | bytes 159752 | tf_op jit(solution)/shard_map/ppermute | solution.py:400
  10.0 5.0 %collective-permute-start = (bf16[16,1664]{1,0:T(8,128)(2,1)S(1)}, bf16[16,1664]{1,0:T(8,128)(2,1)S(1)}, u32[]{:S(2)}, u32[]{:S(2)}) collective-permute-start(bf16[16,1664]{1,0:T(8,128)(2,1)S(1)} %pad_maximum_fusion.1), channel_id=1, source_target_pairs={{0,2},{1,3},{2,0},{3,1},{4,6},{5,7},{6,4},{7,5},{8,10},{9,11},{10,... | collective-permute-start | bytes 159752 | tf_op jit(solution)/shard_map/ppermute | solution.py:400
  15.0 13.6 %collective-permute-start.6 = (bf16[64,1664]{1,0:T(8,128)(2,1)S(1)}, bf16[64,1664]{1,0:T(8,128)(2,1)S(1)}, u32[]{:S(2)}, u32[]{:S(2)}) collective-permute-start(bf16[64,1664]{1,0:T(8,128)(2,1)S(1)} %pad_maximum_fusion.refs_0_), channel_id=1, source_target_pairs={{0,24},{8,16},{16,8},{24,0},{1,25},{9,17},{17,9},{25,1},{2,26},{10... | collective-permute-start | bytes 638984 | tf_op jit(solution)/shard_map/ppermute | solution.py:400
  15.6 13.0 %collective-permute-start.5 = (bf16[64,1664]{1,0:T(8,128)(2,1)S(1)}, bf16[64,1664]{1,0:T(8,128)(2,1)S(1)}, u32[]{:S(2)}, u32[]{:S(2)}) collective-permute-start(bf16[64,1664]{1,0:T(8,128)(2,1)S(1)} %pad_maximum_fusion.refs_0_), channel_id=1, source_target_pairs={{0,16},{8,24},{16,0},{24,8},{1,17},{9,25},{17,1},{25,9},{2,18},{10... | collective-permute-start | bytes 638984 | tf_op jit(solution)/shard_map/ppermute | solution.py:400
  17.1 11.5 %collective-permute-start.4 = (bf16[64,1664]{1,0:T(8,128)(2,1)S(1)}, bf16[64,1664]{1,0:T(8,128)(2,1)S(1)}, u32[]{:S(2)}, u32[]{:S(2)}) collective-permute-start(bf16[64,1664]{1,0:T(8,128)(2,1)S(1)} %pad_maximum_fusion.refs_0_), channel_id=1, source_target_pairs={{0,8},{8,0},{16,24},{24,16},{1,9},{9,1},{17,25},{25,17},{2,10},{10... | collective-permute-start | bytes 638984 | tf_op jit(solution)/shard_map/ppermute | solution.py:400
  18.6 0.9 %copy-start = (f32[32,2,384]{2,1,0:T(2,128)S(1)}, f32[32,2,384]{2,1,0:T(2,128)}, u32[]{:S(2)}) copy-start(f32[32,2,384]{2,1,0:T(2,128)} %refs_8_.1) | copy-start | bytes 294916
  19.5 0.7 %copy-start.2 = (f32[128]{0:T(128)S(1)}, f32[128]{0:T(128)}, u32[]{:S(2)}) copy-start(f32[128]{0:T(128)} %constant.24.clone.trig) | copy-start | bytes 1540
  20.1 1.3 %copy-start.3 = (f32[192,4,384]{2,1,0:T(4,128)S(1)}, f32[192,4,384]{2,1,0:T(4,128)}, u32[]{:S(2)}) copy-start(f32[192,4,384]{2,1,0:T(4,128)} %volume.1) | copy-start | bytes 3538948
  21.4 0.7 %copy-start.4 = (s32[1984]{0:T(1024)S(1)}, s32[1984]{0:T(1024)}, u32[]{:S(2)}) copy-start(s32[1984]{0:T(1024)} %constant.25.clone.table) | copy-start | bytes 23812
  28.7 1.5 %collective-permute-start.7 = (bf16[64,1664]{1,0:T(8,128)(2,1)S(1)}, bf16[64,1664]{1,0:T(8,128)(2,1)S(1)}, u32[]{:S(2)}, u32[]{:S(2)}) collective-permute-start(bf16[64,1664]{1,0:T(8,128)(2,1)S(1)} %pad_maximum_fusion.refs_0_), channel_id=1, source_target_pairs={{0,1},{1,0},{2,3},{3,2},{4,5},{5,4},{6,7},{7,6},{8,9},{9,8},{10,11... | collective-permute-start | bytes 638984 | tf_op jit(solution)/shard_map/ppermute | solution.py:400
  28.8 1.8 %collective-permute-start.8 = (bf16[64,1664]{1,0:T(8,128)(2,1)S(1)}, bf16[64,1664]{1,0:T(8,128)(2,1)S(1)}, u32[]{:S(2)}, u32[]{:S(2)}) collective-permute-start(bf16[64,1664]{1,0:T(8,128)(2,1)S(1)} %collective-permute-done.4.refs_1_), channel_id=1, source_target_pairs={{0,1},{1,0},{2,3},{3,2},{4,5},{5,4},{6,7},{7,6},{8,9},{9,8},{10,11... | collective-permute-start | bytes 638984 | tf_op jit(solution)/shard_map/ppermute | solution.py:400
  29.3 1.6 %collective-permute-start.9 = (bf16[64,1664]{1,0:T(8,128)(2,1)S(1)}, bf16[64,1664]{1,0:T(8,128)(2,1)S(1)}, u32[]{:S(2)}, u32[]{:S(2)}) collective-permute-start(bf16[64,1664]{1,0:T(8,128)(2,1)S(1)} %collective-permute-done.5.refs_2_), channel_id=1, source_target_pairs={{0,1},{1,0},{2,3},{3,2},{4,5},{5,4},{6,7},{7,6},{8,9},{9,8},{10,11... | collective-permute-start | bytes 638984 | tf_op jit(solution)/shard_map/ppermute | solution.py:400
  29.3 1.8 %collective-permute-start.10 = (bf16[64,1664]{1,0:T(8,128)(2,1)S(1)}, bf16[64,1664]{1,0:T(8,128)(2,1)S(1)}, u32[]{:S(2)}, u32[]{:S(2)}) collective-permute-start(bf16[64,1664]{1,0:T(8,128)(2,1)S(1)} %collective-permute-done.6.refs_3_), channel_id=1, source_target_pairs={{0,1},{1,0},{2,3},{3,2},{4,5},{5,4},{6,7},{7,6},{8,9},{9,8},{10,11... | collective-permute-start | bytes 638984 | tf_op jit(solution)/shard_map/ppermute | solution.py:400
  31.1 13.0 %copy-start.1 = (s32[3008]{0:T(1024)S(1)}, s32[3008]{0:T(1024)}, u32[]{:S(2)}) copy-start(s32[3008]{0:T(1024)} %constant.26.clone.table) | copy-start | bytes 36100

commit v6 on v5

--- a/solution.py
+++ b/solution.py
@@ -145,9 +145,44 @@
     return (core * n_gz + lax.axis_index("gz")) * n_z + z
 
 
+def fetch(pairs, sems):
+    copies = [pltpu.make_async_copy(a, b, sems.at[n]) for n, (a, b) in enumerate(pairs)]
+    for copy in copies:
+        copy.start()
+    return copies
+
+
+def pack_kernel(
+    observed_hbm, classes_hbm, bins_hbm, volume, packed, plane, observed, classes, bin_ids, sems
+):
+    copies = fetch(
+        [
+            (observed_hbm, observed),
+            (classes_hbm, classes),
+            (bins_hbm, bin_ids),
+            (volume.at[pl.ds(0, 1)], plane),
+        ],
+        sems,
+    )
+    for copy in copies:
+        copy.wait()
+    count, rows, samples = observed.shape
+    values = observed[...].astype(f32)
+    for r in range(rows):
+        packed[:, r * samples : (r + 1) * samples] = values[:, r, :].astype(bf16)
+    diagonal = lanes_of((count, count), 0) == lanes_of((count, count), 1)
+    lane = lanes_of((count, TILE), 1)
+    tail = jnp.zeros((count, TILE), f32)
+    for n, ids in enumerate((classes, bin_ids)):
+        column = jnp.where(diagonal, ids[...].astype(f32), 0.0)
+        tail = jnp.where(lane == n, jnp.sum(column, axis=1, keepdims=True), tail)
+    packed[:, rows * samples :] = tail.astype(bf16)
+
+
 def extract_kernel(
     groups, length, samples, bins, planes, n_dom,
-    table, trig, volume, above, ctf, slope, pairs, field, vhi, vlo, out, sem,
+    table_hbm, trig_hbm, volume, above, ctf_hbm, slope, pairs, flat,
+    table, trig, ctf, field, vhi, vlo, out, sems,
 ):
     depth = field.shape[0]
     xt_count = vhi.shape[0]
@@ -158,16 +193,21 @@
     first = device * planes
     z0, z1 = first.astype(f32), (first + planes).astype(f32)
 
-    own = pltpu.make_async_copy(
-        volume.at[pl.ds(dom * planes, planes)], field.at[pl.ds(0, planes)], sem.at[0]
+    copies = fetch(
+        [
+            (volume.at[pl.ds(dom * planes, planes)], field.at[pl.ds(0, planes)]),
+            (table_hbm, table),
+            (trig_hbm, trig),
+            (ctf_hbm, ctf),
+        ],
+        sems,
     )
-    own.start()
-
     field[planes] = above[0]
     for z in range(planes + 1, depth):
         field[z] = jnp.zeros(field.shape[1:], f32)
     out[...] = jnp.zeros_like(out)
-    own.wait()
+    for copy in copies:
+        copy.wait()
     for xt in range(xt_count):
         stacked = jnp.concatenate(
             [field[:, r, xt * TILE : (xt + 1) * TILE] for r in range(4)], 0
@@ -229,9 +269,10 @@
             square.append(square_sum)
             mixed.append(mixed_sum)
     moments = jnp.concatenate([jnp.concatenate(square, 1), jnp.concatenate(mixed, 1)], 0)
-    flat = jnp.concatenate([ctf[:, 0, :], ctf[:, 1, :]], 1)
+    contrast = jnp.concatenate([ctf[:, 0, :], ctf[:, 1, :]], 1)
+    flat[...] = contrast
     product = lax.dot_general(
-        flat * flat, moments, NT, precision=lax.Precision.HIGHEST, preferred_element_type=f32
+        contrast * contrast, moments, NT, precision=lax.Precision.HIGHEST, preferred_element_type=f32
     )
     pairs[...] = jnp.concatenate(split3(product), 1)
 
@@ -243,7 +284,7 @@
     joined = max(1, CHUNK // size)
     both = slope.shape[0]
     bins = both // 2
-    flat = jnp.concatenate([ctf[:, 0, :], ctf[:, 1, :]], 1)
+    flat = ctf[...]
     ctf_hi = flat.astype(bf16)
     ctf_lo = (flat - ctf_hi.astype(f32)).astype(bf16)
     upper = jnp.where(lanes_of((8, both), 1) >= bins, 1.0, 0.0)
@@ -410,11 +451,31 @@
     count = mine * devices
     width = rows * samples
     xt_count, ut_count = columns // TILE, samples // TILE
-    ids = jnp.stack([ctf_class, bin_ids], 1).astype(bf16)
-    ids = jnp.pad(ids, ((0, 0), (0, TILE - 2)))
-    packed = jnp.concatenate([observed.reshape(mine, width), ids], 1)
+    smem = pl.BlockSpec(memory_space=pltpu.SMEM)
+    vmem = pl.BlockSpec(memory_space=pltpu.VMEM)
+    hbm = pl.BlockSpec(memory_space=pltpu.HBM)
+    wide = pltpu.CompilerParams(vmem_limit_bytes=60 * 2**20)
+    params = pltpu.CompilerParams(vmem_limit_bytes=min(56, 19 + 37 * count // 4096) * 2**20)
+    packed, plane = pl.pallas_call(
+        pack_kernel,
+        out_shape=[
+            jax.ShapeDtypeStruct((mine, width + TILE), bf16),
+            jax.ShapeDtypeStruct((1, rows, columns), f32),
+        ],
+        in_specs=[hbm] * 4,
+        out_specs=[vmem, vmem],
+        scratch_shapes=[
+            pltpu.VMEM(observed.shape, bf16),
+            pltpu.VMEM((1, mine), jnp.int32),
+            pltpu.VMEM((1, mine), jnp.int32),
+            pltpu.SemaphoreType.DMA((4,)),
+        ],
+        compiler_params=wide,
+        name="pack",
+    )(observed, ctf_class.reshape(1, mine), bin_ids.reshape(1, mine), volume)
+
     n_z = n_dom // 2
-    above = lax.ppermute(volume[:1], "gz", [(i, i - 1) for i in range(1, n_gz)])
+    above = lax.ppermute(plane, "gz", [(i, i - 1) for i in range(1, n_gz)])
     column = jnp.concatenate(
         [packed] + [swap(packed, "dom", n_dom, 2 * k) for k in range(1, n_z)], 0
     )
@@ -429,27 +490,27 @@
     trig = jnp.asarray(trig)
     depth_in = round_up(planes + 1, 8)
 
-    smem = pl.BlockSpec(memory_space=pltpu.SMEM)
-    vmem = pl.BlockSpec(memory_space=pltpu.VMEM)
-    hbm = pl.BlockSpec(memory_space=pl.ANY)
-    params = pltpu.CompilerParams(vmem_limit_bytes=min(56, 19 + 37 * count // 4096) * 2**20)
     table, groups = extract_plan
-    slope, pairs = pl.pallas_call(
+    slope, pairs, flat_ctf = pl.pallas_call(
         functools.partial(
             extract_kernel, groups, table.shape[1], samples, bins, planes, n_dom
         ),
         out_shape=[
             jax.ShapeDtypeStruct((2 * bins, width), bf16),
             jax.ShapeDtypeStruct((NCTF, 6 * bins), bf16),
-        ],
-        in_specs=[smem, smem, hbm, vmem, vmem],
-        out_specs=[vmem, vmem],
+            jax.ShapeDtypeStruct((NCTF, width // 2), f32),
+        ],
+        in_specs=[hbm, hbm, hbm, vmem, hbm],
+        out_specs=[vmem, vmem, vmem],
         scratch_shapes=[
+            pltpu.SMEM((table.size,), jnp.int32),
+            pltpu.SMEM(trig.shape, f32),
+            pltpu.VMEM(ctf_table.shape, f32),
             pltpu.VMEM((depth_in, rows, columns), f32),
             pltpu.VMEM((xt_count, rows * depth_in, TILE), bf16),
             pltpu.VMEM((xt_count, rows * depth_in, TILE), bf16),
             pltpu.VMEM((bins * ut_count * 2 * rows, TILE), f32),
-            pltpu.SemaphoreType.DMA((1,)),
+            pltpu.SemaphoreType.DMA((4,)),
         ],
         compiler_params=params,
         cost_estimate=pl.CostEstimate(flops=6 * 10**9, bytes_accessed=2**20, transcendentals=0),
@@ -469,7 +530,7 @@
         out_specs=[vmem] * 3,
         compiler_params=params,
         name="particles",
-    )(*gathered, ctf_table, slope, pairs)
+    )(*gathered, flat_ctf, slope, pairs)
 
     parts = lax.all_to_all(parts, ("gz", "dom"), 0, 0, tiled=True)
 

time: 51.4 us -> 49 us (0.953)
  local copies, waits for them, and re-layouts: 5.12 us -> 0.03 us
  Pallas kernels: 16.1 us -> 17.8 us
  waiting for transfers between devices: 4.91 us -> 5.88 us
  blocking collectives: 10.2 us -> 11.1 us
  other arithmetic: 1.42 us -> 0.83 us
    unnamed x11 -> x10, local copies, waits for them, and re-layouts: 4.32 us -> 0.03 us
    pallas_call x0 -> x1, Pallas kernels: none -> 1.7 us  [local(): pl.pallas_call(pack_kernel, out_shape=[jax.ShapeDtypeStruct((mine, width...]
    ppermute x10, waiting for transfers between devices: 4.91 us -> 5.88 us  [swap(): return lax.ppermute(x, axis, [(i, i ^ distance) for i in range(size)])]
    all_to_all x1, blocking collectives: 10.2 us -> 11.1 us  [local(): parts = lax.all_to_all(parts, ('gz', 'dom'), 0, 0, tiled=True)]
    concatenate x1, other arithmetic: 0.02 us -> 0.83 us  [local(): jnp.concatenate([packed] + [swap(packed, 'dom', n_dom, 2 * k) for k in ra...]
    slice x1 -> x0, local copies, waits for them, and re-layouts: 0.7 us -> none  [local(): above = lax.ppermute(volume[:1], 'gz', [(i, i - 1) for i in range(1, n_gz)])]
    select_n x1, other arithmetic: 0.7 us -> 0.01 us  [local(): above = jnp.where(lax.axis_index('dom') == n_dom - 1, above, inner)]
    another operation x2 -> x0, other arithmetic: 0.69 us -> none  [local(): ids = jnp.stack([ctf_class, bin_ids], 1).astype(bf16)]
  transfers between devices with their start and end apart: 11 -> 11, of which waited for: 6 -> 7; matrix products, arithmetic and copies ran while one was open for 5% -> 0% of each run, Pallas kernels for 13% -> 13%
where the time goes in v6:
time: 49 us; the launch traced here: 48.7 us
  Pallas kernels  17.8 us (36%)
  starting transfers between devices  12.4 us (25%)
  blocking collectives  11.1 us (23%)
  waiting for transfers between devices  5.88 us (12%)
  other arithmetic  0.83 us (2%)
  between operations  0.73 us (1%)
    all_to_all x1, blocking collectives, local(): parts = lax.all_to_all(parts, ('gz', 'dom'), 0, 0, tiled=True)  11.1 us
    ppermute x10, starting transfers between devices, swap(): return lax.ppermute(x, axis, [(i, i ^ distance) for i in range(size)])  9.03 us
    pallas_call x1, Pallas kernels, local(): pl.pallas_call(functools.partial(spread_kernel, groups, table.shape[1], p...  6.85 us
    pallas_call x1, Pallas kernels, local(): pl.pallas_call(functools.partial(extract_kernel, groups, table.shape[1],...  6.53 us
    ppermute x10, waiting for transfers between devices, swap(): return lax.ppermute(x, axis, [(i, i ^ distance) for i in range(size)])  5.88 us
    ppermute x1, starting transfers between devices, local(): above = lax.ppermute(plane, 'gz', [(i, i - 1) for i in range(1, n_gz)])  3.34 us
    pallas_call x1, Pallas kernels, local(): pl.pallas_call(functools.partial(particle_kernel, width, mine, n_gz, n_do...  2.73 us
    pallas_call x1, Pallas kernels, local(): pl.pallas_call(pack_kernel, out_shape=[jax.ShapeDtypeStruct((mine, width...  1.7 us
  transfers between devices with their start and end apart: 11, of which 7 were waited for; matrix products, arithmetic and copies ran while one was open for 0% of the time, Pallas kernels for 13%

profile of v6, /device:TPU:4, one launch (start us, length us, event | category | flops | bytes accessed | tf_op | source)
XLA Modules:
  0.0 48.7 jit_solution(5215038193905551659)
XLA Ops:
  0.6 0.0 copy-start.2
  0.6 0.0 copy-start.4
  0.7 0.0 copy-start
  0.7 0.0 copy-start.3
  0.7 1.7 %pack.1 = (bf16[16,1664]{1,0:T(8,128)(2,1)}, f32[1,4,384]{2,1,0:T(4,128)}) custom-call(bf16[16,4,384]{2,1,0:T(4,128)(2,1)} %observed_hbm.1, s32[1,16]{1,0:T(1,128)} %bitcast.7, s32[1,16]{1,0:T(1,128)} %bitcast.8, f32[192,4,384]{2,1,0:T(4,128)} %volume.3), custom_call_target="tpu_custom_call" | custom-call | tf_op jit(solution)/shard_map/pack/pallas_call | solution.py:459
  2.4 3.3 %collective-permute-start.3 = (f32[1,4,384]{2,1,0:T(4,128)}, f32[1,4,384]{2,1,0:T(4,128)S(1)}, u32[]{:S(2)}, u32[]{:S(2)}) collective-permute-start(f32[1,4,384]{2,1,0:T(4,128)} %get-tuple-element.20), channel_id=1, source_target_pairs={{8,0},{16,8},{24,16},{9,1},{17,9},{25,17},{10,2},{18,10},{26,18},{... | collective-permute-start | bytes 18440 | tf_op jit(solution)/shard_map/ppermute | solution.py:478
  5.7 3.7 %collective-permute-start.2 = (bf16[16,1664]{1,0:T(8,128)(2,1)}, bf16[16,1664]{1,0:T(8,128)(2,1)S(1)}, u32[]{:S(2)}, u32[]{:S(2)}) collective-permute-start(bf16[16,1664]{1,0:T(8,128)(2,1)} %get-tuple-element.19), channel_id=1, source_target_pairs={{0,6},{1,7},{2,4},{3,5},{4,2},{5,3},{6,0},{7,1},{8,14},{9,15},{10,... | collective-permute-start | bytes 159752 | tf_op jit(solution)/shard_map/ppermute | solution.py:441
  9.4 0.0 collective-permute-start.1
  9.4 0.8 %collective-permute-start = (bf16[16,1664]{1,0:T(8,128)(2,1)}, bf16[16,1664]{1,0:T(8,128)(2,1)S(1)}, u32[]{:S(2)}, u32[]{:S(2)}) collective-permute-start(bf16[16,1664]{1,0:T(8,128)(2,1)} %get-tuple-element.19), channel_id=1, source_target_pairs={{0,2},{1,3},{2,0},{3,1},{4,6},{5,7},{6,4},{7,5},{8,10},{9,11},{10,... | collective-permute-start | bytes 159752 | tf_op jit(solution)/shard_map/ppermute | solution.py:441
  10.2 0.0 collective-permute-done.3
  10.2 0.0 copy-done
  10.2 2.4 %collective-permute-done.2 = bf16[16,1664]{1,0:T(8,128)(2,1)S(1)} collective-permute-done((bf16[16,1664]{1,0:T(8,128)(2,1)}, bf16[16,1664]{1,0:T(8,128)(2,1)S(1)}, u32[]{:S(2)}, u32[]{:S(2)}) %collective-permute-start.2) | collective-permute-done | bytes 53280 | tf_op jit(solution)/shard_map/ppermute | solution.py:441
  12.6 2.1 %collective-permute-done.1 = bf16[16,1664]{1,0:T(8,128)(2,1)S(1)} collective-permute-done((bf16[16,1664]{1,0:T(8,128)(2,1)}, bf16[16,1664]{1,0:T(8,128)(2,1)S(1)}, u32[]{:S(2)}, u32[]{:S(2)}) %collective-permute-start.1) | collective-permute-done | bytes 53280 | tf_op jit(solution)/shard_map/ppermute | solution.py:441
  14.6 0.0 collective-permute-done
  14.6 0.8 %pad_maximum_fusion.refs_0_ = bf16[64,1664]{1,0:T(8,128)(2,1)S(1)} fusion(bf16[16,1664]{1,0:T(8,128)(2,1)S(1)} %collective-permute-done.2, bf16[16,1664]{1,0:T(8,128)(2,1)S(1)} %collective-permute-done.1, bf16[16,1664]{1,0:T(8,128)(2,1)S(1)} %collective-permute-done, bf16[16,1664]{1,0:T(8,128)(2,1)} %get-tuple-element.19), kind=kLoop, calls=%fused_computation | loop fusion | flops 851968 | bytes 425984 | tf_op jit(solution)/shard_map/concatenate | solution.py:479
  15.5 0.6 %collective-permute-start.6 = (bf16[64,1664]{1,0:T(8,128)(2,1)S(1)}, bf16[64,1664]{1,0:T(8,128)(2,1)S(1)}, u32[]{:S(2)}, u32[]{:S(2)}) collective-permute-start(bf16[64,1664]{1,0:T(8,128)(2,1)S(1)} %pad_maximum_fusion.refs_0_), channel_id=1, source_target_pairs={{0,24},{8,16},{16,8},{24,0},{1,25},{9,17},{17,9},{25,1},{2,26},{10... | collective-permute-start | bytes 638984 | tf_op jit(solution)/shard_map/ppermute | solution.py:441
  16.1 1.5 %collective-permute-start.5 = (bf16[64,1664]{1,0:T(8,128)(2,1)S(1)}, bf16[64,1664]{1,0:T(8,128)(2,1)S(1)}, u32[]{:S(2)}, u32[]{:S(2)}) collective-permute-start(bf16[64,1664]{1,0:T(8,128)(2,1)S(1)} %pad_maximum_fusion.refs_0_), channel_id=1, source_target_pairs={{0,16},{8,24},{16,0},{24,8},{1,17},{9,25},{17,1},{25,9},{2,18},{10... | collective-permute-start | bytes 638984 | tf_op jit(solution)/shard_map/ppermute | solution.py:441
  17.6 1.4 %collective-permute-start.4 = (bf16[64,1664]{1,0:T(8,128)(2,1)S(1)}, bf16[64,1664]{1,0:T(8,128)(2,1)S(1)}, u32[]{:S(2)}, u32[]{:S(2)}) collective-permute-start(bf16[64,1664]{1,0:T(8,128)(2,1)S(1)} %pad_maximum_fusion.refs_0_), channel_id=1, source_target_pairs={{0,8},{8,0},{16,24},{24,16},{1,9},{9,1},{17,25},{25,17},{2,10},{10... | collective-permute-start | bytes 638984 | tf_op jit(solution)/shard_map/ppermute | solution.py:441
  19.0 0.0 copy-done.2
  19.0 0.0 copy-done.4
  19.0 0.0 copy-done.3
  19.0 6.5 %extract.1 = (bf16[128,1536]{1,0:T(8,128)(2,1)S(1)}, bf16[32,384]{1,0:T(8,128)(2,1)S(1)}, f32[32,768]{1,0:T(8,128)S(1)}) custom-call(s32[1984]{0:T(1024)S(1)} %copy-done.4, f32[128]{0:T(128)S(1)} %copy-done.2, f32[192,4,384]{2,1,0:T(4,128)S(1)} %copy-done, f32[1,4,384]{2,1,0:T(4,128)S(1)} %dynamic-slice_select_fusion.above, f32[32,2,384]{2,1,0:T(2,128)S(1)} %copy-done.3), custom_call_target="tpu_custom_call" | custom-call | flops 6000000000 | bytes 1048576 | tf_op jit(solution)/shard_map/extract/pallas_call | solution.py:494
  25.6 0.0 collective-permute-done.6.refs_3_
  25.6 0.1 collective-permute-done.5.refs_2_
  25.7 0.0 collective-permute-done.4.refs_1_
  25.7 0.0 collective-permute-start.7
  25.7 0.5 %collective-permute-start.8 = (bf16[64,1664]{1,0:T(8,128)(2,1)S(1)}, bf16[64,1664]{1,0:T(8,128)(2,1)S(1)}, u32[]{:S(2)}, u32[]{:S(2)}) collective-permute-start(bf16[64,1664]{1,0:T(8,128)(2,1)S(1)} %collective-permute-done.4.refs_1_), channel_id=1, source_target_pairs={{0,1},{1,0},{2,3},{3,2},{4,5},{5,4},{6,7},{7,6},{8,9},{9,8},{10,11... | collective-permute-start | bytes 638984 | tf_op jit(solution)/shard_map/ppermute | solution.py:441
  26.2 0.1 collective-permute-start.9
  26.3 0.4 collective-permute-start.10
  26.7 0.4 collective-permute-done.7.refs_4_
  27.1 0.3 collective-permute-done.8.refs_5_
  27.4 0.3 collective-permute-done.9.refs_6_
  27.7 0.3 collective-permute-done.10.refs_7_
  28.1 0.0 copy-start.1
  28.1 2.7 %particles.1 = (bf16[512,1536]{1,0:T(8,128)(2,1)S(1)}, f32[256,128]{1,0:T(8,128)S(1)}, f32[1,512]{1,0:T(1,128)S(1)}) custom-call(bf16[64,1664]{1,0:T(8,128)(2,1)S(1)} %pad_maximum_fusion.refs_0_, bf16[64,1664]{1,0:T(8,128)(2,1)S(1)} %collective-permute-done.4.refs_1_, bf16[64,1664]{1,0:T(8,128)(2,1)S(1)} %collective-permute-done.5.refs_2_, ...), custom_call_target="tpu_custom_call" | custom-call | tf_op jit(solution)/shard_map/particles/pallas_call | solution.py:522
  30.8 11.1 %all_to_all.11 = f32[32,8,128]{2,1,0:T(8,128)S(1)} all-to-all(f32[32,8,128]{2,1,0:T(8,128)S(1)} %bitcast.6), channel_id=1, replica_groups=mesh['gz'=4,'dom'=8] {'gz','dom'}, dimensions={0} | all-to-all | bytes 262144 | tf_op jit(solution)/shard_map/all_to_all | solution.py:535
  41.9 0.0 copy-done.1
  41.9 6.9 %spread.1 = (f32[1,16]{1,0:T(1,128)}, f32[24,4,384]{2,1,0:T(4,128)}) custom-call(s32[3008]{0:T(1024)S(1)} %copy-done.1, f32[128]{0:T(128)S(1)} %copy-done.2, f32[256,128]{1,0:T(8,128)S(1)} %bitcast.5, f32[1,512]{1,0:T(1,128)S(1)} %get-tuple-element.32.bins_row, bf16[512,1536]{1,0:T(8,128)(2,1)S(1)} %get-tuple-element.33.weighted), custom_call_target="tpu_custom_call" | custom-call | tf_op jit(solution)/shard_map/spread/pallas_call | solution.py:539
  (1 shorter events, 0.0 us)
Async XLA Ops:
  0.6 18.4 %copy-start.2 = (f32[128]{0:T(128)S(1)}, f32[128]{0:T(128)}, u32[]{:S(2)}) copy-start(f32[128]{0:T(128)} %constant.22.clone.trig_hbm.trig) | copy-start | bytes 1540
  0.6 18.4 %copy-start.4 = (s32[1984]{0:T(1024)S(1)}, s32[1984]{0:T(1024)}, u32[]{:S(2)}) copy-start(s32[1984]{0:T(1024)} %constant.23.clone.table_hbm) | copy-start | bytes 23812
  0.7 9.5 %copy-start = (f32[192,4,384]{2,1,0:T(4,128)S(1)}, f32[192,4,384]{2,1,0:T(4,128)}, u32[]{:S(2)}) copy-start(f32[192,4,384]{2,1,0:T(4,128)} %volume.3) | copy-start | bytes 3538948
  0.7 18.4 %copy-start.3 = (f32[32,2,384]{2,1,0:T(2,128)S(1)}, f32[32,2,384]{2,1,0:T(2,128)}, u32[]{:S(2)}) copy-start(f32[32,2,384]{2,1,0:T(2,128)} %ctf_hbm.1) | copy-start | bytes 294916
  2.4 7.8 %collective-permute-start.3 = (f32[1,4,384]{2,1,0:T(4,128)}, f32[1,4,384]{2,1,0:T(4,128)S(1)}, u32[]{:S(2)}, u32[]{:S(2)}) collective-permute-start(f32[1,4,384]{2,1,0:T(4,128)} %get-tuple-element.20), channel_id=1, source_target_pairs={{8,0},{16,8},{24,16},{9,1},{17,9},{25,17},{10,2},{18,10},{26,18},{... | collective-permute-start | bytes 18440 | tf_op jit(solution)/shard_map/ppermute | solution.py:478
  5.7 6.8 %collective-permute-start.2 = (bf16[16,1664]{1,0:T(8,128)(2,1)}, bf16[16,1664]{1,0:T(8,128)(2,1)S(1)}, u32[]{:S(2)}, u32[]{:S(2)}) collective-permute-start(bf16[16,1664]{1,0:T(8,128)(2,1)} %get-tuple-element.19), channel_id=1, source_target_pairs={{0,6},{1,7},{2,4},{3,5},{4,2},{5,3},{6,0},{7,1},{8,14},{9,15},{10,... | collective-permute-start | bytes 159752 | tf_op jit(solution)/shard_map/ppermute | solution.py:441
  9.4 5.2 %collective-permute-start.1 = (bf16[16,1664]{1,0:T(8,128)(2,1)}, bf16[16,1664]{1,0:T(8,128)(2,1)S(1)}, u32[]{:S(2)}, u32[]{:S(2)}) collective-permute-start(bf16[16,1664]{1,0:T(8,128)(2,1)} %get-tuple-element.19), channel_id=1, source_target_pairs={{0,4},{1,5},{2,6},{3,7},{4,0},{5,1},{6,2},{7,3},{8,12},{9,13},{10,... | collective-permute-start | bytes 159752 | tf_op jit(solution)/shard_map/ppermute | solution.py:441
  9.4 5.2 %collective-permute-start = (bf16[16,1664]{1,0:T(8,128)(2,1)}, bf16[16,1664]{1,0:T(8,128)(2,1)S(1)}, u32[]{:S(2)}, u32[]{:S(2)}) collective-permute-start(bf16[16,1664]{1,0:T(8,128)(2,1)} %get-tuple-element.19), channel_id=1, source_target_pairs={{0,2},{1,3},{2,0},{3,1},{4,6},{5,7},{6,4},{7,5},{8,10},{9,11},{10,... | collective-permute-start | bytes 159752 | tf_op jit(solution)/shard_map/ppermute | solution.py:441
  15.5 10.1 %collective-permute-start.6 = (bf16[64,1664]{1,0:T(8,128)(2,1)S(1)}, bf16[64,1664]{1,0:T(8,128)(2,1)S(1)}, u32[]{:S(2)}, u32[]{:S(2)}) collective-permute-start(bf16[64,1664]{1,0:T(8,128)(2,1)S(1)} %pad_maximum_fusion.refs_0_), channel_id=1, source_target_pairs={{0,24},{8,16},{16,8},{24,0},{1,25},{9,17},{17,9},{25,1},{2,26},{10... | collective-permute-start | bytes 638984 | tf_op jit(solution)/shard_map/ppermute | solution.py:441
  16.1 9.6 %collective-permute-start.5 = (bf16[64,1664]{1,0:T(8,128)(2,1)S(1)}, bf16[64,1664]{1,0:T(8,128)(2,1)S(1)}, u32[]{:S(2)}, u32[]{:S(2)}) collective-permute-start(bf16[64,1664]{1,0:T(8,128)(2,1)S(1)} %pad_maximum_fusion.refs_0_), channel_id=1, source_target_pairs={{0,16},{8,24},{16,0},{24,8},{1,17},{9,25},{17,1},{25,9},{2,18},{10... | collective-permute-start | bytes 638984 | tf_op jit(solution)/shard_map/ppermute | solution.py:441
  17.6 8.1 %collective-permute-start.4 = (bf16[64,1664]{1,0:T(8,128)(2,1)S(1)}, bf16[64,1664]{1,0:T(8,128)(2,1)S(1)}, u32[]{:S(2)}, u32[]{:S(2)}) collective-permute-start(bf16[64,1664]{1,0:T(8,128)(2,1)S(1)} %pad_maximum_fusion.refs_0_), channel_id=1, source_target_pairs={{0,8},{8,0},{16,24},{24,16},{1,9},{9,1},{17,25},{25,17},{2,10},{10... | collective-permute-start | bytes 638984 | tf_op jit(solution)/shard_map/ppermute | solution.py:441
  25.7 1.5 %collective-permute-start.7 = (bf16[64,1664]{1,0:T(8,128)(2,1)S(1)}, bf16[64,1664]{1,0:T(8,128)(2,1)S(1)}, u32[]{:S(2)}, u32[]{:S(2)}) collective-permute-start(bf16[64,1664]{1,0:T(8,128)(2,1)S(1)} %pad_maximum_fusion.refs_0_), channel_id=1, source_target_pairs={{0,1},{1,0},{2,3},{3,2},{4,5},{5,4},{6,7},{7,6},{8,9},{9,8},{10,11... | collective-permute-start | bytes 638984 | tf_op jit(solution)/shard_map/ppermute | solution.py:441
  25.7 1.8 %collective-permute-start.8 = (bf16[64,1664]{1,0:T(8,128)(2,1)S(1)}, bf16[64,1664]{1,0:T(8,128)(2,1)S(1)}, u32[]{:S(2)}, u32[]{:S(2)}) collective-permute-start(bf16[64,1664]{1,0:T(8,128)(2,1)S(1)} %collective-permute-done.4.refs_1_), channel_id=1, source_target_pairs={{0,1},{1,0},{2,3},{3,2},{4,5},{5,4},{6,7},{7,6},{8,9},{9,8},{10,11... | collective-permute-start | bytes 638984 | tf_op jit(solution)/shard_map/ppermute | solution.py:441
  26.2 1.6 %collective-permute-start.9 = (bf16[64,1664]{1,0:T(8,128)(2,1)S(1)}, bf16[64,1664]{1,0:T(8,128)(2,1)S(1)}, u32[]{:S(2)}, u32[]{:S(2)}) collective-permute-start(bf16[64,1664]{1,0:T(8,128)(2,1)S(1)} %collective-permute-done.5.refs_2_), channel_id=1, source_target_pairs={{0,1},{1,0},{2,3},{3,2},{4,5},{5,4},{6,7},{7,6},{8,9},{9,8},{10,11... | collective-permute-start | bytes 638984 | tf_op jit(solution)/shard_map/ppermute | solution.py:441
  26.3 1.8 %collective-permute-start.10 = (bf16[64,1664]{1,0:T(8,128)(2,1)S(1)}, bf16[64,1664]{1,0:T(8,128)(2,1)S(1)}, u32[]{:S(2)}, u32[]{:S(2)}) collective-permute-start(bf16[64,1664]{1,0:T(8,128)(2,1)S(1)} %collective-permute-done.6.refs_3_), channel_id=1, source_target_pairs={{0,1},{1,0},{2,3},{3,2},{4,5},{5,4},{6,7},{7,6},{8,9},{9,8},{10,11... | collective-permute-start | bytes 638984 | tf_op jit(solution)/shard_map/ppermute | solution.py:441
  28.1 13.8 %copy-start.1 = (s32[3008]{0:T(1024)S(1)}, s32[3008]{0:T(1024)}, u32[]{:S(2)}) copy-start(s32[3008]{0:T(1024)} %constant.24.clone.table) | copy-start | bytes 36100

commit v7 on v6

--- a/solution.py
+++ b/solution.py
@@ -164,7 +164,7 @@
         ],
         sems,
     )
-    for copy in copies:
+    for copy in copies[:3]:
         copy.wait()
     count, rows, samples = observed.shape
     values = observed[...].astype(f32)
@@ -177,6 +177,7 @@
         column = jnp.where(diagonal, ids[...].astype(f32), 0.0)
         tail = jnp.where(lane == n, jnp.sum(column, axis=1, keepdims=True), tail)
     packed[:, rows * samples :] = tail.astype(bf16)
+    copies[3].wait()
 
 
 def extract_kernel(
@@ -331,9 +332,38 @@
         parts[n * rows : (n + 1) * rows, :] = scalars
 
 
+def weight_kernel(groups, length, bins, planes, n_dom, edge_samples, table, trig, right, edges):
+    device = lax.axis_index("gz") * n_dom + lax.axis_index("dom")
+    row = device * length
+    uu = lanes_of((TILE, TILE), 0)
+
+    def step(j, carry):
+        xx = lanes_of((1, TILE), 1) + (table[row + 1 + j] * TILE).astype(f32)
+        for k in range(GROUP):
+            at = row + 1 + groups + j * GROUP + k
+            _, _, _, c, base = block_of(table, trig, at, bins)
+            for n, part in enumerate(bump((xx - base * c) - uu * c)):
+                right[j, (2 * k + n) * TILE : (2 * k + n + 1) * TILE, :] = part.astype(bf16)
+        return carry
+
+    lax.fori_loop(0, table[row], step, 0)
+    tail = row + 1 + groups * (1 + GROUP)
+
+    def edge(j, carry):
+        for k in range(EDGE_GROUP):
+            at = j * EDGE_GROUP + k
+            _, _, _, c, _ = block_of(table, trig, tail + 1 + at, bins)
+            uu = lanes_of((edge_samples, TILE), 0)
+            for n, part in enumerate(bump(lanes_of((1, TILE), 1) - uu * c)):
+                edges[at, n * edge_samples : (n + 1) * edge_samples, :] = part.astype(bf16)
+        return carry
+
+    lax.fori_loop(0, table[tail], edge, 0)
+
+
 def spread_kernel(
     groups, length, planes, samples, edge_samples, mine, n_gz, n_dom,
-    table, trig, parts, bins_row, weighted, pose, out, sums, total, poses,
+    table, trig, right, edges, parts, bins_row, weighted, pose, out, sums, total, poses,
 ):
     tiles, bins = sums.shape[0] // 2, sums.shape[1]
     ut_count = samples // TILE
@@ -379,9 +409,7 @@
 
     def step(j, carry):
         xt = table[row + 1 + j]
-        xx = lanes_of((1, TILE), 1) + (xt * TILE).astype(f32)
-        uu = lanes_of((TILE, TILE), 0)
-        left, right = [], []
+        left = []
         for k in range(GROUP):
             at = row + 1 + groups + j * GROUP + k
             b, ut, s, c, base = block_of(table, trig, at, bins)
@@ -394,12 +422,11 @@
                 first.append(kz * direct + kzd * (tilted * z_factor))
                 second.append(kz * (tilted * x_factor))
             left += [jnp.concatenate(first, 0), jnp.concatenate(second, 0)]
-            right += [k.astype(bf16) for k in bump((xx - base * c) - uu * c)]
         left = jnp.concatenate(left, 1)
         hi = left.astype(bf16)
         lo = (left - hi.astype(f32)).astype(bf16)
         both = jnp.dot(
-            jnp.concatenate([hi, lo], 0), jnp.concatenate(right, 0), preferred_element_type=f32
+            jnp.concatenate([hi, lo], 0), right[j], preferred_element_type=f32
         )
         total[xt] = total[xt] + both[: 4 * depth] + both[4 * depth :]
         return carry
@@ -408,8 +435,8 @@
     tail = row + 1 + groups * (1 + GROUP)
 
     def edge(j, carry):
-        left, right = [], []
-        rest = jnp.zeros((TILE - edge_samples, TILE), f32)
+        left, below = [], []
+        rest = jnp.zeros((TILE - edge_samples, TILE), bf16)
         for k in range(EDGE_GROUP):
             b, _, s, c, _ = block_of(table, trig, tail + 1 + j * EDGE_GROUP + k, bins)
             u = lanes_of((1, TILE), 1)
@@ -421,13 +448,12 @@
                 [sums[tiles + r * ut_count, pl.ds(b, 1), :] for r in range(4)], 0
             )
             left += [kz * direct + (kzd * z_factor) * tilted, (kz * x_factor) * tilted]
-            uu = lanes_of((edge_samples, TILE), 0)
-            for part in bump(lanes_of((1, TILE), 1) - uu * c):
-                right.append(jnp.concatenate([part, rest], 0).astype(bf16))
+            part = edges[j * EDGE_GROUP + k]
+            below += [part[:edge_samples], rest, part[edge_samples:], rest]
         left = jnp.concatenate(left, 1)
         hi = left.astype(bf16).astype(f32)
         split = jnp.concatenate([hi, left - hi], 0).astype(bf16)
-        both = jnp.dot(split, jnp.concatenate(right, 0), preferred_element_type=f32)
+        both = jnp.dot(split, jnp.concatenate(below, 0), preferred_element_type=f32)
         return carry + both[:4] + both[4:]
 
     extra = lax.fori_loop(0, table[tail], edge, jnp.zeros((4, TILE), f32))
@@ -456,6 +482,8 @@
     hbm = pl.BlockSpec(memory_space=pltpu.HBM)
     wide = pltpu.CompilerParams(vmem_limit_bytes=60 * 2**20)
     params = pltpu.CompilerParams(vmem_limit_bytes=min(56, 19 + 37 * count // 4096) * 2**20)
+    extract_plan, spread_plan, edge_samples, trig = make_plan(devices, bins, samples, columns)
+    trig = jnp.asarray(trig)
     packed, plane = pl.pallas_call(
         pack_kernel,
         out_shape=[
@@ -483,11 +511,25 @@
         volume, jnp.minimum((lax.axis_index("dom") + 1) * planes, slab - 1), 1, 0
     )
     above = jnp.where(lax.axis_index("dom") == n_dom - 1, above, inner)
-    column, above = lax.optimization_barrier((column, above))
+    spread_table, spread_groups = spread_plan
+    spread_table_flat = jnp.asarray(spread_table.reshape(-1))
+    right, edges = pl.pallas_call(
+        functools.partial(
+            weight_kernel, spread_groups, spread_table.shape[1], bins, planes, n_dom, edge_samples
+        ),
+        out_shape=[
+            jax.ShapeDtypeStruct((spread_groups, GROUP * 2 * TILE, TILE), bf16),
+            jax.ShapeDtypeStruct((bins // 2, 2 * edge_samples, TILE), bf16),
+        ],
+        in_specs=[smem, smem],
+        out_specs=[vmem, vmem],
+        compiler_params=params,
+        cost_estimate=pl.CostEstimate(flops=3 * 10**9, bytes_accessed=2**21, transcendentals=0),
+        name="weights",
+    )(spread_table_flat, trig)
+    column, above, right, edges = lax.optimization_barrier((column, above, right, edges))
     planes_of = [column] + [swap(column, "gz", n_gz, j) for j in range(1, n_gz)]
 
-    extract_plan, spread_plan, edge_samples, trig = make_plan(devices, bins, samples, columns)
-    trig = jnp.asarray(trig)
     depth_in = round_up(planes + 1, 8)
 
     table, groups = extract_plan
@@ -535,16 +577,15 @@
     parts = lax.all_to_all(parts, ("gz", "dom"), 0, 0, tiled=True)
 
     depth = round_up(planes, 8)
-    table, groups = spread_plan
     pose, spread = pl.pallas_call(
         functools.partial(
-            spread_kernel, groups, table.shape[1], planes, samples, edge_samples, mine, n_gz, n_dom
+            spread_kernel, spread_groups, spread_table.shape[1], planes, samples, edge_samples, mine, n_gz, n_dom
         ),
         out_shape=[
             jax.ShapeDtypeStruct((1, mine), f32),
             jax.ShapeDtypeStruct((planes, rows, columns), f32),
         ],
-        in_specs=[smem, smem, vmem, vmem, vmem],
+        in_specs=[smem, smem] + [vmem] * 5,
         out_specs=[vmem, vmem],
         scratch_shapes=[
             pltpu.VMEM((2 * width // TILE, bins, TILE), f32),
@@ -553,7 +594,7 @@
         ],
         compiler_params=params,
         name="spread",
-    )(jnp.asarray(table.reshape(-1)), trig, parts, bins_row, weighted)
+    )(spread_table_flat, trig, right, edges, parts, bins_row, weighted)
     pose = pose.reshape(mine)
     return pose, spread
 

time: 49 us -> 49.5 us (1.010)
  waiting for transfers between devices: 5.88 us -> 1.37 us
  local copies, waits for them, and re-layouts: 0.03 us -> 3.52 us
  Pallas kernels: 17.8 us -> 19.1 us
    ppermute x10, waiting for transfers between devices: 5.88 us -> 1.37 us  [swap(): return lax.ppermute(x, axis, [(i, i ^ distance) for i in range(size)])]
    unnamed x10 -> x20, local copies, waits for them, and re-layouts: 0.03 us -> 3.52 us
    pallas_call x1 -> x2, Pallas kernels: 6.85 us -> 8.23 us  [the longest x1 6.23 us: local(): pl.pallas_call(functools.partial(spread_kernel, spread_groups, spread_tab...]
    concatenate x1, other arithmetic: 0.83 us -> 0.03 us  [local(): jnp.concatenate([packed] + [swap(packed, 'dom', n_dom, 2 * k) for k in ra...]
    select_n x1, other arithmetic: 0.01 us -> 0.7 us  [local(): above = jnp.where(lax.axis_index('dom') == n_dom - 1, above, inner)]
  transfers between devices with their start and end apart: 11 -> 11, of which waited for: 7 -> 4; matrix products, arithmetic and copies ran while one was open for 0% -> 1% of each run, Pallas kernels for 13% -> 17%
where the time goes in v7:
time: 49.5 us; the launch traced here: 49.1 us
  Pallas kernels  19.1 us (39%)
  starting transfers between devices  12.4 us (25%)
  blocking collectives  11.2 us (23%)
  local copies, waits for them, and re-layouts  3.52 us (7%)
  waiting for transfers between devices  1.37 us (3%)
  between operations  0.78 us (2%)
  other arithmetic  0.72 us (1%)
    all_to_all x1, blocking collectives, local(): parts = lax.all_to_all(parts, ('gz', 'dom'), 0, 0, tiled=True)  11.2 us
    ppermute x10, starting transfers between devices, swap(): return lax.ppermute(x, axis, [(i, i ^ distance) for i in range(size)])  9.08 us
    pallas_call x1, Pallas kernels, local(): pl.pallas_call(functools.partial(extract_kernel, groups, table.shape[1],...  6.56 us
    pallas_call x1, Pallas kernels, local(): pl.pallas_call(functools.partial(spread_kernel, spread_groups, spread_tab...  6.23 us
    unnamed x20, local copies, waits for them, and re-layouts  3.52 us
    ppermute x1, starting transfers between devices, local(): above = lax.ppermute(plane, 'gz', [(i, i - 1) for i in range(1, n_gz)])  3.33 us
    pallas_call x1, Pallas kernels, local(): pl.pallas_call(functools.partial(particle_kernel, width, mine, n_gz, n_do...  2.73 us
    pallas_call x1, Pallas kernels, local(): pl.pallas_call(functools.partial(weight_kernel, spread_groups, spread_tab...  2 us
  transfers between devices with their start and end apart: 11, of which 4 were waited for; matrix products, arithmetic and copies ran while one was open for 1% of the time, Pallas kernels for 17%

profile of v7, /device:TPU:4, one launch (start us, length us, event | category | flops | bytes accessed | tf_op | source)
XLA Modules:
  0.0 49.1 jit_solution(6314897175917416509)
XLA Ops:
  0.6 1.6 %pack.1 = (bf16[16,1664]{1,0:T(8,128)(2,1)}, f32[1,4,384]{2,1,0:T(4,128)}) custom-call(bf16[16,4,384]{2,1,0:T(4,128)(2,1)} %observed_hbm.1, s32[1,16]{1,0:T(1,128)} %bitcast.7, s32[1,16]{1,0:T(1,128)} %bitcast.8, f32[192,4,384]{2,1,0:T(4,128)} %volume.3), custom_call_target="tpu_custom_call" | custom-call | tf_op jit(solution)/shard_map/pack/pallas_call | solution.py:487
  2.2 3.7 %collective-permute-start.2 = (bf16[16,1664]{1,0:T(8,128)(2,1)}, bf16[16,1664]{1,0:T(8,128)(2,1)S(1)}, u32[]{:S(2)}, u32[]{:S(2)}) collective-permute-start(bf16[16,1664]{1,0:T(8,128)(2,1)} %get-tuple-element.23), channel_id=1, source_target_pairs={{0,6},{1,7},{2,4},{3,5},{4,2},{5,3},{6,0},{7,1},{8,14},{9,15},{10,... | collective-permute-start | bytes 159752 | tf_op jit(solution)/shard_map/ppermute | solution.py:467
  5.9 0.0 collective-permute-start.1
  5.9 0.8 %collective-permute-start = (bf16[16,1664]{1,0:T(8,128)(2,1)}, bf16[16,1664]{1,0:T(8,128)(2,1)S(1)}, u32[]{:S(2)}, u32[]{:S(2)}) collective-permute-start(bf16[16,1664]{1,0:T(8,128)(2,1)} %get-tuple-element.23), channel_id=1, source_target_pairs={{0,2},{1,3},{2,0},{3,1},{4,6},{5,7},{6,4},{7,5},{8,10},{9,11},{10,... | collective-permute-start | bytes 159752 | tf_op jit(solution)/shard_map/ppermute | solution.py:467
  6.7 3.3 %collective-permute-start.3 = (f32[1,4,384]{2,1,0:T(4,128)}, f32[1,4,384]{2,1,0:T(4,128)S(1)}, u32[]{:S(2)}, u32[]{:S(2)}) collective-permute-start(f32[1,4,384]{2,1,0:T(4,128)} %get-tuple-element.24), channel_id=1, source_target_pairs={{8,0},{16,8},{24,16},{9,1},{17,9},{25,17},{10,2},{18,10},{26,18},{... | collective-permute-start | bytes 18440 | tf_op jit(solution)/shard_map/ppermute | solution.py:506
  10.0 0.0 copy-start.3
  10.0 0.7 %copy-done.3 = s32[3008]{0:T(1024)S(1)} copy-done((s32[3008]{0:T(1024)S(1)}, s32[3008]{0:T(1024)}, u32[]{:S(2)}) %copy-start.3) | copy-done | bytes 12056
  10.7 0.0 copy-start.5
  10.7 0.7 %copy-done.5 = f32[128]{0:T(128)S(1)} copy-done((f32[128]{0:T(128)S(1)}, f32[128]{0:T(128)}, u32[]{:S(2)}) %copy-start.5) | copy-done | bytes 536
  11.4 0.0 copy-start.9
  11.4 0.0 copy-start.6
  11.4 0.0 copy-start.7
  11.4 0.0 copy-start.8
  11.4 2.0 %weights.1 = (bf16[12,1024,128]{2,1,0:T(8,128)(2,1)S(1)}, bf16[32,96,128]{2,1,0:T(8,128)(2,1)S(1)}) custom-call(s32[3008]{0:T(1024)S(1)} %copy-done.3, f32[128]{0:T(128)S(1)} %copy-done.5), custom_call_target="tpu_custom_call" | custom-call | flops 3000000000 | bytes 2097152 | tf_op jit(solution)/shard_map/weights/pallas_call | solution.py:516
  13.4 0.0 copy-start.1
  13.4 0.9 %copy-done.1 = bf16[32,96,128]{2,1,0:T(8,128)(2,1)} copy-done((bf16[32,96,128]{2,1,0:T(8,128)(2,1)}, bf16[32,96,128]{2,1,0:T(8,128)(2,1)S(1)}, u32[]{:S(2)}) %copy-start.1) | copy-done | bytes 786456
  14.3 0.0 collective-permute-done.3
  14.3 0.7 %dynamic-slice_select_fusion.above = f32[1,4,384]{2,1,0:T(4,128)S(1)} fusion(f32[1,4,384]{2,1,0:T(4,128)S(1)} %collective-permute-done.3, f32[192,4,384]{2,1,0:T(4,128)} %volume.3, s32[]{:T(128)S(6)} %select_n.12, pred[]{:T(512)S(6)} %eq.3), kind=kLoop, calls=%fused_computation.1 | loop fusion | flops 1536 | bytes 18437 | tf_op jit(solution)/shard_map/jit(_where)/select_n | solution.py:513
  15.0 0.0 collective-permute-done.2
  15.0 0.0 collective-permute-done.1
  15.0 0.0 collective-permute-done
  15.0 0.0 copy-done.9
  15.0 0.5 %collective-permute-start.6 = (bf16[64,1664]{1,0:T(8,128)(2,1)S(1)}, bf16[64,1664]{1,0:T(8,128)(2,1)S(1)}, u32[]{:S(2)}, u32[]{:S(2)}) collective-permute-start(bf16[64,1664]{1,0:T(8,128)(2,1)S(1)} %pad_maximum_fusion.refs_0_), channel_id=1, source_target_pairs={{0,24},{8,16},{16,8},{24,0},{1,25},{9,17},{17,9},{25,1},{2,26},{10... | collective-permute-start | bytes 638984 | tf_op jit(solution)/shard_map/ppermute | solution.py:467
  15.6 0.9 %collective-permute-start.5 = (bf16[64,1664]{1,0:T(8,128)(2,1)S(1)}, bf16[64,1664]{1,0:T(8,128)(2,1)S(1)}, u32[]{:S(2)}, u32[]{:S(2)}) collective-permute-start(bf16[64,1664]{1,0:T(8,128)(2,1)S(1)} %pad_maximum_fusion.refs_0_), channel_id=1, source_target_pairs={{0,16},{8,24},{16,0},{24,8},{1,17},{9,25},{17,1},{25,9},{2,18},{10... | collective-permute-start | bytes 638984 | tf_op jit(solution)/shard_map/ppermute | solution.py:467
  16.5 2.1 %collective-permute-start.4 = (bf16[64,1664]{1,0:T(8,128)(2,1)S(1)}, bf16[64,1664]{1,0:T(8,128)(2,1)S(1)}, u32[]{:S(2)}, u32[]{:S(2)}) collective-permute-start(bf16[64,1664]{1,0:T(8,128)(2,1)S(1)} %pad_maximum_fusion.refs_0_), channel_id=1, source_target_pairs={{0,8},{8,0},{16,24},{24,16},{1,9},{9,1},{17,25},{25,17},{2,10},{10... | collective-permute-start | bytes 638984 | tf_op jit(solution)/shard_map/ppermute | solution.py:467
  18.6 0.0 copy-done.6
  18.6 0.0 copy-done.7
  18.6 0.0 copy-done.8
  18.6 0.0 copy-start
  18.6 1.3 %copy-done = f32[192,4,384]{2,1,0:T(4,128)S(1)} copy-done((f32[192,4,384]{2,1,0:T(4,128)S(1)}, f32[192,4,384]{2,1,0:T(4,128)}, u32[]{:S(2)}) %copy-start) | copy-done | bytes 1179672
  19.9 6.6 %extract.1 = (bf16[128,1536]{1,0:T(8,128)(2,1)S(1)}, bf16[32,384]{1,0:T(8,128)(2,1)S(1)}, f32[32,768]{1,0:T(8,128)S(1)}) custom-call(s32[1984]{0:T(1024)S(1)} %copy-done.8, f32[128]{0:T(128)S(1)} %copy-done.6, f32[192,4,384]{2,1,0:T(4,128)S(1)} %copy-done, f32[1,4,384]{2,1,0:T(4,128)S(1)} %dynamic-slice_select_fusion.above, f32[32,2,384]{2,1,0:T(2,128)S(1)} %copy-done.7), custom_call_target="tpu_custom_call" | custom-call | flops 6000000000 | bytes 1048576 | tf_op jit(solution)/shard_map/extract/pallas_call | solution.py:536
  26.4 0.0 copy-start.2
  26.5 0.0 copy-start.4
  26.5 0.0 collective-permute-done.6.refs_3_
  26.5 0.0 collective-permute-done.5.refs_2_
  26.5 0.0 collective-permute-done.4.refs_1_
  26.5 0.1 collective-permute-start.7
  26.6 0.5 %collective-permute-start.8 = (bf16[64,1664]{1,0:T(8,128)(2,1)S(1)}, bf16[64,1664]{1,0:T(8,128)(2,1)S(1)}, u32[]{:S(2)}, u32[]{:S(2)}) collective-permute-start(bf16[64,1664]{1,0:T(8,128)(2,1)S(1)} %collective-permute-done.4.refs_1_), channel_id=1, source_target_pairs={{0,1},{1,0},{2,3},{3,2},{4,5},{5,4},{6,7},{7,6},{8,9},{9,8},{10,11... | collective-permute-start | bytes 638984 | tf_op jit(solution)/shard_map/ppermute | solution.py:467
  27.1 0.1 collective-permute-start.9
  27.2 0.4 collective-permute-start.10
  27.6 0.4 collective-permute-done.7.refs_4_
  28.0 0.3 collective-permute-done.8.refs_5_
  28.3 0.3 collective-permute-done.9.refs_6_
  28.6 0.3 collective-permute-done.10.refs_7_
  28.9 2.7 %particles.1 = (bf16[512,1536]{1,0:T(8,128)(2,1)S(1)}, f32[256,128]{1,0:T(8,128)S(1)}, f32[1,512]{1,0:T(1,128)S(1)}) custom-call(bf16[64,1664]{1,0:T(8,128)(2,1)S(1)} %pad_maximum_fusion.refs_0_, bf16[64,1664]{1,0:T(8,128)(2,1)S(1)} %collective-permute-done.4.refs_1_, bf16[64,1664]{1,0:T(8,128)(2,1)S(1)} %collective-permute-done.5.refs_2_, ...), custom_call_target="tpu_custom_call" | custom-call | tf_op jit(solution)/shard_map/particles/pallas_call | solution.py:564
  31.7 11.2 %all_to_all.11 = f32[32,8,128]{2,1,0:T(8,128)S(1)} all-to-all(f32[32,8,128]{2,1,0:T(8,128)S(1)} %bitcast.6), channel_id=1, replica_groups=mesh['gz'=4,'dom'=8] {'gz','dom'}, dimensions={0} | all-to-all | bytes 262144 | tf_op jit(solution)/shard_map/all_to_all | solution.py:577
  42.9 0.0 copy-done.2
  42.9 0.0 copy-done.4
  42.9 6.2 %spread.1 = (f32[1,16]{1,0:T(1,128)}, f32[24,4,384]{2,1,0:T(4,128)}) custom-call(s32[3008]{0:T(1024)S(1)} %copy-done.4, f32[128]{0:T(128)S(1)} %copy-done.6, bf16[12,1024,128]{2,1,0:T(8,128)(2,1)S(1)} %get-tuple-element.27.right, bf16[32,96,128]{2,1,0:T(8,128)(2,1)S(1)} %copy-done.2, f32[256,128]{1,0:T(8,128)S(1)} %bitcast.5, ...), custom_call_target="tpu_custom_call" | custom-call | tf_op jit(solution)/shard_map/spread/pallas_call | solution.py:580
  (1 shorter events, 0.0 us)
Async XLA Ops:
  2.2 12.8 %collective-permute-start.2 = (bf16[16,1664]{1,0:T(8,128)(2,1)}, bf16[16,1664]{1,0:T(8,128)(2,1)S(1)}, u32[]{:S(2)}, u32[]{:S(2)}) collective-permute-start(bf16[16,1664]{1,0:T(8,128)(2,1)} %get-tuple-element.23), channel_id=1, source_target_pairs={{0,6},{1,7},{2,4},{3,5},{4,2},{5,3},{6,0},{7,1},{8,14},{9,15},{10,... | collective-permute-start | bytes 159752 | tf_op jit(solution)/shard_map/ppermute | solution.py:467
  5.9 9.1 %collective-permute-start.1 = (bf16[16,1664]{1,0:T(8,128)(2,1)}, bf16[16,1664]{1,0:T(8,128)(2,1)S(1)}, u32[]{:S(2)}, u32[]{:S(2)}) collective-permute-start(bf16[16,1664]{1,0:T(8,128)(2,1)} %get-tuple-element.23), channel_id=1, source_target_pairs={{0,4},{1,5},{2,6},{3,7},{4,0},{5,1},{6,2},{7,3},{8,12},{9,13},{10,... | collective-permute-start | bytes 159752 | tf_op jit(solution)/shard_map/ppermute | solution.py:467
  5.9 9.1 %collective-permute-start = (bf16[16,1664]{1,0:T(8,128)(2,1)}, bf16[16,1664]{1,0:T(8,128)(2,1)S(1)}, u32[]{:S(2)}, u32[]{:S(2)}) collective-permute-start(bf16[16,1664]{1,0:T(8,128)(2,1)} %get-tuple-element.23), channel_id=1, source_target_pairs={{0,2},{1,3},{2,0},{3,1},{4,6},{5,7},{6,4},{7,5},{8,10},{9,11},{10,... | collective-permute-start | bytes 159752 | tf_op jit(solution)/shard_map/ppermute | solution.py:467
  6.7 7.6 %collective-permute-start.3 = (f32[1,4,384]{2,1,0:T(4,128)}, f32[1,4,384]{2,1,0:T(4,128)S(1)}, u32[]{:S(2)}, u32[]{:S(2)}) collective-permute-start(f32[1,4,384]{2,1,0:T(4,128)} %get-tuple-element.24), channel_id=1, source_target_pairs={{8,0},{16,8},{24,16},{9,1},{17,9},{25,17},{10,2},{18,10},{26,18},{... | collective-permute-start | bytes 18440 | tf_op jit(solution)/shard_map/ppermute | solution.py:506
  10.0 0.7 %copy-start.3 = (s32[3008]{0:T(1024)S(1)}, s32[3008]{0:T(1024)}, u32[]{:S(2)}) copy-start(s32[3008]{0:T(1024)} %constant.23.clone.table) | copy-start | bytes 36100
  10.7 0.7 %copy-start.5 = (f32[128]{0:T(128)S(1)}, f32[128]{0:T(128)}, u32[]{:S(2)}) copy-start(f32[128]{0:T(128)} %constant.22.clone.trig.trig_hbm) | copy-start | bytes 1540
  11.4 3.6 %copy-start.9 = (bf16[16,1664]{1,0:T(8,128)(2,1)S(1)}, bf16[16,1664]{1,0:T(8,128)(2,1)}, u32[]{:S(2)}) copy-start(bf16[16,1664]{1,0:T(8,128)(2,1)} %get-tuple-element.23) | copy-start | bytes 159748
  11.4 7.2 %copy-start.6 = (f32[128]{0:T(128)S(1)}, f32[128]{0:T(128)}, u32[]{:S(2)}) copy-start(f32[128]{0:T(128)} %constant.22.clone.trig.trig_hbm) | copy-start | bytes 1540
  11.4 7.2 %copy-start.7 = (f32[32,2,384]{2,1,0:T(2,128)S(1)}, f32[32,2,384]{2,1,0:T(2,128)}, u32[]{:S(2)}) copy-start(f32[32,2,384]{2,1,0:T(2,128)} %ctf_hbm.1) | copy-start | bytes 294916
  11.4 7.2 %copy-start.8 = (s32[1984]{0:T(1024)S(1)}, s32[1984]{0:T(1024)}, u32[]{:S(2)}) copy-start(s32[1984]{0:T(1024)} %constant.24.clone.table_hbm) | copy-start | bytes 23812
  13.4 0.9 %copy-start.1 = (bf16[32,96,128]{2,1,0:T(8,128)(2,1)}, bf16[32,96,128]{2,1,0:T(8,128)(2,1)S(1)}, u32[]{:S(2)}) copy-start(bf16[32,96,128]{2,1,0:T(8,128)(2,1)S(1)} %get-tuple-element.28.edges) | copy-start | bytes 2359300
  15.0 11.4 %collective-permute-start.6 = (bf16[64,1664]{1,0:T(8,128)(2,1)S(1)}, bf16[64,1664]{1,0:T(8,128)(2,1)S(1)}, u32[]{:S(2)}, u32[]{:S(2)}) collective-permute-start(bf16[64,1664]{1,0:T(8,128)(2,1)S(1)} %pad_maximum_fusion.refs_0_), channel_id=1, source_target_pairs={{0,24},{8,16},{16,8},{24,0},{1,25},{9,17},{17,9},{25,1},{2,26},{10... | collective-permute-start | bytes 638984 | tf_op jit(solution)/shard_map/ppermute | solution.py:467
  15.6 10.9 %collective-permute-start.5 = (bf16[64,1664]{1,0:T(8,128)(2,1)S(1)}, bf16[64,1664]{1,0:T(8,128)(2,1)S(1)}, u32[]{:S(2)}, u32[]{:S(2)}) collective-permute-start(bf16[64,1664]{1,0:T(8,128)(2,1)S(1)} %pad_maximum_fusion.refs_0_), channel_id=1, source_target_pairs={{0,16},{8,24},{16,0},{24,8},{1,17},{9,25},{17,1},{25,9},{2,18},{10... | collective-permute-start | bytes 638984 | tf_op jit(solution)/shard_map/ppermute | solution.py:467
  16.5 10.0 %collective-permute-start.4 = (bf16[64,1664]{1,0:T(8,128)(2,1)S(1)}, bf16[64,1664]{1,0:T(8,128)(2,1)S(1)}, u32[]{:S(2)}, u32[]{:S(2)}) collective-permute-start(bf16[64,1664]{1,0:T(8,128)(2,1)S(1)} %pad_maximum_fusion.refs_0_), channel_id=1, source_target_pairs={{0,8},{8,0},{16,24},{24,16},{1,9},{9,1},{17,25},{25,17},{2,10},{10... | collective-permute-start | bytes 638984 | tf_op jit(solution)/shard_map/ppermute | solution.py:467
  18.6 1.3 %copy-start = (f32[192,4,384]{2,1,0:T(4,128)S(1)}, f32[192,4,384]{2,1,0:T(4,128)}, u32[]{:S(2)}) copy-start(f32[192,4,384]{2,1,0:T(4,128)} %volume.3) | copy-start | bytes 3538948
  26.4 16.4 %copy-start.2 = (bf16[32,96,128]{2,1,0:T(8,128)(2,1)S(1)}, bf16[32,96,128]{2,1,0:T(8,128)(2,1)}, u32[]{:S(2)}) copy-start(bf16[32,96,128]{2,1,0:T(8,128)(2,1)} %copy-done.1) | copy-start | bytes 2359300
  26.5 16.4 %copy-start.4 = (s32[3008]{0:T(1024)S(1)}, s32[3008]{0:T(1024)}, u32[]{:S(2)}) copy-start(s32[3008]{0:T(1024)} %constant.23.clone.table) | copy-start | bytes 36100
  26.5 1.5 %collective-permute-start.7 = (bf16[64,1664]{1,0:T(8,128)(2,1)S(1)}, bf16[64,1664]{1,0:T(8,128)(2,1)S(1)}, u32[]{:S(2)}, u32[]{:S(2)}) collective-permute-start(bf16[64,1664]{1,0:T(8,128)(2,1)S(1)} %pad_maximum_fusion.refs_0_), channel_id=1, source_target_pairs={{0,1},{1,0},{2,3},{3,2},{4,5},{5,4},{6,7},{7,6},{8,9},{9,8},{10,11... | collective-permute-start | bytes 638984 | tf_op jit(solution)/shard_map/ppermute | solution.py:467
  26.6 1.8 %collective-permute-start.8 = (bf16[64,1664]{1,0:T(8,128)(2,1)S(1)}, bf16[64,1664]{1,0:T(8,128)(2,1)S(1)}, u32[]{:S(2)}, u32[]{:S(2)}) collective-permute-start(bf16[64,1664]{1,0:T(8,128)(2,1)S(1)} %collective-permute-done.4.refs_1_), channel_id=1, source_target_pairs={{0,1},{1,0},{2,3},{3,2},{4,5},{5,4},{6,7},{7,6},{8,9},{9,8},{10,11... | collective-permute-start | bytes 638984 | tf_op jit(solution)/shard_map/ppermute | solution.py:467
  27.1 1.6 %collective-permute-start.9 = (bf16[64,1664]{1,0:T(8,128)(2,1)S(1)}, bf16[64,1664]{1,0:T(8,128)(2,1)S(1)}, u32[]{:S(2)}, u32[]{:S(2)}) collective-permute-start(bf16[64,1664]{1,0:T(8,128)(2,1)S(1)} %collective-permute-done.5.refs_2_), channel_id=1, source_target_pairs={{0,1},{1,0},{2,3},{3,2},{4,5},{5,4},{6,7},{7,6},{8,9},{9,8},{10,11... | collective-permute-start | bytes 638984 | tf_op jit(solution)/shard_map/ppermute | solution.py:467
  27.2 1.8 %collective-permute-start.10 = (bf16[64,1664]{1,0:T(8,128)(2,1)S(1)}, bf16[64,1664]{1,0:T(8,128)(2,1)S(1)}, u32[]{:S(2)}, u32[]{:S(2)}) collective-permute-start(bf16[64,1664]{1,0:T(8,128)(2,1)S(1)} %collective-permute-done.6.refs_3_), channel_id=1, source_target_pairs={{0,1},{1,0},{2,3},{3,2},{4,5},{5,4},{6,7},{7,6},{8,9},{9,8},{10,11... | collective-permute-start | bytes 638984 | tf_op jit(solution)/shard_map/ppermute | solution.py:467

commit v8 on v7

--- a/solution.py
+++ b/solution.py
@@ -16,6 +16,7 @@
 EPS = 1e-05
 TILE = 128
 GROUP = 4
+SPREAD_GROUP = 8
 EDGE_GROUP = 8
 CHUNK = 512
 f32 = jnp.float32
@@ -37,7 +38,7 @@
     slack = 1e-3
     reach = 0
     plans = []
-    for spread in (False, True):
+    for spread, size in ((False, GROUP), (True, SPREAD_GROUP)):
         rows = []
         for device in range(devices):
             z0 = device * planes
@@ -69,12 +70,12 @@
             idle = (bins - 1 if z0 < middle else 0) * 4 + ut_count - 1
             tiles, codes = [], []
             for xt, entries in enumerate(lists):
-                entries = entries + [idle] * (-len(entries) % GROUP)
-                tiles += [xt] * (len(entries) // GROUP)
+                entries = entries + [idle] * (-len(entries) % size)
+                tiles += [xt] * (len(entries) // size)
                 codes += entries
             rows.append((tiles, codes, edge))
         groups = max(len(tiles) for tiles, _, _ in rows)
-        start = 1 + groups * (1 + GROUP)
+        start = 1 + groups * (1 + size)
         table = np.zeros((devices, start + 1 + max(len(edge) for _, _, edge in rows)), np.int32)
         for device, (tiles, codes, edge) in enumerate(rows):
             table[device, 0] = len(tiles)
@@ -182,30 +183,25 @@
 
 def extract_kernel(
     groups, length, samples, bins, planes, n_dom,
-    table_hbm, trig_hbm, volume, above, ctf_hbm, slope, pairs, flat,
-    table, trig, ctf, field, vhi, vlo, out, sems,
+    table_hbm, trig_hbm, field, ctf_hbm, slope, pairs, flat,
+    table, trig, ctf, vhi, vlo, out, sems,
 ):
     depth = field.shape[0]
     xt_count = vhi.shape[0]
     ut_count = samples // TILE
-    dom = lax.axis_index("dom")
-    device = lax.axis_index("gz") * n_dom + dom
+    device = lax.axis_index("gz") * n_dom + lax.axis_index("dom")
     row = device * length
     first = device * planes
     z0, z1 = first.astype(f32), (first + planes).astype(f32)
 
     copies = fetch(
         [
-            (volume.at[pl.ds(dom * planes, planes)], field.at[pl.ds(0, planes)]),
             (table_hbm, table),
             (trig_hbm, trig),
             (ctf_hbm, ctf),
         ],
         sems,
     )
-    field[planes] = above[0]
-    for z in range(planes + 1, depth):
-        field[z] = jnp.zeros(field.shape[1:], f32)
     out[...] = jnp.zeros_like(out)
     for copy in copies:
         copy.wait()
@@ -339,15 +335,15 @@
 
     def step(j, carry):
         xx = lanes_of((1, TILE), 1) + (table[row + 1 + j] * TILE).astype(f32)
-        for k in range(GROUP):
-            at = row + 1 + groups + j * GROUP + k
+        for k in range(SPREAD_GROUP):
+            at = row + 1 + groups + j * SPREAD_GROUP + k
             _, _, _, c, base = block_of(table, trig, at, bins)
             for n, part in enumerate(bump((xx - base * c) - uu * c)):
                 right[j, (2 * k + n) * TILE : (2 * k + n + 1) * TILE, :] = part.astype(bf16)
         return carry
 
     lax.fori_loop(0, table[row], step, 0)
-    tail = row + 1 + groups * (1 + GROUP)
+    tail = row + 1 + groups * (1 + SPREAD_GROUP)
 
     def edge(j, carry):
         for k in range(EDGE_GROUP):
@@ -410,8 +406,8 @@
     def step(j, carry):
         xt = table[row + 1 + j]
         left = []
-        for k in range(GROUP):
-            at = row + 1 + groups + j * GROUP + k
+        for k in range(SPREAD_GROUP):
+            at = row + 1 + groups + j * SPREAD_GROUP + k
             b, ut, s, c, base = block_of(table, trig, at, bins)
             u = lanes_of((1, TILE), 1) + base
             _, kz, kzd, z_factor, x_factor = row_weights(z0, depth, u, s, c, samples)
@@ -432,7 +428,7 @@
         return carry
 
     lax.fori_loop(0, table[row], step, 0)
-    tail = row + 1 + groups * (1 + GROUP)
+    tail = row + 1 + groups * (1 + SPREAD_GROUP)
 
     def edge(j, carry):
         left, below = [], []
@@ -507,10 +503,12 @@
     column = jnp.concatenate(
         [packed] + [swap(packed, "dom", n_dom, 2 * k) for k in range(1, n_z)], 0
     )
-    inner = lax.dynamic_slice_in_dim(
-        volume, jnp.minimum((lax.axis_index("dom") + 1) * planes, slab - 1), 1, 0
-    )
-    above = jnp.where(lax.axis_index("dom") == n_dom - 1, above, inner)
+    dom = lax.axis_index("dom")
+    own = lax.dynamic_slice_in_dim(volume, dom * planes, planes, 0)
+    inner = lax.dynamic_slice_in_dim(volume, jnp.minimum((dom + 1) * planes, slab - 1), 1, 0)
+    halo = jnp.where(dom == n_dom - 1, above, inner)
+    depth_in = round_up(planes + 1, 8)
+    field = jnp.concatenate([own, halo, jnp.zeros((depth_in - planes - 1, rows, columns), f32)], 0)
     spread_table, spread_groups = spread_plan
     spread_table_flat = jnp.asarray(spread_table.reshape(-1))
     right, edges = pl.pallas_call(
@@ -518,7 +516,7 @@
             weight_kernel, spread_groups, spread_table.shape[1], bins, planes, n_dom, edge_samples
         ),
         out_shape=[
-            jax.ShapeDtypeStruct((spread_groups, GROUP * 2 * TILE, TILE), bf16),
+            jax.ShapeDtypeStruct((spread_groups, SPREAD_GROUP * 2 * TILE, TILE), bf16),
             jax.ShapeDtypeStruct((bins // 2, 2 * edge_samples, TILE), bf16),
         ],
         in_specs=[smem, smem],
@@ -527,10 +525,9 @@
         cost_estimate=pl.CostEstimate(flops=3 * 10**9, bytes_accessed=2**21, transcendentals=0),
         name="weights",
     )(spread_table_flat, trig)
-    column, above, right, edges = lax.optimization_barrier((column, above, right, edges))
+    column, field, right, edges = lax.optimization_barrier((column, field, right, edges))
     planes_of = [column] + [swap(column, "gz", n_gz, j) for j in range(1, n_gz)]
 
-    depth_in = round_up(planes + 1, 8)
 
     table, groups = extract_plan
     slope, pairs, flat_ctf = pl.pallas_call(
@@ -542,22 +539,21 @@
             jax.ShapeDtypeStruct((NCTF, 6 * bins), bf16),
             jax.ShapeDtypeStruct((NCTF, width // 2), f32),
         ],
-        in_specs=[hbm, hbm, hbm, vmem, hbm],
+        in_specs=[hbm, hbm, vmem, hbm],
         out_specs=[vmem, vmem, vmem],
         scratch_shapes=[
             pltpu.SMEM((table.size,), jnp.int32),
             pltpu.SMEM(trig.shape, f32),
             pltpu.VMEM(ctf_table.shape, f32),
-            pltpu.VMEM((depth_in, rows, columns), f32),
             pltpu.VMEM((xt_count, rows * depth_in, TILE), bf16),
             pltpu.VMEM((xt_count, rows * depth_in, TILE), bf16),
             pltpu.VMEM((bins * ut_count * 2 * rows, TILE), f32),
-            pltpu.SemaphoreType.DMA((4,)),
+            pltpu.SemaphoreType.DMA((3,)),
         ],
         compiler_params=params,
         cost_estimate=pl.CostEstimate(flops=6 * 10**9, bytes_accessed=2**20, transcendentals=0),
         name="extract",
-    )(jnp.asarray(table.reshape(-1)), trig, volume, above, ctf_table)
+    )(jnp.asarray(table.reshape(-1)), trig, field, ctf_table)
 
     planes_of, slope = lax.optimization_barrier((planes_of, slope))
     gathered = planes_of + [swap(part, "dom", n_dom, 1) for part in planes_of]

time: 49.5 us -> 49.8 us (level)
  blocking collectives: 11.2 us -> 12.4 us
  local copies, waits for them, and re-layouts: 3.52 us -> 2.83 us
  Pallas kernels: 19.1 us -> 18.5 us
    unnamed x20 -> x14, local copies, waits for them, and re-layouts: 3.52 us -> 1.82 us
    all_to_all x1, blocking collectives: 11.2 us -> 12.4 us  [local(): parts = lax.all_to_all(parts, ('gz', 'dom'), 0, 0, tiled=True)]
    dynamic_slice x0 -> x1, local copies, waits for them, and re-layouts: none -> 0.92 us  [local(): own = lax.dynamic_slice_in_dim(volume, dom * planes, planes, 0)]
  transfers between devices with their start and end apart: 11 -> 11, of which waited for: 4 -> 5; matrix products, arithmetic and copies ran while one was open for 1% -> 4% of each run, Pallas kernels for 17% -> 17%
where the time goes in v8:
time: 49.8 us; the launch traced here: 49.5 us
  Pallas kernels  18.5 us (37%)
  blocking collectives  12.4 us (25%)
  starting transfers between devices  12.3 us (25%)
  local copies, waits for them, and re-layouts  2.83 us (6%)
  waiting for transfers between devices  1.78 us (4%)
  between operations  0.83 us (2%)
  other arithmetic  0.82 us (2%)
    all_to_all x1, blocking collectives, local(): parts = lax.all_to_all(parts, ('gz', 'dom'), 0, 0, tiled=True)  12.4 us
    ppermute x10, starting transfers between devices, swap(): return lax.ppermute(x, axis, [(i, i ^ distance) for i in range(size)])  9.02 us
    pallas_call x1, Pallas kernels, local(): pl.pallas_call(functools.partial(extract_kernel, groups, table.shape[1],...  6.35 us
    pallas_call x1, Pallas kernels, local(): pl.pallas_call(functools.partial(spread_kernel, spread_groups, spread_tab...  5.75 us
    ppermute x1, starting transfers between devices, local(): above = lax.ppermute(plane, 'gz', [(i, i - 1) for i in range(1, n_gz)])  3.33 us
    pallas_call x1, Pallas kernels, local(): pl.pallas_call(functools.partial(particle_kernel, width, mine, n_gz, n_do...  2.73 us
    pallas_call x1, Pallas kernels, local(): pl.pallas_call(functools.partial(weight_kernel, spread_groups, spread_tab...  2.09 us
    unnamed x14, local copies, waits for them, and re-layouts  1.82 us
  transfers between devices with their start and end apart: 11, of which 5 were waited for; matrix products, arithmetic and copies ran while one was open for 4% of the time, Pallas kernels for 17%

profile of v8, /device:TPU:4, one launch (start us, length us, event | category | flops | bytes accessed | tf_op | source)
XLA Modules:
  0.0 49.5 jit_solution(17873819466260577179)
XLA Ops:
  0.6 0.0 copy-start.3
  0.6 0.0 copy-start.2
  0.7 1.6 %pack.1 = (bf16[16,1664]{1,0:T(8,128)(2,1)}, f32[1,4,384]{2,1,0:T(4,128)}) custom-call(bf16[16,4,384]{2,1,0:T(4,128)(2,1)} %observed_hbm.1, s32[1,16]{1,0:T(1,128)} %bitcast.7, s32[1,16]{1,0:T(1,128)} %bitcast.8, f32[192,4,384]{2,1,0:T(4,128)} %volume.1), custom_call_target="tpu_custom_call" | custom-call | tf_op jit(solution)/shard_map/pack/pallas_call | solution.py:483
  2.3 3.7 %collective-permute-start.2 = (bf16[16,1664]{1,0:T(8,128)(2,1)}, bf16[16,1664]{1,0:T(8,128)(2,1)S(1)}, u32[]{:S(2)}, u32[]{:S(2)}) collective-permute-start(bf16[16,1664]{1,0:T(8,128)(2,1)} %get-tuple-element.23), channel_id=1, source_target_pairs={{0,6},{1,7},{2,4},{3,5},{4,2},{5,3},{6,0},{7,1},{8,14},{9,15},{10,... | collective-permute-start | bytes 159752 | tf_op jit(solution)/shard_map/ppermute | solution.py:463
  5.9 0.0 collective-permute-start.1
  5.9 0.8 %collective-permute-start = (bf16[16,1664]{1,0:T(8,128)(2,1)}, bf16[16,1664]{1,0:T(8,128)(2,1)S(1)}, u32[]{:S(2)}, u32[]{:S(2)}) collective-permute-start(bf16[16,1664]{1,0:T(8,128)(2,1)} %get-tuple-element.23), channel_id=1, source_target_pairs={{0,2},{1,3},{2,0},{3,1},{4,6},{5,7},{6,4},{7,5},{8,10},{9,11},{10,... | collective-permute-start | bytes 159752 | tf_op jit(solution)/shard_map/ppermute | solution.py:463
  6.7 3.3 %collective-permute-start.3 = (f32[1,4,384]{2,1,0:T(4,128)}, f32[1,4,384]{2,1,0:T(4,128)S(1)}, u32[]{:S(2)}, u32[]{:S(2)}) collective-permute-start(f32[1,4,384]{2,1,0:T(4,128)} %get-tuple-element.24), channel_id=1, source_target_pairs={{8,0},{16,8},{24,16},{9,1},{17,9},{25,17},{10,2},{18,10},{26,18},{... | collective-permute-start | bytes 18440 | tf_op jit(solution)/shard_map/ppermute | solution.py:502
  10.1 0.0 copy-done.3
  10.1 0.0 copy-done.2
  10.1 0.0 copy-start.6
  10.1 0.0 copy-start.4
  10.1 0.0 copy-start.5
  10.1 2.1 %weights.1 = (bf16[7,2048,128]{2,1,0:T(8,128)(2,1)S(1)}, bf16[32,96,128]{2,1,0:T(8,128)(2,1)S(1)}) custom-call(s32[3104]{0:T(1024)S(1)} %copy-done.2, f32[128]{0:T(128)S(1)} %copy-done.3), custom_call_target="tpu_custom_call" | custom-call | flops 3000000000 | bytes 2097152 | tf_op jit(solution)/shard_map/weights/pallas_call | solution.py:514
  12.2 0.0 copy-start
  12.2 1.8 %copy-done = bf16[7,2048,128]{2,1,0:T(8,128)(2,1)} copy-done((bf16[7,2048,128]{2,1,0:T(8,128)(2,1)}, bf16[7,2048,128]{2,1,0:T(8,128)(2,1)S(1)}, u32[]{:S(2)}) %copy-start) | copy-done | bytes 3670040
  14.0 0.9 %constant_dynamic-slice_fusion = f32[24,4,384]{2,1,0:T(4,128)S(1)} fusion(f32[192,4,384]{2,1,0:T(4,128)} %volume.1, s32[]{:T(128)S(6)} %select_n.14), kind=kLoop, calls=%fused_computation.3 | loop fusion | bytes 294916 | tf_op jit(solution)/shard_map/dynamic_slice | solution.py:507
  15.0 0.1 pad.2.clone
  15.0 0.0 collective-permute-done.3
  15.0 0.7 %dynamic-slice_select_fusion = f32[1,4,384]{2,1,0:T(4,128)S(1)} fusion(f32[1,4,384]{2,1,0:T(4,128)S(1)} %collective-permute-done.3, f32[192,4,384]{2,1,0:T(4,128)} %volume.1, s32[]{:T(128)S(6)} %select_n.16, pred[]{:T(512)S(6)} %eq.3), kind=kLoop, calls=%fused_computation.2 | loop fusion | flops 1536 | bytes 18437 | tf_op jit(solution)/shard_map/jit(_where)/select_n | solution.py:509
  15.7 0.1 maximum_maximum_fusion.field
  15.8 0.0 collective-permute-done.2
  15.8 0.0 collective-permute-done.1
  15.9 0.0 collective-permute-done
  15.9 0.0 copy-done.6
  15.9 0.1 collective-permute-start.6
  16.0 1.5 %collective-permute-start.5 = (bf16[64,1664]{1,0:T(8,128)(2,1)S(1)}, bf16[64,1664]{1,0:T(8,128)(2,1)S(1)}, u32[]{:S(2)}, u32[]{:S(2)}) collective-permute-start(bf16[64,1664]{1,0:T(8,128)(2,1)S(1)} %pad_maximum_fusion.refs_0_), channel_id=1, source_target_pairs={{0,16},{8,24},{16,0},{24,8},{1,17},{9,25},{17,1},{25,9},{2,18},{10... | collective-permute-start | bytes 638984 | tf_op jit(solution)/shard_map/ppermute | solution.py:463
  17.5 2.0 %collective-permute-start.4 = (bf16[64,1664]{1,0:T(8,128)(2,1)S(1)}, bf16[64,1664]{1,0:T(8,128)(2,1)S(1)}, u32[]{:S(2)}, u32[]{:S(2)}) collective-permute-start(bf16[64,1664]{1,0:T(8,128)(2,1)S(1)} %pad_maximum_fusion.refs_0_), channel_id=1, source_target_pairs={{0,8},{8,0},{16,24},{24,16},{1,9},{9,1},{17,25},{25,17},{2,10},{10... | collective-permute-start | bytes 638984 | tf_op jit(solution)/shard_map/ppermute | solution.py:463
  19.5 0.0 copy-done.4
  19.5 0.0 copy-done.5
  19.5 0.0 copy-start.1
  19.5 6.3 %extract.1 = (bf16[128,1536]{1,0:T(8,128)(2,1)S(1)}, bf16[32,384]{1,0:T(8,128)(2,1)S(1)}, f32[32,768]{1,0:T(8,128)S(1)}) custom-call(s32[1984]{0:T(1024)S(1)} %copy-done.5, f32[128]{0:T(128)S(1)} %copy-done.3, f32[32,4,384]{2,1,0:T(4,128)S(1)} %maximum_maximum_fusion.field, f32[32,2,384]{2,1,0:T(2,128)S(1)} %copy-done.4), custom_call_target="tpu_custom_call" | custom-call | flops 6000000000 | bytes 1048576 | tf_op jit(solution)/shard_map/extract/pallas_call | solution.py:533
  25.8 0.0 collective-permute-done.6.refs_3_
  25.8 0.4 collective-permute-done.5.refs_2_
  26.2 0.0 collective-permute-done.4.refs_1_
  26.2 0.0 collective-permute-start.7
  26.2 0.5 %collective-permute-start.8 = (bf16[64,1664]{1,0:T(8,128)(2,1)S(1)}, bf16[64,1664]{1,0:T(8,128)(2,1)S(1)}, u32[]{:S(2)}, u32[]{:S(2)}) collective-permute-start(bf16[64,1664]{1,0:T(8,128)(2,1)S(1)} %collective-permute-done.4.refs_1_), channel_id=1, source_target_pairs={{0,1},{1,0},{2,3},{3,2},{4,5},{5,4},{6,7},{7,6},{8,9},{9,8},{10,11... | collective-permute-start | bytes 638984 | tf_op jit(solution)/shard_map/ppermute | solution.py:463
  26.8 0.0 collective-permute-start.9
  26.8 0.5 %collective-permute-start.10 = (bf16[64,1664]{1,0:T(8,128)(2,1)S(1)}, bf16[64,1664]{1,0:T(8,128)(2,1)S(1)}, u32[]{:S(2)}, u32[]{:S(2)}) collective-permute-start(bf16[64,1664]{1,0:T(8,128)(2,1)S(1)} %collective-permute-done.6.refs_3_), channel_id=1, source_target_pairs={{0,1},{1,0},{2,3},{3,2},{4,5},{5,4},{6,7},{7,6},{8,9},{9,8},{10,11... | collective-permute-start | bytes 638984 | tf_op jit(solution)/shard_map/ppermute | solution.py:463
  27.3 0.4 collective-permute-done.7.refs_4_
  27.7 0.3 collective-permute-done.8.refs_5_
  28.0 0.3 collective-permute-done.9.refs_6_
  28.3 0.3 collective-permute-done.10.refs_7_
  28.6 2.7 %particles.1 = (bf16[512,1536]{1,0:T(8,128)(2,1)S(1)}, f32[256,128]{1,0:T(8,128)S(1)}, f32[1,512]{1,0:T(1,128)S(1)}) custom-call(bf16[64,1664]{1,0:T(8,128)(2,1)S(1)} %pad_maximum_fusion.refs_0_, bf16[64,1664]{1,0:T(8,128)(2,1)S(1)} %collective-permute-done.4.refs_1_, bf16[64,1664]{1,0:T(8,128)(2,1)S(1)} %collective-permute-done.5.refs_2_, ...), custom_call_target="tpu_custom_call" | custom-call | tf_op jit(solution)/shard_map/particles/pallas_call | solution.py:560
  31.4 12.4 %all_to_all.11 = f32[32,8,128]{2,1,0:T(8,128)S(1)} all-to-all(f32[32,8,128]{2,1,0:T(8,128)S(1)} %bitcast.6), channel_id=1, replica_groups=mesh['gz'=4,'dom'=8] {'gz','dom'}, dimensions={0} | all-to-all | bytes 262144 | tf_op jit(solution)/shard_map/all_to_all | solution.py:573
  43.8 0.0 copy-done.1
  43.8 5.8 %spread.1 = (f32[1,16]{1,0:T(1,128)}, f32[24,4,384]{2,1,0:T(4,128)}) custom-call(s32[3104]{0:T(1024)S(1)} %copy-done.2, f32[128]{0:T(128)S(1)} %copy-done.3, bf16[7,2048,128]{2,1,0:T(8,128)(2,1)S(1)} %copy-done.1, bf16[32,96,128]{2,1,0:T(8,128)(2,1)S(1)} %get-tuple-element.28.edges, f32[256,128]{1,0:T(8,128)S(1)} %bitcast.5, ...), custom_call_target="tpu_custom_call" | custom-call | tf_op jit(solution)/shard_map/spread/pallas_call | solution.py:576
  (2 shorter events, 0.0 us)
Async XLA Ops:
  0.6 9.4 %copy-start.3 = (f32[128]{0:T(128)S(1)}, f32[128]{0:T(128)}, u32[]{:S(2)}) copy-start(f32[128]{0:T(128)} %constant.24.clone.trig.trig_hbm) | copy-start | bytes 1540
  0.6 9.4 %copy-start.2 = (s32[3104]{0:T(1024)S(1)}, s32[3104]{0:T(1024)}, u32[]{:S(2)}) copy-start(s32[3104]{0:T(1024)} %constant.25.clone.table) | copy-start | bytes 37252
  2.3 13.6 %collective-permute-start.2 = (bf16[16,1664]{1,0:T(8,128)(2,1)}, bf16[16,1664]{1,0:T(8,128)(2,1)S(1)}, u32[]{:S(2)}, u32[]{:S(2)}) collective-permute-start(bf16[16,1664]{1,0:T(8,128)(2,1)} %get-tuple-element.23), channel_id=1, source_target_pairs={{0,6},{1,7},{2,4},{3,5},{4,2},{5,3},{6,0},{7,1},{8,14},{9,15},{10,... | collective-permute-start | bytes 159752 | tf_op jit(solution)/shard_map/ppermute | solution.py:463
  5.9 9.9 %collective-permute-start.1 = (bf16[16,1664]{1,0:T(8,128)(2,1)}, bf16[16,1664]{1,0:T(8,128)(2,1)S(1)}, u32[]{:S(2)}, u32[]{:S(2)}) collective-permute-start(bf16[16,1664]{1,0:T(8,128)(2,1)} %get-tuple-element.23), channel_id=1, source_target_pairs={{0,4},{1,5},{2,6},{3,7},{4,0},{5,1},{6,2},{7,3},{8,12},{9,13},{10,... | collective-permute-start | bytes 159752 | tf_op jit(solution)/shard_map/ppermute | solution.py:463
  5.9 9.9 %collective-permute-start = (bf16[16,1664]{1,0:T(8,128)(2,1)}, bf16[16,1664]{1,0:T(8,128)(2,1)S(1)}, u32[]{:S(2)}, u32[]{:S(2)}) collective-permute-start(bf16[16,1664]{1,0:T(8,128)(2,1)} %get-tuple-element.23), channel_id=1, source_target_pairs={{0,2},{1,3},{2,0},{3,1},{4,6},{5,7},{6,4},{7,5},{8,10},{9,11},{10,... | collective-permute-start | bytes 159752 | tf_op jit(solution)/shard_map/ppermute | solution.py:463
  6.7 8.3 %collective-permute-start.3 = (f32[1,4,384]{2,1,0:T(4,128)}, f32[1,4,384]{2,1,0:T(4,128)S(1)}, u32[]{:S(2)}, u32[]{:S(2)}) collective-permute-start(f32[1,4,384]{2,1,0:T(4,128)} %get-tuple-element.24), channel_id=1, source_target_pairs={{8,0},{16,8},{24,16},{9,1},{17,9},{25,17},{10,2},{18,10},{26,18},{... | collective-permute-start | bytes 18440 | tf_op jit(solution)/shard_map/ppermute | solution.py:502
  10.1 5.8 %copy-start.6 = (bf16[16,1664]{1,0:T(8,128)(2,1)S(1)}, bf16[16,1664]{1,0:T(8,128)(2,1)}, u32[]{:S(2)}) copy-start(bf16[16,1664]{1,0:T(8,128)(2,1)} %get-tuple-element.23) | copy-start | bytes 159748
  10.1 9.4 %copy-start.4 = (f32[32,2,384]{2,1,0:T(2,128)S(1)}, f32[32,2,384]{2,1,0:T(2,128)}, u32[]{:S(2)}) copy-start(f32[32,2,384]{2,1,0:T(2,128)} %ctf_hbm.1) | copy-start | bytes 294916
  10.1 9.4 %copy-start.5 = (s32[1984]{0:T(1024)S(1)}, s32[1984]{0:T(1024)}, u32[]{:S(2)}) copy-start(s32[1984]{0:T(1024)} %constant.26.clone.table_hbm) | copy-start | bytes 23812
  12.2 1.8 %copy-start = (bf16[7,2048,128]{2,1,0:T(8,128)(2,1)}, bf16[7,2048,128]{2,1,0:T(8,128)(2,1)S(1)}, u32[]{:S(2)}) copy-start(bf16[7,2048,128]{2,1,0:T(8,128)(2,1)S(1)} %get-tuple-element.27.right) | copy-start | bytes 11010052
  15.9 9.9 %collective-permute-start.6 = (bf16[64,1664]{1,0:T(8,128)(2,1)S(1)}, bf16[64,1664]{1,0:T(8,128)(2,1)S(1)}, u32[]{:S(2)}, u32[]{:S(2)}) collective-permute-start(bf16[64,1664]{1,0:T(8,128)(2,1)S(1)} %pad_maximum_fusion.refs_0_), channel_id=1, source_target_pairs={{0,24},{8,16},{16,8},{24,0},{1,25},{9,17},{17,9},{25,1},{2,26},{10... | collective-permute-start | bytes 638984 | tf_op jit(solution)/shard_map/ppermute | solution.py:463
  16.0 10.3 %collective-permute-start.5 = (bf16[64,1664]{1,0:T(8,128)(2,1)S(1)}, bf16[64,1664]{1,0:T(8,128)(2,1)S(1)}, u32[]{:S(2)}, u32[]{:S(2)}) collective-permute-start(bf16[64,1664]{1,0:T(8,128)(2,1)S(1)} %pad_maximum_fusion.refs_0_), channel_id=1, source_target_pairs={{0,16},{8,24},{16,0},{24,8},{1,17},{9,25},{17,1},{25,9},{2,18},{10... | collective-permute-start | bytes 638984 | tf_op jit(solution)/shard_map/ppermute | solution.py:463
  17.5 8.8 %collective-permute-start.4 = (bf16[64,1664]{1,0:T(8,128)(2,1)S(1)}, bf16[64,1664]{1,0:T(8,128)(2,1)S(1)}, u32[]{:S(2)}, u32[]{:S(2)}) collective-permute-start(bf16[64,1664]{1,0:T(8,128)(2,1)S(1)} %pad_maximum_fusion.refs_0_), channel_id=1, source_target_pairs={{0,8},{8,0},{16,24},{24,16},{1,9},{9,1},{17,25},{25,17},{2,10},{10... | collective-permute-start | bytes 638984 | tf_op jit(solution)/shard_map/ppermute | solution.py:463
  19.5 24.3 %copy-start.1 = (bf16[7,2048,128]{2,1,0:T(8,128)(2,1)S(1)}, bf16[7,2048,128]{2,1,0:T(8,128)(2,1)}, u32[]{:S(2)}) copy-start(bf16[7,2048,128]{2,1,0:T(8,128)(2,1)} %copy-done) | copy-start | bytes 11010052
  26.2 1.5 %collective-permute-start.7 = (bf16[64,1664]{1,0:T(8,128)(2,1)S(1)}, bf16[64,1664]{1,0:T(8,128)(2,1)S(1)}, u32[]{:S(2)}, u32[]{:S(2)}) collective-permute-start(bf16[64,1664]{1,0:T(8,128)(2,1)S(1)} %pad_maximum_fusion.refs_0_), channel_id=1, source_target_pairs={{0,1},{1,0},{2,3},{3,2},{4,5},{5,4},{6,7},{7,6},{8,9},{9,8},{10,11... | collective-permute-start | bytes 638984 | tf_op jit(solution)/shard_map/ppermute | solution.py:463
  26.2 1.8 %collective-permute-start.8 = (bf16[64,1664]{1,0:T(8,128)(2,1)S(1)}, bf16[64,1664]{1,0:T(8,128)(2,1)S(1)}, u32[]{:S(2)}, u32[]{:S(2)}) collective-permute-start(bf16[64,1664]{1,0:T(8,128)(2,1)S(1)} %collective-permute-done.4.refs_1_), channel_id=1, source_target_pairs={{0,1},{1,0},{2,3},{3,2},{4,5},{5,4},{6,7},{7,6},{8,9},{9,8},{10,11... | collective-permute-start | bytes 638984 | tf_op jit(solution)/shard_map/ppermute | solution.py:463
  26.8 1.6 %collective-permute-start.9 = (bf16[64,1664]{1,0:T(8,128)(2,1)S(1)}, bf16[64,1664]{1,0:T(8,128)(2,1)S(1)}, u32[]{:S(2)}, u32[]{:S(2)}) collective-permute-start(bf16[64,1664]{1,0:T(8,128)(2,1)S(1)} %collective-permute-done.5.refs_2_), channel_id=1, source_target_pairs={{0,1},{1,0},{2,3},{3,2},{4,5},{5,4},{6,7},{7,6},{8,9},{9,8},{10,11... | collective-permute-start | bytes 638984 | tf_op jit(solution)/shard_map/ppermute | solution.py:463
  26.8 1.9 %collective-permute-start.10 = (bf16[64,1664]{1,0:T(8,128)(2,1)S(1)}, bf16[64,1664]{1,0:T(8,128)(2,1)S(1)}, u32[]{:S(2)}, u32[]{:S(2)}) collective-permute-start(bf16[64,1664]{1,0:T(8,128)(2,1)S(1)} %collective-permute-done.6.refs_3_), channel_id=1, source_target_pairs={{0,1},{1,0},{2,3},{3,2},{4,5},{5,4},{6,7},{7,6},{8,9},{9,8},{10,11... | collective-permute-start | bytes 638984 | tf_op jit(solution)/shard_map/ppermute | solution.py:463

commit v9 on v8

--- a/solution.py
+++ b/solution.py
@@ -154,17 +154,24 @@
 
 
 def pack_kernel(
-    observed_hbm, classes_hbm, bins_hbm, volume, packed, plane, observed, classes, bin_ids, sems
+    planes, observed_hbm, classes_hbm, bins_hbm, volume,
+    packed, plane, field, observed, classes, bin_ids, sems,
 ):
+    dom = lax.axis_index("dom")
+    after = jnp.minimum((dom + 1) * planes, volume.shape[0] - 1)
     copies = fetch(
         [
             (observed_hbm, observed),
             (classes_hbm, classes),
             (bins_hbm, bin_ids),
             (volume.at[pl.ds(0, 1)], plane),
+            (volume.at[pl.ds(dom * planes, planes)], field.at[pl.ds(0, planes)]),
+            (volume.at[pl.ds(after, 1)], field.at[pl.ds(planes, 1)]),
         ],
         sems,
     )
+    for z in range(planes + 1, field.shape[0]):
+        field[z] = jnp.zeros(field.shape[1:], f32)
     for copy in copies[:3]:
         copy.wait()
     count, rows, samples = observed.shape
@@ -178,18 +185,20 @@
         column = jnp.where(diagonal, ids[...].astype(f32), 0.0)
         tail = jnp.where(lane == n, jnp.sum(column, axis=1, keepdims=True), tail)
     packed[:, rows * samples :] = tail.astype(bf16)
-    copies[3].wait()
+    for copy in copies[3:]:
+        copy.wait()
 
 
 def extract_kernel(
     groups, length, samples, bins, planes, n_dom,
-    table_hbm, trig_hbm, field, ctf_hbm, slope, pairs, flat,
+    table_hbm, trig_hbm, field, above, ctf_hbm, slope, pairs, flat,
     table, trig, ctf, vhi, vlo, out, sems,
 ):
     depth = field.shape[0]
     xt_count = vhi.shape[0]
     ut_count = samples // TILE
-    device = lax.axis_index("gz") * n_dom + lax.axis_index("dom")
+    dom = lax.axis_index("dom")
+    device = lax.axis_index("gz") * n_dom + dom
     row = device * length
     first = device * planes
     z0, z1 = first.astype(f32), (first + planes).astype(f32)
@@ -205,9 +214,12 @@
     out[...] = jnp.zeros_like(out)
     for copy in copies:
         copy.wait()
+    last = dom == n_dom - 1
     for xt in range(xt_count):
+        lanes = slice(xt * TILE, (xt + 1) * TILE)
+        halo = (lax.broadcasted_iota(jnp.int32, (depth, TILE), 0) == planes) & last
         stacked = jnp.concatenate(
-            [field[:, r, xt * TILE : (xt + 1) * TILE] for r in range(4)], 0
+            [jnp.where(halo, above[0, r : r + 1, lanes], field[:, r, lanes]) for r in range(4)], 0
         )
         hi = stacked.astype(bf16)
         vhi[xt] = hi
@@ -480,19 +492,21 @@
     params = pltpu.CompilerParams(vmem_limit_bytes=min(56, 19 + 37 * count // 4096) * 2**20)
     extract_plan, spread_plan, edge_samples, trig = make_plan(devices, bins, samples, columns)
     trig = jnp.asarray(trig)
-    packed, plane = pl.pallas_call(
-        pack_kernel,
+    depth_in = round_up(planes + 1, 8)
+    packed, plane, field = pl.pallas_call(
+        functools.partial(pack_kernel, planes),
         out_shape=[
             jax.ShapeDtypeStruct((mine, width + TILE), bf16),
             jax.ShapeDtypeStruct((1, rows, columns), f32),
+            jax.ShapeDtypeStruct((depth_in, rows, columns), f32),
         ],
         in_specs=[hbm] * 4,
-        out_specs=[vmem, vmem],
+        out_specs=[vmem] * 3,
         scratch_shapes=[
             pltpu.VMEM(observed.shape, bf16),
             pltpu.VMEM((1, mine), jnp.int32),
             pltpu.VMEM((1, mine), jnp.int32),
-            pltpu.SemaphoreType.DMA((4,)),
+            pltpu.SemaphoreType.DMA((6,)),
         ],
         compiler_params=wide,
         name="pack",
@@ -503,12 +517,6 @@
     column = jnp.concatenate(
         [packed] + [swap(packed, "dom", n_dom, 2 * k) for k in range(1, n_z)], 0
     )
-    dom = lax.axis_index("dom")
-    own = lax.dynamic_slice_in_dim(volume, dom * planes, planes, 0)
-    inner = lax.dynamic_slice_in_dim(volume, jnp.minimum((dom + 1) * planes, slab - 1), 1, 0)
-    halo = jnp.where(dom == n_dom - 1, above, inner)
-    depth_in = round_up(planes + 1, 8)
-    field = jnp.concatenate([own, halo, jnp.zeros((depth_in - planes - 1, rows, columns), f32)], 0)
     spread_table, spread_groups = spread_plan
     spread_table_flat = jnp.asarray(spread_table.reshape(-1))
     right, edges = pl.pallas_call(
@@ -521,11 +529,11 @@
         ],
         in_specs=[smem, smem],
         out_specs=[vmem, vmem],
-        compiler_params=params,
+        compiler_params=wide,
         cost_estimate=pl.CostEstimate(flops=3 * 10**9, bytes_accessed=2**21, transcendentals=0),
         name="weights",
     )(spread_table_flat, trig)
-    column, field, right, edges = lax.optimization_barrier((column, field, right, edges))
+    column, above, right, edges = lax.optimization_barrier((column, above, right, edges))
     planes_of = [column] + [swap(column, "gz", n_gz, j) for j in range(1, n_gz)]
 
 
@@ -539,7 +547,7 @@
             jax.ShapeDtypeStruct((NCTF, 6 * bins), bf16),
             jax.ShapeDtypeStruct((NCTF, width // 2), f32),
         ],
-        in_specs=[hbm, hbm, vmem, hbm],
+        in_specs=[hbm, hbm, vmem, vmem, hbm],
         out_specs=[vmem, vmem, vmem],
         scratch_shapes=[
             pltpu.SMEM((table.size,), jnp.int32),
@@ -553,7 +561,7 @@
         compiler_params=params,
         cost_estimate=pl.CostEstimate(flops=6 * 10**9, bytes_accessed=2**20, transcendentals=0),
         name="extract",
-    )(jnp.asarray(table.reshape(-1)), trig, field, ctf_table)
+    )(jnp.asarray(table.reshape(-1)), trig, field, above, ctf_table)
 
     planes_of, slope = lax.optimization_barrier((planes_of, slope))
     gathered = planes_of + [swap(part, "dom", n_dom, 1) for part in planes_of]

time: 49.8 us -> 48.6 us (0.976)
  local copies, waits for them, and re-layouts: 2.83 us -> 0.04 us
  Pallas kernels: 18.5 us -> 20.8 us
  other arithmetic: 0.82 us -> 0.03 us
    pallas_call x1, Pallas kernels: 2.09 us -> 4.28 us  [local(): pl.pallas_call(functools.partial(weight_kernel, spread_groups, spread_tab...]
    unnamed x14 -> x16, local copies, waits for them, and re-layouts: 1.82 us -> 0.04 us
    dynamic_slice x1 -> x0, local copies, waits for them, and re-layouts: 0.92 us -> none  [local(): own = lax.dynamic_slice_in_dim(volume, dom * planes, planes, 0)]
    select_n x1 -> x0, other arithmetic: 0.7 us -> none  [local(): halo = jnp.where(dom == n_dom - 1, above, inner)]
  transfers between devices with their start and end apart: 11 -> 11, of which waited for: 5 -> 5; matrix products, arithmetic and copies ran while one was open for 4% -> 0% of each run, Pallas kernels for 17% -> 22%
where the time goes in v9:
time: 48.6 us; the launch traced here: 48.3 us
  Pallas kernels  20.8 us (43%)
  starting transfers between devices  12.5 us (26%)
  blocking collectives  12.4 us (26%)
  waiting for transfers between devices  1.76 us (4%)
  between operations  0.74 us (2%)
    all_to_all x1, blocking collectives, local(): parts = lax.all_to_all(parts, ('gz', 'dom'), 0, 0, tiled=True)  12.4 us
    ppermute x10, starting transfers between devices, swap(): return lax.ppermute(x, axis, [(i, i ^ distance) for i in range(size)])  9.03 us
    pallas_call x1, Pallas kernels, local(): pl.pallas_call(functools.partial(extract_kernel, groups, table.shape[1],...  6.32 us
    pallas_call x1, Pallas kernels, local(): pl.pallas_call(functools.partial(spread_kernel, spread_groups, spread_tab...  5.76 us
    pallas_call x1, Pallas kernels, local(): pl.pallas_call(functools.partial(weight_kernel, spread_groups, spread_tab...  4.28 us
    ppermute x1, starting transfers between devices, local(): above = lax.ppermute(plane, 'gz', [(i, i - 1) for i in range(1, n_gz)])  3.47 us
    pallas_call x1, Pallas kernels, local(): pl.pallas_call(functools.partial(particle_kernel, width, mine, n_gz, n_do...  2.73 us
    pallas_call x1, Pallas kernels, local(): pl.pallas_call(functools.partial(pack_kernel, planes), out_shape=[jax.Sha...  1.76 us
  transfers between devices with their start and end apart: 11, of which 5 were waited for; matrix products, arithmetic and copies ran while one was open for 0% of the time, Pallas kernels for 22%

profile of v9, /device:TPU:4, one launch (start us, length us, event | category | flops | bytes accessed | tf_op | source)
XLA Modules:
  0.0 48.3 jit_solution(17229491338994496459)
XLA Ops:
  0.6 1.8 %pack.1 = (bf16[16,1664]{1,0:T(8,128)(2,1)}, f32[1,4,384]{2,1,0:T(4,128)}, f32[32,4,384]{2,1,0:T(4,128)}) custom-call(bf16[16,4,384]{2,1,0:T(4,128)(2,1)} %observed_hbm.1, s32[1,16]{1,0:T(1,128)} %bitcast.7, s32[1,16]{1,0:T(1,128)} %bitcast.8, f32[192,4,384]{2,1,0:T(4,128)} %volume.1), custom_call_target="tpu_custom_call" | custom-call | tf_op jit(solution)/shard_map/pack/pallas_call | solution.py:496
  2.4 3.7 %collective-permute-start.2 = (bf16[16,1664]{1,0:T(8,128)(2,1)}, bf16[16,1664]{1,0:T(8,128)(2,1)S(1)}, u32[]{:S(2)}, u32[]{:S(2)}) collective-permute-start(bf16[16,1664]{1,0:T(8,128)(2,1)} %get-tuple-element.24), channel_id=1, source_target_pairs={{0,6},{1,7},{2,4},{3,5},{4,2},{5,3},{6,0},{7,1},{8,14},{9,15},{10,... | collective-permute-start | bytes 159752 | tf_op jit(solution)/shard_map/ppermute | solution.py:475
  6.1 0.0 collective-permute-start.1
  6.1 0.8 %collective-permute-start = (bf16[16,1664]{1,0:T(8,128)(2,1)}, bf16[16,1664]{1,0:T(8,128)(2,1)S(1)}, u32[]{:S(2)}, u32[]{:S(2)}) collective-permute-start(bf16[16,1664]{1,0:T(8,128)(2,1)} %get-tuple-element.24), channel_id=1, source_target_pairs={{0,2},{1,3},{2,0},{3,1},{4,6},{5,7},{6,4},{7,5},{8,10},{9,11},{10,... | collective-permute-start | bytes 159752 | tf_op jit(solution)/shard_map/ppermute | solution.py:475
  6.8 0.0 copy-start.7
  6.8 0.0 copy-start.3
  6.9 0.0 copy-start.4
  6.9 0.0 copy-start.5
  6.9 0.0 copy-start.6
  6.9 3.5 %collective-permute-start.3 = (f32[1,4,384]{2,1,0:T(4,128)}, f32[1,4,384]{2,1,0:T(4,128)S(1)}, u32[]{:S(2)}, u32[]{:S(2)}) collective-permute-start(f32[1,4,384]{2,1,0:T(4,128)} %get-tuple-element.25), channel_id=1, source_target_pairs={{8,0},{16,8},{24,16},{9,1},{17,9},{25,17},{10,2},{18,10},{26,18},{... | collective-permute-start | bytes 18440 | tf_op jit(solution)/shard_map/ppermute | solution.py:516
  10.4 4.3 %weights.1 = (bf16[7,2048,128]{2,1,0:T(8,128)(2,1)}, bf16[32,96,128]{2,1,0:T(8,128)(2,1)}) custom-call(s32[3104]{0:T(1024)} %constant.7.clone.table, f32[128]{0:T(128)} %constant.6.clone.trig.trig_hbm), custom_call_target="tpu_custom_call" | custom-call | flops 3000000000 | bytes 2097152 | tf_op jit(solution)/shard_map/weights/pallas_call | solution.py:522
  14.6 0.0 collective-permute-done.2
  14.6 0.0 collective-permute-done.1
  14.6 0.0 collective-permute-done
  14.6 0.0 copy-done.7
  14.7 0.0 collective-permute-done.3.above
  14.7 0.4 collective-permute-start.6
  15.1 1.2 %collective-permute-start.5 = (bf16[64,1664]{1,0:T(8,128)(2,1)S(1)}, bf16[64,1664]{1,0:T(8,128)(2,1)S(1)}, u32[]{:S(2)}, u32[]{:S(2)}) collective-permute-start(bf16[64,1664]{1,0:T(8,128)(2,1)S(1)} %pad_maximum_fusion.refs_0_), channel_id=1, source_target_pairs={{0,16},{8,24},{16,0},{24,8},{1,17},{9,25},{17,1},{25,9},{2,18},{10... | collective-permute-start | bytes 638984 | tf_op jit(solution)/shard_map/ppermute | solution.py:475
  16.3 2.0 %collective-permute-start.4 = (bf16[64,1664]{1,0:T(8,128)(2,1)S(1)}, bf16[64,1664]{1,0:T(8,128)(2,1)S(1)}, u32[]{:S(2)}, u32[]{:S(2)}) collective-permute-start(bf16[64,1664]{1,0:T(8,128)(2,1)S(1)} %pad_maximum_fusion.refs_0_), channel_id=1, source_target_pairs={{0,8},{8,0},{16,24},{24,16},{1,9},{9,1},{17,25},{25,17},{2,10},{10... | collective-permute-start | bytes 638984 | tf_op jit(solution)/shard_map/ppermute | solution.py:475
  18.2 0.0 copy-done.3
  18.3 0.0 copy-done.4
  18.3 0.0 copy-done.5
  18.3 0.0 copy-done.6
  18.3 0.0 copy-start
  18.3 6.3 %extract.1 = (bf16[128,1536]{1,0:T(8,128)(2,1)S(1)}, bf16[32,384]{1,0:T(8,128)(2,1)S(1)}, f32[32,768]{1,0:T(8,128)S(1)}) custom-call(s32[1984]{0:T(1024)S(1)} %copy-done.6, f32[128]{0:T(128)S(1)} %copy-done.3, f32[32,4,384]{2,1,0:T(4,128)S(1)} %copy-done.4, f32[1,4,384]{2,1,0:T(4,128)S(1)} %collective-permute-done.3.above, f32[32,2,384]{2,1,0:T(2,128)S(1)} %copy-done.5), custom_call_target="tpu_custom_call" | custom-call | flops 6000000000 | bytes 1048576 | tf_op jit(solution)/shard_map/extract/pallas_call | solution.py:541
  24.6 0.0 copy-start.1
  24.6 0.0 copy-start.2
  24.6 0.0 collective-permute-done.6.refs_3_
  24.6 0.4 collective-permute-done.5.refs_2_
  25.0 0.0 collective-permute-done.4.refs_1_
  25.0 0.0 collective-permute-start.7
  25.0 0.5 %collective-permute-start.8 = (bf16[64,1664]{1,0:T(8,128)(2,1)S(1)}, bf16[64,1664]{1,0:T(8,128)(2,1)S(1)}, u32[]{:S(2)}, u32[]{:S(2)}) collective-permute-start(bf16[64,1664]{1,0:T(8,128)(2,1)S(1)} %collective-permute-done.4.refs_1_), channel_id=1, source_target_pairs={{0,1},{1,0},{2,3},{3,2},{4,5},{5,4},{6,7},{7,6},{8,9},{9,8},{10,11... | collective-permute-start | bytes 638984 | tf_op jit(solution)/shard_map/ppermute | solution.py:475
  25.5 0.0 collective-permute-start.9
  25.5 0.5 %collective-permute-start.10 = (bf16[64,1664]{1,0:T(8,128)(2,1)S(1)}, bf16[64,1664]{1,0:T(8,128)(2,1)S(1)}, u32[]{:S(2)}, u32[]{:S(2)}) collective-permute-start(bf16[64,1664]{1,0:T(8,128)(2,1)S(1)} %collective-permute-done.6.refs_3_), channel_id=1, source_target_pairs={{0,1},{1,0},{2,3},{3,2},{4,5},{5,4},{6,7},{7,6},{8,9},{9,8},{10,11... | collective-permute-start | bytes 638984 | tf_op jit(solution)/shard_map/ppermute | solution.py:475
  26.0 0.4 collective-permute-done.7.refs_4_
  26.5 0.3 collective-permute-done.8.refs_5_
  26.8 0.3 collective-permute-done.9.refs_6_
  27.1 0.3 collective-permute-done.10.refs_7_
  27.4 2.7 %particles.1 = (bf16[512,1536]{1,0:T(8,128)(2,1)S(1)}, f32[256,128]{1,0:T(8,128)S(1)}, f32[1,512]{1,0:T(1,128)S(1)}) custom-call(bf16[64,1664]{1,0:T(8,128)(2,1)S(1)} %pad_maximum_fusion.refs_0_, bf16[64,1664]{1,0:T(8,128)(2,1)S(1)} %collective-permute-done.4.refs_1_, bf16[64,1664]{1,0:T(8,128)(2,1)S(1)} %collective-permute-done.5.refs_2_, ...), custom_call_target="tpu_custom_call" | custom-call | tf_op jit(solution)/shard_map/particles/pallas_call | solution.py:568
  30.1 12.4 %all_to_all.11 = f32[32,8,128]{2,1,0:T(8,128)S(1)} all-to-all(f32[32,8,128]{2,1,0:T(8,128)S(1)} %bitcast.6), channel_id=1, replica_groups=mesh['gz'=4,'dom'=8] {'gz','dom'}, dimensions={0} | all-to-all | bytes 262144 | tf_op jit(solution)/shard_map/all_to_all | solution.py:581
  42.5 0.0 copy-done
  42.5 0.0 copy-done.1
  42.5 0.0 copy-done.2
  42.5 5.8 %spread.1 = (f32[1,16]{1,0:T(1,128)}, f32[24,4,384]{2,1,0:T(4,128)}) custom-call(s32[3104]{0:T(1024)S(1)} %copy-done.2, f32[128]{0:T(128)S(1)} %copy-done.3, bf16[7,2048,128]{2,1,0:T(8,128)(2,1)S(1)} %copy-done, bf16[32,96,128]{2,1,0:T(8,128)(2,1)S(1)} %copy-done.1, f32[256,128]{1,0:T(8,128)S(1)} %bitcast.5, f32[1,512]{1,0:T(1,128)S(1)} %get-tuple-element.42.bins_row, ...), custom_call_target="tpu_custom_call" | custom-call | tf_op jit(solution)/shard_map/spread/pallas_call | solution.py:584
  (1 shorter events, 0.0 us)
Async XLA Ops:
  2.4 12.2 %collective-permute-start.2 = (bf16[16,1664]{1,0:T(8,128)(2,1)}, bf16[16,1664]{1,0:T(8,128)(2,1)S(1)}, u32[]{:S(2)}, u32[]{:S(2)}) collective-permute-start(bf16[16,1664]{1,0:T(8,128)(2,1)} %get-tuple-element.24), channel_id=1, source_target_pairs={{0,6},{1,7},{2,4},{3,5},{4,2},{5,3},{6,0},{7,1},{8,14},{9,15},{10,... | collective-permute-start | bytes 159752 | tf_op jit(solution)/shard_map/ppermute | solution.py:475
  6.1 8.6 %collective-permute-start.1 = (bf16[16,1664]{1,0:T(8,128)(2,1)}, bf16[16,1664]{1,0:T(8,128)(2,1)S(1)}, u32[]{:S(2)}, u32[]{:S(2)}) collective-permute-start(bf16[16,1664]{1,0:T(8,128)(2,1)} %get-tuple-element.24), channel_id=1, source_target_pairs={{0,4},{1,5},{2,6},{3,7},{4,0},{5,1},{6,2},{7,3},{8,12},{9,13},{10,... | collective-permute-start | bytes 159752 | tf_op jit(solution)/shard_map/ppermute | solution.py:475
  6.1 8.6 %collective-permute-start = (bf16[16,1664]{1,0:T(8,128)(2,1)}, bf16[16,1664]{1,0:T(8,128)(2,1)S(1)}, u32[]{:S(2)}, u32[]{:S(2)}) collective-permute-start(bf16[16,1664]{1,0:T(8,128)(2,1)} %get-tuple-element.24), channel_id=1, source_target_pairs={{0,2},{1,3},{2,0},{3,1},{4,6},{5,7},{6,4},{7,5},{8,10},{9,11},{10,... | collective-permute-start | bytes 159752 | tf_op jit(solution)/shard_map/ppermute | solution.py:475
  6.8 7.8 %copy-start.7 = (bf16[16,1664]{1,0:T(8,128)(2,1)S(1)}, bf16[16,1664]{1,0:T(8,128)(2,1)}, u32[]{:S(2)}) copy-start(bf16[16,1664]{1,0:T(8,128)(2,1)} %get-tuple-element.24) | copy-start | bytes 159748
  6.8 11.4 %copy-start.3 = (f32[128]{0:T(128)S(1)}, f32[128]{0:T(128)}, u32[]{:S(2)}) copy-start(f32[128]{0:T(128)} %constant.6.clone.trig.trig_hbm) | copy-start | bytes 1540
  6.9 11.4 %copy-start.4 = (f32[32,4,384]{2,1,0:T(4,128)S(1)}, f32[32,4,384]{2,1,0:T(4,128)}, u32[]{:S(2)}) copy-start(f32[32,4,384]{2,1,0:T(4,128)} %get-tuple-element.31.field) | copy-start | bytes 589828
  6.9 11.4 %copy-start.5 = (f32[32,2,384]{2,1,0:T(2,128)S(1)}, f32[32,2,384]{2,1,0:T(2,128)}, u32[]{:S(2)}) copy-start(f32[32,2,384]{2,1,0:T(2,128)} %ctf_hbm.1) | copy-start | bytes 294916
  6.9 11.4 %copy-start.6 = (s32[1984]{0:T(1024)S(1)}, s32[1984]{0:T(1024)}, u32[]{:S(2)}) copy-start(s32[1984]{0:T(1024)} %constant.8.clone.table_hbm) | copy-start | bytes 23812
  6.9 7.8 %collective-permute-start.3 = (f32[1,4,384]{2,1,0:T(4,128)}, f32[1,4,384]{2,1,0:T(4,128)S(1)}, u32[]{:S(2)}, u32[]{:S(2)}) collective-permute-start(f32[1,4,384]{2,1,0:T(4,128)} %get-tuple-element.25), channel_id=1, source_target_pairs={{8,0},{16,8},{24,16},{9,1},{17,9},{25,17},{10,2},{18,10},{26,18},{... | collective-permute-start | bytes 18440 | tf_op jit(solution)/shard_map/ppermute | solution.py:516
  14.7 9.9 %collective-permute-start.6 = (bf16[64,1664]{1,0:T(8,128)(2,1)S(1)}, bf16[64,1664]{1,0:T(8,128)(2,1)S(1)}, u32[]{:S(2)}, u32[]{:S(2)}) collective-permute-start(bf16[64,1664]{1,0:T(8,128)(2,1)S(1)} %pad_maximum_fusion.refs_0_), channel_id=1, source_target_pairs={{0,24},{8,16},{16,8},{24,0},{1,25},{9,17},{17,9},{25,1},{2,26},{10... | collective-permute-start | bytes 638984 | tf_op jit(solution)/shard_map/ppermute | solution.py:475
  15.1 10.0 %collective-permute-start.5 = (bf16[64,1664]{1,0:T(8,128)(2,1)S(1)}, bf16[64,1664]{1,0:T(8,128)(2,1)S(1)}, u32[]{:S(2)}, u32[]{:S(2)}) collective-permute-start(bf16[64,1664]{1,0:T(8,128)(2,1)S(1)} %pad_maximum_fusion.refs_0_), channel_id=1, source_target_pairs={{0,16},{8,24},{16,0},{24,8},{1,17},{9,25},{17,1},{25,9},{2,18},{10... | collective-permute-start | bytes 638984 | tf_op jit(solution)/shard_map/ppermute | solution.py:475
  16.3 8.8 %collective-permute-start.4 = (bf16[64,1664]{1,0:T(8,128)(2,1)S(1)}, bf16[64,1664]{1,0:T(8,128)(2,1)S(1)}, u32[]{:S(2)}, u32[]{:S(2)}) collective-permute-start(bf16[64,1664]{1,0:T(8,128)(2,1)S(1)} %pad_maximum_fusion.refs_0_), channel_id=1, source_target_pairs={{0,8},{8,0},{16,24},{24,16},{1,9},{9,1},{17,25},{25,17},{2,10},{10... | collective-permute-start | bytes 638984 | tf_op jit(solution)/shard_map/ppermute | solution.py:475
  18.3 24.3 %copy-start = (bf16[7,2048,128]{2,1,0:T(8,128)(2,1)S(1)}, bf16[7,2048,128]{2,1,0:T(8,128)(2,1)}, u32[]{:S(2)}) copy-start(bf16[7,2048,128]{2,1,0:T(8,128)(2,1)} %get-tuple-element.28.right) | copy-start | bytes 11010052
  24.6 17.9 %copy-start.1 = (bf16[32,96,128]{2,1,0:T(8,128)(2,1)S(1)}, bf16[32,96,128]{2,1,0:T(8,128)(2,1)}, u32[]{:S(2)}) copy-start(bf16[32,96,128]{2,1,0:T(8,128)(2,1)} %get-tuple-element.29.edges) | copy-start | bytes 2359300
  24.6 17.9 %copy-start.2 = (s32[3104]{0:T(1024)S(1)}, s32[3104]{0:T(1024)}, u32[]{:S(2)}) copy-start(s32[3104]{0:T(1024)} %constant.7.clone.table) | copy-start | bytes 37252
  25.0 1.5 %collective-permute-start.7 = (bf16[64,1664]{1,0:T(8,128)(2,1)S(1)}, bf16[64,1664]{1,0:T(8,128)(2,1)S(1)}, u32[]{:S(2)}, u32[]{:S(2)}) collective-permute-start(bf16[64,1664]{1,0:T(8,128)(2,1)S(1)} %pad_maximum_fusion.refs_0_), channel_id=1, source_target_pairs={{0,1},{1,0},{2,3},{3,2},{4,5},{5,4},{6,7},{7,6},{8,9},{9,8},{10,11... | collective-permute-start | bytes 638984 | tf_op jit(solution)/shard_map/ppermute | solution.py:475
  25.0 1.8 %collective-permute-start.8 = (bf16[64,1664]{1,0:T(8,128)(2,1)S(1)}, bf16[64,1664]{1,0:T(8,128)(2,1)S(1)}, u32[]{:S(2)}, u32[]{:S(2)}) collective-permute-start(bf16[64,1664]{1,0:T(8,128)(2,1)S(1)} %collective-permute-done.4.refs_1_), channel_id=1, source_target_pairs={{0,1},{1,0},{2,3},{3,2},{4,5},{5,4},{6,7},{7,6},{8,9},{9,8},{10,11... | collective-permute-start | bytes 638984 | tf_op jit(solution)/shard_map/ppermute | solution.py:475
  25.5 1.6 %collective-permute-start.9 = (bf16[64,1664]{1,0:T(8,128)(2,1)S(1)}, bf16[64,1664]{1,0:T(8,128)(2,1)S(1)}, u32[]{:S(2)}, u32[]{:S(2)}) collective-permute-start(bf16[64,1664]{1,0:T(8,128)(2,1)S(1)} %collective-permute-done.5.refs_2_), channel_id=1, source_target_pairs={{0,1},{1,0},{2,3},{3,2},{4,5},{5,4},{6,7},{7,6},{8,9},{9,8},{10,11... | collective-permute-start | bytes 638984 | tf_op jit(solution)/shard_map/ppermute | solution.py:475
  25.5 1.9 %collective-permute-start.10 = (bf16[64,1664]{1,0:T(8,128)(2,1)S(1)}, bf16[64,1664]{1,0:T(8,128)(2,1)S(1)}, u32[]{:S(2)}, u32[]{:S(2)}) collective-permute-start(bf16[64,1664]{1,0:T(8,128)(2,1)S(1)} %collective-permute-done.6.refs_3_), channel_id=1, source_target_pairs={{0,1},{1,0},{2,3},{3,2},{4,5},{5,4},{6,7},{7,6},{8,9},{9,8},{10,11... | collective-permute-start | bytes 638984 | tf_op jit(solution)/shard_map/ppermute | solution.py:475

commit v10 on v9

--- a/solution.py
+++ b/solution.py
@@ -517,23 +517,7 @@
     column = jnp.concatenate(
         [packed] + [swap(packed, "dom", n_dom, 2 * k) for k in range(1, n_z)], 0
     )
-    spread_table, spread_groups = spread_plan
-    spread_table_flat = jnp.asarray(spread_table.reshape(-1))
-    right, edges = pl.pallas_call(
-        functools.partial(
-            weight_kernel, spread_groups, spread_table.shape[1], bins, planes, n_dom, edge_samples
-        ),
-        out_shape=[
-            jax.ShapeDtypeStruct((spread_groups, SPREAD_GROUP * 2 * TILE, TILE), bf16),
-            jax.ShapeDtypeStruct((bins // 2, 2 * edge_samples, TILE), bf16),
-        ],
-        in_specs=[smem, smem],
-        out_specs=[vmem, vmem],
-        compiler_params=wide,
-        cost_estimate=pl.CostEstimate(flops=3 * 10**9, bytes_accessed=2**21, transcendentals=0),
-        name="weights",
-    )(spread_table_flat, trig)
-    column, above, right, edges = lax.optimization_barrier((column, above, right, edges))
+    column, above, trig = lax.optimization_barrier((column, above, trig))
     planes_of = [column] + [swap(column, "gz", n_gz, j) for j in range(1, n_gz)]
 
 
@@ -563,7 +547,23 @@
         name="extract",
     )(jnp.asarray(table.reshape(-1)), trig, field, above, ctf_table)
 
-    planes_of, slope = lax.optimization_barrier((planes_of, slope))
+    spread_table, spread_groups = spread_plan
+    spread_table_flat = jnp.asarray(spread_table.reshape(-1))
+    right, edges = pl.pallas_call(
+        functools.partial(
+            weight_kernel, spread_groups, spread_table.shape[1], bins, planes, n_dom, edge_samples
+        ),
+        out_shape=[
+            jax.ShapeDtypeStruct((spread_groups, SPREAD_GROUP * 2 * TILE, TILE), bf16),
+            jax.ShapeDtypeStruct((bins // 2, 2 * edge_samples, TILE), bf16),
+        ],
+        in_specs=[smem, smem],
+        out_specs=[vmem, vmem],
+        compiler_params=params,
+        cost_estimate=pl.CostEstimate(flops=3 * 10**9, bytes_accessed=2**21, transcendentals=0),
+        name="weights",
+    )(spread_table_flat, trig)
+    planes_of, slope, right, edges = lax.optimization_barrier((planes_of, slope, right, edges))
     gathered = planes_of + [swap(part, "dom", n_dom, 1) for part in planes_of]
     weighted, parts, bins_row = pl.pallas_call(
         functools.partial(particle_kernel, width, mine, n_gz, n_dom),

time: 48.6 us -> 49 us (level)
  Pallas kernels: 20.8 us -> 18.7 us
  waiting for transfers between devices: 1.76 us -> 2.91 us
  local copies, waits for them, and re-layouts: 0.04 us -> 0.95 us
  other arithmetic: 0.03 us -> 0.83 us
    pallas_call x1, Pallas kernels: 4.28 us -> 2.09 us  [local(): pl.pallas_call(functools.partial(weight_kernel, spread_groups, spread_tab...]
    unnamed x16 -> x10, local copies, waits for them, and re-layouts: 0.04 us -> 0.95 us
    concatenate x1, other arithmetic: 0.03 us -> 0.83 us  [local(): jnp.concatenate([packed] + [swap(packed, 'dom', n_dom, 2 * k) for k in ra...]
    ppermute x10, waiting for transfers between devices: 1.75 us -> 2.48 us  [swap(): return lax.ppermute(x, axis, [(i, i ^ distance) for i in range(size)])]
  transfers between devices with their start and end apart: 11 -> 11, of which waited for: 5 -> 6; matrix products, arithmetic and copies ran while one was open for 0% -> 2% of each run, Pallas kernels for 22% -> 17%
where the time goes in v10:
time: 49 us; the launch traced here: 48.7 us
  Pallas kernels  18.7 us (38%)
  starting transfers between devices  12.3 us (25%)
  blocking collectives  12.2 us (25%)
  waiting for transfers between devices  2.91 us (6%)
  local copies, waits for them, and re-layouts  0.95 us (2%)
  other arithmetic  0.83 us (2%)
  between operations  0.76 us (2%)
    all_to_all x1, blocking collectives, local(): parts = lax.all_to_all(parts, ('gz', 'dom'), 0, 0, tiled=True)  12.2 us
    ppermute x10, starting transfers between devices, swap(): return lax.ppermute(x, axis, [(i, i ^ distance) for i in range(size)])  9.02 us
    pallas_call x1, Pallas kernels, local(): pl.pallas_call(functools.partial(extract_kernel, groups, table.shape[1],...  6.35 us
    pallas_call x1, Pallas kernels, local(): pl.pallas_call(functools.partial(spread_kernel, spread_groups, spread_tab...  5.76 us
    ppermute x1, starting transfers between devices, local(): above = lax.ppermute(plane, 'gz', [(i, i - 1) for i in range(1, n_gz)])  3.33 us
    pallas_call x1, Pallas kernels, local(): pl.pallas_call(functools.partial(particle_kernel, width, mine, n_gz, n_do...  2.74 us
    ppermute x10, waiting for transfers between devices, swap(): return lax.ppermute(x, axis, [(i, i ^ distance) for i in range(size)])  2.48 us
    pallas_call x1, Pallas kernels, local(): pl.pallas_call(functools.partial(weight_kernel, spread_groups, spread_tab...  2.09 us
  transfers between devices with their start and end apart: 11, of which 6 were waited for; matrix products, arithmetic and copies ran while one was open for 2% of the time, Pallas kernels for 17%

profile of v10, /device:TPU:4, one launch (start us, length us, event | category | flops | bytes accessed | tf_op | source)
XLA Modules:
  0.0 48.7 jit_solution(6727016975504523023)
XLA Ops:
  0.6 0.0 copy-start.1
  0.6 0.0 copy-start.4
  0.7 0.0 copy-start.3
  0.7 1.8 %pack.1 = (bf16[16,1664]{1,0:T(8,128)(2,1)}, f32[1,4,384]{2,1,0:T(4,128)}, f32[32,4,384]{2,1,0:T(4,128)}) custom-call(bf16[16,4,384]{2,1,0:T(4,128)(2,1)} %observed_hbm.1, s32[1,16]{1,0:T(1,128)} %bitcast.7, s32[1,16]{1,0:T(1,128)} %bitcast.8, f32[192,4,384]{2,1,0:T(4,128)} %volume.1), custom_call_target="tpu_custom_call" | custom-call | tf_op jit(solution)/shard_map/pack/pallas_call | solution.py:496
  2.4 3.7 %collective-permute-start.2 = (bf16[16,1664]{1,0:T(8,128)(2,1)}, bf16[16,1664]{1,0:T(8,128)(2,1)S(1)}, u32[]{:S(2)}, u32[]{:S(2)}) collective-permute-start(bf16[16,1664]{1,0:T(8,128)(2,1)} %get-tuple-element.25), channel_id=1, source_target_pairs={{0,6},{1,7},{2,4},{3,5},{4,2},{5,3},{6,0},{7,1},{8,14},{9,15},{10,... | collective-permute-start | bytes 159752 | tf_op jit(solution)/shard_map/ppermute | solution.py:475
  6.1 0.0 collective-permute-start.1
  6.1 0.8 %collective-permute-start = (bf16[16,1664]{1,0:T(8,128)(2,1)}, bf16[16,1664]{1,0:T(8,128)(2,1)S(1)}, u32[]{:S(2)}, u32[]{:S(2)}) collective-permute-start(bf16[16,1664]{1,0:T(8,128)(2,1)} %get-tuple-element.25), channel_id=1, source_target_pairs={{0,2},{1,3},{2,0},{3,1},{4,6},{5,7},{6,4},{7,5},{8,10},{9,11},{10,... | collective-permute-start | bytes 159752 | tf_op jit(solution)/shard_map/ppermute | solution.py:475
  6.9 3.3 %collective-permute-start.3 = (f32[1,4,384]{2,1,0:T(4,128)}, f32[1,4,384]{2,1,0:T(4,128)S(1)}, u32[]{:S(2)}, u32[]{:S(2)}) collective-permute-start(f32[1,4,384]{2,1,0:T(4,128)} %get-tuple-element.26), channel_id=1, source_target_pairs={{8,0},{16,8},{24,16},{9,1},{17,9},{25,17},{10,2},{18,10},{26,18},{... | collective-permute-start | bytes 18440 | tf_op jit(solution)/shard_map/ppermute | solution.py:516
  10.2 0.0 collective-permute-done.2
  10.2 1.1 %collective-permute-done.1 = bf16[16,1664]{1,0:T(8,128)(2,1)S(1)} collective-permute-done((bf16[16,1664]{1,0:T(8,128)(2,1)}, bf16[16,1664]{1,0:T(8,128)(2,1)S(1)}, u32[]{:S(2)}, u32[]{:S(2)}) %collective-permute-start.1) | collective-permute-done | bytes 53280 | tf_op jit(solution)/shard_map/ppermute | solution.py:475
  11.3 0.0 collective-permute-done
  11.4 0.8 %pad_maximum_fusion.refs_0_ = bf16[64,1664]{1,0:T(8,128)(2,1)S(1)} fusion(bf16[16,1664]{1,0:T(8,128)(2,1)S(1)} %collective-permute-done.2, bf16[16,1664]{1,0:T(8,128)(2,1)S(1)} %collective-permute-done.1, bf16[16,1664]{1,0:T(8,128)(2,1)S(1)} %collective-permute-done, bf16[16,1664]{1,0:T(8,128)(2,1)} %get-tuple-element.25), kind=kLoop, calls=%fused_computation | loop fusion | flops 851968 | bytes 425984 | tf_op jit(solution)/shard_map/concatenate | solution.py:517
  12.2 0.4 collective-permute-done.3.above
  12.6 2.3 %collective-permute-start.6 = (bf16[64,1664]{1,0:T(8,128)(2,1)S(1)}, bf16[64,1664]{1,0:T(8,128)(2,1)S(1)}, u32[]{:S(2)}, u32[]{:S(2)}) collective-permute-start(bf16[64,1664]{1,0:T(8,128)(2,1)S(1)} %pad_maximum_fusion.refs_0_), channel_id=1, source_target_pairs={{0,24},{8,16},{16,8},{24,0},{1,25},{9,17},{17,9},{25,1},{2,26},{10... | collective-permute-start | bytes 638984 | tf_op jit(solution)/shard_map/ppermute | solution.py:475
  14.9 0.3 collective-permute-start.5
  15.2 0.9 %collective-permute-start.4 = (bf16[64,1664]{1,0:T(8,128)(2,1)S(1)}, bf16[64,1664]{1,0:T(8,128)(2,1)S(1)}, u32[]{:S(2)}, u32[]{:S(2)}) collective-permute-start(bf16[64,1664]{1,0:T(8,128)(2,1)S(1)} %pad_maximum_fusion.refs_0_), channel_id=1, source_target_pairs={{0,8},{8,0},{16,24},{24,16},{1,9},{9,1},{17,25},{25,17},{2,10},{10... | collective-permute-start | bytes 638984 | tf_op jit(solution)/shard_map/ppermute | solution.py:475
  16.1 0.0 copy-done.1
  16.1 0.0 copy-done.4
  16.1 0.0 copy-done.3
  16.1 0.0 copy-start.2
  16.1 0.9 %copy-done.2 = f32[32,4,384]{2,1,0:T(4,128)S(1)} copy-done((f32[32,4,384]{2,1,0:T(4,128)S(1)}, f32[32,4,384]{2,1,0:T(4,128)}, u32[]{:S(2)}) %copy-start.2) | copy-done | bytes 196632
  17.0 0.0 copy-start
  17.0 6.3 %extract.1 = (bf16[128,1536]{1,0:T(8,128)(2,1)S(1)}, bf16[32,384]{1,0:T(8,128)(2,1)S(1)}, f32[32,768]{1,0:T(8,128)S(1)}) custom-call(s32[1984]{0:T(1024)S(1)} %copy-done.4, f32[128]{0:T(128)S(1)} %copy-done.1, f32[32,4,384]{2,1,0:T(4,128)S(1)} %copy-done.2, f32[1,4,384]{2,1,0:T(4,128)S(1)} %collective-permute-done.3.above, f32[32,2,384]{2,1,0:T(2,128)S(1)} %copy-done.3), custom_call_target="tpu_custom_call" | custom-call | flops 6000000000 | bytes 1048576 | tf_op jit(solution)/shard_map/extract/pallas_call | solution.py:525
  23.4 0.0 copy-done
  23.4 2.1 %weights.1 = (bf16[7,2048,128]{2,1,0:T(8,128)(2,1)S(1)}, bf16[32,96,128]{2,1,0:T(8,128)(2,1)S(1)}) custom-call(s32[3104]{0:T(1024)S(1)} %copy-done, f32[128]{0:T(128)S(1)} %copy-done.1), custom_call_target="tpu_custom_call" | custom-call | flops 3000000000 | bytes 2097152 | tf_op jit(solution)/shard_map/weights/pallas_call | solution.py:552
  25.5 0.0 collective-permute-done.6.refs_3_
  25.5 0.0 collective-permute-done.5.refs_2_
  25.5 0.0 collective-permute-done.4.refs_1_
  25.5 0.1 collective-permute-start.7
  25.6 0.5 %collective-permute-start.8 = (bf16[64,1664]{1,0:T(8,128)(2,1)S(1)}, bf16[64,1664]{1,0:T(8,128)(2,1)S(1)}, u32[]{:S(2)}, u32[]{:S(2)}) collective-permute-start(bf16[64,1664]{1,0:T(8,128)(2,1)S(1)} %collective-permute-done.4.refs_1_), channel_id=1, source_target_pairs={{0,1},{1,0},{2,3},{3,2},{4,5},{5,4},{6,7},{7,6},{8,9},{9,8},{10,11... | collective-permute-start | bytes 638984 | tf_op jit(solution)/shard_map/ppermute | solution.py:475
  26.1 0.1 collective-permute-start.9
  26.2 0.4 collective-permute-start.10
  26.6 0.4 collective-permute-done.7.refs_4_
  27.1 0.3 collective-permute-done.8.refs_5_
  27.4 0.3 collective-permute-done.9.refs_6_
  27.7 0.3 collective-permute-done.10.refs_7_
  28.0 2.7 %particles.1 = (bf16[512,1536]{1,0:T(8,128)(2,1)S(1)}, f32[256,128]{1,0:T(8,128)S(1)}, f32[1,512]{1,0:T(1,128)S(1)}) custom-call(bf16[64,1664]{1,0:T(8,128)(2,1)S(1)} %pad_maximum_fusion.refs_0_, bf16[64,1664]{1,0:T(8,128)(2,1)S(1)} %collective-permute-done.4.refs_1_, bf16[64,1664]{1,0:T(8,128)(2,1)S(1)} %collective-permute-done.5.refs_2_, ...), custom_call_target="tpu_custom_call" | custom-call | tf_op jit(solution)/shard_map/particles/pallas_call | solution.py:568
  30.7 12.2 %all_to_all.11 = f32[32,8,128]{2,1,0:T(8,128)S(1)} all-to-all(f32[32,8,128]{2,1,0:T(8,128)S(1)} %bitcast.6), channel_id=1, replica_groups=mesh['gz'=4,'dom'=8] {'gz','dom'}, dimensions={0} | all-to-all | bytes 262144 | tf_op jit(solution)/shard_map/all_to_all | solution.py:581
  43.0 5.8 %spread.1 = (f32[1,16]{1,0:T(1,128)}, f32[24,4,384]{2,1,0:T(4,128)}) custom-call(s32[3104]{0:T(1024)S(1)} %copy-done, f32[128]{0:T(128)S(1)} %copy-done.1, bf16[7,2048,128]{2,1,0:T(8,128)(2,1)S(1)} %get-tuple-element.34.right, bf16[32,96,128]{2,1,0:T(8,128)(2,1)S(1)} %get-tuple-element.35.edges, f32[256,128]{1,0:T(8,128)S(1)} %bitcast.5, ...), custom_call_target="tpu_custom_call" | custom-call | tf_op jit(solution)/shard_map/spread/pallas_call | solution.py:584
Async XLA Ops:
  0.6 15.5 %copy-start.1 = (f32[128]{0:T(128)S(1)}, f32[128]{0:T(128)}, u32[]{:S(2)}) copy-start(f32[128]{0:T(128)} %constant.6.clone.trig_hbm.trig) | copy-start | bytes 1540
  0.6 15.5 %copy-start.4 = (s32[1984]{0:T(1024)S(1)}, s32[1984]{0:T(1024)}, u32[]{:S(2)}) copy-start(s32[1984]{0:T(1024)} %constant.7.clone.table_hbm) | copy-start | bytes 23812
  0.7 15.5 %copy-start.3 = (f32[32,2,384]{2,1,0:T(2,128)S(1)}, f32[32,2,384]{2,1,0:T(2,128)}, u32[]{:S(2)}) copy-start(f32[32,2,384]{2,1,0:T(2,128)} %ctf_hbm.1) | copy-start | bytes 294916
  2.4 7.8 %collective-permute-start.2 = (bf16[16,1664]{1,0:T(8,128)(2,1)}, bf16[16,1664]{1,0:T(8,128)(2,1)S(1)}, u32[]{:S(2)}, u32[]{:S(2)}) collective-permute-start(bf16[16,1664]{1,0:T(8,128)(2,1)} %get-tuple-element.25), channel_id=1, source_target_pairs={{0,6},{1,7},{2,4},{3,5},{4,2},{5,3},{6,0},{7,1},{8,14},{9,15},{10,... | collective-permute-start | bytes 159752 | tf_op jit(solution)/shard_map/ppermute | solution.py:475
  6.1 5.2 %collective-permute-start.1 = (bf16[16,1664]{1,0:T(8,128)(2,1)}, bf16[16,1664]{1,0:T(8,128)(2,1)S(1)}, u32[]{:S(2)}, u32[]{:S(2)}) collective-permute-start(bf16[16,1664]{1,0:T(8,128)(2,1)} %get-tuple-element.25), channel_id=1, source_target_pairs={{0,4},{1,5},{2,6},{3,7},{4,0},{5,1},{6,2},{7,3},{8,12},{9,13},{10,... | collective-permute-start | bytes 159752 | tf_op jit(solution)/shard_map/ppermute | solution.py:475
  6.1 5.2 %collective-permute-start = (bf16[16,1664]{1,0:T(8,128)(2,1)}, bf16[16,1664]{1,0:T(8,128)(2,1)S(1)}, u32[]{:S(2)}, u32[]{:S(2)}) collective-permute-start(bf16[16,1664]{1,0:T(8,128)(2,1)} %get-tuple-element.25), channel_id=1, source_target_pairs={{0,2},{1,3},{2,0},{3,1},{4,6},{5,7},{6,4},{7,5},{8,10},{9,11},{10,... | collective-permute-start | bytes 159752 | tf_op jit(solution)/shard_map/ppermute | solution.py:475
  6.9 5.7 %collective-permute-start.3 = (f32[1,4,384]{2,1,0:T(4,128)}, f32[1,4,384]{2,1,0:T(4,128)S(1)}, u32[]{:S(2)}, u32[]{:S(2)}) collective-permute-start(f32[1,4,384]{2,1,0:T(4,128)} %get-tuple-element.26), channel_id=1, source_target_pairs={{8,0},{16,8},{24,16},{9,1},{17,9},{25,17},{10,2},{18,10},{26,18},{... | collective-permute-start | bytes 18440 | tf_op jit(solution)/shard_map/ppermute | solution.py:516
  12.6 12.9 %collective-permute-start.6 = (bf16[64,1664]{1,0:T(8,128)(2,1)S(1)}, bf16[64,1664]{1,0:T(8,128)(2,1)S(1)}, u32[]{:S(2)}, u32[]{:S(2)}) collective-permute-start(bf16[64,1664]{1,0:T(8,128)(2,1)S(1)} %pad_maximum_fusion.refs_0_), channel_id=1, source_target_pairs={{0,24},{8,16},{16,8},{24,0},{1,25},{9,17},{17,9},{25,1},{2,26},{10... | collective-permute-start | bytes 638984 | tf_op jit(solution)/shard_map/ppermute | solution.py:475
  14.9 10.6 %collective-permute-start.5 = (bf16[64,1664]{1,0:T(8,128)(2,1)S(1)}, bf16[64,1664]{1,0:T(8,128)(2,1)S(1)}, u32[]{:S(2)}, u32[]{:S(2)}) collective-permute-start(bf16[64,1664]{1,0:T(8,128)(2,1)S(1)} %pad_maximum_fusion.refs_0_), channel_id=1, source_target_pairs={{0,16},{8,24},{16,0},{24,8},{1,17},{9,25},{17,1},{25,9},{2,18},{10... | collective-permute-start | bytes 638984 | tf_op jit(solution)/shard_map/ppermute | solution.py:475
  15.2 10.3 %collective-permute-start.4 = (bf16[64,1664]{1,0:T(8,128)(2,1)S(1)}, bf16[64,1664]{1,0:T(8,128)(2,1)S(1)}, u32[]{:S(2)}, u32[]{:S(2)}) collective-permute-start(bf16[64,1664]{1,0:T(8,128)(2,1)S(1)} %pad_maximum_fusion.refs_0_), channel_id=1, source_target_pairs={{0,8},{8,0},{16,24},{24,16},{1,9},{9,1},{17,25},{25,17},{2,10},{10... | collective-permute-start | bytes 638984 | tf_op jit(solution)/shard_map/ppermute | solution.py:475
  16.1 0.9 %copy-start.2 = (f32[32,4,384]{2,1,0:T(4,128)S(1)}, f32[32,4,384]{2,1,0:T(4,128)}, u32[]{:S(2)}) copy-start(f32[32,4,384]{2,1,0:T(4,128)} %get-tuple-element.29.field) | copy-start | bytes 589828
  17.0 6.4 %copy-start = (s32[3104]{0:T(1024)S(1)}, s32[3104]{0:T(1024)}, u32[]{:S(2)}) copy-start(s32[3104]{0:T(1024)} %constant.8.clone.table) | copy-start | bytes 37252
  25.5 1.5 %collective-permute-start.7 = (bf16[64,1664]{1,0:T(8,128)(2,1)S(1)}, bf16[64,1664]{1,0:T(8,128)(2,1)S(1)}, u32[]{:S(2)}, u32[]{:S(2)}) collective-permute-start(bf16[64,1664]{1,0:T(8,128)(2,1)S(1)} %pad_maximum_fusion.refs_0_), channel_id=1, source_target_pairs={{0,1},{1,0},{2,3},{3,2},{4,5},{5,4},{6,7},{7,6},{8,9},{9,8},{10,11... | collective-permute-start | bytes 638984 | tf_op jit(solution)/shard_map/ppermute | solution.py:475
  25.6 1.8 %collective-permute-start.8 = (bf16[64,1664]{1,0:T(8,128)(2,1)S(1)}, bf16[64,1664]{1,0:T(8,128)(2,1)S(1)}, u32[]{:S(2)}, u32[]{:S(2)}) collective-permute-start(bf16[64,1664]{1,0:T(8,128)(2,1)S(1)} %collective-permute-done.4.refs_1_), channel_id=1, source_target_pairs={{0,1},{1,0},{2,3},{3,2},{4,5},{5,4},{6,7},{7,6},{8,9},{9,8},{10,11... | collective-permute-start | bytes 638984 | tf_op jit(solution)/shard_map/ppermute | solution.py:475
  26.1 1.6 %collective-permute-start.9 = (bf16[64,1664]{1,0:T(8,128)(2,1)S(1)}, bf16[64,1664]{1,0:T(8,128)(2,1)S(1)}, u32[]{:S(2)}, u32[]{:S(2)}) collective-permute-start(bf16[64,1664]{1,0:T(8,128)(2,1)S(1)} %collective-permute-done.5.refs_2_), channel_id=1, source_target_pairs={{0,1},{1,0},{2,3},{3,2},{4,5},{5,4},{6,7},{7,6},{8,9},{9,8},{10,11... | collective-permute-start | bytes 638984 | tf_op jit(solution)/shard_map/ppermute | solution.py:475
  26.2 1.8 %collective-permute-start.10 = (bf16[64,1664]{1,0:T(8,128)(2,1)S(1)}, bf16[64,1664]{1,0:T(8,128)(2,1)S(1)}, u32[]{:S(2)}, u32[]{:S(2)}) collective-permute-start(bf16[64,1664]{1,0:T(8,128)(2,1)S(1)} %collective-permute-done.6.refs_3_), channel_id=1, source_target_pairs={{0,1},{1,0},{2,3},{3,2},{4,5},{5,4},{6,7},{7,6},{8,9},{9,8},{10,11... | collective-permute-start | bytes 638984 | tf_op jit(solution)/shard_map/ppermute | solution.py:475

commit v11 on v9

--- a/solution.py
+++ b/solution.py
@@ -15,7 +15,7 @@
 ITERS = 3
 EPS = 1e-05
 TILE = 128
-GROUP = 4
+GROUP = 8
 SPREAD_GROUP = 8
 EDGE_GROUP = 8
 CHUNK = 512
@@ -529,7 +529,7 @@
         ],
         in_specs=[smem, smem],
         out_specs=[vmem, vmem],
-        compiler_params=wide,
+        compiler_params=params,
         cost_estimate=pl.CostEstimate(flops=3 * 10**9, bytes_accessed=2**21, transcendentals=0),
         name="weights",
     )(spread_table_flat, trig)

time: 48.6 us -> 47.6 us (0.979)
  Pallas kernels: 20.8 us -> 18.2 us
  local copies, waits for them, and re-layouts: 0.04 us -> 1.4 us
  waiting for transfers between devices: 1.76 us -> 2.44 us
    pallas_call x1, Pallas kernels: 4.28 us -> 2.09 us  [local(): pl.pallas_call(functools.partial(weight_kernel, spread_groups, spread_tab...]
    unnamed x16, local copies, waits for them, and re-layouts: 0.04 us -> 1.4 us
    ppermute x10, waiting for transfers between devices: 1.75 us -> 2.44 us  [swap(): return lax.ppermute(x, axis, [(i, i ^ distance) for i in range(size)])]
  transfers between devices with their start and end apart: 11 -> 11, of which waited for: 5 -> 5; matrix products, arithmetic and copies ran while one was open for 0% -> 0% of each run, Pallas kernels for 22% -> 17%
where the time goes in v11:
time: 47.6 us; the launch traced here: 47.3 us
  Pallas kernels  18.2 us (38%)
  starting transfers between devices  12.4 us (26%)
  blocking collectives  12.2 us (26%)
  waiting for transfers between devices  2.44 us (5%)
  local copies, waits for them, and re-layouts  1.4 us (3%)
  between operations  0.76 us (2%)
    all_to_all x1, blocking collectives, local(): parts = lax.all_to_all(parts, ('gz', 'dom'), 0, 0, tiled=True)  12.2 us
    ppermute x10, starting transfers between devices, swap(): return lax.ppermute(x, axis, [(i, i ^ distance) for i in range(size)])  9.03 us
    pallas_call x1, Pallas kernels, local(): pl.pallas_call(functools.partial(extract_kernel, groups, table.shape[1],...  5.89 us
    pallas_call x1, Pallas kernels, local(): pl.pallas_call(functools.partial(spread_kernel, spread_groups, spread_tab...  5.76 us
    ppermute x1, starting transfers between devices, local(): above = lax.ppermute(plane, 'gz', [(i, i - 1) for i in range(1, n_gz)])  3.33 us
    pallas_call x1, Pallas kernels, local(): pl.pallas_call(functools.partial(particle_kernel, width, mine, n_gz, n_do...  2.74 us
    ppermute x10, waiting for transfers between devices, swap(): return lax.ppermute(x, axis, [(i, i ^ distance) for i in range(size)])  2.44 us
    pallas_call x1, Pallas kernels, local(): pl.pallas_call(functools.partial(weight_kernel, spread_groups, spread_tab...  2.09 us
  transfers between devices with their start and end apart: 11, of which 5 were waited for; matrix products, arithmetic and copies ran while one was open for 0% of the time, Pallas kernels for 17%

profile of v11, /device:TPU:4, one launch (start us, length us, event | category | flops | bytes accessed | tf_op | source)
XLA Modules:
  0.0 47.3 jit_solution(17814319559477615308)
XLA Ops:
  0.6 1.7 %pack.1 = (bf16[16,1664]{1,0:T(8,128)(2,1)}, f32[1,4,384]{2,1,0:T(4,128)}, f32[32,4,384]{2,1,0:T(4,128)}) custom-call(bf16[16,4,384]{2,1,0:T(4,128)(2,1)} %observed_hbm.1, s32[1,16]{1,0:T(1,128)} %bitcast.7, s32[1,16]{1,0:T(1,128)} %bitcast.8, f32[192,4,384]{2,1,0:T(4,128)} %volume.1), custom_call_target="tpu_custom_call" | custom-call | tf_op jit(solution)/shard_map/pack/pallas_call | solution.py:496
  2.4 3.7 %collective-permute-start.2 = (bf16[16,1664]{1,0:T(8,128)(2,1)}, bf16[16,1664]{1,0:T(8,128)(2,1)S(1)}, u32[]{:S(2)}, u32[]{:S(2)}) collective-permute-start(bf16[16,1664]{1,0:T(8,128)(2,1)} %get-tuple-element.24), channel_id=1, source_target_pairs={{0,6},{1,7},{2,4},{3,5},{4,2},{5,3},{6,0},{7,1},{8,14},{9,15},{10,... | collective-permute-start | bytes 159752 | tf_op jit(solution)/shard_map/ppermute | solution.py:475
  6.0 0.0 collective-permute-start.1
  6.0 0.8 %collective-permute-start = (bf16[16,1664]{1,0:T(8,128)(2,1)}, bf16[16,1664]{1,0:T(8,128)(2,1)S(1)}, u32[]{:S(2)}, u32[]{:S(2)}) collective-permute-start(bf16[16,1664]{1,0:T(8,128)(2,1)} %get-tuple-element.24), channel_id=1, source_target_pairs={{0,2},{1,3},{2,0},{3,1},{4,6},{5,7},{6,4},{7,5},{8,10},{9,11},{10,... | collective-permute-start | bytes 159752 | tf_op jit(solution)/shard_map/ppermute | solution.py:475
  6.8 3.3 %collective-permute-start.3 = (f32[1,4,384]{2,1,0:T(4,128)}, f32[1,4,384]{2,1,0:T(4,128)S(1)}, u32[]{:S(2)}, u32[]{:S(2)}) collective-permute-start(f32[1,4,384]{2,1,0:T(4,128)} %get-tuple-element.25), channel_id=1, source_target_pairs={{8,0},{16,8},{24,16},{9,1},{17,9},{25,17},{10,2},{18,10},{26,18},{... | collective-permute-start | bytes 18440 | tf_op jit(solution)/shard_map/ppermute | solution.py:516
  10.2 0.0 copy-start
  10.2 0.7 %copy-done = s32[3104]{0:T(1024)S(1)} copy-done((s32[3104]{0:T(1024)S(1)}, s32[3104]{0:T(1024)}, u32[]{:S(2)}) %copy-start) | copy-done | bytes 12440
  10.9 0.0 copy-start.2
  10.9 0.7 %copy-done.2 = f32[128]{0:T(128)S(1)} copy-done((f32[128]{0:T(128)S(1)}, f32[128]{0:T(128)}, u32[]{:S(2)}) %copy-start.2) | copy-done | bytes 536
  11.5 0.0 copy-start.7
  11.5 0.0 copy-start.3
  11.5 0.0 copy-start.4
  11.5 0.0 copy-start.5
  11.6 0.0 copy-start.6
  11.6 2.1 %weights.1 = (bf16[7,2048,128]{2,1,0:T(8,128)(2,1)S(1)}, bf16[32,96,128]{2,1,0:T(8,128)(2,1)S(1)}) custom-call(s32[3104]{0:T(1024)S(1)} %copy-done, f32[128]{0:T(128)S(1)} %copy-done.2), custom_call_target="tpu_custom_call" | custom-call | flops 3000000000 | bytes 2097152 | tf_op jit(solution)/shard_map/weights/pallas_call | solution.py:522
  13.7 0.0 collective-permute-done.2
  13.7 0.0 collective-permute-done.1
  13.7 0.0 collective-permute-done
  13.7 0.0 copy-done.7
  13.7 0.0 collective-permute-done.3.above
  13.7 1.1 %collective-permute-start.6 = (bf16[64,1664]{1,0:T(8,128)(2,1)S(1)}, bf16[64,1664]{1,0:T(8,128)(2,1)S(1)}, u32[]{:S(2)}, u32[]{:S(2)}) collective-permute-start(bf16[64,1664]{1,0:T(8,128)(2,1)S(1)} %pad_maximum_fusion.refs_0_), channel_id=1, source_target_pairs={{0,24},{8,16},{16,8},{24,0},{1,25},{9,17},{17,9},{25,1},{2,26},{10... | collective-permute-start | bytes 638984 | tf_op jit(solution)/shard_map/ppermute | solution.py:475
  14.9 0.4 collective-permute-start.5
  15.3 2.0 %collective-permute-start.4 = (bf16[64,1664]{1,0:T(8,128)(2,1)S(1)}, bf16[64,1664]{1,0:T(8,128)(2,1)S(1)}, u32[]{:S(2)}, u32[]{:S(2)}) collective-permute-start(bf16[64,1664]{1,0:T(8,128)(2,1)S(1)} %pad_maximum_fusion.refs_0_), channel_id=1, source_target_pairs={{0,8},{8,0},{16,24},{24,16},{1,9},{9,1},{17,25},{25,17},{2,10},{10... | collective-permute-start | bytes 638984 | tf_op jit(solution)/shard_map/ppermute | solution.py:475
  17.3 0.0 copy-done.3
  17.3 0.0 copy-done.4
  17.3 0.0 copy-done.5
  17.3 0.0 copy-done.6
  17.3 5.9 %extract.1 = (bf16[128,1536]{1,0:T(8,128)(2,1)S(1)}, bf16[32,384]{1,0:T(8,128)(2,1)S(1)}, f32[32,768]{1,0:T(8,128)S(1)}) custom-call(s32[2080]{0:T(1024)S(1)} %copy-done.6, f32[128]{0:T(128)S(1)} %copy-done.3, f32[32,4,384]{2,1,0:T(4,128)S(1)} %copy-done.4, f32[1,4,384]{2,1,0:T(4,128)S(1)} %collective-permute-done.3.above, f32[32,2,384]{2,1,0:T(2,128)S(1)} %copy-done.5), custom_call_target="tpu_custom_call" | custom-call | flops 6000000000 | bytes 1048576 | tf_op jit(solution)/shard_map/extract/pallas_call | solution.py:541
  23.2 0.0 copy-start.1
  23.2 0.0 collective-permute-done.6.refs_3_
  23.2 1.1 %collective-permute-done.5.refs_2_ = bf16[64,1664]{1,0:T(8,128)(2,1)S(1)} collective-permute-done((bf16[64,1664]{1,0:T(8,128)(2,1)S(1)}, bf16[64,1664]{1,0:T(8,128)(2,1)S(1)}, u32[]{:S(2)}, u32[]{:S(2)}) %collective-permute-start.5) | collective-permute-done | bytes 213024 | tf_op jit(solution)/shard_map/ppermute | solution.py:475
  24.3 0.0 collective-permute-done.4.refs_1_
  24.3 0.0 collective-permute-start.7
  24.3 0.5 %collective-permute-start.8 = (bf16[64,1664]{1,0:T(8,128)(2,1)S(1)}, bf16[64,1664]{1,0:T(8,128)(2,1)S(1)}, u32[]{:S(2)}, u32[]{:S(2)}) collective-permute-start(bf16[64,1664]{1,0:T(8,128)(2,1)S(1)} %collective-permute-done.4.refs_1_), channel_id=1, source_target_pairs={{0,1},{1,0},{2,3},{3,2},{4,5},{5,4},{6,7},{7,6},{8,9},{9,8},{10,11... | collective-permute-start | bytes 638984 | tf_op jit(solution)/shard_map/ppermute | solution.py:475
  24.8 0.0 collective-permute-start.9
  24.8 0.5 %collective-permute-start.10 = (bf16[64,1664]{1,0:T(8,128)(2,1)S(1)}, bf16[64,1664]{1,0:T(8,128)(2,1)S(1)}, u32[]{:S(2)}, u32[]{:S(2)}) collective-permute-start(bf16[64,1664]{1,0:T(8,128)(2,1)S(1)} %collective-permute-done.6.refs_3_), channel_id=1, source_target_pairs={{0,1},{1,0},{2,3},{3,2},{4,5},{5,4},{6,7},{7,6},{8,9},{9,8},{10,11... | collective-permute-start | bytes 638984 | tf_op jit(solution)/shard_map/ppermute | solution.py:475
  25.3 0.4 collective-permute-done.7.refs_4_
  25.8 0.3 collective-permute-done.8.refs_5_
  26.1 0.3 collective-permute-done.9.refs_6_
  26.4 0.3 collective-permute-done.10.refs_7_
  26.7 2.7 %particles.1 = (bf16[512,1536]{1,0:T(8,128)(2,1)S(1)}, f32[256,128]{1,0:T(8,128)S(1)}, f32[1,512]{1,0:T(1,128)S(1)}) custom-call(bf16[64,1664]{1,0:T(8,128)(2,1)S(1)} %pad_maximum_fusion.refs_0_, bf16[64,1664]{1,0:T(8,128)(2,1)S(1)} %collective-permute-done.4.refs_1_, bf16[64,1664]{1,0:T(8,128)(2,1)S(1)} %collective-permute-done.5.refs_2_, ...), custom_call_target="tpu_custom_call" | custom-call | tf_op jit(solution)/shard_map/particles/pallas_call | solution.py:568
  29.4 12.2 %all_to_all.11 = f32[32,8,128]{2,1,0:T(8,128)S(1)} all-to-all(f32[32,8,128]{2,1,0:T(8,128)S(1)} %bitcast.6), channel_id=1, replica_groups=mesh['gz'=4,'dom'=8] {'gz','dom'}, dimensions={0} | all-to-all | bytes 262144 | tf_op jit(solution)/shard_map/all_to_all | solution.py:581
  41.6 0.0 copy-done.1
  41.6 5.8 %spread.1 = (f32[1,16]{1,0:T(1,128)}, f32[24,4,384]{2,1,0:T(4,128)}) custom-call(s32[3104]{0:T(1024)S(1)} %copy-done.1, f32[128]{0:T(128)S(1)} %copy-done.3, bf16[7,2048,128]{2,1,0:T(8,128)(2,1)S(1)} %get-tuple-element.28.right, bf16[32,96,128]{2,1,0:T(8,128)(2,1)S(1)} %get-tuple-element.29.edges, f32[256,128]{1,0:T(8,128)S(1)} %bitcast.5, ...), custom_call_target="tpu_custom_call" | custom-call | tf_op jit(solution)/shard_map/spread/pallas_call | solution.py:584
  (1 shorter events, 0.0 us)
Async XLA Ops:
  2.4 11.3 %collective-permute-start.2 = (bf16[16,1664]{1,0:T(8,128)(2,1)}, bf16[16,1664]{1,0:T(8,128)(2,1)S(1)}, u32[]{:S(2)}, u32[]{:S(2)}) collective-permute-start(bf16[16,1664]{1,0:T(8,128)(2,1)} %get-tuple-element.24), channel_id=1, source_target_pairs={{0,6},{1,7},{2,4},{3,5},{4,2},{5,3},{6,0},{7,1},{8,14},{9,15},{10,... | collective-permute-start | bytes 159752 | tf_op jit(solution)/shard_map/ppermute | solution.py:475
  6.0 7.6 %collective-permute-start.1 = (bf16[16,1664]{1,0:T(8,128)(2,1)}, bf16[16,1664]{1,0:T(8,128)(2,1)S(1)}, u32[]{:S(2)}, u32[]{:S(2)}) collective-permute-start(bf16[16,1664]{1,0:T(8,128)(2,1)} %get-tuple-element.24), channel_id=1, source_target_pairs={{0,4},{1,5},{2,6},{3,7},{4,0},{5,1},{6,2},{7,3},{8,12},{9,13},{10,... | collective-permute-start | bytes 159752 | tf_op jit(solution)/shard_map/ppermute | solution.py:475
  6.0 7.6 %collective-permute-start = (bf16[16,1664]{1,0:T(8,128)(2,1)}, bf16[16,1664]{1,0:T(8,128)(2,1)S(1)}, u32[]{:S(2)}, u32[]{:S(2)}) collective-permute-start(bf16[16,1664]{1,0:T(8,128)(2,1)} %get-tuple-element.24), channel_id=1, source_target_pairs={{0,2},{1,3},{2,0},{3,1},{4,6},{5,7},{6,4},{7,5},{8,10},{9,11},{10,... | collective-permute-start | bytes 159752 | tf_op jit(solution)/shard_map/ppermute | solution.py:475
  6.8 6.9 %collective-permute-start.3 = (f32[1,4,384]{2,1,0:T(4,128)}, f32[1,4,384]{2,1,0:T(4,128)S(1)}, u32[]{:S(2)}, u32[]{:S(2)}) collective-permute-start(f32[1,4,384]{2,1,0:T(4,128)} %get-tuple-element.25), channel_id=1, source_target_pairs={{8,0},{16,8},{24,16},{9,1},{17,9},{25,17},{10,2},{18,10},{26,18},{... | collective-permute-start | bytes 18440 | tf_op jit(solution)/shard_map/ppermute | solution.py:516
  10.2 0.7 %copy-start = (s32[3104]{0:T(1024)S(1)}, s32[3104]{0:T(1024)}, u32[]{:S(2)}) copy-start(s32[3104]{0:T(1024)} %constant.7.clone.table) | copy-start | bytes 37252
  10.9 0.7 %copy-start.2 = (f32[128]{0:T(128)S(1)}, f32[128]{0:T(128)}, u32[]{:S(2)}) copy-start(f32[128]{0:T(128)} %constant.6.clone.trig.trig_hbm) | copy-start | bytes 1540
  11.5 2.2 %copy-start.7 = (bf16[16,1664]{1,0:T(8,128)(2,1)S(1)}, bf16[16,1664]{1,0:T(8,128)(2,1)}, u32[]{:S(2)}) copy-start(bf16[16,1664]{1,0:T(8,128)(2,1)} %get-tuple-element.24) | copy-start | bytes 159748
  11.5 5.8 %copy-start.3 = (f32[128]{0:T(128)S(1)}, f32[128]{0:T(128)}, u32[]{:S(2)}) copy-start(f32[128]{0:T(128)} %constant.6.clone.trig.trig_hbm) | copy-start | bytes 1540
  11.5 5.8 %copy-start.4 = (f32[32,4,384]{2,1,0:T(4,128)S(1)}, f32[32,4,384]{2,1,0:T(4,128)}, u32[]{:S(2)}) copy-start(f32[32,4,384]{2,1,0:T(4,128)} %get-tuple-element.31.field) | copy-start | bytes 589828
  11.5 5.8 %copy-start.5 = (f32[32,2,384]{2,1,0:T(2,128)S(1)}, f32[32,2,384]{2,1,0:T(2,128)}, u32[]{:S(2)}) copy-start(f32[32,2,384]{2,1,0:T(2,128)} %ctf_hbm.1) | copy-start | bytes 294916
  11.6 5.8 %copy-start.6 = (s32[2080]{0:T(1024)S(1)}, s32[2080]{0:T(1024)}, u32[]{:S(2)}) copy-start(s32[2080]{0:T(1024)} %constant.8.clone.table_hbm) | copy-start | bytes 24964
  13.7 9.5 %collective-permute-start.6 = (bf16[64,1664]{1,0:T(8,128)(2,1)S(1)}, bf16[64,1664]{1,0:T(8,128)(2,1)S(1)}, u32[]{:S(2)}, u32[]{:S(2)}) collective-permute-start(bf16[64,1664]{1,0:T(8,128)(2,1)S(1)} %pad_maximum_fusion.refs_0_), channel_id=1, source_target_pairs={{0,24},{8,16},{16,8},{24,0},{1,25},{9,17},{17,9},{25,1},{2,26},{10... | collective-permute-start | bytes 638984 | tf_op jit(solution)/shard_map/ppermute | solution.py:475
  14.9 9.4 %collective-permute-start.5 = (bf16[64,1664]{1,0:T(8,128)(2,1)S(1)}, bf16[64,1664]{1,0:T(8,128)(2,1)S(1)}, u32[]{:S(2)}, u32[]{:S(2)}) collective-permute-start(bf16[64,1664]{1,0:T(8,128)(2,1)S(1)} %pad_maximum_fusion.refs_0_), channel_id=1, source_target_pairs={{0,16},{8,24},{16,0},{24,8},{1,17},{9,25},{17,1},{25,9},{2,18},{10... | collective-permute-start | bytes 638984 | tf_op jit(solution)/shard_map/ppermute | solution.py:475
  15.3 9.0 %collective-permute-start.4 = (bf16[64,1664]{1,0:T(8,128)(2,1)S(1)}, bf16[64,1664]{1,0:T(8,128)(2,1)S(1)}, u32[]{:S(2)}, u32[]{:S(2)}) collective-permute-start(bf16[64,1664]{1,0:T(8,128)(2,1)S(1)} %pad_maximum_fusion.refs_0_), channel_id=1, source_target_pairs={{0,8},{8,0},{16,24},{24,16},{1,9},{9,1},{17,25},{25,17},{2,10},{10... | collective-permute-start | bytes 638984 | tf_op jit(solution)/shard_map/ppermute | solution.py:475
  23.2 18.4 %copy-start.1 = (s32[3104]{0:T(1024)S(1)}, s32[3104]{0:T(1024)}, u32[]{:S(2)}) copy-start(s32[3104]{0:T(1024)} %constant.7.clone.table) | copy-start | bytes 37252
  24.3 1.5 %collective-permute-start.7 = (bf16[64,1664]{1,0:T(8,128)(2,1)S(1)}, bf16[64,1664]{1,0:T(8,128)(2,1)S(1)}, u32[]{:S(2)}, u32[]{:S(2)}) collective-permute-start(bf16[64,1664]{1,0:T(8,128)(2,1)S(1)} %pad_maximum_fusion.refs_0_), channel_id=1, source_target_pairs={{0,1},{1,0},{2,3},{3,2},{4,5},{5,4},{6,7},{7,6},{8,9},{9,8},{10,11... | collective-permute-start | bytes 638984 | tf_op jit(solution)/shard_map/ppermute | solution.py:475
  24.3 1.8 %collective-permute-start.8 = (bf16[64,1664]{1,0:T(8,128)(2,1)S(1)}, bf16[64,1664]{1,0:T(8,128)(2,1)S(1)}, u32[]{:S(2)}, u32[]{:S(2)}) collective-permute-start(bf16[64,1664]{1,0:T(8,128)(2,1)S(1)} %collective-permute-done.4.refs_1_), channel_id=1, source_target_pairs={{0,1},{1,0},{2,3},{3,2},{4,5},{5,4},{6,7},{7,6},{8,9},{9,8},{10,11... | collective-permute-start | bytes 638984 | tf_op jit(solution)/shard_map/ppermute | solution.py:475
  24.8 1.6 %collective-permute-start.9 = (bf16[64,1664]{1,0:T(8,128)(2,1)S(1)}, bf16[64,1664]{1,0:T(8,128)(2,1)S(1)}, u32[]{:S(2)}, u32[]{:S(2)}) collective-permute-start(bf16[64,1664]{1,0:T(8,128)(2,1)S(1)} %collective-permute-done.5.refs_2_), channel_id=1, source_target_pairs={{0,1},{1,0},{2,3},{3,2},{4,5},{5,4},{6,7},{7,6},{8,9},{9,8},{10,11... | collective-permute-start | bytes 638984 | tf_op jit(solution)/shard_map/ppermute | solution.py:475
  24.8 1.9 %collective-permute-start.10 = (bf16[64,1664]{1,0:T(8,128)(2,1)S(1)}, bf16[64,1664]{1,0:T(8,128)(2,1)S(1)}, u32[]{:S(2)}, u32[]{:S(2)}) collective-permute-start(bf16[64,1664]{1,0:T(8,128)(2,1)S(1)} %collective-permute-done.6.refs_3_), channel_id=1, source_target_pairs={{0,1},{1,0},{2,3},{3,2},{4,5},{5,4},{6,7},{7,6},{8,9},{9,8},{10,11... | collective-permute-start | bytes 638984 | tf_op jit(solution)/shard_map/ppermute | solution.py:475

commit v12 on v11

--- a/solution.py
+++ b/solution.py
@@ -286,9 +286,12 @@
     pairs[...] = jnp.concatenate(split3(product), 1)
 
 
-def particle_kernel(width, mine, n_gz, n_dom, *refs):
-    blocks = refs[: 2 * n_gz]
-    ctf, slope, pairs, weighted, parts, bins_row = refs[2 * n_gz :]
+def particle_kernel(width, mine, n_gz, n_dom, final, *refs):
+    blocks = refs[:n_gz]
+    if final:
+        ctf, slope, pairs, before, weighted, bins_row, parts = refs[n_gz:]
+    else:
+        ctf, slope, pairs, weighted, bins_row, parts = refs[n_gz:]
     size = blocks[0].shape[0]
     joined = max(1, CHUNK // size)
     both = slope.shape[0]
@@ -302,7 +305,7 @@
     slopes = slope[...]
     scalars = [[], []]
 
-    for i in range(0, 2 * n_gz, joined):
+    for i in range(0, n_gz, joined):
         packed = jnp.concatenate([ref[...] for ref in blocks[i : i + joined]], 0)
         count = packed.shape[0]
         span = slice(i * size, i * size + count)
@@ -333,7 +336,13 @@
         pick = jnp.where(lanes_of((8, TILE), 1) == 1.0, 1.0, 0.0).astype(bf16)
         bins_row[:, span] = lax.dot_general(pick, ids, NT, preferred_element_type=f32)[0:1]
 
-    scalars = jnp.concatenate(scalars[0] + scalars[1], 0)
+    if not final:
+        parts[...] = jnp.concatenate(scalars[0] + scalars[1], 0)
+        return
+    half = before.shape[0] // 2
+    scalars = jnp.concatenate(
+        [before[:half]] + scalars[0] + [before[half:]] + scalars[1], 0
+    )
     scalars = reorder(scalars, position(n_gz, n_dom), mine)
     rows = scalars.shape[0]
     for n in range(parts.shape[0] // rows):
@@ -371,13 +380,15 @@
 
 def spread_kernel(
     groups, length, planes, samples, edge_samples, mine, n_gz, n_dom,
-    table, trig, right, edges, parts, bins_row, weighted, pose, out, sums, total, poses,
+    table, trig, right, edges, parts, bins_own, weighted_own, bins_row, weighted,
+    pose, out, sums, total, poses,
 ):
     tiles, bins = sums.shape[0] // 2, sums.shape[1]
     ut_count = samples // TILE
     depth = total.shape[1] // 4
-    count = bins_row.shape[1]
-    chunk = min(CHUNK, count)
+    half = bins_row.shape[1]
+    count = 2 * half
+    chunk = min(CHUNK, half)
     device = lax.axis_index("gz") * n_dom + lax.axis_index("dom")
     row = device * length
     z0 = (device * planes).astype(f32)
@@ -399,14 +410,15 @@
 
     bin_sums = jnp.zeros((3 * bins, tiles * TILE), f32)
     for i in range(count // chunk):
-        span = slice(i * chunk, (i + 1) * chunk)
-        belongs = lanes_of((bins, chunk), 0) == bins_row[:, span]
-        scaled = jnp.where(belongs, shift[:, span], 0.0)
+        ids, values = (bins_own, weighted_own) if i * chunk < half else (bins_row, weighted)
+        span = slice(i * chunk % half, i * chunk % half + chunk)
+        belongs = lanes_of((bins, chunk), 0) == ids[:, span]
+        scaled = jnp.where(belongs, shift[:, i * chunk : (i + 1) * chunk], 0.0)
         hi = scaled.astype(bf16)
         lo = (scaled - hi.astype(f32)).astype(bf16)
         onehot = jnp.where(belongs, 1.0, 0.0).astype(bf16)
         bin_sums = bin_sums + jnp.dot(
-            jnp.concatenate([onehot, hi, lo], 0), weighted[span, :], preferred_element_type=f32
+            jnp.concatenate([onehot, hi, lo], 0), values[span, :], preferred_element_type=f32
         )
     plain = bin_sums[:bins]
     slope_sum = bin_sums[bins : 2 * bins] + bin_sums[2 * bins :]
@@ -564,19 +576,31 @@
     )(jnp.asarray(table.reshape(-1)), trig, field, above, ctf_table)
 
     planes_of, slope = lax.optimization_barrier((planes_of, slope))
-    gathered = planes_of + [swap(part, "dom", n_dom, 1) for part in planes_of]
-    weighted, parts, bins_row = pl.pallas_call(
-        functools.partial(particle_kernel, width, mine, n_gz, n_dom),
-        out_shape=[
-            jax.ShapeDtypeStruct((count, width), bf16),
-            jax.ShapeDtypeStruct((devices * 2 * count // TILE, TILE), f32),
-            jax.ShapeDtypeStruct((1, count), f32),
-        ],
-        in_specs=[vmem] * (len(gathered) + 3),
-        out_specs=[vmem] * 3,
-        compiler_params=params,
-        name="particles",
-    )(*gathered, flat_ctf, slope, pairs)
+    others = [swap(part, "dom", n_dom, 1) for part in planes_of]
+    per_device = 2 * count // TILE
+
+    def particles(blocks, before):
+        final = len(before) > 0
+        return pl.pallas_call(
+            functools.partial(particle_kernel, width, mine, n_gz, n_dom, final),
+            out_shape=[
+                jax.ShapeDtypeStruct((count // 2, width), bf16),
+                jax.ShapeDtypeStruct((1, count // 2), f32),
+                jax.ShapeDtypeStruct(
+                    (devices * per_device if final else per_device // 2, TILE), f32
+                ),
+            ],
+            in_specs=[vmem] * (len(blocks) + 3 + len(before)),
+            out_specs=[vmem] * 3,
+            compiler_params=params,
+            cost_estimate=pl.CostEstimate(
+                flops=2 * 10**9, bytes_accessed=2**20, transcendentals=0
+            ),
+            name="particles",
+        )(*blocks, flat_ctf, slope, pairs, *before)
+
+    weighted_own, bins_own, before = particles(planes_of, [])
+    weighted, bins_row, parts = particles(others, [before])
 
     parts = lax.all_to_all(parts, ("gz", "dom"), 0, 0, tiled=True)
 
@@ -589,7 +613,7 @@
             jax.ShapeDtypeStruct((1, mine), f32),
             jax.ShapeDtypeStruct((planes, rows, columns), f32),
         ],
-        in_specs=[smem, smem] + [vmem] * 5,
+        in_specs=[smem, smem] + [vmem] * 7,
         out_specs=[vmem, vmem],
         scratch_shapes=[
             pltpu.VMEM((2 * width // TILE, bins, TILE), f32),
@@ -598,7 +622,9 @@
         ],
         compiler_params=params,
         name="spread",
-    )(spread_table_flat, trig, right, edges, parts, bins_row, weighted)
+    )(
+        spread_table_flat, trig, right, edges, parts, bins_own, weighted_own, bins_row, weighted
+    )
     pose = pose.reshape(mine)
     return pose, spread
 

time: 47.6 us -> 46.8 us (0.983)
  waiting for transfers between devices: 2.44 us -> 1.13 us
  Pallas kernels: 18.2 us -> 18.7 us
    ppermute x10, waiting for transfers between devices: 2.44 us -> 1.13 us  [swap(): return lax.ppermute(x, axis, [(i, i ^ distance) for i in range(size)])]
    pallas_call x1 -> x2, Pallas kernels: 2.74 us -> 3.2 us  [particles(): pl.pallas_call(functools.partial(particle_kernel, width, mine, n_gz, n_do...]
  transfers between devices with their start and end apart: 11 -> 11, of which waited for: 5 -> 1; matrix products, arithmetic and copies ran while one was open for 0% -> 0% of each run, Pallas kernels for 17% -> 20%
where the time goes in v12:
time: 46.8 us; the launch traced here: 46.5 us
  Pallas kernels  18.7 us (40%)
  starting transfers between devices  12.4 us (26%)
  blocking collectives  12.2 us (26%)
  local copies, waits for them, and re-layouts  1.4 us (3%)
  waiting for transfers between devices  1.13 us (2%)
  between operations  0.8 us (2%)
    all_to_all x1, blocking collectives, local(): parts = lax.all_to_all(parts, ('gz', 'dom'), 0, 0, tiled=True)  12.2 us
    ppermute x10, starting transfers between devices, swap(): return lax.ppermute(x, axis, [(i, i ^ distance) for i in range(size)])  9.03 us
    pallas_call x1, Pallas kernels, local(): pl.pallas_call(functools.partial(extract_kernel, groups, table.shape[1],...  5.89 us
    pallas_call x1, Pallas kernels, local(): pl.pallas_call(functools.partial(spread_kernel, spread_groups, spread_tab...  5.73 us
    ppermute x1, starting transfers between devices, local(): above = lax.ppermute(plane, 'gz', [(i, i - 1) for i in range(1, n_gz)])  3.33 us
    pallas_call x2, Pallas kernels, particles(): pl.pallas_call(functools.partial(particle_kernel, width, mine, n_gz, n_do...  3.2 us
    pallas_call x1, Pallas kernels, local(): pl.pallas_call(functools.partial(weight_kernel, spread_groups, spread_tab...  2.09 us
    pallas_call x1, Pallas kernels, local(): pl.pallas_call(functools.partial(pack_kernel, planes), out_shape=[jax.Sha...  1.75 us
  transfers between devices with their start and end apart: 11, of which 1 were waited for; matrix products, arithmetic and copies ran while one was open for 0% of the time, Pallas kernels for 20%

profile of v12, /device:TPU:4, one launch (start us, length us, event | category | flops | bytes accessed | tf_op | source)
XLA Modules:
  0.0 46.5 jit_solution(450672857923509390)
XLA Ops:
  0.6 1.7 %pack.1 = (bf16[16,1664]{1,0:T(8,128)(2,1)}, f32[1,4,384]{2,1,0:T(4,128)}, f32[32,4,384]{2,1,0:T(4,128)}) custom-call(bf16[16,4,384]{2,1,0:T(4,128)(2,1)} %observed_hbm.1, s32[1,16]{1,0:T(1,128)} %bitcast.7, s32[1,16]{1,0:T(1,128)} %bitcast.8, f32[192,4,384]{2,1,0:T(4,128)} %volume.1), custom_call_target="tpu_custom_call" | custom-call | tf_op jit(solution)/shard_map/pack/pallas_call | solution.py:508
  2.4 3.7 %collective-permute-start.2 = (bf16[16,1664]{1,0:T(8,128)(2,1)}, bf16[16,1664]{1,0:T(8,128)(2,1)S(1)}, u32[]{:S(2)}, u32[]{:S(2)}) collective-permute-start(bf16[16,1664]{1,0:T(8,128)(2,1)} %get-tuple-element.27), channel_id=1, source_target_pairs={{0,6},{1,7},{2,4},{3,5},{4,2},{5,3},{6,0},{7,1},{8,14},{9,15},{10,... | collective-permute-start | bytes 159752 | tf_op jit(solution)/shard_map/ppermute | solution.py:487
  6.0 0.0 collective-permute-start.1
  6.1 0.8 %collective-permute-start = (bf16[16,1664]{1,0:T(8,128)(2,1)}, bf16[16,1664]{1,0:T(8,128)(2,1)S(1)}, u32[]{:S(2)}, u32[]{:S(2)}) collective-permute-start(bf16[16,1664]{1,0:T(8,128)(2,1)} %get-tuple-element.27), channel_id=1, source_target_pairs={{0,2},{1,3},{2,0},{3,1},{4,6},{5,7},{6,4},{7,5},{8,10},{9,11},{10,... | collective-permute-start | bytes 159752 | tf_op jit(solution)/shard_map/ppermute | solution.py:487
  6.8 3.3 %collective-permute-start.3 = (f32[1,4,384]{2,1,0:T(4,128)}, f32[1,4,384]{2,1,0:T(4,128)S(1)}, u32[]{:S(2)}, u32[]{:S(2)}) collective-permute-start(f32[1,4,384]{2,1,0:T(4,128)} %get-tuple-element.28), channel_id=1, source_target_pairs={{8,0},{16,8},{24,16},{9,1},{17,9},{25,17},{10,2},{18,10},{26,18},{... | collective-permute-start | bytes 18440 | tf_op jit(solution)/shard_map/ppermute | solution.py:528
  10.2 0.0 copy-start
  10.2 0.7 %copy-done = s32[3104]{0:T(1024)S(1)} copy-done((s32[3104]{0:T(1024)S(1)}, s32[3104]{0:T(1024)}, u32[]{:S(2)}) %copy-start) | copy-done | bytes 12440
  10.9 0.0 copy-start.2
  10.9 0.7 %copy-done.2 = f32[128]{0:T(128)S(1)} copy-done((f32[128]{0:T(128)S(1)}, f32[128]{0:T(128)}, u32[]{:S(2)}) %copy-start.2) | copy-done | bytes 536
  11.6 0.0 copy-start.7
  11.6 0.0 copy-start.3
  11.6 0.0 copy-start.4
  11.6 0.0 copy-start.5
  11.6 0.0 copy-start.6
  11.6 2.1 %weights.1 = (bf16[7,2048,128]{2,1,0:T(8,128)(2,1)S(1)}, bf16[32,96,128]{2,1,0:T(8,128)(2,1)S(1)}) custom-call(s32[3104]{0:T(1024)S(1)} %copy-done, f32[128]{0:T(128)S(1)} %copy-done.2), custom_call_target="tpu_custom_call" | custom-call | flops 3000000000 | bytes 2097152 | tf_op jit(solution)/shard_map/weights/pallas_call | solution.py:534
  13.7 0.0 collective-permute-done.2
  13.7 0.0 collective-permute-done.1
  13.7 0.0 collective-permute-done
  13.7 0.0 copy-done.7
  13.7 0.0 collective-permute-done.3.above
  13.8 1.1 %collective-permute-start.6 = (bf16[64,1664]{1,0:T(8,128)(2,1)S(1)}, bf16[64,1664]{1,0:T(8,128)(2,1)S(1)}, u32[]{:S(2)}, u32[]{:S(2)}) collective-permute-start(bf16[64,1664]{1,0:T(8,128)(2,1)S(1)} %pad_maximum_fusion.refs_0_), channel_id=1, source_target_pairs={{0,24},{8,16},{16,8},{24,0},{1,25},{9,17},{17,9},{25,1},{2,26},{10... | collective-permute-start | bytes 638984 | tf_op jit(solution)/shard_map/ppermute | solution.py:487
  14.9 0.4 collective-permute-start.5
  15.3 2.0 %collective-permute-start.4 = (bf16[64,1664]{1,0:T(8,128)(2,1)S(1)}, bf16[64,1664]{1,0:T(8,128)(2,1)S(1)}, u32[]{:S(2)}, u32[]{:S(2)}) collective-permute-start(bf16[64,1664]{1,0:T(8,128)(2,1)S(1)} %pad_maximum_fusion.refs_0_), channel_id=1, source_target_pairs={{0,8},{8,0},{16,24},{24,16},{1,9},{9,1},{17,25},{25,17},{2,10},{10... | collective-permute-start | bytes 638984 | tf_op jit(solution)/shard_map/ppermute | solution.py:487
  17.3 0.0 copy-done.3
  17.3 0.0 copy-done.4
  17.3 0.0 copy-done.5
  17.3 0.0 copy-done.6
  17.3 5.9 %extract.1 = (bf16[128,1536]{1,0:T(8,128)(2,1)S(1)}, bf16[32,384]{1,0:T(8,128)(2,1)S(1)}, f32[32,768]{1,0:T(8,128)S(1)}) custom-call(s32[2080]{0:T(1024)S(1)} %copy-done.6, f32[128]{0:T(128)S(1)} %copy-done.3, f32[32,4,384]{2,1,0:T(4,128)S(1)} %copy-done.4, f32[1,4,384]{2,1,0:T(4,128)S(1)} %collective-permute-done.3.above, f32[32,2,384]{2,1,0:T(2,128)S(1)} %copy-done.5), custom_call_target="tpu_custom_call" | custom-call | flops 6000000000 | bytes 1048576 | tf_op jit(solution)/shard_map/extract/pallas_call | solution.py:553
  23.2 0.0 collective-permute-done.6.refs_3_
  23.2 1.1 %collective-permute-done.5.refs_2_ = bf16[64,1664]{1,0:T(8,128)(2,1)S(1)} collective-permute-done((bf16[64,1664]{1,0:T(8,128)(2,1)S(1)}, bf16[64,1664]{1,0:T(8,128)(2,1)S(1)}, u32[]{:S(2)}, u32[]{:S(2)}) %collective-permute-start.5) | collective-permute-done | bytes 213024 | tf_op jit(solution)/shard_map/ppermute | solution.py:487
  24.3 0.0 collective-permute-done.4.refs_1_
  24.3 0.0 collective-permute-start.7
  24.3 0.5 %collective-permute-start.8 = (bf16[64,1664]{1,0:T(8,128)(2,1)S(1)}, bf16[64,1664]{1,0:T(8,128)(2,1)S(1)}, u32[]{:S(2)}, u32[]{:S(2)}) collective-permute-start(bf16[64,1664]{1,0:T(8,128)(2,1)S(1)} %collective-permute-done.4.refs_1_), channel_id=1, source_target_pairs={{0,1},{1,0},{2,3},{3,2},{4,5},{5,4},{6,7},{7,6},{8,9},{9,8},{10,11... | collective-permute-start | bytes 638984 | tf_op jit(solution)/shard_map/ppermute | solution.py:487
  24.8 0.0 collective-permute-start.9
  24.8 0.5 %collective-permute-start.10 = (bf16[64,1664]{1,0:T(8,128)(2,1)S(1)}, bf16[64,1664]{1,0:T(8,128)(2,1)S(1)}, u32[]{:S(2)}, u32[]{:S(2)}) collective-permute-start(bf16[64,1664]{1,0:T(8,128)(2,1)S(1)} %collective-permute-done.6.refs_3_), channel_id=1, source_target_pairs={{0,1},{1,0},{2,3},{3,2},{4,5},{5,4},{6,7},{7,6},{8,9},{9,8},{10,11... | collective-permute-start | bytes 638984 | tf_op jit(solution)/shard_map/ppermute | solution.py:487
  25.3 1.5 %particles.2 = (bf16[256,1536]{1,0:T(8,128)(2,1)S(1)}, f32[1,256]{1,0:T(1,128)S(1)}, f32[4,128]{1,0:T(4,128)S(1)}) custom-call(bf16[64,1664]{1,0:T(8,128)(2,1)S(1)} %pad_maximum_fusion.refs_0_, bf16[64,1664]{1,0:T(8,128)(2,1)S(1)} %collective-permute-done.4.refs_1_, bf16[64,1664]{1,0:T(8,128)(2,1)S(1)} %collective-permute-done.5.refs_2_, ...), custom_call_target="tpu_custom_call" | custom-call | flops 2000000000 | bytes 1048576 | tf_op jit(solution)/shard_map/particles/pallas_call | solution.py:584
  26.8 0.0 collective-permute-done.7.refs_0_
  26.8 0.0 collective-permute-done.8.refs_1_
  26.9 0.0 collective-permute-done.9.refs_2_
  26.9 0.0 collective-permute-done.10.refs_3_
  26.9 0.0 copy-start.1
  26.9 1.7 %particles.3 = (bf16[256,1536]{1,0:T(8,128)(2,1)S(1)}, f32[1,256]{1,0:T(1,128)S(1)}, f32[256,128]{1,0:T(8,128)S(1)}) custom-call(bf16[64,1664]{1,0:T(8,128)(2,1)S(1)} %collective-permute-done.7.refs_0_, bf16[64,1664]{1,0:T(8,128)(2,1)S(1)} %collective-permute-done.8.refs_1_, bf16[64,1664]{1,0:T(8,128)(2,1)S(1)} %collective-permute-done.9.refs_2_, ...), custom_call_target="tpu_custom_call" | custom-call | flops 2000000000 | bytes 1048576 | tf_op jit(solution)/shard_map/particles/pallas_call | solution.py:584
  28.6 12.2 %all_to_all.11 = f32[32,8,128]{2,1,0:T(8,128)S(1)} all-to-all(f32[32,8,128]{2,1,0:T(8,128)S(1)} %bitcast.6), channel_id=1, replica_groups=mesh['gz'=4,'dom'=8] {'gz','dom'}, dimensions={0} | all-to-all | bytes 262144 | tf_op jit(solution)/shard_map/all_to_all | solution.py:605
  40.8 0.0 copy-done.1
  40.8 5.7 %spread.1 = (f32[1,16]{1,0:T(1,128)}, f32[24,4,384]{2,1,0:T(4,128)}) custom-call(s32[3104]{0:T(1024)S(1)} %copy-done.1, f32[128]{0:T(128)S(1)} %copy-done.3, bf16[7,2048,128]{2,1,0:T(8,128)(2,1)S(1)} %get-tuple-element.31.right, bf16[32,96,128]{2,1,0:T(8,128)(2,1)S(1)} %get-tuple-element.32.edges, f32[256,128]{1,0:T(8,128)S(1)} %bitcast.5, ...), custom_call_target="tpu_custom_call" | custom-call | tf_op jit(solution)/shard_map/spread/pallas_call | solution.py:608
  (1 shorter events, 0.0 us)
Async XLA Ops:
  2.4 11.3 %collective-permute-start.2 = (bf16[16,1664]{1,0:T(8,128)(2,1)}, bf16[16,1664]{1,0:T(8,128)(2,1)S(1)}, u32[]{:S(2)}, u32[]{:S(2)}) collective-permute-start(bf16[16,1664]{1,0:T(8,128)(2,1)} %get-tuple-element.27), channel_id=1, source_target_pairs={{0,6},{1,7},{2,4},{3,5},{4,2},{5,3},{6,0},{7,1},{8,14},{9,15},{10,... | collective-permute-start | bytes 159752 | tf_op jit(solution)/shard_map/ppermute | solution.py:487
  6.0 7.6 %collective-permute-start.1 = (bf16[16,1664]{1,0:T(8,128)(2,1)}, bf16[16,1664]{1,0:T(8,128)(2,1)S(1)}, u32[]{:S(2)}, u32[]{:S(2)}) collective-permute-start(bf16[16,1664]{1,0:T(8,128)(2,1)} %get-tuple-element.27), channel_id=1, source_target_pairs={{0,4},{1,5},{2,6},{3,7},{4,0},{5,1},{6,2},{7,3},{8,12},{9,13},{10,... | collective-permute-start | bytes 159752 | tf_op jit(solution)/shard_map/ppermute | solution.py:487
  6.1 7.6 %collective-permute-start = (bf16[16,1664]{1,0:T(8,128)(2,1)}, bf16[16,1664]{1,0:T(8,128)(2,1)S(1)}, u32[]{:S(2)}, u32[]{:S(2)}) collective-permute-start(bf16[16,1664]{1,0:T(8,128)(2,1)} %get-tuple-element.27), channel_id=1, source_target_pairs={{0,2},{1,3},{2,0},{3,1},{4,6},{5,7},{6,4},{7,5},{8,10},{9,11},{10,... | collective-permute-start | bytes 159752 | tf_op jit(solution)/shard_map/ppermute | solution.py:487
  6.8 6.9 %collective-permute-start.3 = (f32[1,4,384]{2,1,0:T(4,128)}, f32[1,4,384]{2,1,0:T(4,128)S(1)}, u32[]{:S(2)}, u32[]{:S(2)}) collective-permute-start(f32[1,4,384]{2,1,0:T(4,128)} %get-tuple-element.28), channel_id=1, source_target_pairs={{8,0},{16,8},{24,16},{9,1},{17,9},{25,17},{10,2},{18,10},{26,18},{... | collective-permute-start | bytes 18440 | tf_op jit(solution)/shard_map/ppermute | solution.py:528
  10.2 0.7 %copy-start = (s32[3104]{0:T(1024)S(1)}, s32[3104]{0:T(1024)}, u32[]{:S(2)}) copy-start(s32[3104]{0:T(1024)} %constant.7.clone.table) | copy-start | bytes 37252
  10.9 0.7 %copy-start.2 = (f32[128]{0:T(128)S(1)}, f32[128]{0:T(128)}, u32[]{:S(2)}) copy-start(f32[128]{0:T(128)} %constant.6.clone.trig.trig_hbm) | copy-start | bytes 1540
  11.6 2.2 %copy-start.7 = (bf16[16,1664]{1,0:T(8,128)(2,1)S(1)}, bf16[16,1664]{1,0:T(8,128)(2,1)}, u32[]{:S(2)}) copy-start(bf16[16,1664]{1,0:T(8,128)(2,1)} %get-tuple-element.27) | copy-start | bytes 159748
  11.6 5.8 %copy-start.3 = (f32[128]{0:T(128)S(1)}, f32[128]{0:T(128)}, u32[]{:S(2)}) copy-start(f32[128]{0:T(128)} %constant.6.clone.trig.trig_hbm) | copy-start | bytes 1540
  11.6 5.8 %copy-start.4 = (f32[32,4,384]{2,1,0:T(4,128)S(1)}, f32[32,4,384]{2,1,0:T(4,128)}, u32[]{:S(2)}) copy-start(f32[32,4,384]{2,1,0:T(4,128)} %get-tuple-element.34.field) | copy-start | bytes 589828
  11.6 5.8 %copy-start.5 = (f32[32,2,384]{2,1,0:T(2,128)S(1)}, f32[32,2,384]{2,1,0:T(2,128)}, u32[]{:S(2)}) copy-start(f32[32,2,384]{2,1,0:T(2,128)} %ctf_hbm.1) | copy-start | bytes 294916
  11.6 5.8 %copy-start.6 = (s32[2080]{0:T(1024)S(1)}, s32[2080]{0:T(1024)}, u32[]{:S(2)}) copy-start(s32[2080]{0:T(1024)} %constant.8.clone.table_hbm) | copy-start | bytes 24964
  13.8 9.5 %collective-permute-start.6 = (bf16[64,1664]{1,0:T(8,128)(2,1)S(1)}, bf16[64,1664]{1,0:T(8,128)(2,1)S(1)}, u32[]{:S(2)}, u32[]{:S(2)}) collective-permute-start(bf16[64,1664]{1,0:T(8,128)(2,1)S(1)} %pad_maximum_fusion.refs_0_), channel_id=1, source_target_pairs={{0,24},{8,16},{16,8},{24,0},{1,25},{9,17},{17,9},{25,1},{2,26},{10... | collective-permute-start | bytes 638984 | tf_op jit(solution)/shard_map/ppermute | solution.py:487
  14.9 9.4 %collective-permute-start.5 = (bf16[64,1664]{1,0:T(8,128)(2,1)S(1)}, bf16[64,1664]{1,0:T(8,128)(2,1)S(1)}, u32[]{:S(2)}, u32[]{:S(2)}) collective-permute-start(bf16[64,1664]{1,0:T(8,128)(2,1)S(1)} %pad_maximum_fusion.refs_0_), channel_id=1, source_target_pairs={{0,16},{8,24},{16,0},{24,8},{1,17},{9,25},{17,1},{25,9},{2,18},{10... | collective-permute-start | bytes 638984 | tf_op jit(solution)/shard_map/ppermute | solution.py:487
  15.3 9.0 %collective-permute-start.4 = (bf16[64,1664]{1,0:T(8,128)(2,1)S(1)}, bf16[64,1664]{1,0:T(8,128)(2,1)S(1)}, u32[]{:S(2)}, u32[]{:S(2)}) collective-permute-start(bf16[64,1664]{1,0:T(8,128)(2,1)S(1)} %pad_maximum_fusion.refs_0_), channel_id=1, source_target_pairs={{0,8},{8,0},{16,24},{24,16},{1,9},{9,1},{17,25},{25,17},{2,10},{10... | collective-permute-start | bytes 638984 | tf_op jit(solution)/shard_map/ppermute | solution.py:487
  24.3 2.5 %collective-permute-start.7 = (bf16[64,1664]{1,0:T(8,128)(2,1)S(1)}, bf16[64,1664]{1,0:T(8,128)(2,1)S(1)}, u32[]{:S(2)}, u32[]{:S(2)}) collective-permute-start(bf16[64,1664]{1,0:T(8,128)(2,1)S(1)} %pad_maximum_fusion.refs_0_), channel_id=1, source_target_pairs={{0,1},{1,0},{2,3},{3,2},{4,5},{5,4},{6,7},{7,6},{8,9},{9,8},{10,11... | collective-permute-start | bytes 638984 | tf_op jit(solution)/shard_map/ppermute | solution.py:487
  24.3 2.5 %collective-permute-start.8 = (bf16[64,1664]{1,0:T(8,128)(2,1)S(1)}, bf16[64,1664]{1,0:T(8,128)(2,1)S(1)}, u32[]{:S(2)}, u32[]{:S(2)}) collective-permute-start(bf16[64,1664]{1,0:T(8,128)(2,1)S(1)} %collective-permute-done.4.refs_1_), channel_id=1, source_target_pairs={{0,1},{1,0},{2,3},{3,2},{4,5},{5,4},{6,7},{7,6},{8,9},{9,8},{10,11... | collective-permute-start | bytes 638984 | tf_op jit(solution)/shard_map/ppermute | solution.py:487
  24.8 2.0 %collective-permute-start.9 = (bf16[64,1664]{1,0:T(8,128)(2,1)S(1)}, bf16[64,1664]{1,0:T(8,128)(2,1)S(1)}, u32[]{:S(2)}, u32[]{:S(2)}) collective-permute-start(bf16[64,1664]{1,0:T(8,128)(2,1)S(1)} %collective-permute-done.5.refs_2_), channel_id=1, source_target_pairs={{0,1},{1,0},{2,3},{3,2},{4,5},{5,4},{6,7},{7,6},{8,9},{9,8},{10,11... | collective-permute-start | bytes 638984 | tf_op jit(solution)/shard_map/ppermute | solution.py:487
  24.8 2.0 %collective-permute-start.10 = (bf16[64,1664]{1,0:T(8,128)(2,1)S(1)}, bf16[64,1664]{1,0:T(8,128)(2,1)S(1)}, u32[]{:S(2)}, u32[]{:S(2)}) collective-permute-start(bf16[64,1664]{1,0:T(8,128)(2,1)S(1)} %collective-permute-done.6.refs_3_), channel_id=1, source_target_pairs={{0,1},{1,0},{2,3},{3,2},{4,5},{5,4},{6,7},{7,6},{8,9},{9,8},{10,11... | collective-permute-start | bytes 638984 | tf_op jit(solution)/shard_map/ppermute | solution.py:487
  26.9 13.9 %copy-start.1 = (s32[3104]{0:T(1024)S(1)}, s32[3104]{0:T(1024)}, u32[]{:S(2)}) copy-start(s32[3104]{0:T(1024)} %constant.7.clone.table) | copy-start | bytes 37252

commit v13 on v12

--- a/solution.py
+++ b/solution.py
@@ -575,8 +575,9 @@
         name="extract",
     )(jnp.asarray(table.reshape(-1)), trig, field, above, ctf_table)
 
-    planes_of, slope = lax.optimization_barrier((planes_of, slope))
-    others = [swap(part, "dom", n_dom, 1) for part in planes_of]
+    early = swap(column, "dom", n_dom, 1)
+    planes_of, slope, early = lax.optimization_barrier((planes_of, slope, early))
+    others = [early] + [swap(part, "dom", n_dom, 1) for part in planes_of[1:]]
     per_device = 2 * count // TILE
 
     def particles(blocks, before):

time: 46.8 us -> 48.7 us (1.041)
  waiting for transfers between devices: 1.13 us -> 3.61 us
  starting transfers between devices: 12.4 us -> 11.9 us
    ppermute x10, waiting for transfers between devices: 1.13 us -> 3.61 us  [swap(): return lax.ppermute(x, axis, [(i, i ^ distance) for i in range(size)])]
where the time goes in v13:
time: 48.7 us; the launch traced here: 48.4 us
  Pallas kernels  18.6 us (38%)
  blocking collectives  12.1 us (25%)
  starting transfers between devices  11.9 us (24%)
  waiting for transfers between devices  3.61 us (7%)
  local copies, waits for them, and re-layouts  1.39 us (3%)
  between operations  0.79 us (2%)
    all_to_all x1, blocking collectives, local(): parts = lax.all_to_all(parts, ('gz', 'dom'), 0, 0, tiled=True)  12.1 us
    ppermute x10, starting transfers between devices, swap(): return lax.ppermute(x, axis, [(i, i ^ distance) for i in range(size)])  8.59 us
    pallas_call x1, Pallas kernels, local(): pl.pallas_call(functools.partial(extract_kernel, groups, table.shape[1],...  5.88 us
    pallas_call x1, Pallas kernels, local(): pl.pallas_call(functools.partial(spread_kernel, spread_groups, spread_tab...  5.73 us
    ppermute x10, waiting for transfers between devices, swap(): return lax.ppermute(x, axis, [(i, i ^ distance) for i in range(size)])  3.61 us
    ppermute x1, starting transfers between devices, local(): above = lax.ppermute(plane, 'gz', [(i, i - 1) for i in range(1, n_gz)])  3.33 us
    pallas_call x2, Pallas kernels, particles(): pl.pallas_call(functools.partial(particle_kernel, width, mine, n_gz, n_do...  3.19 us
    pallas_call x1, Pallas kernels, local(): pl.pallas_call(functools.partial(weight_kernel, spread_groups, spread_tab...  2.09 us
  transfers between devices with their start and end apart: 11, of which 1 were waited for; matrix products, arithmetic and copies ran while one was open for 0% of the time, Pallas kernels for 20%

profile of v13, /device:TPU:4, one launch (start us, length us, event | category | flops | bytes accessed | tf_op | source)
XLA Modules:
  0.0 48.4 jit_solution(4726101052305954831)
XLA Ops:
  0.6 1.7 %pack.1 = (bf16[16,1664]{1,0:T(8,128)(2,1)}, f32[1,4,384]{2,1,0:T(4,128)}, f32[32,4,384]{2,1,0:T(4,128)}) custom-call(bf16[16,4,384]{2,1,0:T(4,128)(2,1)} %observed_hbm.1, s32[1,16]{1,0:T(1,128)} %bitcast.7, s32[1,16]{1,0:T(1,128)} %bitcast.8, f32[192,4,384]{2,1,0:T(4,128)} %volume.1), custom_call_target="tpu_custom_call" | custom-call | tf_op jit(solution)/shard_map/pack/pallas_call | solution.py:508
  2.4 3.7 %collective-permute-start.2 = (bf16[16,1664]{1,0:T(8,128)(2,1)}, bf16[16,1664]{1,0:T(8,128)(2,1)S(1)}, u32[]{:S(2)}, u32[]{:S(2)}) collective-permute-start(bf16[16,1664]{1,0:T(8,128)(2,1)} %get-tuple-element.28), channel_id=1, source_target_pairs={{0,6},{1,7},{2,4},{3,5},{4,2},{5,3},{6,0},{7,1},{8,14},{9,15},{10,... | collective-permute-start | bytes 159752 | tf_op jit(solution)/shard_map/ppermute | solution.py:487
  6.0 0.0 collective-permute-start.1
  6.1 0.8 %collective-permute-start = (bf16[16,1664]{1,0:T(8,128)(2,1)}, bf16[16,1664]{1,0:T(8,128)(2,1)S(1)}, u32[]{:S(2)}, u32[]{:S(2)}) collective-permute-start(bf16[16,1664]{1,0:T(8,128)(2,1)} %get-tuple-element.28), channel_id=1, source_target_pairs={{0,2},{1,3},{2,0},{3,1},{4,6},{5,7},{6,4},{7,5},{8,10},{9,11},{10,... | collective-permute-start | bytes 159752 | tf_op jit(solution)/shard_map/ppermute | solution.py:487
  6.8 3.3 %collective-permute-start.3 = (f32[1,4,384]{2,1,0:T(4,128)}, f32[1,4,384]{2,1,0:T(4,128)S(1)}, u32[]{:S(2)}, u32[]{:S(2)}) collective-permute-start(f32[1,4,384]{2,1,0:T(4,128)} %get-tuple-element.29), channel_id=1, source_target_pairs={{8,0},{16,8},{24,16},{9,1},{17,9},{25,17},{10,2},{18,10},{26,18},{... | collective-permute-start | bytes 18440 | tf_op jit(solution)/shard_map/ppermute | solution.py:528
  10.2 0.0 copy-start
  10.2 0.7 %copy-done = s32[3104]{0:T(1024)S(1)} copy-done((s32[3104]{0:T(1024)S(1)}, s32[3104]{0:T(1024)}, u32[]{:S(2)}) %copy-start) | copy-done | bytes 12440
  10.9 0.0 copy-start.2
  10.9 0.7 %copy-done.2 = f32[128]{0:T(128)S(1)} copy-done((f32[128]{0:T(128)S(1)}, f32[128]{0:T(128)}, u32[]{:S(2)}) %copy-start.2) | copy-done | bytes 536
  11.6 0.0 copy-start.7
  11.6 0.0 copy-start.3
  11.6 0.0 copy-start.4
  11.6 0.0 copy-start.5
  11.6 0.0 copy-start.6
  11.6 2.1 %weights.1 = (bf16[7,2048,128]{2,1,0:T(8,128)(2,1)S(1)}, bf16[32,96,128]{2,1,0:T(8,128)(2,1)S(1)}) custom-call(s32[3104]{0:T(1024)S(1)} %copy-done, f32[128]{0:T(128)S(1)} %copy-done.2), custom_call_target="tpu_custom_call" | custom-call | flops 3000000000 | bytes 2097152 | tf_op jit(solution)/shard_map/weights/pallas_call | solution.py:534
  13.7 0.0 collective-permute-done.2
  13.7 0.0 collective-permute-done.1
  13.7 0.0 collective-permute-done
  13.7 0.0 copy-done.7
  13.7 0.0 collective-permute-done.3.above
  13.8 0.1 collective-permute-start.7
  13.8 1.1 %collective-permute-start.6 = (bf16[64,1664]{1,0:T(8,128)(2,1)S(1)}, bf16[64,1664]{1,0:T(8,128)(2,1)S(1)}, u32[]{:S(2)}, u32[]{:S(2)}) collective-permute-start(bf16[64,1664]{1,0:T(8,128)(2,1)S(1)} %pad_maximum_fusion.refs_0_), channel_id=1, source_target_pairs={{0,24},{8,16},{16,8},{24,0},{1,25},{9,17},{17,9},{25,1},{2,26},{10... | collective-permute-start | bytes 638984 | tf_op jit(solution)/shard_map/ppermute | solution.py:487
  14.9 0.5 %collective-permute-start.5 = (bf16[64,1664]{1,0:T(8,128)(2,1)S(1)}, bf16[64,1664]{1,0:T(8,128)(2,1)S(1)}, u32[]{:S(2)}, u32[]{:S(2)}) collective-permute-start(bf16[64,1664]{1,0:T(8,128)(2,1)S(1)} %pad_maximum_fusion.refs_0_), channel_id=1, source_target_pairs={{0,16},{8,24},{16,0},{24,8},{1,17},{9,25},{17,1},{25,9},{2,18},{10... | collective-permute-start | bytes 638984 | tf_op jit(solution)/shard_map/ppermute | solution.py:487
  15.4 2.0 %collective-permute-start.4 = (bf16[64,1664]{1,0:T(8,128)(2,1)S(1)}, bf16[64,1664]{1,0:T(8,128)(2,1)S(1)}, u32[]{:S(2)}, u32[]{:S(2)}) collective-permute-start(bf16[64,1664]{1,0:T(8,128)(2,1)S(1)} %pad_maximum_fusion.refs_0_), channel_id=1, source_target_pairs={{0,8},{8,0},{16,24},{24,16},{1,9},{9,1},{17,25},{25,17},{2,10},{10... | collective-permute-start | bytes 638984 | tf_op jit(solution)/shard_map/ppermute | solution.py:487
  17.4 0.0 copy-done.3
  17.4 0.0 copy-done.4
  17.4 0.0 copy-done.5
  17.4 0.0 copy-done.6
  17.4 5.9 %extract.1 = (bf16[128,1536]{1,0:T(8,128)(2,1)S(1)}, bf16[32,384]{1,0:T(8,128)(2,1)S(1)}, f32[32,768]{1,0:T(8,128)S(1)}) custom-call(s32[2080]{0:T(1024)S(1)} %copy-done.6, f32[128]{0:T(128)S(1)} %copy-done.3, f32[32,4,384]{2,1,0:T(4,128)S(1)} %copy-done.4, f32[1,4,384]{2,1,0:T(4,128)S(1)} %collective-permute-done.3.above, f32[32,2,384]{2,1,0:T(2,128)S(1)} %copy-done.5), custom_call_target="tpu_custom_call" | custom-call | flops 6000000000 | bytes 1048576 | tf_op jit(solution)/shard_map/extract/pallas_call | solution.py:553
  23.3 0.0 collective-permute-done.7.refs_0_
  23.3 0.0 collective-permute-done.6.refs_3_
  23.3 3.5 %collective-permute-done.5.refs_2_ = bf16[64,1664]{1,0:T(8,128)(2,1)S(1)} collective-permute-done((bf16[64,1664]{1,0:T(8,128)(2,1)S(1)}, bf16[64,1664]{1,0:T(8,128)(2,1)S(1)}, u32[]{:S(2)}, u32[]{:S(2)}) %collective-permute-start.5) | collective-permute-done | bytes 213024 | tf_op jit(solution)/shard_map/ppermute | solution.py:487
  26.8 0.0 collective-permute-done.4.refs_1_
  26.9 0.0 collective-permute-start.8
  26.9 0.5 %collective-permute-start.9 = (bf16[64,1664]{1,0:T(8,128)(2,1)S(1)}, bf16[64,1664]{1,0:T(8,128)(2,1)S(1)}, u32[]{:S(2)}, u32[]{:S(2)}) collective-permute-start(bf16[64,1664]{1,0:T(8,128)(2,1)S(1)} %collective-permute-done.5.refs_2_), channel_id=1, source_target_pairs={{0,1},{1,0},{2,3},{3,2},{4,5},{5,4},{6,7},{7,6},{8,9},{9,8},{10,11... | collective-permute-start | bytes 638984 | tf_op jit(solution)/shard_map/ppermute | solution.py:487
  27.4 0.0 collective-permute-start.10
  27.4 1.5 %particles.2 = (bf16[256,1536]{1,0:T(8,128)(2,1)S(1)}, f32[1,256]{1,0:T(1,128)S(1)}, f32[4,128]{1,0:T(4,128)S(1)}) custom-call(bf16[64,1664]{1,0:T(8,128)(2,1)S(1)} %pad_maximum_fusion.refs_0_, bf16[64,1664]{1,0:T(8,128)(2,1)S(1)} %collective-permute-done.4.refs_1_, bf16[64,1664]{1,0:T(8,128)(2,1)S(1)} %collective-permute-done.5.refs_2_, ...), custom_call_target="tpu_custom_call" | custom-call | flops 2000000000 | bytes 1048576 | tf_op jit(solution)/shard_map/particles/pallas_call | solution.py:585
  28.9 0.0 collective-permute-done.8.refs_1_
  28.9 0.0 collective-permute-done.9.refs_2_
  28.9 0.0 collective-permute-done.10.refs_3_
  28.9 0.0 copy-start.1
  28.9 1.7 %particles.3 = (bf16[256,1536]{1,0:T(8,128)(2,1)S(1)}, f32[1,256]{1,0:T(1,128)S(1)}, f32[256,128]{1,0:T(8,128)S(1)}) custom-call(bf16[64,1664]{1,0:T(8,128)(2,1)S(1)} %collective-permute-done.7.refs_0_, bf16[64,1664]{1,0:T(8,128)(2,1)S(1)} %collective-permute-done.8.refs_1_, bf16[64,1664]{1,0:T(8,128)(2,1)S(1)} %collective-permute-done.9.refs_2_, ...), custom_call_target="tpu_custom_call" | custom-call | flops 2000000000 | bytes 1048576 | tf_op jit(solution)/shard_map/particles/pallas_call | solution.py:585
  30.6 12.1 %all_to_all.11 = f32[32,8,128]{2,1,0:T(8,128)S(1)} all-to-all(f32[32,8,128]{2,1,0:T(8,128)S(1)} %bitcast.6), channel_id=1, replica_groups=mesh['gz'=4,'dom'=8] {'gz','dom'}, dimensions={0} | all-to-all | bytes 262144 | tf_op jit(solution)/shard_map/all_to_all | solution.py:606
  42.7 0.0 copy-done.1
  42.7 5.7 %spread.1 = (f32[1,16]{1,0:T(1,128)}, f32[24,4,384]{2,1,0:T(4,128)}) custom-call(s32[3104]{0:T(1024)S(1)} %copy-done.1, f32[128]{0:T(128)S(1)} %copy-done.3, bf16[7,2048,128]{2,1,0:T(8,128)(2,1)S(1)} %get-tuple-element.32.right, bf16[32,96,128]{2,1,0:T(8,128)(2,1)S(1)} %get-tuple-element.33.edges, f32[256,128]{1,0:T(8,128)S(1)} %bitcast.5, ...), custom_call_target="tpu_custom_call" | custom-call | tf_op jit(solution)/shard_map/spread/pallas_call | solution.py:609
  (1 shorter events, 0.0 us)
Async XLA Ops:
  2.4 11.3 %collective-permute-start.2 = (bf16[16,1664]{1,0:T(8,128)(2,1)}, bf16[16,1664]{1,0:T(8,128)(2,1)S(1)}, u32[]{:S(2)}, u32[]{:S(2)}) collective-permute-start(bf16[16,1664]{1,0:T(8,128)(2,1)} %get-tuple-element.28), channel_id=1, source_target_pairs={{0,6},{1,7},{2,4},{3,5},{4,2},{5,3},{6,0},{7,1},{8,14},{9,15},{10,... | collective-permute-start | bytes 159752 | tf_op jit(solution)/shard_map/ppermute | solution.py:487
  6.0 7.6 %collective-permute-start.1 = (bf16[16,1664]{1,0:T(8,128)(2,1)}, bf16[16,1664]{1,0:T(8,128)(2,1)S(1)}, u32[]{:S(2)}, u32[]{:S(2)}) collective-permute-start(bf16[16,1664]{1,0:T(8,128)(2,1)} %get-tuple-element.28), channel_id=1, source_target_pairs={{0,4},{1,5},{2,6},{3,7},{4,0},{5,1},{6,2},{7,3},{8,12},{9,13},{10,... | collective-permute-start | bytes 159752 | tf_op jit(solution)/shard_map/ppermute | solution.py:487
  6.1 7.6 %collective-permute-start = (bf16[16,1664]{1,0:T(8,128)(2,1)}, bf16[16,1664]{1,0:T(8,128)(2,1)S(1)}, u32[]{:S(2)}, u32[]{:S(2)}) collective-permute-start(bf16[16,1664]{1,0:T(8,128)(2,1)} %get-tuple-element.28), channel_id=1, source_target_pairs={{0,2},{1,3},{2,0},{3,1},{4,6},{5,7},{6,4},{7,5},{8,10},{9,11},{10,... | collective-permute-start | bytes 159752 | tf_op jit(solution)/shard_map/ppermute | solution.py:487
  6.8 6.9 %collective-permute-start.3 = (f32[1,4,384]{2,1,0:T(4,128)}, f32[1,4,384]{2,1,0:T(4,128)S(1)}, u32[]{:S(2)}, u32[]{:S(2)}) collective-permute-start(f32[1,4,384]{2,1,0:T(4,128)} %get-tuple-element.29), channel_id=1, source_target_pairs={{8,0},{16,8},{24,16},{9,1},{17,9},{25,17},{10,2},{18,10},{26,18},{... | collective-permute-start | bytes 18440 | tf_op jit(solution)/shard_map/ppermute | solution.py:528
  10.2 0.7 %copy-start = (s32[3104]{0:T(1024)S(1)}, s32[3104]{0:T(1024)}, u32[]{:S(2)}) copy-start(s32[3104]{0:T(1024)} %constant.7.clone.table) | copy-start | bytes 37252
  10.9 0.7 %copy-start.2 = (f32[128]{0:T(128)S(1)}, f32[128]{0:T(128)}, u32[]{:S(2)}) copy-start(f32[128]{0:T(128)} %constant.6.clone.trig.trig_hbm) | copy-start | bytes 1540
  11.6 2.2 %copy-start.7 = (bf16[16,1664]{1,0:T(8,128)(2,1)S(1)}, bf16[16,1664]{1,0:T(8,128)(2,1)}, u32[]{:S(2)}) copy-start(bf16[16,1664]{1,0:T(8,128)(2,1)} %get-tuple-element.28) | copy-start | bytes 159748
  11.6 5.8 %copy-start.3 = (f32[128]{0:T(128)S(1)}, f32[128]{0:T(128)}, u32[]{:S(2)}) copy-start(f32[128]{0:T(128)} %constant.6.clone.trig.trig_hbm) | copy-start | bytes 1540
  11.6 5.8 %copy-start.4 = (f32[32,4,384]{2,1,0:T(4,128)S(1)}, f32[32,4,384]{2,1,0:T(4,128)}, u32[]{:S(2)}) copy-start(f32[32,4,384]{2,1,0:T(4,128)} %get-tuple-element.35.field) | copy-start | bytes 589828
  11.6 5.8 %copy-start.5 = (f32[32,2,384]{2,1,0:T(2,128)S(1)}, f32[32,2,384]{2,1,0:T(2,128)}, u32[]{:S(2)}) copy-start(f32[32,2,384]{2,1,0:T(2,128)} %ctf_hbm.1) | copy-start | bytes 294916
  11.6 5.8 %copy-start.6 = (s32[2080]{0:T(1024)S(1)}, s32[2080]{0:T(1024)}, u32[]{:S(2)}) copy-start(s32[2080]{0:T(1024)} %constant.8.clone.table_hbm) | copy-start | bytes 24964
  13.8 9.5 %collective-permute-start.7 = (bf16[64,1664]{1,0:T(8,128)(2,1)S(1)}, bf16[64,1664]{1,0:T(8,128)(2,1)S(1)}, u32[]{:S(2)}, u32[]{:S(2)}) collective-permute-start(bf16[64,1664]{1,0:T(8,128)(2,1)S(1)} %pad_maximum_fusion.refs_0_), channel_id=1, source_target_pairs={{0,1},{1,0},{2,3},{3,2},{4,5},{5,4},{6,7},{7,6},{8,9},{9,8},{10,11... | collective-permute-start | bytes 638984 | tf_op jit(solution)/shard_map/ppermute | solution.py:487
  13.8 9.5 %collective-permute-start.6 = (bf16[64,1664]{1,0:T(8,128)(2,1)S(1)}, bf16[64,1664]{1,0:T(8,128)(2,1)S(1)}, u32[]{:S(2)}, u32[]{:S(2)}) collective-permute-start(bf16[64,1664]{1,0:T(8,128)(2,1)S(1)} %pad_maximum_fusion.refs_0_), channel_id=1, source_target_pairs={{0,24},{8,16},{16,8},{24,0},{1,25},{9,17},{17,9},{25,1},{2,26},{10... | collective-permute-start | bytes 638984 | tf_op jit(solution)/shard_map/ppermute | solution.py:487
  14.9 11.9 %collective-permute-start.5 = (bf16[64,1664]{1,0:T(8,128)(2,1)S(1)}, bf16[64,1664]{1,0:T(8,128)(2,1)S(1)}, u32[]{:S(2)}, u32[]{:S(2)}) collective-permute-start(bf16[64,1664]{1,0:T(8,128)(2,1)S(1)} %pad_maximum_fusion.refs_0_), channel_id=1, source_target_pairs={{0,16},{8,24},{16,0},{24,8},{1,17},{9,25},{17,1},{25,9},{2,18},{10... | collective-permute-start | bytes 638984 | tf_op jit(solution)/shard_map/ppermute | solution.py:487
  15.4 11.5 %collective-permute-start.4 = (bf16[64,1664]{1,0:T(8,128)(2,1)S(1)}, bf16[64,1664]{1,0:T(8,128)(2,1)S(1)}, u32[]{:S(2)}, u32[]{:S(2)}) collective-permute-start(bf16[64,1664]{1,0:T(8,128)(2,1)S(1)} %pad_maximum_fusion.refs_0_), channel_id=1, source_target_pairs={{0,8},{8,0},{16,24},{24,16},{1,9},{9,1},{17,25},{25,17},{2,10},{10... | collective-permute-start | bytes 638984 | tf_op jit(solution)/shard_map/ppermute | solution.py:487
  26.9 2.0 %collective-permute-start.8 = (bf16[64,1664]{1,0:T(8,128)(2,1)S(1)}, bf16[64,1664]{1,0:T(8,128)(2,1)S(1)}, u32[]{:S(2)}, u32[]{:S(2)}) collective-permute-start(bf16[64,1664]{1,0:T(8,128)(2,1)S(1)} %collective-permute-done.4.refs_1_), channel_id=1, source_target_pairs={{0,1},{1,0},{2,3},{3,2},{4,5},{5,4},{6,7},{7,6},{8,9},{9,8},{10,11... | collective-permute-start | bytes 638984 | tf_op jit(solution)/shard_map/ppermute | solution.py:487
  26.9 2.0 %collective-permute-start.9 = (bf16[64,1664]{1,0:T(8,128)(2,1)S(1)}, bf16[64,1664]{1,0:T(8,128)(2,1)S(1)}, u32[]{:S(2)}, u32[]{:S(2)}) collective-permute-start(bf16[64,1664]{1,0:T(8,128)(2,1)S(1)} %collective-permute-done.5.refs_2_), channel_id=1, source_target_pairs={{0,1},{1,0},{2,3},{3,2},{4,5},{5,4},{6,7},{7,6},{8,9},{9,8},{10,11... | collective-permute-start | bytes 638984 | tf_op jit(solution)/shard_map/ppermute | solution.py:487
  27.4 1.6 %collective-permute-start.10 = (bf16[64,1664]{1,0:T(8,128)(2,1)S(1)}, bf16[64,1664]{1,0:T(8,128)(2,1)S(1)}, u32[]{:S(2)}, u32[]{:S(2)}) collective-permute-start(bf16[64,1664]{1,0:T(8,128)(2,1)S(1)} %collective-permute-done.6.refs_3_), channel_id=1, source_target_pairs={{0,1},{1,0},{2,3},{3,2},{4,5},{5,4},{6,7},{7,6},{8,9},{9,8},{10,11... | collective-permute-start | bytes 638984 | tf_op jit(solution)/shard_map/ppermute | solution.py:487
  28.9 13.8 %copy-start.1 = (s32[3104]{0:T(1024)S(1)}, s32[3104]{0:T(1024)}, u32[]{:S(2)}) copy-start(s32[3104]{0:T(1024)} %constant.7.clone.table) | copy-start | bytes 37252

commit v14 on v12

--- a/solution.py
+++ b/solution.py
@@ -545,7 +545,7 @@
         cost_estimate=pl.CostEstimate(flops=3 * 10**9, bytes_accessed=2**21, transcendentals=0),
         name="weights",
     )(spread_table_flat, trig)
-    column, above, right, edges = lax.optimization_barrier((column, above, right, edges))
+    column, trig, right, edges = lax.optimization_barrier((column, trig, right, edges))
     planes_of = [column] + [swap(column, "gz", n_gz, j) for j in range(1, n_gz)]
 
 

time: 46.8 us -> 46.8 us (level)
  no operation moved by 1% of the time
where the time goes in v14:
time: 46.8 us; the launch traced here: 46.5 us
  Pallas kernels  18.7 us (40%)
  blocking collectives  12.4 us (26%)
  starting transfers between devices  12.3 us (26%)
  local copies, waits for them, and re-layouts  1.4 us (3%)
  waiting for transfers between devices  0.88 us (2%)
  between operations  0.81 us (2%)
    all_to_all x1, blocking collectives, local(): parts = lax.all_to_all(parts, ('gz', 'dom'), 0, 0, tiled=True)  12.4 us
    ppermute x10, starting transfers between devices, swap(): return lax.ppermute(x, axis, [(i, i ^ distance) for i in range(size)])  9.02 us
    pallas_call x1, Pallas kernels, local(): pl.pallas_call(functools.partial(extract_kernel, groups, table.shape[1],...  5.89 us
    pallas_call x1, Pallas kernels, local(): pl.pallas_call(functools.partial(spread_kernel, spread_groups, spread_tab...  5.73 us
    ppermute x1, starting transfers between devices, local(): above = lax.ppermute(plane, 'gz', [(i, i - 1) for i in range(1, n_gz)])  3.33 us
    pallas_call x2, Pallas kernels, particles(): pl.pallas_call(functools.partial(particle_kernel, width, mine, n_gz, n_do...  3.19 us
    pallas_call x1, Pallas kernels, local(): pl.pallas_call(functools.partial(weight_kernel, spread_groups, spread_tab...  2.09 us
    pallas_call x1, Pallas kernels, local(): pl.pallas_call(functools.partial(pack_kernel, planes), out_shape=[jax.Sha...  1.75 us
  transfers between devices with their start and end apart: 11, of which 1 were waited for; matrix products, arithmetic and copies ran while one was open for 0% of the time, Pallas kernels for 20%

profile of v14, /device:TPU:4, one launch (start us, length us, event | category | flops | bytes accessed | tf_op | source)
XLA Modules:
  0.0 46.5 jit_solution(10449534151276410928)
XLA Ops:
  0.6 1.7 %pack.1 = (bf16[16,1664]{1,0:T(8,128)(2,1)}, f32[1,4,384]{2,1,0:T(4,128)}, f32[32,4,384]{2,1,0:T(4,128)}) custom-call(bf16[16,4,384]{2,1,0:T(4,128)(2,1)} %observed_hbm.1, s32[1,16]{1,0:T(1,128)} %bitcast.7, s32[1,16]{1,0:T(1,128)} %bitcast.8, f32[192,4,384]{2,1,0:T(4,128)} %volume.1), custom_call_target="tpu_custom_call" | custom-call | tf_op jit(solution)/shard_map/pack/pallas_call | solution.py:508
  2.4 3.7 %collective-permute-start.2 = (bf16[16,1664]{1,0:T(8,128)(2,1)}, bf16[16,1664]{1,0:T(8,128)(2,1)S(1)}, u32[]{:S(2)}, u32[]{:S(2)}) collective-permute-start(bf16[16,1664]{1,0:T(8,128)(2,1)} %get-tuple-element.27), channel_id=1, source_target_pairs={{0,6},{1,7},{2,4},{3,5},{4,2},{5,3},{6,0},{7,1},{8,14},{9,15},{10,... | collective-permute-start | bytes 159752 | tf_op jit(solution)/shard_map/ppermute | solution.py:487
  6.0 0.0 collective-permute-start.1
  6.1 0.8 %collective-permute-start = (bf16[16,1664]{1,0:T(8,128)(2,1)}, bf16[16,1664]{1,0:T(8,128)(2,1)S(1)}, u32[]{:S(2)}, u32[]{:S(2)}) collective-permute-start(bf16[16,1664]{1,0:T(8,128)(2,1)} %get-tuple-element.27), channel_id=1, source_target_pairs={{0,2},{1,3},{2,0},{3,1},{4,6},{5,7},{6,4},{7,5},{8,10},{9,11},{10,... | collective-permute-start | bytes 159752 | tf_op jit(solution)/shard_map/ppermute | solution.py:487
  6.8 3.3 %collective-permute-start.6 = (f32[1,4,384]{2,1,0:T(4,128)}, f32[1,4,384]{2,1,0:T(4,128)S(1)}, u32[]{:S(2)}, u32[]{:S(2)}) collective-permute-start(f32[1,4,384]{2,1,0:T(4,128)} %get-tuple-element.35), channel_id=1, source_target_pairs={{8,0},{16,8},{24,16},{9,1},{17,9},{25,17},{10,2},{18,10},{26,18},{... | collective-permute-start | bytes 18440 | tf_op jit(solution)/shard_map/ppermute | solution.py:528
  10.2 0.0 copy-start
  10.2 0.7 %copy-done = s32[3104]{0:T(1024)S(1)} copy-done((s32[3104]{0:T(1024)S(1)}, s32[3104]{0:T(1024)}, u32[]{:S(2)}) %copy-start) | copy-done | bytes 12440
  10.9 0.0 copy-start.2
  10.9 0.7 %copy-done.2 = f32[128]{0:T(128)S(1)} copy-done((f32[128]{0:T(128)S(1)}, f32[128]{0:T(128)}, u32[]{:S(2)}) %copy-start.2) | copy-done | bytes 536
  11.6 0.0 copy-start.7
  11.6 0.0 copy-start.3
  11.6 0.0 copy-start.4
  11.6 0.0 copy-start.5
  11.6 0.0 copy-start.6
  11.6 2.1 %weights.1 = (bf16[7,2048,128]{2,1,0:T(8,128)(2,1)S(1)}, bf16[32,96,128]{2,1,0:T(8,128)(2,1)S(1)}) custom-call(s32[3104]{0:T(1024)S(1)} %copy-done, f32[128]{0:T(128)S(1)} %copy-done.2), custom_call_target="tpu_custom_call" | custom-call | flops 3000000000 | bytes 2097152 | tf_op jit(solution)/shard_map/weights/pallas_call | solution.py:534
  13.7 0.0 collective-permute-done.2
  13.7 0.0 collective-permute-done.1
  13.7 0.0 collective-permute-done
  13.7 0.0 copy-done.7
  13.7 0.1 collective-permute-start.5
  13.8 1.5 %collective-permute-start.4 = (bf16[64,1664]{1,0:T(8,128)(2,1)S(1)}, bf16[64,1664]{1,0:T(8,128)(2,1)S(1)}, u32[]{:S(2)}, u32[]{:S(2)}) collective-permute-start(bf16[64,1664]{1,0:T(8,128)(2,1)S(1)} %pad_maximum_fusion.refs_0_), channel_id=1, source_target_pairs={{0,16},{8,24},{16,0},{24,8},{1,17},{9,25},{17,1},{25,9},{2,18},{10... | collective-permute-start | bytes 638984 | tf_op jit(solution)/shard_map/ppermute | solution.py:487
  15.3 2.0 %collective-permute-start.3 = (bf16[64,1664]{1,0:T(8,128)(2,1)S(1)}, bf16[64,1664]{1,0:T(8,128)(2,1)S(1)}, u32[]{:S(2)}, u32[]{:S(2)}) collective-permute-start(bf16[64,1664]{1,0:T(8,128)(2,1)S(1)} %pad_maximum_fusion.refs_0_), channel_id=1, source_target_pairs={{0,8},{8,0},{16,24},{24,16},{1,9},{9,1},{17,25},{25,17},{2,10},{10... | collective-permute-start | bytes 638984 | tf_op jit(solution)/shard_map/ppermute | solution.py:487
  17.3 0.0 collective-permute-done.6.above
  17.3 0.0 copy-done.3
  17.3 0.0 copy-done.4
  17.3 0.0 copy-done.5
  17.3 0.0 copy-done.6
  17.3 5.9 %extract.1 = (bf16[128,1536]{1,0:T(8,128)(2,1)S(1)}, bf16[32,384]{1,0:T(8,128)(2,1)S(1)}, f32[32,768]{1,0:T(8,128)S(1)}) custom-call(s32[2080]{0:T(1024)S(1)} %copy-done.6, f32[128]{0:T(128)S(1)} %copy-done.3, f32[32,4,384]{2,1,0:T(4,128)S(1)} %copy-done.4, f32[1,4,384]{2,1,0:T(4,128)S(1)} %collective-permute-done.6.above, f32[32,2,384]{2,1,0:T(2,128)S(1)} %copy-done.5), custom_call_target="tpu_custom_call" | custom-call | flops 6000000000 | bytes 1048576 | tf_op jit(solution)/shard_map/extract/pallas_call | solution.py:553
  23.2 0.0 collective-permute-done.5.refs_3_
  23.2 0.8 %collective-permute-done.4.refs_2_ = bf16[64,1664]{1,0:T(8,128)(2,1)S(1)} collective-permute-done((bf16[64,1664]{1,0:T(8,128)(2,1)S(1)}, bf16[64,1664]{1,0:T(8,128)(2,1)S(1)}, u32[]{:S(2)}, u32[]{:S(2)}) %collective-permute-start.4) | collective-permute-done | bytes 213024 | tf_op jit(solution)/shard_map/ppermute | solution.py:487
  24.1 0.0 collective-permute-done.3.refs_1_
  24.1 0.0 collective-permute-start.7
  24.1 0.5 %collective-permute-start.8 = (bf16[64,1664]{1,0:T(8,128)(2,1)S(1)}, bf16[64,1664]{1,0:T(8,128)(2,1)S(1)}, u32[]{:S(2)}, u32[]{:S(2)}) collective-permute-start(bf16[64,1664]{1,0:T(8,128)(2,1)S(1)} %collective-permute-done.3.refs_1_), channel_id=1, source_target_pairs={{0,1},{1,0},{2,3},{3,2},{4,5},{5,4},{6,7},{7,6},{8,9},{9,8},{10,11... | collective-permute-start | bytes 638984 | tf_op jit(solution)/shard_map/ppermute | solution.py:487
  24.6 0.0 collective-permute-start.9
  24.6 0.5 %collective-permute-start.10 = (bf16[64,1664]{1,0:T(8,128)(2,1)S(1)}, bf16[64,1664]{1,0:T(8,128)(2,1)S(1)}, u32[]{:S(2)}, u32[]{:S(2)}) collective-permute-start(bf16[64,1664]{1,0:T(8,128)(2,1)S(1)} %collective-permute-done.5.refs_3_), channel_id=1, source_target_pairs={{0,1},{1,0},{2,3},{3,2},{4,5},{5,4},{6,7},{7,6},{8,9},{9,8},{10,11... | collective-permute-start | bytes 638984 | tf_op jit(solution)/shard_map/ppermute | solution.py:487
  25.1 1.5 %particles.2 = (bf16[256,1536]{1,0:T(8,128)(2,1)S(1)}, f32[1,256]{1,0:T(1,128)S(1)}, f32[4,128]{1,0:T(4,128)S(1)}) custom-call(bf16[64,1664]{1,0:T(8,128)(2,1)S(1)} %pad_maximum_fusion.refs_0_, bf16[64,1664]{1,0:T(8,128)(2,1)S(1)} %collective-permute-done.3.refs_1_, bf16[64,1664]{1,0:T(8,128)(2,1)S(1)} %collective-permute-done.4.refs_2_, ...), custom_call_target="tpu_custom_call" | custom-call | flops 2000000000 | bytes 1048576 | tf_op jit(solution)/shard_map/particles/pallas_call | solution.py:584
  26.6 0.0 collective-permute-done.7.refs_0_
  26.6 0.0 collective-permute-done.8.refs_1_
  26.6 0.0 collective-permute-done.9.refs_2_
  26.6 0.0 collective-permute-done.10.refs_3_
  26.6 0.0 copy-start.1
  26.7 1.7 %particles.3 = (bf16[256,1536]{1,0:T(8,128)(2,1)S(1)}, f32[1,256]{1,0:T(1,128)S(1)}, f32[256,128]{1,0:T(8,128)S(1)}) custom-call(bf16[64,1664]{1,0:T(8,128)(2,1)S(1)} %collective-permute-done.7.refs_0_, bf16[64,1664]{1,0:T(8,128)(2,1)S(1)} %collective-permute-done.8.refs_1_, bf16[64,1664]{1,0:T(8,128)(2,1)S(1)} %collective-permute-done.9.refs_2_, ...), custom_call_target="tpu_custom_call" | custom-call | flops 2000000000 | bytes 1048576 | tf_op jit(solution)/shard_map/particles/pallas_call | solution.py:584
  28.4 12.4 %all_to_all.11 = f32[32,8,128]{2,1,0:T(8,128)S(1)} all-to-all(f32[32,8,128]{2,1,0:T(8,128)S(1)} %bitcast.6), channel_id=1, replica_groups=mesh['gz'=4,'dom'=8] {'gz','dom'}, dimensions={0} | all-to-all | bytes 262144 | tf_op jit(solution)/shard_map/all_to_all | solution.py:605
  40.8 0.0 copy-done.1
  40.8 5.7 %spread.1 = (f32[1,16]{1,0:T(1,128)}, f32[24,4,384]{2,1,0:T(4,128)}) custom-call(s32[3104]{0:T(1024)S(1)} %copy-done.1, f32[128]{0:T(128)S(1)} %copy-done.3, bf16[7,2048,128]{2,1,0:T(8,128)(2,1)S(1)} %get-tuple-element.31.right, bf16[32,96,128]{2,1,0:T(8,128)(2,1)S(1)} %get-tuple-element.32.edges, f32[256,128]{1,0:T(8,128)S(1)} %bitcast.5, ...), custom_call_target="tpu_custom_call" | custom-call | tf_op jit(solution)/shard_map/spread/pallas_call | solution.py:608
  (1 shorter events, 0.0 us)
Async XLA Ops:
  2.4 11.3 %collective-permute-start.2 = (bf16[16,1664]{1,0:T(8,128)(2,1)}, bf16[16,1664]{1,0:T(8,128)(2,1)S(1)}, u32[]{:S(2)}, u32[]{:S(2)}) collective-permute-start(bf16[16,1664]{1,0:T(8,128)(2,1)} %get-tuple-element.27), channel_id=1, source_target_pairs={{0,6},{1,7},{2,4},{3,5},{4,2},{5,3},{6,0},{7,1},{8,14},{9,15},{10,... | collective-permute-start | bytes 159752 | tf_op jit(solution)/shard_map/ppermute | solution.py:487
  6.0 7.6 %collective-permute-start.1 = (bf16[16,1664]{1,0:T(8,128)(2,1)}, bf16[16,1664]{1,0:T(8,128)(2,1)S(1)}, u32[]{:S(2)}, u32[]{:S(2)}) collective-permute-start(bf16[16,1664]{1,0:T(8,128)(2,1)} %get-tuple-element.27), channel_id=1, source_target_pairs={{0,4},{1,5},{2,6},{3,7},{4,0},{5,1},{6,2},{7,3},{8,12},{9,13},{10,... | collective-permute-start | bytes 159752 | tf_op jit(solution)/shard_map/ppermute | solution.py:487
  6.1 7.6 %collective-permute-start = (bf16[16,1664]{1,0:T(8,128)(2,1)}, bf16[16,1664]{1,0:T(8,128)(2,1)S(1)}, u32[]{:S(2)}, u32[]{:S(2)}) collective-permute-start(bf16[16,1664]{1,0:T(8,128)(2,1)} %get-tuple-element.27), channel_id=1, source_target_pairs={{0,2},{1,3},{2,0},{3,1},{4,6},{5,7},{6,4},{7,5},{8,10},{9,11},{10,... | collective-permute-start | bytes 159752 | tf_op jit(solution)/shard_map/ppermute | solution.py:487
  6.8 10.5 %collective-permute-start.6 = (f32[1,4,384]{2,1,0:T(4,128)}, f32[1,4,384]{2,1,0:T(4,128)S(1)}, u32[]{:S(2)}, u32[]{:S(2)}) collective-permute-start(f32[1,4,384]{2,1,0:T(4,128)} %get-tuple-element.35), channel_id=1, source_target_pairs={{8,0},{16,8},{24,16},{9,1},{17,9},{25,17},{10,2},{18,10},{26,18},{... | collective-permute-start | bytes 18440 | tf_op jit(solution)/shard_map/ppermute | solution.py:528
  10.2 0.7 %copy-start = (s32[3104]{0:T(1024)S(1)}, s32[3104]{0:T(1024)}, u32[]{:S(2)}) copy-start(s32[3104]{0:T(1024)} %constant.7.clone.table) | copy-start | bytes 37252
  10.9 0.7 %copy-start.2 = (f32[128]{0:T(128)S(1)}, f32[128]{0:T(128)}, u32[]{:S(2)}) copy-start(f32[128]{0:T(128)} %constant.6.clone.trig.trig_hbm) | copy-start | bytes 1540
  11.6 2.2 %copy-start.7 = (bf16[16,1664]{1,0:T(8,128)(2,1)S(1)}, bf16[16,1664]{1,0:T(8,128)(2,1)}, u32[]{:S(2)}) copy-start(bf16[16,1664]{1,0:T(8,128)(2,1)} %get-tuple-element.27) | copy-start | bytes 159748
  11.6 5.7 %copy-start.3 = (f32[128]{0:T(128)S(1)}, f32[128]{0:T(128)}, u32[]{:S(2)}) copy-start(f32[128]{0:T(128)} %constant.6.clone.trig.trig_hbm) | copy-start | bytes 1540
  11.6 5.7 %copy-start.4 = (f32[32,4,384]{2,1,0:T(4,128)S(1)}, f32[32,4,384]{2,1,0:T(4,128)}, u32[]{:S(2)}) copy-start(f32[32,4,384]{2,1,0:T(4,128)} %get-tuple-element.34.field) | copy-start | bytes 589828
  11.6 5.7 %copy-start.5 = (f32[32,2,384]{2,1,0:T(2,128)S(1)}, f32[32,2,384]{2,1,0:T(2,128)}, u32[]{:S(2)}) copy-start(f32[32,2,384]{2,1,0:T(2,128)} %ctf_hbm.1) | copy-start | bytes 294916
  11.6 5.8 %copy-start.6 = (s32[2080]{0:T(1024)S(1)}, s32[2080]{0:T(1024)}, u32[]{:S(2)}) copy-start(s32[2080]{0:T(1024)} %constant.8.clone.table_hbm) | copy-start | bytes 24964
  13.7 9.5 %collective-permute-start.5 = (bf16[64,1664]{1,0:T(8,128)(2,1)S(1)}, bf16[64,1664]{1,0:T(8,128)(2,1)S(1)}, u32[]{:S(2)}, u32[]{:S(2)}) collective-permute-start(bf16[64,1664]{1,0:T(8,128)(2,1)S(1)} %pad_maximum_fusion.refs_0_), channel_id=1, source_target_pairs={{0,24},{8,16},{16,8},{24,0},{1,25},{9,17},{17,9},{25,1},{2,26},{10... | collective-permute-start | bytes 638984 | tf_op jit(solution)/shard_map/ppermute | solution.py:487
  13.8 10.2 %collective-permute-start.4 = (bf16[64,1664]{1,0:T(8,128)(2,1)S(1)}, bf16[64,1664]{1,0:T(8,128)(2,1)S(1)}, u32[]{:S(2)}, u32[]{:S(2)}) collective-permute-start(bf16[64,1664]{1,0:T(8,128)(2,1)S(1)} %pad_maximum_fusion.refs_0_), channel_id=1, source_target_pairs={{0,16},{8,24},{16,0},{24,8},{1,17},{9,25},{17,1},{25,9},{2,18},{10... | collective-permute-start | bytes 638984 | tf_op jit(solution)/shard_map/ppermute | solution.py:487
  15.3 8.8 %collective-permute-start.3 = (bf16[64,1664]{1,0:T(8,128)(2,1)S(1)}, bf16[64,1664]{1,0:T(8,128)(2,1)S(1)}, u32[]{:S(2)}, u32[]{:S(2)}) collective-permute-start(bf16[64,1664]{1,0:T(8,128)(2,1)S(1)} %pad_maximum_fusion.refs_0_), channel_id=1, source_target_pairs={{0,8},{8,0},{16,24},{24,16},{1,9},{9,1},{17,25},{25,17},{2,10},{10... | collective-permute-start | bytes 638984 | tf_op jit(solution)/shard_map/ppermute | solution.py:487
  24.1 2.5 %collective-permute-start.7 = (bf16[64,1664]{1,0:T(8,128)(2,1)S(1)}, bf16[64,1664]{1,0:T(8,128)(2,1)S(1)}, u32[]{:S(2)}, u32[]{:S(2)}) collective-permute-start(bf16[64,1664]{1,0:T(8,128)(2,1)S(1)} %pad_maximum_fusion.refs_0_), channel_id=1, source_target_pairs={{0,1},{1,0},{2,3},{3,2},{4,5},{5,4},{6,7},{7,6},{8,9},{9,8},{10,11... | collective-permute-start | bytes 638984 | tf_op jit(solution)/shard_map/ppermute | solution.py:487
  24.1 2.5 %collective-permute-start.8 = (bf16[64,1664]{1,0:T(8,128)(2,1)S(1)}, bf16[64,1664]{1,0:T(8,128)(2,1)S(1)}, u32[]{:S(2)}, u32[]{:S(2)}) collective-permute-start(bf16[64,1664]{1,0:T(8,128)(2,1)S(1)} %collective-permute-done.3.refs_1_), channel_id=1, source_target_pairs={{0,1},{1,0},{2,3},{3,2},{4,5},{5,4},{6,7},{7,6},{8,9},{9,8},{10,11... | collective-permute-start | bytes 638984 | tf_op jit(solution)/shard_map/ppermute | solution.py:487
  24.6 2.0 %collective-permute-start.9 = (bf16[64,1664]{1,0:T(8,128)(2,1)S(1)}, bf16[64,1664]{1,0:T(8,128)(2,1)S(1)}, u32[]{:S(2)}, u32[]{:S(2)}) collective-permute-start(bf16[64,1664]{1,0:T(8,128)(2,1)S(1)} %collective-permute-done.4.refs_2_), channel_id=1, source_target_pairs={{0,1},{1,0},{2,3},{3,2},{4,5},{5,4},{6,7},{7,6},{8,9},{9,8},{10,11... | collective-permute-start | bytes 638984 | tf_op jit(solution)/shard_map/ppermute | solution.py:487
  24.6 2.0 %collective-permute-start.10 = (bf16[64,1664]{1,0:T(8,128)(2,1)S(1)}, bf16[64,1664]{1,0:T(8,128)(2,1)S(1)}, u32[]{:S(2)}, u32[]{:S(2)}) collective-permute-start(bf16[64,1664]{1,0:T(8,128)(2,1)S(1)} %collective-permute-done.5.refs_3_), channel_id=1, source_target_pairs={{0,1},{1,0},{2,3},{3,2},{4,5},{5,4},{6,7},{7,6},{8,9},{9,8},{10,11... | collective-permute-start | bytes 638984 | tf_op jit(solution)/shard_map/ppermute | solution.py:487
  26.6 14.1 %copy-start.1 = (s32[3104]{0:T(1024)S(1)}, s32[3104]{0:T(1024)}, u32[]{:S(2)}) copy-start(s32[3104]{0:T(1024)} %constant.7.clone.table) | copy-start | bytes 37252

commit v15 on v14

--- a/solution.py
+++ b/solution.py
@@ -349,7 +349,16 @@
         parts[n * rows : (n + 1) * rows, :] = scalars
 
 
-def weight_kernel(groups, length, bins, planes, n_dom, edge_samples, table, trig, right, edges):
+class Codes:
+    def __init__(self, ref, start):
+        self.ref, self.start = ref, start
+
+    def __getitem__(self, at):
+        return self.ref[self.start + at].astype(jnp.int32)
+
+
+def weight_kernel(groups, length, bins, planes, n_dom, edge_samples, trig, right, edges):
+    table = Codes(trig, 2 * bins)
     device = lax.axis_index("gz") * n_dom + lax.axis_index("dom")
     row = device * length
     uu = lanes_of((TILE, TILE), 0)
@@ -539,12 +548,12 @@
             jax.ShapeDtypeStruct((spread_groups, SPREAD_GROUP * 2 * TILE, TILE), bf16),
             jax.ShapeDtypeStruct((bins // 2, 2 * edge_samples, TILE), bf16),
         ],
-        in_specs=[smem, smem],
+        in_specs=[smem],
         out_specs=[vmem, vmem],
         compiler_params=params,
         cost_estimate=pl.CostEstimate(flops=3 * 10**9, bytes_accessed=2**21, transcendentals=0),
         name="weights",
-    )(spread_table_flat, trig)
+    )(jnp.concatenate([trig, spread_table_flat.astype(f32)]))
     column, trig, right, edges = lax.optimization_barrier((column, trig, right, edges))
     planes_of = [column] + [swap(column, "gz", n_gz, j) for j in range(1, n_gz)]
 

time: 46.8 us -> 46.3 us (0.989)
  local copies, waits for them, and re-layouts: 1.4 us -> 0.74 us
    unnamed x16 -> x14, local copies, waits for them, and re-layouts: 1.4 us -> 0.74 us
  transfers between devices with their start and end apart: 11 -> 11, of which waited for: 1 -> 1; matrix products, arithmetic and copies ran while one was open for 0% -> 0% of each run, Pallas kernels for 20% -> 21%
where the time goes in v15:
time: 46.3 us; the launch traced here: 46 us
  Pallas kernels  18.7 us (40%)
  starting transfers between devices  12.5 us (27%)
  blocking collectives  12.4 us (27%)
  waiting for transfers between devices  0.86 us (2%)
  between operations  0.8 us (2%)
  local copies, waits for them, and re-layouts  0.74 us (2%)
    all_to_all x1, blocking collectives, local(): parts = lax.all_to_all(parts, ('gz', 'dom'), 0, 0, tiled=True)  12.4 us
    ppermute x10, starting transfers between devices, swap(): return lax.ppermute(x, axis, [(i, i ^ distance) for i in range(size)])  9.02 us
    pallas_call x1, Pallas kernels, local(): pl.pallas_call(functools.partial(extract_kernel, groups, table.shape[1],...  5.89 us
    pallas_call x1, Pallas kernels, local(): pl.pallas_call(functools.partial(spread_kernel, spread_groups, spread_tab...  5.73 us
    ppermute x1, starting transfers between devices, local(): above = lax.ppermute(plane, 'gz', [(i, i - 1) for i in range(1, n_gz)])  3.46 us
    pallas_call x2, Pallas kernels, particles(): pl.pallas_call(functools.partial(particle_kernel, width, mine, n_gz, n_do...  3.2 us
    pallas_call x1, Pallas kernels, local(): pl.pallas_call(functools.partial(weight_kernel, spread_groups, spread_tab...  2.14 us
    pallas_call x1, Pallas kernels, local(): pl.pallas_call(functools.partial(pack_kernel, planes), out_shape=[jax.Sha...  1.74 us
  transfers between devices with their start and end apart: 11, of which 1 were waited for; matrix products, arithmetic and copies ran while one was open for 0% of the time, Pallas kernels for 21%

profile of v15, /device:TPU:4, one launch (start us, length us, event | category | flops | bytes accessed | tf_op | source)
XLA Modules:
  0.0 46.0 jit_solution(4680392608005341926)
XLA Ops:
  0.6 1.7 %pack.1 = (bf16[16,1664]{1,0:T(8,128)(2,1)}, f32[1,4,384]{2,1,0:T(4,128)}, f32[32,4,384]{2,1,0:T(4,128)}) custom-call(bf16[16,4,384]{2,1,0:T(4,128)(2,1)} %observed_hbm.1, s32[1,16]{1,0:T(1,128)} %bitcast.7, s32[1,16]{1,0:T(1,128)} %bitcast.8, f32[192,4,384]{2,1,0:T(4,128)} %volume.1), custom_call_target="tpu_custom_call" | custom-call | tf_op jit(solution)/shard_map/pack/pallas_call | solution.py:517
  2.4 3.7 %collective-permute-start.2 = (bf16[16,1664]{1,0:T(8,128)(2,1)}, bf16[16,1664]{1,0:T(8,128)(2,1)S(1)}, u32[]{:S(2)}, u32[]{:S(2)}) collective-permute-start(bf16[16,1664]{1,0:T(8,128)(2,1)} %get-tuple-element.27), channel_id=1, source_target_pairs={{0,6},{1,7},{2,4},{3,5},{4,2},{5,3},{6,0},{7,1},{8,14},{9,15},{10,... | collective-permute-start | bytes 159752 | tf_op jit(solution)/shard_map/ppermute | solution.py:496
  6.0 0.0 collective-permute-start.1
  6.0 0.8 %collective-permute-start = (bf16[16,1664]{1,0:T(8,128)(2,1)}, bf16[16,1664]{1,0:T(8,128)(2,1)S(1)}, u32[]{:S(2)}, u32[]{:S(2)}) collective-permute-start(bf16[16,1664]{1,0:T(8,128)(2,1)} %get-tuple-element.27), channel_id=1, source_target_pairs={{0,2},{1,3},{2,0},{3,1},{4,6},{5,7},{6,4},{7,5},{8,10},{9,11},{10,... | collective-permute-start | bytes 159752 | tf_op jit(solution)/shard_map/ppermute | solution.py:496
  6.8 0.0 copy-start.1
  6.8 0.0 copy-start.2
  6.8 0.0 copy-start.3
  6.8 3.5 %collective-permute-start.6 = (f32[1,4,384]{2,1,0:T(4,128)}, f32[1,4,384]{2,1,0:T(4,128)S(1)}, u32[]{:S(2)}, u32[]{:S(2)}) collective-permute-start(f32[1,4,384]{2,1,0:T(4,128)} %get-tuple-element.35), channel_id=1, source_target_pairs={{8,0},{16,8},{24,16},{9,1},{17,9},{25,17},{10,2},{18,10},{26,18},{... | collective-permute-start | bytes 18440 | tf_op jit(solution)/shard_map/ppermute | solution.py:537
  10.3 0.0 copy-start.4
  10.3 0.7 %copy-done.4 = f32[3232]{0:T(1024)S(1)} copy-done((f32[3232]{0:T(1024)S(1)}, f32[3232]{0:T(1024)}, u32[]{:S(2)}) %copy-start.4) | copy-done | bytes 12952
  11.0 0.0 copy-start.6
  11.0 0.0 copy-start.5
  11.0 2.1 %weights.1 = (bf16[7,2048,128]{2,1,0:T(8,128)(2,1)S(1)}, bf16[32,96,128]{2,1,0:T(8,128)(2,1)S(1)}) custom-call(f32[3232]{0:T(1024)S(1)} %copy-done.4), custom_call_target="tpu_custom_call" | custom-call | flops 3000000000 | bytes 2097152 | tf_op jit(solution)/shard_map/weights/pallas_call | solution.py:543
  13.2 0.0 collective-permute-done.2
  13.2 0.0 collective-permute-done.1
  13.2 0.0 collective-permute-done
  13.2 0.0 copy-done.6
  13.2 0.1 collective-permute-start.5
  13.3 1.5 %collective-permute-start.4 = (bf16[64,1664]{1,0:T(8,128)(2,1)S(1)}, bf16[64,1664]{1,0:T(8,128)(2,1)S(1)}, u32[]{:S(2)}, u32[]{:S(2)}) collective-permute-start(bf16[64,1664]{1,0:T(8,128)(2,1)S(1)} %pad_maximum_fusion.refs_0_), channel_id=1, source_target_pairs={{0,16},{8,24},{16,0},{24,8},{1,17},{9,25},{17,1},{25,9},{2,18},{10... | collective-permute-start | bytes 638984 | tf_op jit(solution)/shard_map/ppermute | solution.py:496
  14.8 2.0 %collective-permute-start.3 = (bf16[64,1664]{1,0:T(8,128)(2,1)S(1)}, bf16[64,1664]{1,0:T(8,128)(2,1)S(1)}, u32[]{:S(2)}, u32[]{:S(2)}) collective-permute-start(bf16[64,1664]{1,0:T(8,128)(2,1)S(1)} %pad_maximum_fusion.refs_0_), channel_id=1, source_target_pairs={{0,8},{8,0},{16,24},{24,16},{1,9},{9,1},{17,25},{25,17},{2,10},{10... | collective-permute-start | bytes 638984 | tf_op jit(solution)/shard_map/ppermute | solution.py:496
  16.8 0.0 collective-permute-done.6.above
  16.8 0.0 copy-done.1
  16.8 0.0 copy-done.2
  16.8 0.0 copy-done.3
  16.8 0.0 copy-done.5
  16.8 5.9 %extract.1 = (bf16[128,1536]{1,0:T(8,128)(2,1)S(1)}, bf16[32,384]{1,0:T(8,128)(2,1)S(1)}, f32[32,768]{1,0:T(8,128)S(1)}) custom-call(s32[2080]{0:T(1024)S(1)} %copy-done.5, f32[128]{0:T(128)S(1)} %copy-done.1, f32[32,4,384]{2,1,0:T(4,128)S(1)} %copy-done.2, f32[1,4,384]{2,1,0:T(4,128)S(1)} %collective-permute-done.6.above, f32[32,2,384]{2,1,0:T(2,128)S(1)} %copy-done.3), custom_call_target="tpu_custom_call" | custom-call | flops 6000000000 | bytes 1048576 | tf_op jit(solution)/shard_map/extract/pallas_call | solution.py:562
  22.7 0.0 collective-permute-done.5.refs_3_
  22.7 0.8 %collective-permute-done.4.refs_2_ = bf16[64,1664]{1,0:T(8,128)(2,1)S(1)} collective-permute-done((bf16[64,1664]{1,0:T(8,128)(2,1)S(1)}, bf16[64,1664]{1,0:T(8,128)(2,1)S(1)}, u32[]{:S(2)}, u32[]{:S(2)}) %collective-permute-start.4) | collective-permute-done | bytes 213024 | tf_op jit(solution)/shard_map/ppermute | solution.py:496
  23.6 0.0 collective-permute-done.3.refs_1_
  23.6 0.0 collective-permute-start.7
  23.6 0.5 %collective-permute-start.8 = (bf16[64,1664]{1,0:T(8,128)(2,1)S(1)}, bf16[64,1664]{1,0:T(8,128)(2,1)S(1)}, u32[]{:S(2)}, u32[]{:S(2)}) collective-permute-start(bf16[64,1664]{1,0:T(8,128)(2,1)S(1)} %collective-permute-done.3.refs_1_), channel_id=1, source_target_pairs={{0,1},{1,0},{2,3},{3,2},{4,5},{5,4},{6,7},{7,6},{8,9},{9,8},{10,11... | collective-permute-start | bytes 638984 | tf_op jit(solution)/shard_map/ppermute | solution.py:496
  24.1 0.0 collective-permute-start.9
  24.1 0.5 %collective-permute-start.10 = (bf16[64,1664]{1,0:T(8,128)(2,1)S(1)}, bf16[64,1664]{1,0:T(8,128)(2,1)S(1)}, u32[]{:S(2)}, u32[]{:S(2)}) collective-permute-start(bf16[64,1664]{1,0:T(8,128)(2,1)S(1)} %collective-permute-done.5.refs_3_), channel_id=1, source_target_pairs={{0,1},{1,0},{2,3},{3,2},{4,5},{5,4},{6,7},{7,6},{8,9},{9,8},{10,11... | collective-permute-start | bytes 638984 | tf_op jit(solution)/shard_map/ppermute | solution.py:496
  24.6 1.5 %particles.2 = (bf16[256,1536]{1,0:T(8,128)(2,1)S(1)}, f32[1,256]{1,0:T(1,128)S(1)}, f32[4,128]{1,0:T(4,128)S(1)}) custom-call(bf16[64,1664]{1,0:T(8,128)(2,1)S(1)} %pad_maximum_fusion.refs_0_, bf16[64,1664]{1,0:T(8,128)(2,1)S(1)} %collective-permute-done.3.refs_1_, bf16[64,1664]{1,0:T(8,128)(2,1)S(1)} %collective-permute-done.4.refs_2_, ...), custom_call_target="tpu_custom_call" | custom-call | flops 2000000000 | bytes 1048576 | tf_op jit(solution)/shard_map/particles/pallas_call | solution.py:593
  26.1 0.0 collective-permute-done.7.refs_0_
  26.1 0.0 collective-permute-done.8.refs_1_
  26.1 0.0 collective-permute-done.9.refs_2_
  26.1 0.0 collective-permute-done.10.refs_3_
  26.1 0.0 copy-start
  26.1 1.7 %particles.3 = (bf16[256,1536]{1,0:T(8,128)(2,1)S(1)}, f32[1,256]{1,0:T(1,128)S(1)}, f32[256,128]{1,0:T(8,128)S(1)}) custom-call(bf16[64,1664]{1,0:T(8,128)(2,1)S(1)} %collective-permute-done.7.refs_0_, bf16[64,1664]{1,0:T(8,128)(2,1)S(1)} %collective-permute-done.8.refs_1_, bf16[64,1664]{1,0:T(8,128)(2,1)S(1)} %collective-permute-done.9.refs_2_, ...), custom_call_target="tpu_custom_call" | custom-call | flops 2000000000 | bytes 1048576 | tf_op jit(solution)/shard_map/particles/pallas_call | solution.py:593
  27.9 12.4 %all_to_all.11 = f32[32,8,128]{2,1,0:T(8,128)S(1)} all-to-all(f32[32,8,128]{2,1,0:T(8,128)S(1)} %bitcast.6), channel_id=1, replica_groups=mesh['gz'=4,'dom'=8] {'gz','dom'}, dimensions={0} | all-to-all | bytes 262144 | tf_op jit(solution)/shard_map/all_to_all | solution.py:614
  40.3 0.0 copy-done
  40.3 5.7 %spread.1 = (f32[1,16]{1,0:T(1,128)}, f32[24,4,384]{2,1,0:T(4,128)}) custom-call(s32[3104]{0:T(1024)S(1)} %copy-done, f32[128]{0:T(128)S(1)} %copy-done.1, bf16[7,2048,128]{2,1,0:T(8,128)(2,1)S(1)} %get-tuple-element.31.right, bf16[32,96,128]{2,1,0:T(8,128)(2,1)S(1)} %get-tuple-element.32.edges, f32[256,128]{1,0:T(8,128)S(1)} %bitcast.5, ...), custom_call_target="tpu_custom_call" | custom-call | tf_op jit(solution)/shard_map/spread/pallas_call | solution.py:617
  (1 shorter events, 0.0 us)
Async XLA Ops:
  2.4 10.8 %collective-permute-start.2 = (bf16[16,1664]{1,0:T(8,128)(2,1)}, bf16[16,1664]{1,0:T(8,128)(2,1)S(1)}, u32[]{:S(2)}, u32[]{:S(2)}) collective-permute-start(bf16[16,1664]{1,0:T(8,128)(2,1)} %get-tuple-element.27), channel_id=1, source_target_pairs={{0,6},{1,7},{2,4},{3,5},{4,2},{5,3},{6,0},{7,1},{8,14},{9,15},{10,... | collective-permute-start | bytes 159752 | tf_op jit(solution)/shard_map/ppermute | solution.py:496
  6.0 7.2 %collective-permute-start.1 = (bf16[16,1664]{1,0:T(8,128)(2,1)}, bf16[16,1664]{1,0:T(8,128)(2,1)S(1)}, u32[]{:S(2)}, u32[]{:S(2)}) collective-permute-start(bf16[16,1664]{1,0:T(8,128)(2,1)} %get-tuple-element.27), channel_id=1, source_target_pairs={{0,4},{1,5},{2,6},{3,7},{4,0},{5,1},{6,2},{7,3},{8,12},{9,13},{10,... | collective-permute-start | bytes 159752 | tf_op jit(solution)/shard_map/ppermute | solution.py:496
  6.0 7.2 %collective-permute-start = (bf16[16,1664]{1,0:T(8,128)(2,1)}, bf16[16,1664]{1,0:T(8,128)(2,1)S(1)}, u32[]{:S(2)}, u32[]{:S(2)}) collective-permute-start(bf16[16,1664]{1,0:T(8,128)(2,1)} %get-tuple-element.27), channel_id=1, source_target_pairs={{0,2},{1,3},{2,0},{3,1},{4,6},{5,7},{6,4},{7,5},{8,10},{9,11},{10,... | collective-permute-start | bytes 159752 | tf_op jit(solution)/shard_map/ppermute | solution.py:496
  6.8 10.0 %copy-start.1 = (f32[128]{0:T(128)S(1)}, f32[128]{0:T(128)}, u32[]{:S(2)}) copy-start(f32[128]{0:T(128)} %constant.6.clone.trig_hbm.trig) | copy-start | bytes 1540
  6.8 10.0 %copy-start.2 = (f32[32,4,384]{2,1,0:T(4,128)S(1)}, f32[32,4,384]{2,1,0:T(4,128)}, u32[]{:S(2)}) copy-start(f32[32,4,384]{2,1,0:T(4,128)} %get-tuple-element.34.field) | copy-start | bytes 589828
  6.8 10.0 %copy-start.3 = (f32[32,2,384]{2,1,0:T(2,128)S(1)}, f32[32,2,384]{2,1,0:T(2,128)}, u32[]{:S(2)}) copy-start(f32[32,2,384]{2,1,0:T(2,128)} %ctf_hbm.1) | copy-start | bytes 294916
  6.8 10.0 %collective-permute-start.6 = (f32[1,4,384]{2,1,0:T(4,128)}, f32[1,4,384]{2,1,0:T(4,128)S(1)}, u32[]{:S(2)}, u32[]{:S(2)}) collective-permute-start(f32[1,4,384]{2,1,0:T(4,128)} %get-tuple-element.35), channel_id=1, source_target_pairs={{8,0},{16,8},{24,16},{9,1},{17,9},{25,17},{10,2},{18,10},{26,18},{... | collective-permute-start | bytes 18440 | tf_op jit(solution)/shard_map/ppermute | solution.py:537
  10.3 0.7 %copy-start.4 = (f32[3232]{0:T(1024)S(1)}, f32[3232]{0:T(1024)}, u32[]{:S(2)}) copy-start(f32[3232]{0:T(1024)} %constant.13.trig) | copy-start | bytes 38788
  11.0 2.2 %copy-start.6 = (bf16[16,1664]{1,0:T(8,128)(2,1)S(1)}, bf16[16,1664]{1,0:T(8,128)(2,1)}, u32[]{:S(2)}) copy-start(bf16[16,1664]{1,0:T(8,128)(2,1)} %get-tuple-element.27) | copy-start | bytes 159748
  11.0 5.8 %copy-start.5 = (s32[2080]{0:T(1024)S(1)}, s32[2080]{0:T(1024)}, u32[]{:S(2)}) copy-start(s32[2080]{0:T(1024)} %constant.8.clone.table_hbm) | copy-start | bytes 24964
  13.2 9.5 %collective-permute-start.5 = (bf16[64,1664]{1,0:T(8,128)(2,1)S(1)}, bf16[64,1664]{1,0:T(8,128)(2,1)S(1)}, u32[]{:S(2)}, u32[]{:S(2)}) collective-permute-start(bf16[64,1664]{1,0:T(8,128)(2,1)S(1)} %pad_maximum_fusion.refs_0_), channel_id=1, source_target_pairs={{0,24},{8,16},{16,8},{24,0},{1,25},{9,17},{17,9},{25,1},{2,26},{10... | collective-permute-start | bytes 638984 | tf_op jit(solution)/shard_map/ppermute | solution.py:496
  13.3 10.2 %collective-permute-start.4 = (bf16[64,1664]{1,0:T(8,128)(2,1)S(1)}, bf16[64,1664]{1,0:T(8,128)(2,1)S(1)}, u32[]{:S(2)}, u32[]{:S(2)}) collective-permute-start(bf16[64,1664]{1,0:T(8,128)(2,1)S(1)} %pad_maximum_fusion.refs_0_), channel_id=1, source_target_pairs={{0,16},{8,24},{16,0},{24,8},{1,17},{9,25},{17,1},{25,9},{2,18},{10... | collective-permute-start | bytes 638984 | tf_op jit(solution)/shard_map/ppermute | solution.py:496
  14.8 8.8 %collective-permute-start.3 = (bf16[64,1664]{1,0:T(8,128)(2,1)S(1)}, bf16[64,1664]{1,0:T(8,128)(2,1)S(1)}, u32[]{:S(2)}, u32[]{:S(2)}) collective-permute-start(bf16[64,1664]{1,0:T(8,128)(2,1)S(1)} %pad_maximum_fusion.refs_0_), channel_id=1, source_target_pairs={{0,8},{8,0},{16,24},{24,16},{1,9},{9,1},{17,25},{25,17},{2,10},{10... | collective-permute-start | bytes 638984 | tf_op jit(solution)/shard_map/ppermute | solution.py:496
  23.6 2.5 %collective-permute-start.7 = (bf16[64,1664]{1,0:T(8,128)(2,1)S(1)}, bf16[64,1664]{1,0:T(8,128)(2,1)S(1)}, u32[]{:S(2)}, u32[]{:S(2)}) collective-permute-start(bf16[64,1664]{1,0:T(8,128)(2,1)S(1)} %pad_maximum_fusion.refs_0_), channel_id=1, source_target_pairs={{0,1},{1,0},{2,3},{3,2},{4,5},{5,4},{6,7},{7,6},{8,9},{9,8},{10,11... | collective-permute-start | bytes 638984 | tf_op jit(solution)/shard_map/ppermute | solution.py:496
  23.6 2.5 %collective-permute-start.8 = (bf16[64,1664]{1,0:T(8,128)(2,1)S(1)}, bf16[64,1664]{1,0:T(8,128)(2,1)S(1)}, u32[]{:S(2)}, u32[]{:S(2)}) collective-permute-start(bf16[64,1664]{1,0:T(8,128)(2,1)S(1)} %collective-permute-done.3.refs_1_), channel_id=1, source_target_pairs={{0,1},{1,0},{2,3},{3,2},{4,5},{5,4},{6,7},{7,6},{8,9},{9,8},{10,11... | collective-permute-start | bytes 638984 | tf_op jit(solution)/shard_map/ppermute | solution.py:496
  24.1 2.0 %collective-permute-start.9 = (bf16[64,1664]{1,0:T(8,128)(2,1)S(1)}, bf16[64,1664]{1,0:T(8,128)(2,1)S(1)}, u32[]{:S(2)}, u32[]{:S(2)}) collective-permute-start(bf16[64,1664]{1,0:T(8,128)(2,1)S(1)} %collective-permute-done.4.refs_2_), channel_id=1, source_target_pairs={{0,1},{1,0},{2,3},{3,2},{4,5},{5,4},{6,7},{7,6},{8,9},{9,8},{10,11... | collective-permute-start | bytes 638984 | tf_op jit(solution)/shard_map/ppermute | solution.py:496
  24.1 2.0 %collective-permute-start.10 = (bf16[64,1664]{1,0:T(8,128)(2,1)S(1)}, bf16[64,1664]{1,0:T(8,128)(2,1)S(1)}, u32[]{:S(2)}, u32[]{:S(2)}) collective-permute-start(bf16[64,1664]{1,0:T(8,128)(2,1)S(1)} %collective-permute-done.5.refs_3_), channel_id=1, source_target_pairs={{0,1},{1,0},{2,3},{3,2},{4,5},{5,4},{6,7},{7,6},{8,9},{9,8},{10,11... | collective-permute-start | bytes 638984 | tf_op jit(solution)/shard_map/ppermute | solution.py:496
  26.1 14.1 %copy-start = (s32[3104]{0:T(1024)S(1)}, s32[3104]{0:T(1024)}, u32[]{:S(2)}) copy-start(s32[3104]{0:T(1024)} %constant.7.clone.table) | copy-start | bytes 37252
